TPU v7x, 128 devices: a whole 4x4x4 slice. The times are simulated.
128 devices in a mesh: query: 4 (over y_lo, core), corpus: 32 (over z, y_hi, x).
Axes of the slice: x: 4, y: 4 (y_hi: 2, y_lo: 2; y = y_hi * 2 + y_lo), z: 4, core: 2. Of those that a mesh axis runs over, the one named last changes fastest.
Arguments:
- queries: bfloat16 [1024, 32, 128], P('corpus', 'query'), may hold values from -6 to 6
- passages: bfloat16 [1024, 128, 128], P(('query', 'corpus')), may hold values from -0.5 to 0.5
- lengths: int32 [1024], P(('query', 'corpus')), may hold values from 8 to 128, as said below
Outputs:
- scores: float32 [1024, 1024], P('corpus', 'query')
Inputs may be any that keep to these rules, and one draw needn't show every extreme that they name: `lengths`: every length is a multiple of 8; some passage uses all 128 slots.
All inputs are finite; a program needn't handle non-finite values.
Results may differ from a plain program's by a relative error of at most 0.0003.
Values may be sent and summed in bfloat16 or wider, within the bound.
No kernel may reach another device: no remote copies, remote signals or barrier semaphores. Data moves between devices by JAX's collectives and lax.ppermute only.
A program may use at most 64 MiB of HBM per device.

v0:
```python
import jax
import jax.numpy as jnp
from jax import lax
from jax.sharding import PartitionSpec as P

masked_value = -1e30


def block_scores(flat_rows, piece, piece_lengths, query_len):
    count = piece.shape[0]
    slots = piece.shape[1]
    width = piece.shape[2]
    row_count = flat_rows.shape[0]
    dots = lax.dot_general(
        flat_rows,
        piece.reshape(count * slots, width),
        (((1,), (1,)), ((), ())),
        preferred_element_type=jnp.float32,
    )
    dots = dots.reshape(row_count, count, slots)
    usable = lax.broadcasted_iota(jnp.int32, (count, slots), 1) < piece_lengths[:, None]
    top_dot = jnp.max(jnp.where(usable[None], dots, masked_value), axis=2)
    return jnp.mean(top_dot.reshape(row_count // query_len, query_len, count), axis=1)


def grouped_scores(flat_rows, piece, piece_lengths, query_len):
    count = piece.shape[0]
    slots = piece.shape[1]
    width = piece.shape[2]
    limit = min(16, max(1, (1 << 22) // (flat_rows.shape[0] * slots)))
    group_size = 1
    while group_size * 2 <= limit and count % (group_size * 2) == 0:
        group_size = group_size * 2
    steps_count = count // group_size

    def one_group(pieces):
        return block_scores(flat_rows, pieces[0], pieces[1], query_len)

    blocks = lax.map(
        one_group,
        (
            piece.reshape(steps_count, group_size, slots, width),
            piece_lengths.reshape(steps_count, group_size),
        ),
    )
    return jnp.transpose(blocks, (1, 0, 2)).reshape(flat_rows.shape[0] // query_len, count)


def per_device(queries, passages, lengths):
    width = queries.shape[2]
    gathered = lax.all_gather(queries, "query", axis=1, tiled=True)
    query_len = gathered.shape[1]
    piece = lax.all_gather(gathered, "corpus", axis=0, tiled=True)
    flat_piece = piece.reshape(piece.shape[0] * query_len, width)
    terms = grouped_scores(flat_piece, passages, lengths, query_len)
    return lax.all_to_all(terms, "corpus", split_axis=0, concat_axis=1, tiled=True)


def solution(mesh):
    placed = (
        P("corpus", "query", None),
        P(("query", "corpus"), None, None),
        P(("query", "corpus")),
    )
    return jax.shard_map(
        per_device, mesh=mesh, in_specs=placed, out_specs=P("corpus", "query"), check_vma=False
    )
```

profile of v0, /device:TPU:0, one launch (start us, length us, event | category | flops | bytes accessed | tf_op | source)
XLA Modules:
  0.0 209.1 jit_solution(7045147887331968042)
XLA Ops:
  6.5 0.0 all-gather.2.cloned.1.call-start
  6.5 7.6 %all_gather.6 = bf16[32,32,128]{2,1,0:T(8,128)(2,1)} all-gather(bf16[32,8,128]{2,1,0:T(8,128)(2,1)} %param.5), channel_id=1, replica_groups=mesh['query'=4,'corpus'=32] {'query'}, dimensions={1}, use_global_device_ids=true | all-gather | bytes 327680 | tf_op jit(solution)/shard_map/all_gather | solution.py:51
  14.1 0.0 all-gather.2.cloned.1.call-update
  14.1 106.5 %all-gather.2.cloned.1.call-done = bf16[1024,32,128]{2,1,0:T(8,128)(2,1)} async-done(((bf16[32,32,128]{2,1,0:T(8,128)(2,1)}), bf16[1024,32,128]{2,1,0:T(8,128)(2,1)}) %all-gather.2.cloned.1.call-update) | async-done | bytes 8388624 | tf_op jit(solution)/shard_map/all_gather | solution.py:53
  120.7 63.9 %while.10 = (s32[]{:T(128)}, f32[8,1024,1]{1,2,0:T(1,128)S(1)}, s32[8,1]{0,1:T(1,128)}, bf16[8,1,128,128]{3,2,1,0:T(8,128)(2,1)}, bf16[32768,128]{1,0:T(8,128)(2,1)}, /*index=5*/s32[]{:T(128)}, f32[]{:T(128)}) while((s32[]{:T(128)}, f32[8,1024,1]{1,2,0:T(1,128)S(1)}, s32[8,1]{0,1:T(1,128)}, bf16[8,1,128,128]{3,2,1,0:T(8,128)(2,1)}, ...), condition=%wide.region_3.4_spmd, body=%wide.region_0.3_spmd.sunk | while | flops 1082130560 | bytes 8967013 | solution.py:39
  120.7 1.2 constant_dynamic-slice_fusion.2
  121.9 0.6 iota_compare_fusion.2
  122.4 5.8 %fusion.10 = f32[32768]{0:T(1024)S(1)} fusion(bf16[32768,128]{1,0:T(8,128)(2,1)} %get-tuple-element.92, pred[128]{0:T(512)(128)(4,1)S(1)} %iota_compare_fusion.2, bf16[8,1,128,128]{3,2,1,0:T(8,128)(2,1)} %get-tuple-element.91, s32[]{:T(128)} %get-tuple-element.81), kind=kOutput, calls=%fused_computation.1.clone.1 | convolution fusion | flops 1082097664 | bytes 8553088 | tf_op jit(solution)/shard_map/while/body/eval_jaxpr/dot_general | solution.py:14
  128.2 0.2 reshape.55
  128.4 0.2 reduce_sum.10
  128.6 1.2 constant_dynamic-slice_fusion.2
  129.9 0.6 iota_compare_fusion.2
  130.4 5.8 %fusion.10 = f32[32768]{0:T(1024)S(1)} fusion(bf16[32768,128]{1,0:T(8,128)(2,1)} %get-tuple-element.92, pred[128]{0:T(512)(128)(4,1)S(1)} %iota_compare_fusion.2, bf16[8,1,128,128]{3,2,1,0:T(8,128)(2,1)} %get-tuple-element.91, s32[]{:T(128)} %get-tuple-element.81), kind=kOutput, calls=%fused_computation.1.clone.1 | convolution fusion | flops 1082097664 | bytes 8553088 | tf_op jit(solution)/shard_map/while/body/eval_jaxpr/dot_general | solution.py:14
  136.2 0.2 reshape.55
  136.4 0.2 reduce_sum.10
  136.6 1.2 constant_dynamic-slice_fusion.2
  137.9 0.6 iota_compare_fusion.2
  138.4 5.8 %fusion.10 = f32[32768]{0:T(1024)S(1)} fusion(bf16[32768,128]{1,0:T(8,128)(2,1)} %get-tuple-element.92, pred[128]{0:T(512)(128)(4,1)S(1)} %iota_compare_fusion.2, bf16[8,1,128,128]{3,2,1,0:T(8,128)(2,1)} %get-tuple-element.91, s32[]{:T(128)} %get-tuple-element.81), kind=kOutput, calls=%fused_computation.1.clone.1 | convolution fusion | flops 1082097664 | bytes 8553088 | tf_op jit(solution)/shard_map/while/body/eval_jaxpr/dot_general | solution.py:14
  144.2 0.2 reshape.55
  144.4 0.2 reduce_sum.10
  144.6 1.2 constant_dynamic-slice_fusion.2
  145.8 0.6 iota_compare_fusion.2
  146.4 5.8 %fusion.10 = f32[32768]{0:T(1024)S(1)} fusion(bf16[32768,128]{1,0:T(8,128)(2,1)} %get-tuple-element.92, pred[128]{0:T(512)(128)(4,1)S(1)} %iota_compare_fusion.2, bf16[8,1,128,128]{3,2,1,0:T(8,128)(2,1)} %get-tuple-element.91, s32[]{:T(128)} %get-tuple-element.81), kind=kOutput, calls=%fused_computation.1.clone.1 | convolution fusion | flops 1082097664 | bytes 8553088 | tf_op jit(solution)/shard_map/while/body/eval_jaxpr/dot_general | solution.py:14
  152.2 0.2 reshape.55
  152.4 0.2 reduce_sum.10
  152.6 1.2 constant_dynamic-slice_fusion.2
  153.8 0.6 iota_compare_fusion.2
  154.4 5.8 %fusion.10 = f32[32768]{0:T(1024)S(1)} fusion(bf16[32768,128]{1,0:T(8,128)(2,1)} %get-tuple-element.92, pred[128]{0:T(512)(128)(4,1)S(1)} %iota_compare_fusion.2, bf16[8,1,128,128]{3,2,1,0:T(8,128)(2,1)} %get-tuple-element.91, s32[]{:T(128)} %get-tuple-element.81), kind=kOutput, calls=%fused_computation.1.clone.1 | convolution fusion | flops 1082097664 | bytes 8553088 | tf_op jit(solution)/shard_map/while/body/eval_jaxpr/dot_general | solution.py:14
  160.2 0.2 reshape.55
  160.4 0.2 reduce_sum.10
  160.6 1.2 constant_dynamic-slice_fusion.2
  161.8 0.6 iota_compare_fusion.2
  162.4 5.8 %fusion.10 = f32[32768]{0:T(1024)S(1)} fusion(bf16[32768,128]{1,0:T(8,128)(2,1)} %get-tuple-element.92, pred[128]{0:T(512)(128)(4,1)S(1)} %iota_compare_fusion.2, bf16[8,1,128,128]{3,2,1,0:T(8,128)(2,1)} %get-tuple-element.91, s32[]{:T(128)} %get-tuple-element.81), kind=kOutput, calls=%fused_computation.1.clone.1 | convolution fusion | flops 1082097664 | bytes 8553088 | tf_op jit(solution)/shard_map/while/body/eval_jaxpr/dot_general | solution.py:14
  168.2 0.2 reshape.55
  168.4 0.2 reduce_sum.10
  168.6 1.2 constant_dynamic-slice_fusion.2
  169.8 0.6 iota_compare_fusion.2
  170.4 5.8 %fusion.10 = f32[32768]{0:T(1024)S(1)} fusion(bf16[32768,128]{1,0:T(8,128)(2,1)} %get-tuple-element.92, pred[128]{0:T(512)(128)(4,1)S(1)} %iota_compare_fusion.2, bf16[8,1,128,128]{3,2,1,0:T(8,128)(2,1)} %get-tuple-element.91, s32[]{:T(128)} %get-tuple-element.81), kind=kOutput, calls=%fused_computation.1.clone.1 | convolution fusion | flops 1082097664 | bytes 8553088 | tf_op jit(solution)/shard_map/while/body/eval_jaxpr/dot_general | solution.py:14
  176.2 0.2 reshape.55
  176.4 0.2 reduce_sum.10
  176.6 1.2 constant_dynamic-slice_fusion.2
  177.8 0.6 iota_compare_fusion.2
  178.4 5.8 %fusion.10 = f32[32768]{0:T(1024)S(1)} fusion(bf16[32768,128]{1,0:T(8,128)(2,1)} %get-tuple-element.92, pred[128]{0:T(512)(128)(4,1)S(1)} %iota_compare_fusion.2, bf16[8,1,128,128]{3,2,1,0:T(8,128)(2,1)} %get-tuple-element.91, s32[]{:T(128)} %get-tuple-element.81), kind=kOutput, calls=%fused_computation.1.clone.1 | convolution fusion | flops 1082097664 | bytes 8553088 | tf_op jit(solution)/shard_map/while/body/eval_jaxpr/dot_general | solution.py:14
  184.2 0.2 reshape.55
  184.4 0.2 reduce_sum.10
  184.6 0.1 bitcast_reduce_fusion
  184.7 0.1 all_to_all.14
  184.8 0.1 copy.10
  184.9 0.1 reshape.52
  185.0 15.2 %all_to_all.19 = f32[32,1,256]{2,1,0:T(1,128)S(1)} all-to-all(f32[32,1,256]{2,1,0:T(1,128)S(1)} %reshape.52), channel_id=1, replica_groups=mesh['query'=4,'corpus'=32] {'corpus'}, dimensions={0} | all-to-all | bytes 65536 | tf_op jit(solution)/shard_map/all_to_all | solution.py:56
  200.2 0.5 broadcast.30
  200.7 0.7 reduce.6
  201.5 0.1 reshape.53
  201.6 0.7 copy.8
  (18 shorter events, 0.1 us)
Async XLA Ops:
  6.5 114.1 %all-gather.2.cloned.1.call-start = ((), (), s32[]{:S(2)}) async-start(), calls=%async_computation.1 | async-start | bytes 8650752 | tf_op jit(solution)/shard_map/all_gather | solution.py:53
Sparse Core Ops, SparseCore 0:
  14.2 106.3 all-gather.1
where the time goes:
time: 210 us; the launch traced here: 209 us
  waiting for transfers between devices  107 us (51%)
  matrix products  46.1 us (22%)
  blocking collectives  22.8 us (11%)
  between operations  13.4 us (6%)
  local copies, waits for them, and re-layouts  12.8 us (6%)
  other arithmetic  6.95 us (3%)
    all_gather x1, waiting for transfers between devices, per_device(): piece = lax.all_gather(gathered, 'corpus', axis=0, tiled=True)  107 us
    dot_general x8, matrix products, block_scores(): lax.dot_general(flat_rows, piece.reshape(count * slots, width), (((1,), (...  46.1 us
    all_to_all x1, blocking collectives, per_device(): lax.all_to_all(terms, 'corpus', split_axis=0, concat_axis=1, tiled=True)  15.2 us
    dynamic_slice x8, local copies, waits for them, and re-layouts, grouped_scores(): lax.map(one_group, (piece.reshape(steps_count, group_size, slots, width),...  9.7 us
    all_gather x1, blocking collectives, per_device(): gathered = lax.all_gather(queries, 'query', axis=1, tiled=True)  7.55 us
    lt x8, other arithmetic, block_scores(): lax.broadcasted_iota(jnp.int32, (count, slots), 1) < piece_lengths[:, None]  4.57 us
  transfers between devices with their start and end apart: 1, of which 1 were waited for; matrix products, arithmetic and copies ran while one was open for 0% of the time, Pallas kernels for 0%

commit v1 on v0

v1 whole, which is shorter than its diff:
```python
import functools

import jax
import jax.numpy as jnp
from jax import lax
from jax.experimental import pallas as pl
from jax.experimental.pallas import tpu as pltpu
from jax.sharding import Mesh
from jax.sharding import PartitionSpec as P

NAMES = ("ylo", "core", "z", "yhi", "x")
SIZES = (2, 2, 4, 2, 4)
PLANE = ("ylo", "core", "z", "yhi")
SHIFTS = (0, 1, -1, 2)


def plane_pairs(move):
    def index(ylo, core, z, yhi):
        return ((ylo * 2 + core) * 4 + z) * 2 + yhi

    pairs = []
    for ylo in range(2):
        for core in range(2):
            for z in range(4):
                for yhi in range(2):
                    y2, core2, z2 = move(2 * yhi + ylo, core, z)
                    y2, z2 = y2 % 4, z2 % 4
                    pairs.append((index(ylo, core, z, yhi), index(y2 % 2, core2, z2, y2 // 2)))
    return pairs


def along(first, shift):
    def move(y, core, z):
        if (core == 0) == first:
            return y + shift, core, z
        return y, core, z + shift

    return plane_pairs(move)


def to_core(v):
    return lax.ppermute(v, "core", [(0, 1), (1, 0)])


def on_x(v, shift):
    return lax.ppermute(v, "x", [(i, (i + shift) % 4) for i in range(4)])


def fill_kernel(len_ref, p_ref, o_ref):
    slot = lax.broadcasted_iota(jnp.int32, p_ref.shape[1:], 0)
    for i in range(p_ref.shape[0]):
        v = p_ref[i].astype(jnp.float32)
        o_ref[i] = jnp.where(slot < len_ref[i], v, v[0:1]).astype(o_ref.dtype)


def fill(passages, lengths):
    return pl.pallas_call(
        fill_kernel,
        out_shape=jax.ShapeDtypeStruct(passages.shape, passages.dtype),
        in_specs=[pl.BlockSpec(memory_space=pltpu.SMEM), pl.BlockSpec(memory_space=pltpu.VMEM)],
        out_specs=pl.BlockSpec(memory_space=pltpu.VMEM),
    )(lengths, passages)


def dot_nt(a, b, precision=None):
    return lax.dot_general(
        a, b, (((1,), (1,)), ((), ())), preferred_element_type=jnp.float32, precision=precision
    )


def score_kernel(info_ref, *refs):
    rows, pieces, out_ref, acc_ref = refs[:8], refs[8:12], refs[12], refs[13]
    z, y, core, x = info_ref[0], info_ref[1], info_ref[2], info_ref[3]
    acc_ref[...] = jnp.zeros_like(acc_ref)
    for a in range(8):
        kind = core if a < 4 else 1 - core
        far = SHIFTS[a % 4]
        w = rows[a][...].reshape(1024, 128)
        places = []
        for j in range(4):
            near = SHIFTS[j]
            y_from = lax.rem(y + 4 - jnp.where(kind == 0, near, far), 4)
            z_from = lax.rem(z + 4 - jnp.where(kind == 0, far, near), 4)
            places.append(z_from * 2 + y_from // 2)
        for m in range(4):
            p_ref = pieces[m]
            g = pl.multiple_of(8 * lax.rem(x + 4 - SHIFTS[m], 4), 8)
            tops = []
            for i in range(8):
                d = dot_nt(p_ref[i], w)
                tops.append(jnp.max(d.reshape(16, 8, 1024), axis=0)[None])
            top = jnp.max(jnp.concatenate(tops, axis=0), axis=1)
            for j in range(4):
                acc_ref[places[j], pl.ds(g, 8), :] += top[:, 256 * j : 256 * j + 256]
    lane = lax.broadcasted_iota(jnp.int32, (32, 256), 1)
    row = lax.broadcasted_iota(jnp.int32, (32, 256), 0)
    pick = jnp.where(lane // 8 == row, 1.0 / 32, 0.0).astype(jnp.float32)
    for c in range(8):
        r = dot_nt(pick, acc_ref[c], lax.Precision.HIGHEST)
        out_ref[c] = jnp.concatenate([r[0:8], r[8:16], r[16:24], r[24:32]], axis=1)


def score(info, rows, pieces):
    return pl.pallas_call(
        score_kernel,
        out_shape=jax.ShapeDtypeStruct((8, 8, 128), jnp.float32),
        in_specs=[pl.BlockSpec(memory_space=pltpu.SMEM)]
        + [pl.BlockSpec(memory_space=pltpu.VMEM)] * 12,
        out_specs=pl.BlockSpec(memory_space=pltpu.VMEM),
        scratch_shapes=[pltpu.VMEM((8, 32, 256), jnp.float32)],
        compiler_params=pltpu.CompilerParams(vmem_limit_bytes=48 << 20),
    )(info, *rows, *pieces)


def place_kernel(r_ref, o_ref):
    for g in range(4):
        o_ref[8 * g : 8 * g + 8, :] = jnp.concatenate(
            [r_ref[s][:, 32 * g : 32 * g + 32] for s in range(8)], axis=1
        )


def place(received):
    return pl.pallas_call(
        place_kernel,
        out_shape=jax.ShapeDtypeStruct((32, 256), jnp.float32),
        in_specs=[pl.BlockSpec(memory_space=pltpu.VMEM)],
        out_specs=pl.BlockSpec(memory_space=pltpu.VMEM),
    )(received)


def per_device(queries, passages, lengths):
    own = queries.reshape(256, 128)
    z = lax.axis_index("z")
    y = lax.axis_index("yhi") * 2 + lax.axis_index("ylo")
    core = lax.axis_index("core")
    x = lax.axis_index("x")
    info = jnp.stack([z, y, core, x]).astype(jnp.int32)

    near = [own] + [lax.ppermute(own, PLANE, along(True, k)) for k in SHIFTS[1:]]
    filled = fill(passages, lengths)
    moved = [filled] + [on_x(filled, k) for k in SHIFTS[1:]]
    block = jnp.stack(near)
    mine = [block] + [lax.ppermute(block, PLANE, along(False, k)) for k in SHIFTS[1:]]
    other = [to_core(v) for v in mine]
    terms = score(info, mine + other, moved)
    received = lax.all_to_all(terms, ("z", "yhi"), 0, 0, tiled=True)
    return place(received)


def solution(mesh):
    fine = Mesh(mesh.devices.reshape(SIZES), NAMES)
    corpus = ("z", "yhi", "x")
    query = ("ylo", "core")
    return jax.shard_map(
        per_device,
        mesh=fine,
        in_specs=(P(corpus, query, None), P(query + corpus, None, None), P(query + corpus)),
        out_specs=P(corpus, query),
        check_vma=False,
    )
```

time: 210 us -> 59.6 us (0.28)
  waiting for transfers between devices: 107 us -> 4.83 us
  matrix products: 46.1 us -> 0 us
  Pallas kernels: 0 us -> 22 us
  starting transfers between devices: 0.01 us -> 18.6 us
  between operations: 13.4 us -> 0.05 us
  local copies, waits for them, and re-layouts: 12.8 us -> 0.01 us
  blocking collectives: 22.8 us -> 13.4 us
  other arithmetic: 6.95 us -> 0.11 us
    all_gather x1 -> x0, waiting for transfers between devices: 107 us -> none  [per_device(): piece = lax.all_gather(gathered, 'corpus', axis=0, tiled=True)]
    dot_general x8 -> x0, matrix products: 46.1 us -> none  [block_scores(): lax.dot_general(flat_rows, piece.reshape(count * slots, width), (((1,), (...]
    pallas_call x0 -> x3, Pallas kernels: none -> 22 us  [the longest x1 18.9 us: score(): pl.pallas_call(score_kernel, out_shape=jax.ShapeDtypeStruct((8, 8, 128),...]
    ppermute x0 -> x13, starting transfers between devices: none -> 18.6 us  [the longest x3 6.4 us: on_x(): return lax.ppermute(v, 'x', [(i, (i + shift) % 4) for i in range(4)])]
    dynamic_slice x8 -> x0, local copies, waits for them, and re-layouts: 9.7 us -> none  [grouped_scores(): lax.map(one_group, (piece.reshape(steps_count, group_size, slots, width),...]
    all_gather x1 -> x0, blocking collectives: 7.55 us -> none  [per_device(): gathered = lax.all_gather(queries, 'query', axis=1, tiled=True)]
    ppermute x0 -> x13, waiting for transfers between devices: none -> 4.83 us  [the longest x3 3.96 us: on_x(): return lax.ppermute(v, 'x', [(i, (i + shift) % 4) for i in range(4)])]
    lt x8 -> x0, other arithmetic: 4.57 us -> none  [block_scores(): lax.broadcasted_iota(jnp.int32, (count, slots), 1) < piece_lengths[:, None]]
  transfers between devices with their start and end apart: 1 -> 13, of which waited for: 1 -> 5; matrix products, arithmetic and copies ran while one was open for 0% -> 0% of each run, Pallas kernels for 0% -> 3%
where the time goes in v1:
time: 59.6 us; the launch traced here: 59.1 us
  Pallas kernels  22 us (37%)
  starting transfers between devices  18.6 us (31%)
  blocking collectives  13.4 us (22%)
  waiting for transfers between devices  4.83 us (8%)
    pallas_call x1, Pallas kernels, score(): pl.pallas_call(score_kernel, out_shape=jax.ShapeDtypeStruct((8, 8, 128),...  18.9 us
    all_to_all x1, blocking collectives, per_device(): received = lax.all_to_all(terms, ('z', 'yhi'), 0, 0, tiled=True)  13.4 us
    ppermute x3, starting transfers between devices, on_x(): return lax.ppermute(v, 'x', [(i, (i + shift) % 4) for i in range(4)])  6.4 us
    ppermute x3, starting transfers between devices, per_device(): lax.ppermute(block, PLANE, along(False, k))  5.98 us
    ppermute x3, starting transfers between devices, per_device(): lax.ppermute(own, PLANE, along(True, k))  5.3 us
    ppermute x3, waiting for transfers between devices, on_x(): return lax.ppermute(v, 'x', [(i, (i + shift) % 4) for i in range(4)])  3.96 us
    pallas_call x1, Pallas kernels, fill(): pl.pallas_call(fill_kernel, out_shape=jax.ShapeDtypeStruct(passages.shape...  1.73 us
    pallas_call x1, Pallas kernels, place(): pl.pallas_call(place_kernel, out_shape=jax.ShapeDtypeStruct((32, 256), jn...  1.46 us
  transfers between devices with their start and end apart: 13, of which 5 were waited for; matrix products, arithmetic and copies ran while one was open for 0% of the time, Pallas kernels for 3%

profile of v1, /device:TPU:0, one launch (start us, length us, event | category | flops | bytes accessed | tf_op | source)
XLA Modules:
  0.0 59.1 jit_solution(17626660351820490390)
XLA Ops:
  0.0 0.0 copy-start.1
  0.0 3.3 %collective-permute-start.2 = (bf16[256,128]{1,0:T(8,128)(2,1)}, bf16[256,128]{1,0:T(8,128)(2,1)S(1)}, u32[]{:S(2)}, u32[]{:S(2)}) collective-permute-start(bf16[256,128]{1,0:T(8,128)(2,1)} %bitcast.9), channel_id=1, source_target_pairs={{0,4},{4,0},{8,12},{12,8},{16,20},{20,16},{24,28},{28,24},{32,48},... | collective-permute-start | bytes 196616 | tf_op jit(solution)/shard_map/ppermute | solution.py:139
  3.3 1.1 %collective-permute-start.1 = (bf16[256,128]{1,0:T(8,128)(2,1)}, bf16[256,128]{1,0:T(8,128)(2,1)S(1)}, u32[]{:S(2)}, u32[]{:S(2)}) collective-permute-start(bf16[256,128]{1,0:T(8,128)(2,1)} %bitcast.10), channel_id=1, source_target_pairs={{0,68},{4,64},{8,76},{12,72},{16,84},{20,80},{24,92},{28,88},{32,5... | collective-permute-start | bytes 196616 | tf_op jit(solution)/shard_map/ppermute | solution.py:139
  4.3 1.0 %collective-permute-start = (bf16[256,128]{1,0:T(8,128)(2,1)}, bf16[256,128]{1,0:T(8,128)(2,1)S(1)}, u32[]{:S(2)}, u32[]{:S(2)}) collective-permute-start(bf16[256,128]{1,0:T(8,128)(2,1)} %bitcast.11), channel_id=1, source_target_pairs={{0,64},{4,68},{8,72},{12,76},{16,80},{20,84},{24,88},{28,92},{32,4... | collective-permute-start | bytes 196616 | tf_op jit(solution)/shard_map/ppermute | solution.py:139
  5.3 1.7 %shard_map.37.refs_8_ = bf16[8,128,128]{2,1,0:T(8,128)(2,1)} custom-call(s32[8]{0:T(128)} %len_ref.1, bf16[8,128,128]{2,1,0:T(8,128)(2,1)} %p_ref.1), custom_call_target="tpu_custom_call" | custom-call | tf_op jit(solution)/shard_map/pallas_call | solution.py:57
  7.0 3.0 %collective-permute-start.12 = (bf16[8,128,128]{2,1,0:T(8,128)(2,1)}, bf16[8,128,128]{2,1,0:T(8,128)(2,1)S(1)}, u32[]{:S(2)}, u32[]{:S(2)}) collective-permute-start(bf16[8,128,128]{2,1,0:T(8,128)(2,1)} %shard_map.37.refs_8_), channel_id=1, source_target_pairs={{0,2},{1,3},{2,0},{3,1},{4,6},{5,7},{6,4},{7,5},{8,10},{9,11},{10,... | collective-permute-start | bytes 786440 | tf_op jit(solution)/shard_map/ppermute | solution.py:46
  10.1 1.1 %collective-permute-start.11 = (bf16[8,128,128]{2,1,0:T(8,128)(2,1)}, bf16[8,128,128]{2,1,0:T(8,128)(2,1)S(1)}, u32[]{:S(2)}, u32[]{:S(2)}) collective-permute-start(bf16[8,128,128]{2,1,0:T(8,128)(2,1)} %shard_map.37.refs_8_), channel_id=1, source_target_pairs={{0,3},{1,0},{2,1},{3,2},{4,7},{5,4},{6,5},{7,6},{8,11},{9,8},{10,9... | collective-permute-start | bytes 786440 | tf_op jit(solution)/shard_map/ppermute | solution.py:46
  11.2 0.0 collective-permute-done.2
  11.2 0.0 collective-permute-done.1
  11.2 0.0 collective-permute-done
  11.2 0.0 copy-done.1
  11.2 0.0 copy-start
  11.3 4.0 %collective-permute-start.5 = (bf16[4,256,128]{2,1,0:T(8,128)(2,1)S(1)}, bf16[4,256,128]{2,1,0:T(8,128)(2,1)S(1)}, u32[]{:S(2)}, u32[]{:S(2)}) collective-permute-start(bf16[4,256,128]{2,1,0:T(8,128)(2,1)S(1)} %pad_maximum_fusion.refs_0_), channel_id=1, source_target_pairs={{0,16},{4,20},{8,24},{12,28},{16,0},{20,4},{24,8},{28,12},{32,36},... | collective-permute-start | bytes 786440 | tf_op jit(solution)/shard_map/ppermute | solution.py:143
  15.2 0.7 %collective-permute-start.4 = (bf16[4,256,128]{2,1,0:T(8,128)(2,1)S(1)}, bf16[4,256,128]{2,1,0:T(8,128)(2,1)S(1)}, u32[]{:S(2)}, u32[]{:S(2)}) collective-permute-start(bf16[4,256,128]{2,1,0:T(8,128)(2,1)S(1)} %pad_maximum_fusion.refs_0_), channel_id=1, source_target_pairs={{0,24},{4,28},{8,0},{12,4},{16,8},{20,12},{24,16},{28,20},{32,100}... | collective-permute-start | bytes 786440 | tf_op jit(solution)/shard_map/ppermute | solution.py:143
  15.9 1.3 %collective-permute-start.3 = (bf16[4,256,128]{2,1,0:T(8,128)(2,1)S(1)}, bf16[4,256,128]{2,1,0:T(8,128)(2,1)S(1)}, u32[]{:S(2)}, u32[]{:S(2)}) collective-permute-start(bf16[4,256,128]{2,1,0:T(8,128)(2,1)S(1)} %pad_maximum_fusion.refs_0_), channel_id=1, source_target_pairs={{0,8},{4,12},{8,16},{12,20},{16,24},{20,28},{24,0},{28,4},{32,96},... | collective-permute-start | bytes 786440 | tf_op jit(solution)/shard_map/ppermute | solution.py:143
  17.3 0.0 collective-permute-done.12.refs_11_
  17.3 0.0 copy-done
  17.3 2.2 %collective-permute-start.10 = (bf16[8,128,128]{2,1,0:T(8,128)(2,1)S(1)}, bf16[8,128,128]{2,1,0:T(8,128)(2,1)S(1)}, u32[]{:S(2)}, u32[]{:S(2)}) collective-permute-start(bf16[8,128,128]{2,1,0:T(8,128)(2,1)S(1)} %copy-done), channel_id=1, source_target_pairs={{0,1},{1,2},{2,3},{3,0},{4,5},{5,6},{6,7},{7,4},{8,9},{9,10},{10,1... | collective-permute-start | bytes 786440 | tf_op jit(solution)/shard_map/ppermute | solution.py:46
  19.5 2.9 %collective-permute-done.11.refs_10_ = bf16[8,128,128]{2,1,0:T(8,128)(2,1)S(1)} collective-permute-done((bf16[8,128,128]{2,1,0:T(8,128)(2,1)}, bf16[8,128,128]{2,1,0:T(8,128)(2,1)S(1)}, u32[]{:S(2)}, u32[]{:S(2)}) %collective-permute-start.11) | collective-permute-done | bytes 262176 | tf_op jit(solution)/shard_map/ppermute | solution.py:46
  22.4 0.0 collective-permute-start.6
  22.4 0.0 collective-permute-done.5.refs_3_
  22.4 0.5 collective-permute-start.9
  22.9 0.5 collective-permute-done.4.refs_2_
  23.5 0.0 collective-permute-start.8
  23.5 0.1 collective-permute-done.3.refs_1_
  23.5 0.4 collective-permute-start.7
  24.0 0.1 pad_add_fusion.info_ref
  24.0 1.1 %collective-permute-done.10.refs_9_ = bf16[8,128,128]{2,1,0:T(8,128)(2,1)S(1)} collective-permute-done((bf16[8,128,128]{2,1,0:T(8,128)(2,1)S(1)}, bf16[8,128,128]{2,1,0:T(8,128)(2,1)S(1)}, u32[]{:S(2)}, u32[]{:S(2)}) %collective-permute-start.10) | collective-permute-done | bytes 262176 | tf_op jit(solution)/shard_map/ppermute | solution.py:46
  25.1 0.0 collective-permute-done.6.refs_4_
  25.1 0.0 collective-permute-done.9.refs_7_
  25.1 0.0 collective-permute-done.8.refs_6_
  25.1 0.2 collective-permute-done.7.refs_5_
  25.4 18.9 %shard_map.38 = f32[8,8,128]{2,1,0:T(8,128)S(1)} custom-call(s32[4]{0:T(128)S(1)} %pad_add_fusion.info_ref, bf16[4,256,128]{2,1,0:T(8,128)(2,1)S(1)} %pad_maximum_fusion.refs_0_, bf16[4,256,128]{2,1,0:T(8,128)(2,1)S(1)} %collective-permute-done.3.refs_1_, bf16[4,256,128]{2,1,0:T(8,128)(2,1)S(1)} %collective-permute-done.4.refs_2_, ...), custom_call_target="tpu_custom_call" | custom-call | tf_op jit(solution)/shard_map/pallas_call | solution.py:104
  44.2 13.4 %all_to_all.5.r_ref = f32[8,8,128]{2,1,0:T(8,128)} all-to-all(f32[8,8,128]{2,1,0:T(8,128)S(1)} %shard_map.38), channel_id=1, replica_groups=mesh['ylo'=2,'core'=2,'z'=4,'yhi'=2,'x'=4] {'z','yhi'}, dimensions={0} | all-to-all | bytes 65536 | tf_op jit(solution)/shard_map/all_to_all | solution.py:146
  57.6 1.5 %shard_map.39 = f32[32,256]{1,0:T(8,128)} custom-call(f32[8,8,128]{2,1,0:T(8,128)} %all_to_all.5.r_ref), custom_call_target="tpu_custom_call" | custom-call | tf_op jit(solution)/shard_map/pallas_call | solution.py:123
  (1 shorter events, 0.0 us)
Async XLA Ops:
  0.0 11.2 %copy-start.1 = (bf16[32,8,128]{2,1,0:T(8,128)(2,1)S(1)}, bf16[32,8,128]{2,1,0:T(8,128)(2,1)}, u32[]{:S(2)}) copy-start(bf16[32,8,128]{2,1,0:T(8,128)(2,1)} %param.3) | copy-start | bytes 196612
  0.0 11.2 %collective-permute-start.2 = (bf16[256,128]{1,0:T(8,128)(2,1)}, bf16[256,128]{1,0:T(8,128)(2,1)S(1)}, u32[]{:S(2)}, u32[]{:S(2)}) collective-permute-start(bf16[256,128]{1,0:T(8,128)(2,1)} %bitcast.9), channel_id=1, source_target_pairs={{0,4},{4,0},{8,12},{12,8},{16,20},{20,16},{24,28},{28,24},{32,48},... | collective-permute-start | bytes 196616 | tf_op jit(solution)/shard_map/ppermute | solution.py:139
  3.3 7.9 %collective-permute-start.1 = (bf16[256,128]{1,0:T(8,128)(2,1)}, bf16[256,128]{1,0:T(8,128)(2,1)S(1)}, u32[]{:S(2)}, u32[]{:S(2)}) collective-permute-start(bf16[256,128]{1,0:T(8,128)(2,1)} %bitcast.10), channel_id=1, source_target_pairs={{0,68},{4,64},{8,76},{12,72},{16,84},{20,80},{24,92},{28,88},{32,5... | collective-permute-start | bytes 196616 | tf_op jit(solution)/shard_map/ppermute | solution.py:139
  4.3 6.9 %collective-permute-start = (bf16[256,128]{1,0:T(8,128)(2,1)}, bf16[256,128]{1,0:T(8,128)(2,1)S(1)}, u32[]{:S(2)}, u32[]{:S(2)}) collective-permute-start(bf16[256,128]{1,0:T(8,128)(2,1)} %bitcast.11), channel_id=1, source_target_pairs={{0,64},{4,68},{8,72},{12,76},{16,80},{20,84},{24,88},{28,92},{32,4... | collective-permute-start | bytes 196616 | tf_op jit(solution)/shard_map/ppermute | solution.py:139
  7.0 10.2 %collective-permute-start.12 = (bf16[8,128,128]{2,1,0:T(8,128)(2,1)}, bf16[8,128,128]{2,1,0:T(8,128)(2,1)S(1)}, u32[]{:S(2)}, u32[]{:S(2)}) collective-permute-start(bf16[8,128,128]{2,1,0:T(8,128)(2,1)} %shard_map.37.refs_8_), channel_id=1, source_target_pairs={{0,2},{1,3},{2,0},{3,1},{4,6},{5,7},{6,4},{7,5},{8,10},{9,11},{10,... | collective-permute-start | bytes 786440 | tf_op jit(solution)/shard_map/ppermute | solution.py:46
  10.1 12.3 %collective-permute-start.11 = (bf16[8,128,128]{2,1,0:T(8,128)(2,1)}, bf16[8,128,128]{2,1,0:T(8,128)(2,1)S(1)}, u32[]{:S(2)}, u32[]{:S(2)}) collective-permute-start(bf16[8,128,128]{2,1,0:T(8,128)(2,1)} %shard_map.37.refs_8_), channel_id=1, source_target_pairs={{0,3},{1,0},{2,1},{3,2},{4,7},{5,4},{6,5},{7,6},{8,11},{9,8},{10,9... | collective-permute-start | bytes 786440 | tf_op jit(solution)/shard_map/ppermute | solution.py:46
  11.2 6.0 %copy-start = (bf16[8,128,128]{2,1,0:T(8,128)(2,1)S(1)}, bf16[8,128,128]{2,1,0:T(8,128)(2,1)}, u32[]{:S(2)}) copy-start(bf16[8,128,128]{2,1,0:T(8,128)(2,1)} %shard_map.37.refs_8_) | copy-start | bytes 786436
  11.3 11.1 %collective-permute-start.5 = (bf16[4,256,128]{2,1,0:T(8,128)(2,1)S(1)}, bf16[4,256,128]{2,1,0:T(8,128)(2,1)S(1)}, u32[]{:S(2)}, u32[]{:S(2)}) collective-permute-start(bf16[4,256,128]{2,1,0:T(8,128)(2,1)S(1)} %pad_maximum_fusion.refs_0_), channel_id=1, source_target_pairs={{0,16},{4,20},{8,24},{12,28},{16,0},{20,4},{24,8},{28,12},{32,36},... | collective-permute-start | bytes 786440 | tf_op jit(solution)/shard_map/ppermute | solution.py:143
  15.2 8.2 %collective-permute-start.4 = (bf16[4,256,128]{2,1,0:T(8,128)(2,1)S(1)}, bf16[4,256,128]{2,1,0:T(8,128)(2,1)S(1)}, u32[]{:S(2)}, u32[]{:S(2)}) collective-permute-start(bf16[4,256,128]{2,1,0:T(8,128)(2,1)S(1)} %pad_maximum_fusion.refs_0_), channel_id=1, source_target_pairs={{0,24},{4,28},{8,0},{12,4},{16,8},{20,12},{24,16},{28,20},{32,100}... | collective-permute-start | bytes 786440 | tf_op jit(solution)/shard_map/ppermute | solution.py:143
  15.9 7.6 %collective-permute-start.3 = (bf16[4,256,128]{2,1,0:T(8,128)(2,1)S(1)}, bf16[4,256,128]{2,1,0:T(8,128)(2,1)S(1)}, u32[]{:S(2)}, u32[]{:S(2)}) collective-permute-start(bf16[4,256,128]{2,1,0:T(8,128)(2,1)S(1)} %pad_maximum_fusion.refs_0_), channel_id=1, source_target_pairs={{0,8},{4,12},{8,16},{12,20},{16,24},{20,28},{24,0},{28,4},{32,96},... | collective-permute-start | bytes 786440 | tf_op jit(solution)/shard_map/ppermute | solution.py:143
  17.3 7.9 %collective-permute-start.10 = (bf16[8,128,128]{2,1,0:T(8,128)(2,1)S(1)}, bf16[8,128,128]{2,1,0:T(8,128)(2,1)S(1)}, u32[]{:S(2)}, u32[]{:S(2)}) collective-permute-start(bf16[8,128,128]{2,1,0:T(8,128)(2,1)S(1)} %copy-done), channel_id=1, source_target_pairs={{0,1},{1,2},{2,3},{3,0},{4,5},{5,6},{6,7},{7,4},{8,9},{9,10},{10,1... | collective-permute-start | bytes 786440 | tf_op jit(solution)/shard_map/ppermute | solution.py:46
  22.4 2.7 %collective-permute-start.6 = (bf16[4,256,128]{2,1,0:T(8,128)(2,1)S(1)}, bf16[4,256,128]{2,1,0:T(8,128)(2,1)S(1)}, u32[]{:S(2)}, u32[]{:S(2)}) collective-permute-start(bf16[4,256,128]{2,1,0:T(8,128)(2,1)S(1)} %pad_maximum_fusion.refs_0_), channel_id=1, source_target_pairs={{0,32},{32,0},{1,33},{33,1},{2,34},{34,2},{3,35},{35,3},{4,36},{36... | collective-permute-start | bytes 786440 | tf_op jit(solution)/shard_map/ppermute | solution.py:42
  22.4 2.7 %collective-permute-start.9 = (bf16[4,256,128]{2,1,0:T(8,128)(2,1)S(1)}, bf16[4,256,128]{2,1,0:T(8,128)(2,1)S(1)}, u32[]{:S(2)}, u32[]{:S(2)}) collective-permute-start(bf16[4,256,128]{2,1,0:T(8,128)(2,1)S(1)} %collective-permute-done.5.refs_3_), channel_id=1, source_target_pairs={{0,32},{32,0},{1,33},{33,1},{2,34},{34,2},{3,35},{35,3},{4,36},{36... | collective-permute-start | bytes 786440 | tf_op jit(solution)/shard_map/ppermute | solution.py:42
  23.5 1.7 %collective-permute-start.8 = (bf16[4,256,128]{2,1,0:T(8,128)(2,1)S(1)}, bf16[4,256,128]{2,1,0:T(8,128)(2,1)S(1)}, u32[]{:S(2)}, u32[]{:S(2)}) collective-permute-start(bf16[4,256,128]{2,1,0:T(8,128)(2,1)S(1)} %collective-permute-done.4.refs_2_), channel_id=1, source_target_pairs={{0,32},{32,0},{1,33},{33,1},{2,34},{34,2},{3,35},{35,3},{4,36},{36... | collective-permute-start | bytes 786440 | tf_op jit(solution)/shard_map/ppermute | solution.py:42
  23.5 1.8 %collective-permute-start.7 = (bf16[4,256,128]{2,1,0:T(8,128)(2,1)S(1)}, bf16[4,256,128]{2,1,0:T(8,128)(2,1)S(1)}, u32[]{:S(2)}, u32[]{:S(2)}) collective-permute-start(bf16[4,256,128]{2,1,0:T(8,128)(2,1)S(1)} %collective-permute-done.3.refs_1_), channel_id=1, source_target_pairs={{0,32},{32,0},{1,33},{33,1},{2,34},{34,2},{3,35},{35,3},{4,36},{36... | collective-permute-start | bytes 786440 | tf_op jit(solution)/shard_map/ppermute | solution.py:42

commit v2 on v1

v2 whole, which is shorter than its diff:
```python
import jax
import jax.numpy as jnp
from jax import lax
from jax.experimental import pallas as pl
from jax.experimental.pallas import tpu as pltpu
from jax.sharding import Mesh
from jax.sharding import PartitionSpec as P

NAMES = ("ylo", "core", "z", "yhi", "x")
SIZES = (2, 2, 4, 2, 4)
SHIFTS = (0, 1, -1, 2)
FROM = tuple((k, flip) for k in SHIFTS for flip in range(2))


def on_y(v, shift):
    def index(y):
        return (y % 2) * 2 + y // 2

    return lax.ppermute(v, ("ylo", "yhi"), [(index(i), index((i + shift) % 4)) for i in range(4)])


def on_z(v, shift):
    return lax.ppermute(v, "z", [(i, (i + shift) % 4) for i in range(4)])


def on_z_yhi(v, shift, flip):
    pairs = [
        (z * 2 + yhi, ((z + shift) % 4) * 2 + (yhi ^ flip)) for z in range(4) for yhi in range(2)
    ]
    return lax.ppermute(v, ("z", "yhi"), pairs)


def to_core(v):
    return lax.ppermute(v, "core", [(0, 1), (1, 0)])


def on_x(v, shift):
    return lax.ppermute(v, "x", [(i, (i + shift) % 4) for i in range(4)])


def fill_kernel(len_ref, p_ref, o_ref):
    slot = lax.broadcasted_iota(jnp.int32, p_ref.shape[1:], 0)
    for i in range(p_ref.shape[0]):
        v = p_ref[i].astype(jnp.float32)
        o_ref[i] = jnp.where(slot < len_ref[i], v, v[0:1]).astype(o_ref.dtype)


def fill(passages, lengths):
    return pl.pallas_call(
        fill_kernel,
        out_shape=jax.ShapeDtypeStruct(passages.shape, passages.dtype),
        in_specs=[pl.BlockSpec(memory_space=pltpu.SMEM), pl.BlockSpec(memory_space=pltpu.VMEM)],
        out_specs=pl.BlockSpec(memory_space=pltpu.VMEM),
    )(lengths, passages)


def dot_nt(a, b, precision=None):
    return lax.dot_general(
        a, b, (((1,), (1,)), ((), ())), preferred_element_type=jnp.float32, precision=precision
    )


def score_kernel(info_ref, mine_ref, other_ref, *refs):
    pieces, outs, acc_ref = refs[:4], refs[4:6], refs[6]
    x, ylo = info_ref[0], info_ref[1]
    mate = 2 - ylo
    lane = lax.broadcasted_iota(jnp.int32, (32, 256), 1)
    row = lax.broadcasted_iota(jnp.int32, (32, 256), 0)
    pick = jnp.where(lane // 8 == row, 1.0 / 32, 0.0).astype(jnp.float32)
    for half, pair in ((1, (3 - mate, 3)), (0, (0, mate))):
        w = jnp.concatenate([ref[j] for ref in (mine_ref, other_ref) for j in pair], axis=0)
        for m in range(4):
            tops = []
            for i in range(8):
                d = dot_nt(pieces[m][i], w)
                tops.append(jnp.max(d.reshape(16, 8, 1024), axis=0)[None])
            top = jnp.max(jnp.concatenate(tops, axis=0), axis=1)
            total = top[:, 0:256] + top[:, 256:512] + top[:, 512:768] + top[:, 768:1024]
            place = pl.multiple_of(8 * lax.rem(x + 4 - SHIFTS[m], 4), 8)
            acc_ref[pl.ds(place, 8), :] = total
        r = dot_nt(pick, acc_ref[...], lax.Precision.HIGHEST)
        outs[half][...] = jnp.concatenate([r[0:8], r[8:16], r[16:24], r[24:32]], axis=1)


def score(info, mine, other, pieces):
    return pl.pallas_call(
        score_kernel,
        out_shape=[jax.ShapeDtypeStruct((8, 128), jnp.float32)] * 2,
        in_specs=[pl.BlockSpec(memory_space=pltpu.SMEM)]
        + [pl.BlockSpec(memory_space=pltpu.VMEM)] * 6,
        out_specs=[pl.BlockSpec(memory_space=pltpu.VMEM)] * 2,
        scratch_shapes=[pltpu.VMEM((32, 256), jnp.float32)],
        compiler_params=pltpu.CompilerParams(vmem_limit_bytes=32 << 20),
        cost_estimate=pl.CostEstimate(
            flops=2 * 2048 * 4096 * 128 * 2, bytes_accessed=1 << 20, transcendentals=0
        ),
    )(info, mine, other, *pieces)


def place_kernel(info_ref, *refs):
    parts, o_ref, held_ref = refs[:8], refs[8], refs[9]
    z, yhi = info_ref[2], info_ref[3]
    for n, (shift, flip) in enumerate(FROM):
        source = lax.rem(z + 4 + shift, 4) * 2 + (yhi if flip == 0 else 1 - yhi)
        held_ref[source] = parts[n][...]
    for g in range(4):
        o_ref[8 * g : 8 * g + 8, :] = jnp.concatenate(
            [held_ref[s][:, 32 * g : 32 * g + 32] for s in range(8)], axis=1
        )


def place(info, parts):
    return pl.pallas_call(
        place_kernel,
        out_shape=jax.ShapeDtypeStruct((32, 256), jnp.float32),
        in_specs=[pl.BlockSpec(memory_space=pltpu.SMEM)]
        + [pl.BlockSpec(memory_space=pltpu.VMEM)] * 8,
        out_specs=pl.BlockSpec(memory_space=pltpu.VMEM),
        scratch_shapes=[pltpu.VMEM((8, 8, 128), jnp.float32)],
    )(info, *parts)


def per_device(queries, passages, lengths):
    own = queries.reshape(256, 128)
    places = [lax.axis_index(name) for name in ("x", "ylo", "z", "yhi")]
    info = jnp.stack(places).astype(jnp.int32)

    near = [own] + [on_y(own, k) for k in SHIFTS[1:]]
    filled = fill(passages, lengths)
    pieces = [filled] + [on_x(filled, k) for k in SHIFTS[1:]]
    block = jnp.stack(near)
    parts = []
    for k in SHIFTS:
        mine = block if k == 0 else on_z(block, k)
        terms = score(info, mine, to_core(mine), pieces)
        for flip in range(2):
            parts.append(terms[flip] if (k, flip) == (0, 0) else on_z_yhi(terms[flip], -k, flip))
    return place(info, parts)


def solution(mesh):
    fine = Mesh(mesh.devices.reshape(SIZES), NAMES)
    corpus = ("z", "yhi", "x")
    query = ("ylo", "core")
    return jax.shard_map(
        per_device,
        mesh=fine,
        in_specs=(P(corpus, query, None), P(query + corpus, None, None), P(query + corpus)),
        out_specs=P(corpus, query),
        check_vma=False,
    )
```

time: 59.6 us -> 68 us (1.14)
  starting transfers between devices: 18.6 us -> 36.5 us
  blocking collectives: 13.4 us -> 0 us
  Pallas kernels: 22 us -> 25.3 us
  local copies, waits for them, and re-layouts: 0.01 us -> 1.29 us
  waiting for transfers between devices: 4.83 us -> 4.02 us
    ppermute x6 -> x13, starting transfers between devices: 11.3 us -> 31.2 us  [the longest x7 14.5 us: on_z_yhi(): return lax.ppermute(v, ('z', 'yhi'), pairs)]
    all_to_all x1 -> x0, blocking collectives: 13.4 us -> none  [per_device(): received = lax.all_to_all(terms, ('z', 'yhi'), 0, 0, tiled=True)]
    ppermute x3, waiting for transfers between devices: 3.96 us -> 0.01 us  [on_x(): return lax.ppermute(v, 'x', [(i, (i + shift) % 4) for i in range(4)])]
    ppermute x6 -> x13, waiting for transfers between devices: 0.64 us -> 4.01 us  [the longest x7 3.77 us: on_z_yhi(): return lax.ppermute(v, ('z', 'yhi'), pairs)]
    pallas_call x1 -> x4, Pallas kernels: 18.9 us -> 22 us  [score(): pl.pallas_call(score_kernel, out_shape=[jax.ShapeDtypeStruct((8, 128), jn...]
    ppermute x3, starting transfers between devices: 6.4 us -> 5.05 us  [on_x(): return lax.ppermute(v, 'x', [(i, (i + shift) % 4) for i in range(4)])]
    unnamed x4 -> x22, local copies, waits for them, and re-layouts: 0.01 us -> 1.29 us
  transfers between devices with their start and end apart: 13 -> 20, of which waited for: 5 -> 2; matrix products, arithmetic and copies ran while one was open for 0% -> 0% of each run, Pallas kernels for 3% -> 35%
where the time goes in v2:
time: 68 us; the launch traced here: 67.4 us
  starting transfers between devices  36.5 us (54%)
  Pallas kernels  25.3 us (37%)
  waiting for transfers between devices  4.02 us (6%)
  local copies, waits for them, and re-layouts  1.29 us (2%)
    pallas_call x4, Pallas kernels, score(): pl.pallas_call(score_kernel, out_shape=[jax.ShapeDtypeStruct((8, 128), jn...  22 us
    ppermute x7, starting transfers between devices, on_z_yhi(): return lax.ppermute(v, ('z', 'yhi'), pairs)  14.5 us
    ppermute x3, starting transfers between devices, on_z(): return lax.ppermute(v, 'z', [(i, (i + shift) % 4) for i in range(4)])  11.4 us
    ppermute x3, starting transfers between devices, on_y(): lax.ppermute(v, ('ylo', 'yhi'), [(index(i), index((i + shift) % 4)) for i...  5.3 us
    ppermute x3, starting transfers between devices, on_x(): return lax.ppermute(v, 'x', [(i, (i + shift) % 4) for i in range(4)])  5.05 us
    ppermute x7, waiting for transfers between devices, on_z_yhi(): return lax.ppermute(v, ('z', 'yhi'), pairs)  3.77 us
    pallas_call x1, Pallas kernels, fill(): pl.pallas_call(fill_kernel, out_shape=jax.ShapeDtypeStruct(passages.shape...  1.72 us
    pallas_call x1, Pallas kernels, place(): pl.pallas_call(place_kernel, out_shape=jax.ShapeDtypeStruct((32, 256), jn...  1.54 us
  transfers between devices with their start and end apart: 20, of which 2 were waited for; matrix products, arithmetic and copies ran while one was open for 0% of the time, Pallas kernels for 35%

profile of v2, /device:TPU:0, one launch (start us, length us, event | category | flops | bytes accessed | tf_op | source)
XLA Modules:
  0.0 67.4 jit_solution(3725735005267983868)
XLA Ops:
  0.0 3.3 %collective-permute-start.2 = (bf16[256,128]{1,0:T(8,128)(2,1)}, bf16[256,128]{1,0:T(8,128)(2,1)S(1)}, u32[]{:S(2)}, u32[]{:S(2)}) collective-permute-start(bf16[256,128]{1,0:T(8,128)(2,1)} %bitcast.9), channel_id=1, source_target_pairs={{0,4},{64,68},{4,0},{68,64},{1,5},{65,69},{5,1},{69,65},{2,6},{66,... | collective-permute-start | bytes 196616 | tf_op jit(solution)/shard_map/ppermute | solution.py:19
  3.3 1.1 %collective-permute-start.1 = (bf16[256,128]{1,0:T(8,128)(2,1)}, bf16[256,128]{1,0:T(8,128)(2,1)S(1)}, u32[]{:S(2)}, u32[]{:S(2)}) collective-permute-start(bf16[256,128]{1,0:T(8,128)(2,1)} %bitcast.10), channel_id=1, source_target_pairs={{0,68},{64,0},{4,64},{68,4},{1,69},{65,1},{5,65},{69,5},{2,70},{66... | collective-permute-start | bytes 196616 | tf_op jit(solution)/shard_map/ppermute | solution.py:19
  4.3 1.0 %collective-permute-start = (bf16[256,128]{1,0:T(8,128)(2,1)}, bf16[256,128]{1,0:T(8,128)(2,1)S(1)}, u32[]{:S(2)}, u32[]{:S(2)}) collective-permute-start(bf16[256,128]{1,0:T(8,128)(2,1)} %bitcast.11), channel_id=1, source_target_pairs={{0,64},{64,4},{4,68},{68,0},{1,65},{65,5},{5,69},{69,1},{2,66},{66... | collective-permute-start | bytes 196616 | tf_op jit(solution)/shard_map/ppermute | solution.py:19
  5.3 1.7 %shard_map.37.refs_0_ = bf16[8,128,128]{2,1,0:T(8,128)(2,1)} custom-call(s32[8]{0:T(128)} %len_ref.1, bf16[8,128,128]{2,1,0:T(8,128)(2,1)} %p_ref.1), custom_call_target="tpu_custom_call" | custom-call | tf_op jit(solution)/shard_map/pallas_call | solution.py:49
  7.0 3.0 %collective-permute-start.6 = (bf16[8,128,128]{2,1,0:T(8,128)(2,1)}, bf16[8,128,128]{2,1,0:T(8,128)(2,1)S(1)}, u32[]{:S(2)}, u32[]{:S(2)}) collective-permute-start(bf16[8,128,128]{2,1,0:T(8,128)(2,1)} %shard_map.37.refs_0_), channel_id=1, source_target_pairs={{0,2},{1,3},{2,0},{3,1},{4,6},{5,7},{6,4},{7,5},{8,10},{9,11},{10,... | collective-permute-start | bytes 786440 | tf_op jit(solution)/shard_map/ppermute | solution.py:38
  10.0 1.1 %collective-permute-start.5 = (bf16[8,128,128]{2,1,0:T(8,128)(2,1)}, bf16[8,128,128]{2,1,0:T(8,128)(2,1)S(1)}, u32[]{:S(2)}, u32[]{:S(2)}) collective-permute-start(bf16[8,128,128]{2,1,0:T(8,128)(2,1)} %shard_map.37.refs_0_), channel_id=1, source_target_pairs={{0,3},{1,0},{2,1},{3,2},{4,7},{5,4},{6,5},{7,6},{8,11},{9,8},{10,9... | collective-permute-start | bytes 786440 | tf_op jit(solution)/shard_map/ppermute | solution.py:38
  11.2 0.0 collective-permute-done.2
  11.2 0.0 collective-permute-done.1
  11.2 0.0 collective-permute-done
  11.2 0.0 copy-done.3
  11.2 0.0 copy-start
  11.3 4.0 %collective-permute-start.16 = (bf16[4,256,128]{2,1,0:T(8,128)(2,1)S(1)}, bf16[4,256,128]{2,1,0:T(8,128)(2,1)S(1)}, u32[]{:S(2)}, u32[]{:S(2)}) collective-permute-start(bf16[4,256,128]{2,1,0:T(8,128)(2,1)S(1)} %pad_maximum_fusion.mine_ref), channel_id=1, source_target_pairs={{0,16},{8,24},{16,0},{24,8},{1,17},{9,25},{17,1},{25,9},{2,18},{10... | collective-permute-start | bytes 786440 | tf_op jit(solution)/shard_map/ppermute | solution.py:23
  15.2 0.0 copy-done
  15.2 0.9 %collective-permute-start.4 = (bf16[8,128,128]{2,1,0:T(8,128)(2,1)S(1)}, bf16[8,128,128]{2,1,0:T(8,128)(2,1)S(1)}, u32[]{:S(2)}, u32[]{:S(2)}) collective-permute-start(bf16[8,128,128]{2,1,0:T(8,128)(2,1)S(1)} %copy-done), channel_id=1, source_target_pairs={{0,1},{1,2},{2,3},{3,0},{4,5},{5,6},{6,7},{7,4},{8,9},{9,10},{10,1... | collective-permute-start | bytes 786440 | tf_op jit(solution)/shard_map/ppermute | solution.py:38
  16.1 0.0 collective-permute-start.3
  16.1 0.1 pad_add_fusion.info_ref
  16.2 0.0 collective-permute-done.6.refs_3_
  16.2 5.8 %collective-permute-start.12 = (bf16[4,256,128]{2,1,0:T(8,128)(2,1)S(1)}, bf16[4,256,128]{2,1,0:T(8,128)(2,1)S(1)}, u32[]{:S(2)}, u32[]{:S(2)}) collective-permute-start(bf16[4,256,128]{2,1,0:T(8,128)(2,1)S(1)} %pad_maximum_fusion.mine_ref), channel_id=1, source_target_pairs={{0,24},{8,0},{16,8},{24,16},{1,25},{9,1},{17,9},{25,17},{2,26},{10... | collective-permute-start | bytes 786440 | tf_op jit(solution)/shard_map/ppermute | solution.py:23
  22.0 0.0 collective-permute-done.5.refs_2_
  22.0 1.6 %collective-permute-start.8 = (bf16[4,256,128]{2,1,0:T(8,128)(2,1)S(1)}, bf16[4,256,128]{2,1,0:T(8,128)(2,1)S(1)}, u32[]{:S(2)}, u32[]{:S(2)}) collective-permute-start(bf16[4,256,128]{2,1,0:T(8,128)(2,1)S(1)} %pad_maximum_fusion.mine_ref), channel_id=1, source_target_pairs={{0,8},{8,16},{16,24},{24,0},{1,9},{9,17},{17,25},{25,1},{2,10},{10... | collective-permute-start | bytes 786440 | tf_op jit(solution)/shard_map/ppermute | solution.py:23
  23.6 0.0 collective-permute-done.16.mine_ref
  23.6 0.0 collective-permute-start.17
  23.6 0.0 collective-permute-done.4.refs_1_
  23.6 0.0 collective-permute-done.3.other_ref
  23.6 5.5 %shard_map.38 = (f32[8,128]{1,0:T(8,128)S(1)}, f32[8,128]{1,0:T(8,128)S(1)}) custom-call(s32[4]{0:T(128)S(1)} %pad_add_fusion.info_ref, bf16[4,256,128]{2,1,0:T(8,128)(2,1)S(1)} %pad_maximum_fusion.mine_ref, bf16[4,256,128]{2,1,0:T(8,128)(2,1)S(1)} %collective-permute-done.3.other_ref, bf16[8,128,128]{2,1,0:T(8,128)(2,1)S(1)} %copy-done, ...), custom_call_target="tpu_custom_call" | custom-call | flops 4294967296 | bytes 1048576 | tf_op jit(solution)/shard_map/pallas_call | solution.py:86
  29.1 0.0 copy-start.1
  29.2 0.7 copy-done.1
  29.8 1.0 %collective-permute-start.7 = (f32[8,128]{1,0:T(8,128)S(1)}, f32[8,128]{1,0:T(8,128)S(1)}, u32[]{:S(2)}, u32[]{:S(2)}) collective-permute-start(f32[8,128]{1,0:T(8,128)S(1)} %get-tuple-element.14), channel_id=1, source_target_pairs={{0,4},{4,0},{8,12},{12,8},{16,20},{20,16},{24,28},{28,24},{1,5},{5... | collective-permute-start | bytes 12296 | tf_op jit(solution)/shard_map/ppermute | solution.py:30
  30.8 0.0 collective-permute-done.12.mine_ref
  30.8 0.2 collective-permute-start.13
  31.0 0.2 collective-permute-done.8.mine_ref
  31.3 0.1 collective-permute-start.9
  31.3 0.0 collective-permute-done.17.other_ref
  31.3 5.5 %shard_map.41 = (f32[8,128]{1,0:T(8,128)S(1)}, f32[8,128]{1,0:T(8,128)S(1)}) custom-call(s32[4]{0:T(128)S(1)} %pad_add_fusion.info_ref, bf16[4,256,128]{2,1,0:T(8,128)(2,1)S(1)} %collective-permute-done.16.mine_ref, bf16[4,256,128]{2,1,0:T(8,128)(2,1)S(1)} %collective-permute-done.17.other_ref, bf16[8,128,128]{2,1,0:T(8,128)(2,1)S(1)} %copy-done, ...), custom_call_target="tpu_custom_call" | custom-call | flops 4294967296 | bytes 1048576 | tf_op jit(solution)/shard_map/pallas_call | solution.py:86
  36.8 3.7 %collective-permute-start.18 = (f32[8,128]{1,0:T(8,128)S(1)}, f32[8,128]{1,0:T(8,128)S(1)}, u32[]{:S(2)}, u32[]{:S(2)}) collective-permute-start(f32[8,128]{1,0:T(8,128)S(1)} %get-tuple-element.19), channel_id=1, source_target_pairs={{0,16},{4,20},{8,24},{12,28},{16,0},{20,4},{24,8},{28,12},{1,17},{... | collective-permute-start | bytes 12296 | tf_op jit(solution)/shard_map/ppermute | solution.py:30
  40.5 2.0 %collective-permute-start.19 = (f32[8,128]{1,0:T(8,128)S(1)}, f32[8,128]{1,0:T(8,128)S(1)}, u32[]{:S(2)}, u32[]{:S(2)}) collective-permute-start(f32[8,128]{1,0:T(8,128)S(1)} %get-tuple-element.20), channel_id=1, source_target_pairs={{0,20},{4,16},{8,28},{12,24},{16,4},{20,0},{24,12},{28,8},{1,21},{... | collective-permute-start | bytes 12296 | tf_op jit(solution)/shard_map/ppermute | solution.py:30
  42.5 0.0 collective-permute-done.13.other_ref
  42.5 5.5 %shard_map.40 = (f32[8,128]{1,0:T(8,128)S(1)}, f32[8,128]{1,0:T(8,128)S(1)}) custom-call(s32[4]{0:T(128)S(1)} %pad_add_fusion.info_ref, bf16[4,256,128]{2,1,0:T(8,128)(2,1)S(1)} %collective-permute-done.12.mine_ref, bf16[4,256,128]{2,1,0:T(8,128)(2,1)S(1)} %collective-permute-done.13.other_ref, bf16[8,128,128]{2,1,0:T(8,128)(2,1)S(1)} %copy-done, ...), custom_call_target="tpu_custom_call" | custom-call | flops 4294967296 | bytes 1048576 | tf_op jit(solution)/shard_map/pallas_call | solution.py:86
  48.1 1.9 %collective-permute-start.14 = (f32[8,128]{1,0:T(8,128)S(1)}, f32[8,128]{1,0:T(8,128)S(1)}, u32[]{:S(2)}, u32[]{:S(2)}) collective-permute-start(f32[8,128]{1,0:T(8,128)S(1)} %get-tuple-element.17), channel_id=1, source_target_pairs={{0,8},{4,12},{8,16},{12,20},{16,24},{20,28},{24,0},{28,4},{1,9},{5... | collective-permute-start | bytes 12296 | tf_op jit(solution)/shard_map/ppermute | solution.py:30
  49.9 0.0 collective-permute-done.9.other_ref
  49.9 2.1 %collective-permute-start.15 = (f32[8,128]{1,0:T(8,128)S(1)}, f32[8,128]{1,0:T(8,128)S(1)}, u32[]{:S(2)}, u32[]{:S(2)}) collective-permute-start(f32[8,128]{1,0:T(8,128)S(1)} %get-tuple-element.18), channel_id=1, source_target_pairs={{0,12},{4,8},{8,20},{12,16},{16,28},{20,24},{24,4},{28,0},{1,13},{... | collective-permute-start | bytes 12296 | tf_op jit(solution)/shard_map/ppermute | solution.py:30
  52.0 0.0 copy-done.2
  52.0 5.5 %shard_map.39 = (f32[8,128]{1,0:T(8,128)S(1)}, f32[8,128]{1,0:T(8,128)S(1)}) custom-call(s32[4]{0:T(128)S(1)} %pad_add_fusion.info_ref, bf16[4,256,128]{2,1,0:T(8,128)(2,1)S(1)} %collective-permute-done.8.mine_ref, bf16[4,256,128]{2,1,0:T(8,128)(2,1)S(1)} %collective-permute-done.9.other_ref, bf16[8,128,128]{2,1,0:T(8,128)(2,1)S(1)} %copy-done, ...), custom_call_target="tpu_custom_call" | custom-call | flops 4294967296 | bytes 1048576 | tf_op jit(solution)/shard_map/pallas_call | solution.py:86
  57.5 0.0 collective-permute-done.7.refs_1_
  57.5 0.1 copy-start.4
  57.6 1.7 %collective-permute-start.10 = (f32[8,128]{1,0:T(8,128)S(1)}, f32[8,128]{1,0:T(8,128)S(1)}, u32[]{:S(2)}, u32[]{:S(2)}) collective-permute-start(f32[8,128]{1,0:T(8,128)S(1)} %get-tuple-element.15), channel_id=1, source_target_pairs={{0,24},{4,28},{8,0},{12,4},{16,8},{20,12},{24,16},{28,20},{1,25},{... | collective-permute-start | bytes 12296 | tf_op jit(solution)/shard_map/ppermute | solution.py:30
  59.3 0.0 collective-permute-done.18.refs_6_
  59.3 2.2 %collective-permute-start.11 = (f32[8,128]{1,0:T(8,128)S(1)}, f32[8,128]{1,0:T(8,128)S(1)}, u32[]{:S(2)}, u32[]{:S(2)}) collective-permute-start(f32[8,128]{1,0:T(8,128)S(1)} %get-tuple-element.16), channel_id=1, source_target_pairs={{0,28},{4,24},{8,4},{12,0},{16,12},{20,8},{24,20},{28,16},{1,29},{... | collective-permute-start | bytes 12296 | tf_op jit(solution)/shard_map/ppermute | solution.py:30
  61.5 0.0 collective-permute-done.19.refs_7_
  61.5 0.0 collective-permute-done.14.refs_4_
  61.5 0.0 copy-start.7
  61.5 0.0 collective-permute-done.15.refs_5_
  61.5 0.0 copy-start.8
  61.5 0.0 collective-permute-done.10.refs_2_
  61.5 0.0 copy-start.9
  61.5 3.7 %collective-permute-done.11.refs_3_ = f32[8,128]{1,0:T(8,128)S(1)} collective-permute-done((f32[8,128]{1,0:T(8,128)S(1)}, f32[8,128]{1,0:T(8,128)S(1)}, u32[]{:S(2)}, u32[]{:S(2)}) %collective-permute-start.11) | collective-permute-done | bytes 4128 | tf_op jit(solution)/shard_map/ppermute | solution.py:30
  65.3 0.0 copy-done.4
  65.3 0.0 copy-done.5
  65.3 0.0 copy-done.6
  65.3 0.0 copy-done.7
  65.3 0.0 copy-done.8
  65.3 0.0 copy-done.9
  65.3 0.5 copy-done.10
  65.9 1.5 %shard_map.42 = f32[32,256]{1,0:T(8,128)} custom-call(s32[4]{0:T(128)} %copy-done.2, f32[8,128]{1,0:T(8,128)} %copy-done.1, f32[8,128]{1,0:T(8,128)} %copy-done.4, f32[8,128]{1,0:T(8,128)} %copy-done.9, f32[8,128]{1,0:T(8,128)} %copy-done.10, f32[8,128]{1,0:T(8,128)} %copy-done.7, f32[8,128]{1,0:T(8,128)} %copy-done.8, f32[8,128]{1,0:T(8,128)} %copy-done.5, ...), custom_call_target="tpu_custom_call" | custom-call | tf_op jit(solution)/shard_map/pallas_call | solution.py:113
  (6 shorter events, 0.0 us)
Async XLA Ops:
  0.0 11.2 %copy-start.3 = (bf16[32,8,128]{2,1,0:T(8,128)(2,1)S(1)}, bf16[32,8,128]{2,1,0:T(8,128)(2,1)}, u32[]{:S(2)}) copy-start(bf16[32,8,128]{2,1,0:T(8,128)(2,1)} %param.3) | copy-start | bytes 196612
  0.0 11.2 %collective-permute-start.2 = (bf16[256,128]{1,0:T(8,128)(2,1)}, bf16[256,128]{1,0:T(8,128)(2,1)S(1)}, u32[]{:S(2)}, u32[]{:S(2)}) collective-permute-start(bf16[256,128]{1,0:T(8,128)(2,1)} %bitcast.9), channel_id=1, source_target_pairs={{0,4},{64,68},{4,0},{68,64},{1,5},{65,69},{5,1},{69,65},{2,6},{66,... | collective-permute-start | bytes 196616 | tf_op jit(solution)/shard_map/ppermute | solution.py:19
  3.3 7.9 %collective-permute-start.1 = (bf16[256,128]{1,0:T(8,128)(2,1)}, bf16[256,128]{1,0:T(8,128)(2,1)S(1)}, u32[]{:S(2)}, u32[]{:S(2)}) collective-permute-start(bf16[256,128]{1,0:T(8,128)(2,1)} %bitcast.10), channel_id=1, source_target_pairs={{0,68},{64,0},{4,64},{68,4},{1,69},{65,1},{5,65},{69,5},{2,70},{66... | collective-permute-start | bytes 196616 | tf_op jit(solution)/shard_map/ppermute | solution.py:19
  4.3 6.9 %collective-permute-start = (bf16[256,128]{1,0:T(8,128)(2,1)}, bf16[256,128]{1,0:T(8,128)(2,1)S(1)}, u32[]{:S(2)}, u32[]{:S(2)}) collective-permute-start(bf16[256,128]{1,0:T(8,128)(2,1)} %bitcast.11), channel_id=1, source_target_pairs={{0,64},{64,4},{4,68},{68,0},{1,65},{65,5},{5,69},{69,1},{2,66},{66... | collective-permute-start | bytes 196616 | tf_op jit(solution)/shard_map/ppermute | solution.py:19
  7.0 9.2 %collective-permute-start.6 = (bf16[8,128,128]{2,1,0:T(8,128)(2,1)}, bf16[8,128,128]{2,1,0:T(8,128)(2,1)S(1)}, u32[]{:S(2)}, u32[]{:S(2)}) collective-permute-start(bf16[8,128,128]{2,1,0:T(8,128)(2,1)} %shard_map.37.refs_0_), channel_id=1, source_target_pairs={{0,2},{1,3},{2,0},{3,1},{4,6},{5,7},{6,4},{7,5},{8,10},{9,11},{10,... | collective-permute-start | bytes 786440 | tf_op jit(solution)/shard_map/ppermute | solution.py:38
  10.0 12.0 %collective-permute-start.5 = (bf16[8,128,128]{2,1,0:T(8,128)(2,1)}, bf16[8,128,128]{2,1,0:T(8,128)(2,1)S(1)}, u32[]{:S(2)}, u32[]{:S(2)}) collective-permute-start(bf16[8,128,128]{2,1,0:T(8,128)(2,1)} %shard_map.37.refs_0_), channel_id=1, source_target_pairs={{0,3},{1,0},{2,1},{3,2},{4,7},{5,4},{6,5},{7,6},{8,11},{9,8},{10,9... | collective-permute-start | bytes 786440 | tf_op jit(solution)/shard_map/ppermute | solution.py:38
  11.2 4.0 %copy-start = (bf16[8,128,128]{2,1,0:T(8,128)(2,1)S(1)}, bf16[8,128,128]{2,1,0:T(8,128)(2,1)}, u32[]{:S(2)}) copy-start(bf16[8,128,128]{2,1,0:T(8,128)(2,1)} %shard_map.37.refs_0_) | copy-start | bytes 786436
  11.3 12.3 %collective-permute-start.16 = (bf16[4,256,128]{2,1,0:T(8,128)(2,1)S(1)}, bf16[4,256,128]{2,1,0:T(8,128)(2,1)S(1)}, u32[]{:S(2)}, u32[]{:S(2)}) collective-permute-start(bf16[4,256,128]{2,1,0:T(8,128)(2,1)S(1)} %pad_maximum_fusion.mine_ref), channel_id=1, source_target_pairs={{0,16},{8,24},{16,0},{24,8},{1,17},{9,25},{17,1},{25,9},{2,18},{10... | collective-permute-start | bytes 786440 | tf_op jit(solution)/shard_map/ppermute | solution.py:23
  15.2 8.4 %collective-permute-start.4 = (bf16[8,128,128]{2,1,0:T(8,128)(2,1)S(1)}, bf16[8,128,128]{2,1,0:T(8,128)(2,1)S(1)}, u32[]{:S(2)}, u32[]{:S(2)}) collective-permute-start(bf16[8,128,128]{2,1,0:T(8,128)(2,1)S(1)} %copy-done), channel_id=1, source_target_pairs={{0,1},{1,2},{2,3},{3,0},{4,5},{5,6},{6,7},{7,4},{8,9},{9,10},{10,1... | collective-permute-start | bytes 786440 | tf_op jit(solution)/shard_map/ppermute | solution.py:38
  16.1 7.5 %collective-permute-start.3 = (bf16[4,256,128]{2,1,0:T(8,128)(2,1)S(1)}, bf16[4,256,128]{2,1,0:T(8,128)(2,1)S(1)}, u32[]{:S(2)}, u32[]{:S(2)}) collective-permute-start(bf16[4,256,128]{2,1,0:T(8,128)(2,1)S(1)} %pad_maximum_fusion.mine_ref), channel_id=1, source_target_pairs={{0,32},{32,0},{1,33},{33,1},{2,34},{34,2},{3,35},{35,3},{4,36},{36... | collective-permute-start | bytes 786440 | tf_op jit(solution)/shard_map/ppermute | solution.py:34
  16.2 35.8 %copy-start.2 = (s32[4]{0:T(128)}, s32[4]{0:T(128)S(1)}, u32[]{:S(2)}) copy-start(s32[4]{0:T(128)S(1)} %pad_add_fusion.info_ref) | copy-start | bytes 52
  16.2 14.6 %collective-permute-start.12 = (bf16[4,256,128]{2,1,0:T(8,128)(2,1)S(1)}, bf16[4,256,128]{2,1,0:T(8,128)(2,1)S(1)}, u32[]{:S(2)}, u32[]{:S(2)}) collective-permute-start(bf16[4,256,128]{2,1,0:T(8,128)(2,1)S(1)} %pad_maximum_fusion.mine_ref), channel_id=1, source_target_pairs={{0,24},{8,0},{16,8},{24,16},{1,25},{9,1},{17,9},{25,17},{2,26},{10... | collective-permute-start | bytes 786440 | tf_op jit(solution)/shard_map/ppermute | solution.py:23
  22.0 9.2 %collective-permute-start.8 = (bf16[4,256,128]{2,1,0:T(8,128)(2,1)S(1)}, bf16[4,256,128]{2,1,0:T(8,128)(2,1)S(1)}, u32[]{:S(2)}, u32[]{:S(2)}) collective-permute-start(bf16[4,256,128]{2,1,0:T(8,128)(2,1)S(1)} %pad_maximum_fusion.mine_ref), channel_id=1, source_target_pairs={{0,8},{8,16},{16,24},{24,0},{1,9},{9,17},{17,25},{25,1},{2,10},{10... | collective-permute-start | bytes 786440 | tf_op jit(solution)/shard_map/ppermute | solution.py:23
  23.6 7.7 %collective-permute-start.17 = (bf16[4,256,128]{2,1,0:T(8,128)(2,1)S(1)}, bf16[4,256,128]{2,1,0:T(8,128)(2,1)S(1)}, u32[]{:S(2)}, u32[]{:S(2)}) collective-permute-start(bf16[4,256,128]{2,1,0:T(8,128)(2,1)S(1)} %collective-permute-done.16.mine_ref), channel_id=1, source_target_pairs={{0,32},{32,0},{1,33},{33,1},{2,34},{34,2},{3,35},{35,3},{4,36},{36... | collective-permute-start | bytes 786440 | tf_op jit(solution)/shard_map/ppermute | solution.py:34
  29.1 0.7 copy-start.1
  29.8 27.7 %collective-permute-start.7 = (f32[8,128]{1,0:T(8,128)S(1)}, f32[8,128]{1,0:T(8,128)S(1)}, u32[]{:S(2)}, u32[]{:S(2)}) collective-permute-start(f32[8,128]{1,0:T(8,128)S(1)} %get-tuple-element.14), channel_id=1, source_target_pairs={{0,4},{4,0},{8,12},{12,8},{16,20},{20,16},{24,28},{28,24},{1,5},{5... | collective-permute-start | bytes 12296 | tf_op jit(solution)/shard_map/ppermute | solution.py:30
  30.8 11.7 %collective-permute-start.13 = (bf16[4,256,128]{2,1,0:T(8,128)(2,1)S(1)}, bf16[4,256,128]{2,1,0:T(8,128)(2,1)S(1)}, u32[]{:S(2)}, u32[]{:S(2)}) collective-permute-start(bf16[4,256,128]{2,1,0:T(8,128)(2,1)S(1)} %collective-permute-done.12.mine_ref), channel_id=1, source_target_pairs={{0,32},{32,0},{1,33},{33,1},{2,34},{34,2},{3,35},{35,3},{4,36},{36... | collective-permute-start | bytes 786440 | tf_op jit(solution)/shard_map/ppermute | solution.py:34
  31.3 18.7 %collective-permute-start.9 = (bf16[4,256,128]{2,1,0:T(8,128)(2,1)S(1)}, bf16[4,256,128]{2,1,0:T(8,128)(2,1)S(1)}, u32[]{:S(2)}, u32[]{:S(2)}) collective-permute-start(bf16[4,256,128]{2,1,0:T(8,128)(2,1)S(1)} %collective-permute-done.8.mine_ref), channel_id=1, source_target_pairs={{0,32},{32,0},{1,33},{33,1},{2,34},{34,2},{3,35},{35,3},{4,36},{36... | collective-permute-start | bytes 786440 | tf_op jit(solution)/shard_map/ppermute | solution.py:34
  36.8 22.4 %collective-permute-start.18 = (f32[8,128]{1,0:T(8,128)S(1)}, f32[8,128]{1,0:T(8,128)S(1)}, u32[]{:S(2)}, u32[]{:S(2)}) collective-permute-start(f32[8,128]{1,0:T(8,128)S(1)} %get-tuple-element.19), channel_id=1, source_target_pairs={{0,16},{4,20},{8,24},{12,28},{16,0},{20,4},{24,8},{28,12},{1,17},{... | collective-permute-start | bytes 12296 | tf_op jit(solution)/shard_map/ppermute | solution.py:30
  40.5 21.0 %collective-permute-start.19 = (f32[8,128]{1,0:T(8,128)S(1)}, f32[8,128]{1,0:T(8,128)S(1)}, u32[]{:S(2)}, u32[]{:S(2)}) collective-permute-start(f32[8,128]{1,0:T(8,128)S(1)} %get-tuple-element.20), channel_id=1, source_target_pairs={{0,20},{4,16},{8,28},{12,24},{16,4},{20,0},{24,12},{28,8},{1,21},{... | collective-permute-start | bytes 12296 | tf_op jit(solution)/shard_map/ppermute | solution.py:30
  48.1 13.4 %collective-permute-start.14 = (f32[8,128]{1,0:T(8,128)S(1)}, f32[8,128]{1,0:T(8,128)S(1)}, u32[]{:S(2)}, u32[]{:S(2)}) collective-permute-start(f32[8,128]{1,0:T(8,128)S(1)} %get-tuple-element.17), channel_id=1, source_target_pairs={{0,8},{4,12},{8,16},{12,20},{16,24},{20,28},{24,0},{28,4},{1,9},{5... | collective-permute-start | bytes 12296 | tf_op jit(solution)/shard_map/ppermute | solution.py:30
  49.9 11.6 %collective-permute-start.15 = (f32[8,128]{1,0:T(8,128)S(1)}, f32[8,128]{1,0:T(8,128)S(1)}, u32[]{:S(2)}, u32[]{:S(2)}) collective-permute-start(f32[8,128]{1,0:T(8,128)S(1)} %get-tuple-element.18), channel_id=1, source_target_pairs={{0,12},{4,8},{8,20},{12,16},{16,28},{20,24},{24,4},{28,0},{1,13},{... | collective-permute-start | bytes 12296 | tf_op jit(solution)/shard_map/ppermute | solution.py:30
  57.5 7.8 %copy-start.4 = (f32[8,128]{1,0:T(8,128)}, f32[8,128]{1,0:T(8,128)S(1)}, u32[]{:S(2)}) copy-start(f32[8,128]{1,0:T(8,128)S(1)} %collective-permute-done.7.refs_1_) | copy-start | bytes 12292
  57.6 3.9 %collective-permute-start.10 = (f32[8,128]{1,0:T(8,128)S(1)}, f32[8,128]{1,0:T(8,128)S(1)}, u32[]{:S(2)}, u32[]{:S(2)}) collective-permute-start(f32[8,128]{1,0:T(8,128)S(1)} %get-tuple-element.15), channel_id=1, source_target_pairs={{0,24},{4,28},{8,0},{12,4},{16,8},{20,12},{24,16},{28,20},{1,25},{... | collective-permute-start | bytes 12296 | tf_op jit(solution)/shard_map/ppermute | solution.py:30
  59.3 6.0 %copy-start.5 = (f32[8,128]{1,0:T(8,128)}, f32[8,128]{1,0:T(8,128)S(1)}, u32[]{:S(2)}) copy-start(f32[8,128]{1,0:T(8,128)S(1)} %collective-permute-done.18.refs_6_) | copy-start | bytes 12292
  59.3 6.0 %collective-permute-start.11 = (f32[8,128]{1,0:T(8,128)S(1)}, f32[8,128]{1,0:T(8,128)S(1)}, u32[]{:S(2)}, u32[]{:S(2)}) collective-permute-start(f32[8,128]{1,0:T(8,128)S(1)} %get-tuple-element.16), channel_id=1, source_target_pairs={{0,28},{4,24},{8,4},{12,0},{16,12},{20,8},{24,20},{28,16},{1,29},{... | collective-permute-start | bytes 12296 | tf_op jit(solution)/shard_map/ppermute | solution.py:30
  61.5 3.8 %copy-start.6 = (f32[8,128]{1,0:T(8,128)}, f32[8,128]{1,0:T(8,128)S(1)}, u32[]{:S(2)}) copy-start(f32[8,128]{1,0:T(8,128)S(1)} %collective-permute-done.19.refs_7_) | copy-start | bytes 12292
  61.5 3.8 %copy-start.7 = (f32[8,128]{1,0:T(8,128)}, f32[8,128]{1,0:T(8,128)S(1)}, u32[]{:S(2)}) copy-start(f32[8,128]{1,0:T(8,128)S(1)} %collective-permute-done.14.refs_4_) | copy-start | bytes 12292
  61.5 3.8 %copy-start.8 = (f32[8,128]{1,0:T(8,128)}, f32[8,128]{1,0:T(8,128)S(1)}, u32[]{:S(2)}) copy-start(f32[8,128]{1,0:T(8,128)S(1)} %collective-permute-done.15.refs_5_) | copy-start | bytes 12292
  61.5 3.8 %copy-start.9 = (f32[8,128]{1,0:T(8,128)}, f32[8,128]{1,0:T(8,128)S(1)}, u32[]{:S(2)}) copy-start(f32[8,128]{1,0:T(8,128)S(1)} %collective-permute-done.10.refs_2_) | copy-start | bytes 12292
  65.3 0.6 copy-start.10

commit v3 on v1

v3 whole, which is shorter than its diff:
```python
import functools

import jax
import jax.numpy as jnp
from jax import lax
from jax.experimental import pallas as pl
from jax.experimental.pallas import tpu as pltpu
from jax.sharding import Mesh
from jax.sharding import PartitionSpec as P

NAMES = ("ylo", "core", "z", "yhi", "x")
SIZES = (2, 2, 4, 2, 4)
PLANE = ("ylo", "core", "z", "yhi")
SHIFTS = (0, 1, -1, 2)
OWN, SLOTS, WIDTH = 8, 128, 128
DEPTH = 16
LOWEST = -3.0e38


def plane_pairs(move):
    def index(ylo, core, z, yhi):
        return ((ylo * 2 + core) * 4 + z) * 2 + yhi

    pairs = []
    for ylo in range(2):
        for core in range(2):
            for z in range(4):
                for yhi in range(2):
                    y2, core2, z2 = move(2 * yhi + ylo, core, z)
                    y2, z2 = y2 % 4, z2 % 4
                    pairs.append((index(ylo, core, z, yhi), index(y2 % 2, core2, z2, y2 // 2)))
    return pairs


def along(first, shift):
    def move(y, core, z):
        if (core == 0) == first:
            return y + shift, core, z
        return y, core, z + shift

    return plane_pairs(move)


def to_core(v):
    return lax.ppermute(v, "core", [(0, 1), (1, 0)])


def on_x(v, shift):
    return lax.ppermute(v, "x", [(i, (i + shift) % 4) for i in range(4)])


def fill_kernel(len_ref, p_ref, o_ref):
    slot = lax.broadcasted_iota(jnp.int32, (SLOTS, WIDTH), 0)
    lane = lax.broadcasted_iota(jnp.int32, (16, WIDTH), 1)
    lengths = jnp.zeros((16, WIDTH), jnp.float32)
    for i in range(OWN):
        v = p_ref[i].astype(jnp.float32)
        o_ref[SLOTS * i : SLOTS * i + SLOTS, :] = jnp.where(slot < len_ref[i], v, v[0:1]).astype(o_ref.dtype)
        lengths = jnp.where(lane == i, len_ref[i].astype(jnp.float32), lengths)
    o_ref[OWN * SLOTS :, :] = lengths.astype(o_ref.dtype)


def fill(passages, lengths):
    return pl.pallas_call(
        fill_kernel,
        out_shape=jax.ShapeDtypeStruct((OWN * SLOTS + 16, WIDTH), passages.dtype),
        in_specs=[pl.BlockSpec(memory_space=pltpu.SMEM), pl.BlockSpec(memory_space=pltpu.VMEM)],
        out_specs=pl.BlockSpec(memory_space=pltpu.VMEM),
    )(lengths, passages)


def merge(values, sublane):
    step = 1
    while len(values) > 1:
        low = (sublane & step) == 0
        joined = []
        for a, b in zip(values[0::2], values[1::2]):
            kept, moved = jnp.where(low, a, b), jnp.where(low, b, a)
            joined.append(jnp.maximum(kept, pltpu.roll(moved, step, 0)))
        values = joined
        step *= 2
    return values[0]


def best_dots(w_ref, p_ref, m_ref, s_ref, unit_ref, turns, *acc):
    acc = (acc[:DEPTH], acc[DEPTH:])
    m_ref[...] = jnp.full_like(m_ref, LOWEST)
    nothing = jnp.zeros((16, 128), jnp.bfloat16)

    def push(g):
        for u in range(2):
            pltpu.matmul_push_rhs(w_ref[g * 2 + u], 0, u, transpose=True)

    def issue(unit, j, fresh=False):
        slots = p_ref[pl.ds(pl.multiple_of(unit, 16), 16), :]
        lhs = jnp.concatenate(
            [
                jnp.concatenate([slots, nothing], axis=1),
                jnp.concatenate([nothing, slots], axis=1),
            ],
            axis=0,
        )
        for u in range(2):
            pltpu.matmul_acc_lhs(acc[u][j], lhs, load_staged_rhs=0 if fresh else None)

    def take(unit, j):
        p = lax.shift_right_logical(unit, 7)
        for u in range(2):
            d = pltpu.matmul_pop(acc[u][j])
            for half in range(2):
                top = jnp.maximum(d[16 * half : 16 * half + 8], d[16 * half + 8 : 16 * half + 16])
                m_ref[p, 2 * u + half] = jnp.maximum(m_ref[p, 2 * u + half], top)

    push(0)
    for j in range(DEPTH):
        issue(unit_ref[j], j, fresh=j == 0)

    def group(g, carry):
        push(jnp.minimum(g + 1, 7))

        def turn(t, c):
            for j in range(DEPTH):
                take(unit_ref[t * DEPTH + j], j)
                issue(unit_ref[t * DEPTH + DEPTH + j], j)
            return c

        lax.fori_loop(0, turns - 1, turn, 0)
        last = (turns - 1) * DEPTH
        for j in range(DEPTH):
            take(unit_ref[last + j], j)
            issue(unit_ref[j], j, fresh=j == 0)
        sublane = lax.broadcasted_iota(jnp.int32, (8, 256), 0)
        lowest = jnp.full((8, 256), LOWEST, jnp.float32)
        for o in range(4):
            total = None
            for b in range(4):
                top = merge([m_ref[8 * o + i, b] for i in range(8)], sublane)
                for i in range(8):
                    m_ref[8 * o + i, b] = lowest
                total = top if total is None else total + top
            s_ref[g, 8 * o : 8 * o + 8, :] = total
        return carry

    lax.fori_loop(0, 8, group, 0)
    for u in range(2):
        for j in range(DEPTH):
            m_ref[0, 0] = pltpu.matmul_pop(acc[u][j])[0:8]


def score_kernel(info_ref, *refs):
    rows, pieces, out_ref = refs[:8], refs[8:12], refs[12]
    w_ref, p_ref, m_ref, s_ref, unit_ref = refs[13:]
    z, yhi, core, x, ylo = (info_ref[i] for i in range(5))
    mate = 2 - ylo

    for kind in range(2):

        @pl.when(core == kind)
        def _():
            for a in range(8):
                for j in range(4):
                    same = (a < 4) == (kind == 0)
                    dz, dy = (a % 4, j) if same else (j, a % 4)
                    h = {0: 0, 3: 1}.get(dy, (mate != dy).astype(jnp.int32))
                    half = 128 * (dy in (1, 2))
                    w_ref[(dz * 2 + h) * 2 + a // 4, :, half : half + 128] = rows[a][j]

    count = jnp.int32(0)
    for m in range(4):
        from_x = lax.rem(x + 4 - SHIFTS[m], 4)
        p_ref[pl.ds(pl.multiple_of(from_x * 1024, 1024), 1024), :] = pieces[m][0:1024, :]
        lengths = pieces[m][1024:1040, :].astype(jnp.float32)[0:8].astype(jnp.int32)
        units = lax.shift_right_logical(lengths + 15, 4)
        for i in range(OWN):
            for n in range(8):
                unit_ref[count + n] = from_x * 1024 + i * SLOTS + n * 16
            count = count + units[0, i]
    for i in range(2 * DEPTH):
        unit_ref[count + i] = unit_ref[0]
    turns = lax.div(count + DEPTH - 1, DEPTH)

    pl.run_scoped(
        functools.partial(best_dots, w_ref, p_ref, m_ref, s_ref, unit_ref, turns),
        *[pltpu.ACC(u)((32, 256), jnp.float32) for u in range(2) for _ in range(DEPTH)],
    )

    lane = lax.broadcasted_iota(jnp.int32, (32, 256), 1)
    row = lax.broadcasted_iota(jnp.int32, (32, 256), 0)
    pick = jnp.where(lane // 8 == row, 1.0 / 32, 0.0).astype(jnp.bfloat16)
    rest = s_ref[...].reshape(256, 256)
    parts = []
    for _ in range(3):
        parts.append(rest.astype(jnp.bfloat16))
        rest = rest - parts[-1].astype(jnp.float32)

    def add_up(acc):
        for part in parts:
            pltpu.matmul_push_rhs(part, 0, 0, transpose=True)
            pltpu.matmul_acc_lhs(acc, pick, load_staged_rhs=0)
        return pltpu.matmul_pop(acc)

    r = pl.run_scoped(add_up, pltpu.ACC(0)((32, 256), jnp.float32))
    for g in range(8):
        c = r[:, 32 * g : 32 * g + 32]
        place = lax.rem(z + 4 - SHIFTS[g // 2], 4) * 2 + (yhi if g % 2 == 0 else 1 - yhi)
        out_ref[place] = jnp.concatenate([c[0:8], c[8:16], c[16:24], c[24:32]], axis=1)


def score(info, rows, pieces):
    return pl.pallas_call(
        score_kernel,
        out_shape=jax.ShapeDtypeStruct((8, 8, 128), jnp.float32),
        in_specs=[pl.BlockSpec(memory_space=pltpu.SMEM)]
        + [pl.BlockSpec(memory_space=pltpu.VMEM)] * 12,
        out_specs=pl.BlockSpec(memory_space=pltpu.VMEM),
        scratch_shapes=[
            pltpu.VMEM((16, 256, 256), jnp.bfloat16),
            pltpu.VMEM((4096, 128), jnp.bfloat16),
            pltpu.VMEM((32, 4, 8, 256), jnp.float32),
            pltpu.VMEM((8, 32, 256), jnp.float32),
            pltpu.SMEM((256 + 2 * DEPTH,), jnp.int32),
        ],
        compiler_params=pltpu.CompilerParams(vmem_limit_bytes=32 << 20),
    )(info, *rows, *pieces)


def place_kernel(r_ref, o_ref):
    for g in range(4):
        o_ref[8 * g : 8 * g + 8, :] = jnp.concatenate(
            [r_ref[s][:, 32 * g : 32 * g + 32] for s in range(8)], axis=1
        )


def place(received):
    return pl.pallas_call(
        place_kernel,
        out_shape=jax.ShapeDtypeStruct((32, 256), jnp.float32),
        in_specs=[pl.BlockSpec(memory_space=pltpu.VMEM)],
        out_specs=pl.BlockSpec(memory_space=pltpu.VMEM),
    )(received)


def per_device(queries, passages, lengths):
    own = queries.reshape(256, 128)
    info = jnp.stack([lax.axis_index(name) for name in ("z", "yhi", "core", "x", "ylo")]).astype(jnp.int32)

    near = [own] + [lax.ppermute(own, PLANE, along(True, k)) for k in SHIFTS[1:]]
    filled = fill(passages, lengths)
    moved = [filled] + [on_x(filled, k) for k in SHIFTS[1:]]
    block = jnp.stack(near)
    mine = [block] + [lax.ppermute(block, PLANE, along(False, k)) for k in SHIFTS[1:]]
    other = [to_core(v) for v in mine]
    terms = score(info, mine + other, moved)
    received = lax.all_to_all(terms, ("z", "yhi"), 0, 0, tiled=True)
    return place(received)


def solution(mesh):
    fine = Mesh(mesh.devices.reshape(SIZES), NAMES)
    corpus = ("z", "yhi", "x")
    query = ("ylo", "core")
    return jax.shard_map(
        per_device,
        mesh=fine,
        in_specs=(P(corpus, query, None), P(query + corpus, None, None), P(query + corpus)),
        out_specs=P(corpus, query),
        check_vma=False,
    )
```

time: 59.6 us -> 57.6 us (0.966); the launches traced: 59.1 us -> 58.1 us
  Pallas kernels: 22 us -> 17.1 us
  blocking collectives: 13.4 us -> 17.3 us
    pallas_call x1, Pallas kernels: 18.9 us -> 13.9 us  [score(): pl.pallas_call(score_kernel, out_shape=jax.ShapeDtypeStruct((8, 8, 128),...]
    all_to_all x1, blocking collectives: 13.4 us -> 17.3 us  [per_device(): received = lax.all_to_all(terms, ('z', 'yhi'), 0, 0, tiled=True)]
where the time goes in v3:
time: 57.6 us; the launch traced here: 58.1 us
  starting transfers between devices  18.7 us (32%)
  blocking collectives  17.3 us (30%)
  Pallas kernels  17.1 us (30%)
  waiting for transfers between devices  4.73 us (8%)
    all_to_all x1, blocking collectives, per_device(): received = lax.all_to_all(terms, ('z', 'yhi'), 0, 0, tiled=True)  17.3 us
    pallas_call x1, Pallas kernels, score(): pl.pallas_call(score_kernel, out_shape=jax.ShapeDtypeStruct((8, 8, 128),...  13.9 us
    ppermute x3, starting transfers between devices, on_x(): return lax.ppermute(v, 'x', [(i, (i + shift) % 4) for i in range(4)])  6.5 us
    ppermute x3, starting transfers between devices, per_device(): lax.ppermute(block, PLANE, along(False, k))  5.98 us
    ppermute x3, starting transfers between devices, per_device(): lax.ppermute(own, PLANE, along(True, k))  5.3 us
    ppermute x3, waiting for transfers between devices, on_x(): return lax.ppermute(v, 'x', [(i, (i + shift) % 4) for i in range(4)])  4.18 us
    pallas_call x1, Pallas kernels, fill(): pl.pallas_call(fill_kernel, out_shape=jax.ShapeDtypeStruct((OWN * SLOTS +...  1.73 us
    pallas_call x1, Pallas kernels, place(): pl.pallas_call(place_kernel, out_shape=jax.ShapeDtypeStruct((32, 256), jn...  1.46 us
  transfers between devices with their start and end apart: 13, of which 5 were waited for; matrix products, arithmetic and copies ran while one was open for 0% of the time, Pallas kernels for 3%

profile of v3, /device:TPU:0, one launch (start us, length us, event | category | flops | bytes accessed | tf_op | source)
XLA Modules:
  0.0 58.1 jit_solution(9558184683864029641)
XLA Ops:
  0.0 0.0 copy-start.1
  0.0 3.3 %collective-permute-start.2 = (bf16[256,128]{1,0:T(8,128)(2,1)}, bf16[256,128]{1,0:T(8,128)(2,1)S(1)}, u32[]{:S(2)}, u32[]{:S(2)}) collective-permute-start(bf16[256,128]{1,0:T(8,128)(2,1)} %bitcast.10), channel_id=1, source_target_pairs={{0,4},{4,0},{8,12},{12,8},{16,20},{20,16},{24,28},{28,24},{32,48},... | collective-permute-start | bytes 196616 | tf_op jit(solution)/shard_map/ppermute | solution.py:247
  3.3 1.1 %collective-permute-start.1 = (bf16[256,128]{1,0:T(8,128)(2,1)}, bf16[256,128]{1,0:T(8,128)(2,1)S(1)}, u32[]{:S(2)}, u32[]{:S(2)}) collective-permute-start(bf16[256,128]{1,0:T(8,128)(2,1)} %bitcast.11), channel_id=1, source_target_pairs={{0,68},{4,64},{8,76},{12,72},{16,84},{20,80},{24,92},{28,88},{32,5... | collective-permute-start | bytes 196616 | tf_op jit(solution)/shard_map/ppermute | solution.py:247
  4.3 1.0 %collective-permute-start = (bf16[256,128]{1,0:T(8,128)(2,1)}, bf16[256,128]{1,0:T(8,128)(2,1)S(1)}, u32[]{:S(2)}, u32[]{:S(2)}) collective-permute-start(bf16[256,128]{1,0:T(8,128)(2,1)} %bitcast.12), channel_id=1, source_target_pairs={{0,64},{4,68},{8,72},{12,76},{16,80},{20,84},{24,88},{28,92},{32,4... | collective-permute-start | bytes 196616 | tf_op jit(solution)/shard_map/ppermute | solution.py:247
  5.3 1.7 %shard_map.37.refs_8_ = bf16[1040,128]{1,0:T(8,128)(2,1)} custom-call(s32[8]{0:T(128)} %len_ref.1, bf16[8,128,128]{2,1,0:T(8,128)(2,1)} %p_ref.1), custom_call_target="tpu_custom_call" | custom-call | tf_op jit(solution)/shard_map/pallas_call | solution.py:64
  7.0 0.0 copy-start
  7.0 3.0 %collective-permute-start.12 = (bf16[1040,128]{1,0:T(8,128)(2,1)}, bf16[1040,128]{1,0:T(8,128)(2,1)S(1)}, u32[]{:S(2)}, u32[]{:S(2)}) collective-permute-start(bf16[1040,128]{1,0:T(8,128)(2,1)} %shard_map.37.refs_8_), channel_id=1, source_target_pairs={{0,2},{1,3},{2,0},{3,1},{4,6},{5,7},{6,4},{7,5},{8,10},{9,11},{10,... | collective-permute-start | bytes 798728 | tf_op jit(solution)/shard_map/ppermute | solution.py:49
  10.1 1.1 %collective-permute-start.11 = (bf16[1040,128]{1,0:T(8,128)(2,1)}, bf16[1040,128]{1,0:T(8,128)(2,1)S(1)}, u32[]{:S(2)}, u32[]{:S(2)}) collective-permute-start(bf16[1040,128]{1,0:T(8,128)(2,1)} %shard_map.37.refs_8_), channel_id=1, source_target_pairs={{0,3},{1,0},{2,1},{3,2},{4,7},{5,4},{6,5},{7,6},{8,11},{9,8},{10,9... | collective-permute-start | bytes 798728 | tf_op jit(solution)/shard_map/ppermute | solution.py:49
  11.2 0.0 collective-permute-done.2
  11.2 0.0 collective-permute-done.1
  11.2 0.0 collective-permute-done
  11.2 0.0 copy-done.1
  11.3 4.0 %collective-permute-start.5 = (bf16[4,256,128]{2,1,0:T(8,128)(2,1)S(1)}, bf16[4,256,128]{2,1,0:T(8,128)(2,1)S(1)}, u32[]{:S(2)}, u32[]{:S(2)}) collective-permute-start(bf16[4,256,128]{2,1,0:T(8,128)(2,1)S(1)} %pad_maximum_fusion.refs_0_), channel_id=1, source_target_pairs={{0,16},{4,20},{8,24},{12,28},{16,0},{20,4},{24,8},{28,12},{32,36},... | collective-permute-start | bytes 786440 | tf_op jit(solution)/shard_map/ppermute | solution.py:251
  15.2 0.7 %collective-permute-start.4 = (bf16[4,256,128]{2,1,0:T(8,128)(2,1)S(1)}, bf16[4,256,128]{2,1,0:T(8,128)(2,1)S(1)}, u32[]{:S(2)}, u32[]{:S(2)}) collective-permute-start(bf16[4,256,128]{2,1,0:T(8,128)(2,1)S(1)} %pad_maximum_fusion.refs_0_), channel_id=1, source_target_pairs={{0,24},{4,28},{8,0},{12,4},{16,8},{20,12},{24,16},{28,20},{32,100}... | collective-permute-start | bytes 786440 | tf_op jit(solution)/shard_map/ppermute | solution.py:251
  15.9 1.3 %collective-permute-start.3 = (bf16[4,256,128]{2,1,0:T(8,128)(2,1)S(1)}, bf16[4,256,128]{2,1,0:T(8,128)(2,1)S(1)}, u32[]{:S(2)}, u32[]{:S(2)}) collective-permute-start(bf16[4,256,128]{2,1,0:T(8,128)(2,1)S(1)} %pad_maximum_fusion.refs_0_), channel_id=1, source_target_pairs={{0,8},{4,12},{8,16},{12,20},{16,24},{20,28},{24,0},{28,4},{32,96},... | collective-permute-start | bytes 786440 | tf_op jit(solution)/shard_map/ppermute | solution.py:251
  17.3 0.0 collective-permute-done.12.refs_11_
  17.3 0.0 copy-done
  17.3 2.3 %collective-permute-start.10 = (bf16[1040,128]{1,0:T(8,128)(2,1)S(1)}, bf16[1040,128]{1,0:T(8,128)(2,1)S(1)}, u32[]{:S(2)}, u32[]{:S(2)}) collective-permute-start(bf16[1040,128]{1,0:T(8,128)(2,1)S(1)} %copy-done), channel_id=1, source_target_pairs={{0,1},{1,2},{2,3},{3,0},{4,5},{5,6},{6,7},{7,4},{8,9},{9,10},{10,1... | collective-permute-start | bytes 798728 | tf_op jit(solution)/shard_map/ppermute | solution.py:49
  19.6 3.0 %collective-permute-done.11.refs_10_ = bf16[1040,128]{1,0:T(8,128)(2,1)S(1)} collective-permute-done((bf16[1040,128]{1,0:T(8,128)(2,1)}, bf16[1040,128]{1,0:T(8,128)(2,1)S(1)}, u32[]{:S(2)}, u32[]{:S(2)}) %collective-permute-start.11) | collective-permute-done | bytes 266272 | tf_op jit(solution)/shard_map/ppermute | solution.py:49
  22.6 0.0 collective-permute-start.6
  22.6 0.0 collective-permute-done.5.refs_3_
  22.6 0.5 collective-permute-start.9
  23.1 0.4 collective-permute-done.4.refs_2_
  23.4 0.0 collective-permute-start.8
  23.5 0.1 collective-permute-done.3.refs_1_
  23.5 0.4 collective-permute-start.7
  24.0 0.1 stack.35.info_ref
  24.0 1.2 %collective-permute-done.10.refs_9_ = bf16[1040,128]{1,0:T(8,128)(2,1)S(1)} collective-permute-done((bf16[1040,128]{1,0:T(8,128)(2,1)S(1)}, bf16[1040,128]{1,0:T(8,128)(2,1)S(1)}, u32[]{:S(2)}, u32[]{:S(2)}) %collective-permute-start.10) | collective-permute-done | bytes 266272 | tf_op jit(solution)/shard_map/ppermute | solution.py:49
  25.3 0.0 collective-permute-done.6.refs_4_
  25.3 0.0 collective-permute-done.9.refs_7_
  25.3 0.0 collective-permute-done.8.refs_6_
  25.3 0.1 collective-permute-done.7.refs_5_
  25.4 13.9 %shard_map.38 = f32[8,8,128]{2,1,0:T(8,128)S(1)} custom-call(s32[5]{0:T(128)S(1)} %stack.35.info_ref, bf16[4,256,128]{2,1,0:T(8,128)(2,1)S(1)} %pad_maximum_fusion.refs_0_, bf16[4,256,128]{2,1,0:T(8,128)(2,1)S(1)} %collective-permute-done.3.refs_1_, bf16[4,256,128]{2,1,0:T(8,128)(2,1)S(1)} %collective-permute-done.4.refs_2_, ...), custom_call_target="tpu_custom_call" | custom-call | tf_op jit(solution)/shard_map/pallas_call | solution.py:210
  39.3 17.3 %all_to_all.5.r_ref = f32[8,8,128]{2,1,0:T(8,128)} all-to-all(f32[8,8,128]{2,1,0:T(8,128)S(1)} %shard_map.38), channel_id=1, replica_groups=mesh['ylo'=2,'core'=2,'z'=4,'yhi'=2,'x'=4] {'z','yhi'}, dimensions={0} | all-to-all | bytes 65536 | tf_op jit(solution)/shard_map/all_to_all | solution.py:254
  56.6 1.5 %shard_map.39 = f32[32,256]{1,0:T(8,128)} custom-call(f32[8,8,128]{2,1,0:T(8,128)} %all_to_all.5.r_ref), custom_call_target="tpu_custom_call" | custom-call | tf_op jit(solution)/shard_map/pallas_call | solution.py:235
  (1 shorter events, 0.0 us)
Async XLA Ops:
  0.0 11.2 %copy-start.1 = (bf16[32,8,128]{2,1,0:T(8,128)(2,1)S(1)}, bf16[32,8,128]{2,1,0:T(8,128)(2,1)}, u32[]{:S(2)}) copy-start(bf16[32,8,128]{2,1,0:T(8,128)(2,1)} %param.3) | copy-start | bytes 196612
  0.0 11.2 %collective-permute-start.2 = (bf16[256,128]{1,0:T(8,128)(2,1)}, bf16[256,128]{1,0:T(8,128)(2,1)S(1)}, u32[]{:S(2)}, u32[]{:S(2)}) collective-permute-start(bf16[256,128]{1,0:T(8,128)(2,1)} %bitcast.10), channel_id=1, source_target_pairs={{0,4},{4,0},{8,12},{12,8},{16,20},{20,16},{24,28},{28,24},{32,48},... | collective-permute-start | bytes 196616 | tf_op jit(solution)/shard_map/ppermute | solution.py:247
  3.3 7.9 %collective-permute-start.1 = (bf16[256,128]{1,0:T(8,128)(2,1)}, bf16[256,128]{1,0:T(8,128)(2,1)S(1)}, u32[]{:S(2)}, u32[]{:S(2)}) collective-permute-start(bf16[256,128]{1,0:T(8,128)(2,1)} %bitcast.11), channel_id=1, source_target_pairs={{0,68},{4,64},{8,76},{12,72},{16,84},{20,80},{24,92},{28,88},{32,5... | collective-permute-start | bytes 196616 | tf_op jit(solution)/shard_map/ppermute | solution.py:247
  4.3 6.9 %collective-permute-start = (bf16[256,128]{1,0:T(8,128)(2,1)}, bf16[256,128]{1,0:T(8,128)(2,1)S(1)}, u32[]{:S(2)}, u32[]{:S(2)}) collective-permute-start(bf16[256,128]{1,0:T(8,128)(2,1)} %bitcast.12), channel_id=1, source_target_pairs={{0,64},{4,68},{8,72},{12,76},{16,80},{20,84},{24,88},{28,92},{32,4... | collective-permute-start | bytes 196616 | tf_op jit(solution)/shard_map/ppermute | solution.py:247
  7.0 10.2 %copy-start = (bf16[1040,128]{1,0:T(8,128)(2,1)S(1)}, bf16[1040,128]{1,0:T(8,128)(2,1)}, u32[]{:S(2)}) copy-start(bf16[1040,128]{1,0:T(8,128)(2,1)} %shard_map.37.refs_8_) | copy-start | bytes 798724
  7.0 10.2 %collective-permute-start.12 = (bf16[1040,128]{1,0:T(8,128)(2,1)}, bf16[1040,128]{1,0:T(8,128)(2,1)S(1)}, u32[]{:S(2)}, u32[]{:S(2)}) collective-permute-start(bf16[1040,128]{1,0:T(8,128)(2,1)} %shard_map.37.refs_8_), channel_id=1, source_target_pairs={{0,2},{1,3},{2,0},{3,1},{4,6},{5,7},{6,4},{7,5},{8,10},{9,11},{10,... | collective-permute-start | bytes 798728 | tf_op jit(solution)/shard_map/ppermute | solution.py:49
  10.1 12.5 %collective-permute-start.11 = (bf16[1040,128]{1,0:T(8,128)(2,1)}, bf16[1040,128]{1,0:T(8,128)(2,1)S(1)}, u32[]{:S(2)}, u32[]{:S(2)}) collective-permute-start(bf16[1040,128]{1,0:T(8,128)(2,1)} %shard_map.37.refs_8_), channel_id=1, source_target_pairs={{0,3},{1,0},{2,1},{3,2},{4,7},{5,4},{6,5},{7,6},{8,11},{9,8},{10,9... | collective-permute-start | bytes 798728 | tf_op jit(solution)/shard_map/ppermute | solution.py:49
  11.3 11.3 %collective-permute-start.5 = (bf16[4,256,128]{2,1,0:T(8,128)(2,1)S(1)}, bf16[4,256,128]{2,1,0:T(8,128)(2,1)S(1)}, u32[]{:S(2)}, u32[]{:S(2)}) collective-permute-start(bf16[4,256,128]{2,1,0:T(8,128)(2,1)S(1)} %pad_maximum_fusion.refs_0_), channel_id=1, source_target_pairs={{0,16},{4,20},{8,24},{12,28},{16,0},{20,4},{24,8},{28,12},{32,36},... | collective-permute-start | bytes 786440 | tf_op jit(solution)/shard_map/ppermute | solution.py:251
  15.2 8.2 %collective-permute-start.4 = (bf16[4,256,128]{2,1,0:T(8,128)(2,1)S(1)}, bf16[4,256,128]{2,1,0:T(8,128)(2,1)S(1)}, u32[]{:S(2)}, u32[]{:S(2)}) collective-permute-start(bf16[4,256,128]{2,1,0:T(8,128)(2,1)S(1)} %pad_maximum_fusion.refs_0_), channel_id=1, source_target_pairs={{0,24},{4,28},{8,0},{12,4},{16,8},{20,12},{24,16},{28,20},{32,100}... | collective-permute-start | bytes 786440 | tf_op jit(solution)/shard_map/ppermute | solution.py:251
  15.9 7.6 %collective-permute-start.3 = (bf16[4,256,128]{2,1,0:T(8,128)(2,1)S(1)}, bf16[4,256,128]{2,1,0:T(8,128)(2,1)S(1)}, u32[]{:S(2)}, u32[]{:S(2)}) collective-permute-start(bf16[4,256,128]{2,1,0:T(8,128)(2,1)S(1)} %pad_maximum_fusion.refs_0_), channel_id=1, source_target_pairs={{0,8},{4,12},{8,16},{12,20},{16,24},{20,28},{24,0},{28,4},{32,96},... | collective-permute-start | bytes 786440 | tf_op jit(solution)/shard_map/ppermute | solution.py:251
  17.3 8.0 %collective-permute-start.10 = (bf16[1040,128]{1,0:T(8,128)(2,1)S(1)}, bf16[1040,128]{1,0:T(8,128)(2,1)S(1)}, u32[]{:S(2)}, u32[]{:S(2)}) collective-permute-start(bf16[1040,128]{1,0:T(8,128)(2,1)S(1)} %copy-done), channel_id=1, source_target_pairs={{0,1},{1,2},{2,3},{3,0},{4,5},{5,6},{6,7},{7,4},{8,9},{9,10},{10,1... | collective-permute-start | bytes 798728 | tf_op jit(solution)/shard_map/ppermute | solution.py:49
  22.6 2.7 %collective-permute-start.6 = (bf16[4,256,128]{2,1,0:T(8,128)(2,1)S(1)}, bf16[4,256,128]{2,1,0:T(8,128)(2,1)S(1)}, u32[]{:S(2)}, u32[]{:S(2)}) collective-permute-start(bf16[4,256,128]{2,1,0:T(8,128)(2,1)S(1)} %pad_maximum_fusion.refs_0_), channel_id=1, source_target_pairs={{0,32},{32,0},{1,33},{33,1},{2,34},{34,2},{3,35},{35,3},{4,36},{36... | collective-permute-start | bytes 786440 | tf_op jit(solution)/shard_map/ppermute | solution.py:45
  22.6 2.7 %collective-permute-start.9 = (bf16[4,256,128]{2,1,0:T(8,128)(2,1)S(1)}, bf16[4,256,128]{2,1,0:T(8,128)(2,1)S(1)}, u32[]{:S(2)}, u32[]{:S(2)}) collective-permute-start(bf16[4,256,128]{2,1,0:T(8,128)(2,1)S(1)} %collective-permute-done.5.refs_3_), channel_id=1, source_target_pairs={{0,32},{32,0},{1,33},{33,1},{2,34},{34,2},{3,35},{35,3},{4,36},{36... | collective-permute-start | bytes 786440 | tf_op jit(solution)/shard_map/ppermute | solution.py:45
  23.4 1.8 %collective-permute-start.8 = (bf16[4,256,128]{2,1,0:T(8,128)(2,1)S(1)}, bf16[4,256,128]{2,1,0:T(8,128)(2,1)S(1)}, u32[]{:S(2)}, u32[]{:S(2)}) collective-permute-start(bf16[4,256,128]{2,1,0:T(8,128)(2,1)S(1)} %collective-permute-done.4.refs_2_), channel_id=1, source_target_pairs={{0,32},{32,0},{1,33},{33,1},{2,34},{34,2},{3,35},{35,3},{4,36},{36... | collective-permute-start | bytes 786440 | tf_op jit(solution)/shard_map/ppermute | solution.py:45
  23.5 1.8 %collective-permute-start.7 = (bf16[4,256,128]{2,1,0:T(8,128)(2,1)S(1)}, bf16[4,256,128]{2,1,0:T(8,128)(2,1)S(1)}, u32[]{:S(2)}, u32[]{:S(2)}) collective-permute-start(bf16[4,256,128]{2,1,0:T(8,128)(2,1)S(1)} %collective-permute-done.3.refs_1_), channel_id=1, source_target_pairs={{0,32},{32,0},{1,33},{33,1},{2,34},{34,2},{3,35},{35,3},{4,36},{36... | collective-permute-start | bytes 786440 | tf_op jit(solution)/shard_map/ppermute | solution.py:45

commit v4 on v3

--- a/solution.py
+++ b/solution.py
@@ -49,42 +49,15 @@
     return lax.ppermute(v, "x", [(i, (i + shift) % 4) for i in range(4)])
 
 
-def fill_kernel(len_ref, p_ref, o_ref):
-    slot = lax.broadcasted_iota(jnp.int32, (SLOTS, WIDTH), 0)
-    lane = lax.broadcasted_iota(jnp.int32, (16, WIDTH), 1)
-    lengths = jnp.zeros((16, WIDTH), jnp.float32)
-    for i in range(OWN):
-        v = p_ref[i].astype(jnp.float32)
-        o_ref[SLOTS * i : SLOTS * i + SLOTS, :] = jnp.where(slot < len_ref[i], v, v[0:1]).astype(o_ref.dtype)
-        lengths = jnp.where(lane == i, len_ref[i].astype(jnp.float32), lengths)
-    o_ref[OWN * SLOTS :, :] = lengths.astype(o_ref.dtype)
-
-
-def fill(passages, lengths):
-    return pl.pallas_call(
-        fill_kernel,
-        out_shape=jax.ShapeDtypeStruct((OWN * SLOTS + 16, WIDTH), passages.dtype),
-        in_specs=[pl.BlockSpec(memory_space=pltpu.SMEM), pl.BlockSpec(memory_space=pltpu.VMEM)],
-        out_specs=pl.BlockSpec(memory_space=pltpu.VMEM),
-    )(lengths, passages)
-
-
-def merge(values, sublane):
-    step = 1
-    while len(values) > 1:
-        low = (sublane & step) == 0
-        joined = []
-        for a, b in zip(values[0::2], values[1::2]):
-            kept, moved = jnp.where(low, a, b), jnp.where(low, b, a)
-            joined.append(jnp.maximum(kept, pltpu.roll(moved, step, 0)))
-        values = joined
-        step *= 2
-    return values[0]
+def with_lengths(passages, lengths):
+    tail = jnp.pad(lengths.astype(passages.dtype), (0, WIDTH - OWN))
+    return jnp.concatenate(
+        [passages.reshape(OWN * SLOTS, WIDTH), jnp.broadcast_to(tail, (16, WIDTH))], axis=0
+    )
 
 
 def best_dots(w_ref, p_ref, m_ref, s_ref, unit_ref, turns, *acc):
     acc = (acc[:DEPTH], acc[DEPTH:])
-    m_ref[...] = jnp.full_like(m_ref, LOWEST)
     nothing = jnp.zeros((16, 128), jnp.bfloat16)
 
     def push(g):
@@ -104,13 +77,19 @@
             pltpu.matmul_acc_lhs(acc[u][j], lhs, load_staged_rhs=0 if fresh else None)
 
     def take(unit, j):
-        p = lax.shift_right_logical(unit, 7)
+        at = lax.shift_right_logical(unit, 7)
+        begin = jnp.where(lax.bitwise_and(unit, 127) == 0, 32, at)
+        tops = []
+        held = [m_ref[b, begin] for b in range(8)]
         for u in range(2):
             d = pltpu.matmul_pop(acc[u][j])
             for half in range(2):
                 top = jnp.maximum(d[16 * half : 16 * half + 8], d[16 * half + 8 : 16 * half + 16])
-                m_ref[p, 2 * u + half] = jnp.maximum(m_ref[p, 2 * u + half], top)
-
+                tops += [top[:, 0:128], top[:, 128:256]]
+        for b in range(8):
+            m_ref[b, at] = jnp.maximum(held[b], tops[b])
+
+    m_ref[:, 32] = jnp.full((8, 8, 128), LOWEST, jnp.float32)
     push(0)
     for j in range(DEPTH):
         issue(unit_ref[j], j, fresh=j == 0)
@@ -129,22 +108,22 @@
         for j in range(DEPTH):
             take(unit_ref[last + j], j)
             issue(unit_ref[j], j, fresh=j == 0)
-        sublane = lax.broadcasted_iota(jnp.int32, (8, 256), 0)
-        lowest = jnp.full((8, 256), LOWEST, jnp.float32)
+        rows_ref = m_ref.reshape(8, 264, 128)
         for o in range(4):
-            total = None
-            for b in range(4):
-                top = merge([m_ref[8 * o + i, b] for i in range(8)], sublane)
-                for i in range(8):
-                    m_ref[8 * o + i, b] = lowest
-                total = top if total is None else total + top
-            s_ref[g, 8 * o : 8 * o + 8, :] = total
+            for side in range(2):
+                total = None
+                for b in range(side, 8, 2):
+                    top = rows_ref[b, pl.ds(64 * o, 8, stride=8), :]
+                    for i in range(1, 8):
+                        top = jnp.maximum(top, rows_ref[b, pl.ds(64 * o + i, 8, stride=8), :])
+                    total = top if total is None else total + top
+                s_ref[g, 8 * o : 8 * o + 8, 128 * side : 128 * side + 128] = total
         return carry
 
     lax.fori_loop(0, 8, group, 0)
     for u in range(2):
         for j in range(DEPTH):
-            m_ref[0, 0] = pltpu.matmul_pop(acc[u][j])[0:8]
+            m_ref[0, 0] = pltpu.matmul_pop(acc[u][j])[0:8, 0:128]
 
 
 def score_kernel(info_ref, *refs):
@@ -175,8 +154,13 @@
             for n in range(8):
                 unit_ref[count + n] = from_x * 1024 + i * SLOTS + n * 16
             count = count + units[0, i]
-    for i in range(2 * DEPTH):
-        unit_ref[count + i] = unit_ref[0]
+            used = units[0, i]
+            last = pl.multiple_of(from_x * 1024 + i * SLOTS + (used - 1) * 16, 16)
+            both = p_ref[pl.ds(last, 16), :].astype(jnp.float32)
+            second = jnp.where(lengths[0, i] == used * 16, both[8:16], both[0:8])
+            p_ref[pl.ds(last, 16), :] = jnp.concatenate([both[0:8], second], axis=0).astype(p_ref.dtype)
+    for i in range(DEPTH):
+        unit_ref[count + i] = unit_ref[count - 1]
     turns = lax.div(count + DEPTH - 1, DEPTH)
 
     pl.run_scoped(
@@ -216,9 +200,9 @@
         scratch_shapes=[
             pltpu.VMEM((16, 256, 256), jnp.bfloat16),
             pltpu.VMEM((4096, 128), jnp.bfloat16),
-            pltpu.VMEM((32, 4, 8, 256), jnp.float32),
+            pltpu.VMEM((8, 33, 8, 128), jnp.float32),
             pltpu.VMEM((8, 32, 256), jnp.float32),
-            pltpu.SMEM((256 + 2 * DEPTH,), jnp.int32),
+            pltpu.SMEM((256 + DEPTH,), jnp.int32),
         ],
         compiler_params=pltpu.CompilerParams(vmem_limit_bytes=32 << 20),
     )(info, *rows, *pieces)
@@ -245,7 +229,7 @@
     info = jnp.stack([lax.axis_index(name) for name in ("z", "yhi", "core", "x", "ylo")]).astype(jnp.int32)
 
     near = [own] + [lax.ppermute(own, PLANE, along(True, k)) for k in SHIFTS[1:]]
-    filled = fill(passages, lengths)
+    filled = with_lengths(passages, lengths)
     moved = [filled] + [on_x(filled, k) for k in SHIFTS[1:]]
     block = jnp.stack(near)
     mine = [block] + [lax.ppermute(block, PLANE, along(False, k)) for k in SHIFTS[1:]]

time: 57.6 us -> 56.8 us (0.986)
  the two profiles are of different devices: /device:TPU:0 before, /device:TPU:8 now
where the time goes in v4:
time: 56.8 us; the launch traced here: 56.1 us
  Pallas kernels  19.1 us (34%)
  starting transfers between devices  17.4 us (31%)
  blocking collectives  11.9 us (21%)
  waiting for transfers between devices  6.55 us (12%)
  other arithmetic  1.04 us (2%)
    pallas_call x1, Pallas kernels, score(): pl.pallas_call(score_kernel, out_shape=jax.ShapeDtypeStruct((8, 8, 128),...  17.6 us
    all_to_all x1, blocking collectives, per_device(): received = lax.all_to_all(terms, ('z', 'yhi'), 0, 0, tiled=True)  11.9 us
    ppermute x3, waiting for transfers between devices, on_x(): return lax.ppermute(v, 'x', [(i, (i + shift) % 4) for i in range(4)])  6.53 us
    ppermute x3, starting transfers between devices, on_x(): return lax.ppermute(v, 'x', [(i, (i + shift) % 4) for i in range(4)])  6.08 us
    ppermute x3, starting transfers between devices, per_device(): lax.ppermute(block, PLANE, along(False, k))  5.98 us
    ppermute x3, starting transfers between devices, per_device(): lax.ppermute(own, PLANE, along(True, k))  4.32 us
    pallas_call x1, Pallas kernels, place(): pl.pallas_call(place_kernel, out_shape=jax.ShapeDtypeStruct((32, 256), jn...  1.46 us
  transfers between devices with their start and end apart: 13, of which 3 were waited for; matrix products, arithmetic and copies ran while one was open for 2% of the time, Pallas kernels for 0%

profile of v4, /device:TPU:8, one launch (start us, length us, event | category | flops | bytes accessed | tf_op | source)
XLA Modules:
  0.0 56.1 jit_solution(8290652769348754294)
XLA Ops:
  0.0 0.0 copy-start.1
  0.0 2.3 %collective-permute-start.2 = (bf16[256,128]{1,0:T(8,128)(2,1)}, bf16[256,128]{1,0:T(8,128)(2,1)S(1)}, u32[]{:S(2)}, u32[]{:S(2)}) collective-permute-start(bf16[256,128]{1,0:T(8,128)(2,1)} %bitcast.12), channel_id=1, source_target_pairs={{0,4},{4,0},{8,12},{12,8},{16,20},{20,16},{24,28},{28,24},{32,48},... | collective-permute-start | bytes 196616 | tf_op jit(solution)/shard_map/ppermute | solution.py:231
  2.3 1.3 %collective-permute-start.1 = (bf16[256,128]{1,0:T(8,128)(2,1)}, bf16[256,128]{1,0:T(8,128)(2,1)S(1)}, u32[]{:S(2)}, u32[]{:S(2)}) collective-permute-start(bf16[256,128]{1,0:T(8,128)(2,1)} %bitcast.13), channel_id=1, source_target_pairs={{0,68},{4,64},{8,76},{12,72},{16,84},{20,80},{24,92},{28,88},{32,5... | collective-permute-start | bytes 196616 | tf_op jit(solution)/shard_map/ppermute | solution.py:231
  3.6 0.7 %collective-permute-start = (bf16[256,128]{1,0:T(8,128)(2,1)}, bf16[256,128]{1,0:T(8,128)(2,1)S(1)}, u32[]{:S(2)}, u32[]{:S(2)}) collective-permute-start(bf16[256,128]{1,0:T(8,128)(2,1)} %bitcast.14), channel_id=1, source_target_pairs={{0,64},{4,68},{8,72},{12,76},{16,80},{20,84},{24,88},{28,92},{32,4... | collective-permute-start | bytes 196616 | tf_op jit(solution)/shard_map/ppermute | solution.py:231
  4.3 0.0 copy-done.1
  4.3 0.0 copy-start
  4.4 1.0 %pad_maximum_fusion.refs_8_ = bf16[1040,128]{1,0:T(8,128)(2,1)S(1)} fusion(bf16[16,128]{1,0:T(8,128)(2,1)S(1)} %broadcast_in_dim.3, bf16[1024,128]{1,0:T(8,128)(2,1)} %bitcast.11), kind=kLoop, calls=%fused_computation | loop fusion | flops 532480 | bytes 532480 | tf_op jit(solution)/shard_map/concatenate | solution.py:54
  5.4 3.1 %collective-permute-start.12 = (bf16[1040,128]{1,0:T(8,128)(2,1)S(1)}, bf16[1040,128]{1,0:T(8,128)(2,1)S(1)}, u32[]{:S(2)}, u32[]{:S(2)}) collective-permute-start(bf16[1040,128]{1,0:T(8,128)(2,1)S(1)} %pad_maximum_fusion.refs_8_), channel_id=1, source_target_pairs={{0,2},{1,3},{2,0},{3,1},{4,6},{5,7},{6,4},{7,5},{8,10},{9,11},{10,... | collective-permute-start | bytes 798728 | tf_op jit(solution)/shard_map/ppermute | solution.py:49
  8.5 1.1 %collective-permute-start.11 = (bf16[1040,128]{1,0:T(8,128)(2,1)S(1)}, bf16[1040,128]{1,0:T(8,128)(2,1)S(1)}, u32[]{:S(2)}, u32[]{:S(2)}) collective-permute-start(bf16[1040,128]{1,0:T(8,128)(2,1)S(1)} %pad_maximum_fusion.refs_8_), channel_id=1, source_target_pairs={{0,3},{1,0},{2,1},{3,2},{4,7},{5,4},{6,5},{7,6},{8,11},{9,8},{10,9... | collective-permute-start | bytes 798728 | tf_op jit(solution)/shard_map/ppermute | solution.py:49
  9.6 0.0 collective-permute-done.2
  9.6 0.0 collective-permute-done.1
  9.6 0.0 collective-permute-done
  9.6 0.0 copy-done
  9.7 4.0 %collective-permute-start.5 = (bf16[4,256,128]{2,1,0:T(8,128)(2,1)S(1)}, bf16[4,256,128]{2,1,0:T(8,128)(2,1)S(1)}, u32[]{:S(2)}, u32[]{:S(2)}) collective-permute-start(bf16[4,256,128]{2,1,0:T(8,128)(2,1)S(1)} %pad_maximum_fusion.1.refs_0_), channel_id=1, source_target_pairs={{0,16},{4,20},{8,24},{12,28},{16,0},{20,4},{24,8},{28,12},{32,36},... | collective-permute-start | bytes 786440 | tf_op jit(solution)/shard_map/ppermute | solution.py:235
  13.6 0.7 %collective-permute-start.4 = (bf16[4,256,128]{2,1,0:T(8,128)(2,1)S(1)}, bf16[4,256,128]{2,1,0:T(8,128)(2,1)S(1)}, u32[]{:S(2)}, u32[]{:S(2)}) collective-permute-start(bf16[4,256,128]{2,1,0:T(8,128)(2,1)S(1)} %pad_maximum_fusion.1.refs_0_), channel_id=1, source_target_pairs={{0,24},{4,28},{8,0},{12,4},{16,8},{20,12},{24,16},{28,20},{32,100}... | collective-permute-start | bytes 786440 | tf_op jit(solution)/shard_map/ppermute | solution.py:235
  14.3 1.3 %collective-permute-start.3 = (bf16[4,256,128]{2,1,0:T(8,128)(2,1)S(1)}, bf16[4,256,128]{2,1,0:T(8,128)(2,1)S(1)}, u32[]{:S(2)}, u32[]{:S(2)}) collective-permute-start(bf16[4,256,128]{2,1,0:T(8,128)(2,1)S(1)} %pad_maximum_fusion.1.refs_0_), channel_id=1, source_target_pairs={{0,8},{4,12},{8,16},{12,20},{16,24},{20,28},{24,0},{28,4},{32,96},... | collective-permute-start | bytes 786440 | tf_op jit(solution)/shard_map/ppermute | solution.py:235
  15.7 0.2 collective-permute-done.12.refs_11_
  15.8 1.8 %collective-permute-start.10 = (bf16[1040,128]{1,0:T(8,128)(2,1)S(1)}, bf16[1040,128]{1,0:T(8,128)(2,1)S(1)}, u32[]{:S(2)}, u32[]{:S(2)}) collective-permute-start(bf16[1040,128]{1,0:T(8,128)(2,1)S(1)} %pad_maximum_fusion.refs_8_), channel_id=1, source_target_pairs={{0,1},{1,2},{2,3},{3,0},{4,5},{5,6},{6,7},{7,4},{8,9},{9,10},{10,1... | collective-permute-start | bytes 798728 | tf_op jit(solution)/shard_map/ppermute | solution.py:49
  17.7 4.0 %collective-permute-done.11.refs_10_ = bf16[1040,128]{1,0:T(8,128)(2,1)S(1)} collective-permute-done((bf16[1040,128]{1,0:T(8,128)(2,1)S(1)}, bf16[1040,128]{1,0:T(8,128)(2,1)S(1)}, u32[]{:S(2)}, u32[]{:S(2)}) %collective-permute-start.11) | collective-permute-done | bytes 266272 | tf_op jit(solution)/shard_map/ppermute | solution.py:49
  21.7 0.0 collective-permute-start.6
  21.7 0.0 collective-permute-done.5.refs_3_
  21.7 0.5 collective-permute-start.9
  22.2 0.0 collective-permute-done.4.refs_2_
  22.2 0.1 collective-permute-start.8
  22.3 0.0 collective-permute-done.3.refs_1_
  22.3 0.4 collective-permute-start.7
  22.7 0.1 stack.35.info_ref
  22.8 2.4 %collective-permute-done.10.refs_9_ = bf16[1040,128]{1,0:T(8,128)(2,1)S(1)} collective-permute-done((bf16[1040,128]{1,0:T(8,128)(2,1)S(1)}, bf16[1040,128]{1,0:T(8,128)(2,1)S(1)}, u32[]{:S(2)}, u32[]{:S(2)}) %collective-permute-start.10) | collective-permute-done | bytes 266272 | tf_op jit(solution)/shard_map/ppermute | solution.py:49
  25.1 0.0 collective-permute-done.6.refs_4_
  25.1 0.0 collective-permute-done.9.refs_7_
  25.1 0.0 collective-permute-done.8.refs_6_
  25.2 0.0 collective-permute-done.7.refs_5_
  25.2 17.6 %shard_map.37 = f32[8,8,128]{2,1,0:T(8,128)S(1)} custom-call(s32[5]{0:T(128)S(1)} %stack.35.info_ref, bf16[4,256,128]{2,1,0:T(8,128)(2,1)S(1)} %pad_maximum_fusion.1.refs_0_, bf16[4,256,128]{2,1,0:T(8,128)(2,1)S(1)} %collective-permute-done.3.refs_1_, bf16[4,256,128]{2,1,0:T(8,128)(2,1)S(1)} %collective-permute-done.4.refs_2_, ...), custom_call_target="tpu_custom_call" | custom-call | tf_op jit(solution)/shard_map/pallas_call | solution.py:194
  42.8 11.9 %all_to_all.5.r_ref = f32[8,8,128]{2,1,0:T(8,128)} all-to-all(f32[8,8,128]{2,1,0:T(8,128)S(1)} %shard_map.37), channel_id=1, replica_groups=mesh['ylo'=2,'core'=2,'z'=4,'yhi'=2,'x'=4] {'z','yhi'}, dimensions={0} | all-to-all | bytes 65536 | tf_op jit(solution)/shard_map/all_to_all | solution.py:238
  54.7 1.5 %shard_map.38 = f32[32,256]{1,0:T(8,128)} custom-call(f32[8,8,128]{2,1,0:T(8,128)} %all_to_all.5.r_ref), custom_call_target="tpu_custom_call" | custom-call | tf_op jit(solution)/shard_map/pallas_call | solution.py:219
  (4 shorter events, 0.1 us)
Async XLA Ops:
  0.0 4.3 %copy-start.1 = (s32[8]{0:T(128)S(1)}, s32[8]{0:T(128)}, u32[]{:S(2)}) copy-start(s32[8]{0:T(128)} %param.5) | copy-start | bytes 100
  0.0 9.6 %collective-permute-start.2 = (bf16[256,128]{1,0:T(8,128)(2,1)}, bf16[256,128]{1,0:T(8,128)(2,1)S(1)}, u32[]{:S(2)}, u32[]{:S(2)}) collective-permute-start(bf16[256,128]{1,0:T(8,128)(2,1)} %bitcast.12), channel_id=1, source_target_pairs={{0,4},{4,0},{8,12},{12,8},{16,20},{20,16},{24,28},{28,24},{32,48},... | collective-permute-start | bytes 196616 | tf_op jit(solution)/shard_map/ppermute | solution.py:231
  2.3 7.3 %collective-permute-start.1 = (bf16[256,128]{1,0:T(8,128)(2,1)}, bf16[256,128]{1,0:T(8,128)(2,1)S(1)}, u32[]{:S(2)}, u32[]{:S(2)}) collective-permute-start(bf16[256,128]{1,0:T(8,128)(2,1)} %bitcast.13), channel_id=1, source_target_pairs={{0,68},{4,64},{8,76},{12,72},{16,84},{20,80},{24,92},{28,88},{32,5... | collective-permute-start | bytes 196616 | tf_op jit(solution)/shard_map/ppermute | solution.py:231
  3.6 6.0 %collective-permute-start = (bf16[256,128]{1,0:T(8,128)(2,1)}, bf16[256,128]{1,0:T(8,128)(2,1)S(1)}, u32[]{:S(2)}, u32[]{:S(2)}) collective-permute-start(bf16[256,128]{1,0:T(8,128)(2,1)} %bitcast.14), channel_id=1, source_target_pairs={{0,64},{4,68},{8,72},{12,76},{16,80},{20,84},{24,88},{28,92},{32,4... | collective-permute-start | bytes 196616 | tf_op jit(solution)/shard_map/ppermute | solution.py:231
  4.3 5.3 %copy-start = (bf16[32,8,128]{2,1,0:T(8,128)(2,1)S(1)}, bf16[32,8,128]{2,1,0:T(8,128)(2,1)}, u32[]{:S(2)}) copy-start(bf16[32,8,128]{2,1,0:T(8,128)(2,1)} %param.3) | copy-start | bytes 196612
  5.4 10.5 %collective-permute-start.12 = (bf16[1040,128]{1,0:T(8,128)(2,1)S(1)}, bf16[1040,128]{1,0:T(8,128)(2,1)S(1)}, u32[]{:S(2)}, u32[]{:S(2)}) collective-permute-start(bf16[1040,128]{1,0:T(8,128)(2,1)S(1)} %pad_maximum_fusion.refs_8_), channel_id=1, source_target_pairs={{0,2},{1,3},{2,0},{3,1},{4,6},{5,7},{6,4},{7,5},{8,10},{9,11},{10,... | collective-permute-start | bytes 798728 | tf_op jit(solution)/shard_map/ppermute | solution.py:49
  8.5 13.2 %collective-permute-start.11 = (bf16[1040,128]{1,0:T(8,128)(2,1)S(1)}, bf16[1040,128]{1,0:T(8,128)(2,1)S(1)}, u32[]{:S(2)}, u32[]{:S(2)}) collective-permute-start(bf16[1040,128]{1,0:T(8,128)(2,1)S(1)} %pad_maximum_fusion.refs_8_), channel_id=1, source_target_pairs={{0,3},{1,0},{2,1},{3,2},{4,7},{5,4},{6,5},{7,6},{8,11},{9,8},{10,9... | collective-permute-start | bytes 798728 | tf_op jit(solution)/shard_map/ppermute | solution.py:49
  9.7 12.0 %collective-permute-start.5 = (bf16[4,256,128]{2,1,0:T(8,128)(2,1)S(1)}, bf16[4,256,128]{2,1,0:T(8,128)(2,1)S(1)}, u32[]{:S(2)}, u32[]{:S(2)}) collective-permute-start(bf16[4,256,128]{2,1,0:T(8,128)(2,1)S(1)} %pad_maximum_fusion.1.refs_0_), channel_id=1, source_target_pairs={{0,16},{4,20},{8,24},{12,28},{16,0},{20,4},{24,8},{28,12},{32,36},... | collective-permute-start | bytes 786440 | tf_op jit(solution)/shard_map/ppermute | solution.py:235
  13.6 8.5 %collective-permute-start.4 = (bf16[4,256,128]{2,1,0:T(8,128)(2,1)S(1)}, bf16[4,256,128]{2,1,0:T(8,128)(2,1)S(1)}, u32[]{:S(2)}, u32[]{:S(2)}) collective-permute-start(bf16[4,256,128]{2,1,0:T(8,128)(2,1)S(1)} %pad_maximum_fusion.1.refs_0_), channel_id=1, source_target_pairs={{0,24},{4,28},{8,0},{12,4},{16,8},{20,12},{24,16},{28,20},{32,100}... | collective-permute-start | bytes 786440 | tf_op jit(solution)/shard_map/ppermute | solution.py:235
  14.3 7.9 %collective-permute-start.3 = (bf16[4,256,128]{2,1,0:T(8,128)(2,1)S(1)}, bf16[4,256,128]{2,1,0:T(8,128)(2,1)S(1)}, u32[]{:S(2)}, u32[]{:S(2)}) collective-permute-start(bf16[4,256,128]{2,1,0:T(8,128)(2,1)S(1)} %pad_maximum_fusion.1.refs_0_), channel_id=1, source_target_pairs={{0,8},{4,12},{8,16},{12,20},{16,24},{20,28},{24,0},{28,4},{32,96},... | collective-permute-start | bytes 786440 | tf_op jit(solution)/shard_map/ppermute | solution.py:235
  15.8 9.3 %collective-permute-start.10 = (bf16[1040,128]{1,0:T(8,128)(2,1)S(1)}, bf16[1040,128]{1,0:T(8,128)(2,1)S(1)}, u32[]{:S(2)}, u32[]{:S(2)}) collective-permute-start(bf16[1040,128]{1,0:T(8,128)(2,1)S(1)} %pad_maximum_fusion.refs_8_), channel_id=1, source_target_pairs={{0,1},{1,2},{2,3},{3,0},{4,5},{5,6},{6,7},{7,4},{8,9},{9,10},{10,1... | collective-permute-start | bytes 798728 | tf_op jit(solution)/shard_map/ppermute | solution.py:49
  21.7 3.5 %collective-permute-start.6 = (bf16[4,256,128]{2,1,0:T(8,128)(2,1)S(1)}, bf16[4,256,128]{2,1,0:T(8,128)(2,1)S(1)}, u32[]{:S(2)}, u32[]{:S(2)}) collective-permute-start(bf16[4,256,128]{2,1,0:T(8,128)(2,1)S(1)} %pad_maximum_fusion.1.refs_0_), channel_id=1, source_target_pairs={{0,32},{32,0},{1,33},{33,1},{2,34},{34,2},{3,35},{35,3},{4,36},{36... | collective-permute-start | bytes 786440 | tf_op jit(solution)/shard_map/ppermute | solution.py:45
  21.7 3.5 %collective-permute-start.9 = (bf16[4,256,128]{2,1,0:T(8,128)(2,1)S(1)}, bf16[4,256,128]{2,1,0:T(8,128)(2,1)S(1)}, u32[]{:S(2)}, u32[]{:S(2)}) collective-permute-start(bf16[4,256,128]{2,1,0:T(8,128)(2,1)S(1)} %collective-permute-done.5.refs_3_), channel_id=1, source_target_pairs={{0,32},{32,0},{1,33},{33,1},{2,34},{34,2},{3,35},{35,3},{4,36},{36... | collective-permute-start | bytes 786440 | tf_op jit(solution)/shard_map/ppermute | solution.py:45
  22.2 3.0 %collective-permute-start.8 = (bf16[4,256,128]{2,1,0:T(8,128)(2,1)S(1)}, bf16[4,256,128]{2,1,0:T(8,128)(2,1)S(1)}, u32[]{:S(2)}, u32[]{:S(2)}) collective-permute-start(bf16[4,256,128]{2,1,0:T(8,128)(2,1)S(1)} %collective-permute-done.4.refs_2_), channel_id=1, source_target_pairs={{0,32},{32,0},{1,33},{33,1},{2,34},{34,2},{3,35},{35,3},{4,36},{36... | collective-permute-start | bytes 786440 | tf_op jit(solution)/shard_map/ppermute | solution.py:45
  22.3 2.9 %collective-permute-start.7 = (bf16[4,256,128]{2,1,0:T(8,128)(2,1)S(1)}, bf16[4,256,128]{2,1,0:T(8,128)(2,1)S(1)}, u32[]{:S(2)}, u32[]{:S(2)}) collective-permute-start(bf16[4,256,128]{2,1,0:T(8,128)(2,1)S(1)} %collective-permute-done.3.refs_1_), channel_id=1, source_target_pairs={{0,32},{32,0},{1,33},{33,1},{2,34},{34,2},{3,35},{35,3},{4,36},{36... | collective-permute-start | bytes 786440 | tf_op jit(solution)/shard_map/ppermute | solution.py:45

commit v5 on v4

--- a/solution.py
+++ b/solution.py
@@ -46,7 +46,12 @@
 
 
 def on_x(v, shift):
-    return lax.ppermute(v, "x", [(i, (i + shift) % 4) for i in range(4)])
+    pairs = [
+        (core * 4 + i, core * 4 + (i + (shift if core == 0 else -shift)) % 4)
+        for core in range(2)
+        for i in range(4)
+    ]
+    return lax.ppermute(v, ("core", "x"), pairs)
 
 
 def with_lengths(passages, lengths):
@@ -146,7 +151,7 @@
 
     count = jnp.int32(0)
     for m in range(4):
-        from_x = lax.rem(x + 4 - SHIFTS[m], 4)
+        from_x = lax.rem(x + 4 - jnp.where(core == 0, SHIFTS[m], -SHIFTS[m]), 4)
         p_ref[pl.ds(pl.multiple_of(from_x * 1024, 1024), 1024), :] = pieces[m][0:1024, :]
         lengths = pieces[m][1024:1040, :].astype(jnp.float32)[0:8].astype(jnp.int32)
         units = lax.shift_right_logical(lengths + 15, 4)
@@ -230,7 +235,8 @@
 
     near = [own] + [lax.ppermute(own, PLANE, along(True, k)) for k in SHIFTS[1:]]
     filled = with_lengths(passages, lengths)
-    moved = [filled] + [on_x(filled, k) for k in SHIFTS[1:]]
+    once = on_x(filled, 1)
+    moved = [filled, once, on_x(filled, -1), on_x(once, 1)]
     block = jnp.stack(near)
     mine = [block] + [lax.ppermute(block, PLANE, along(False, k)) for k in SHIFTS[1:]]
     other = [to_core(v) for v in mine]

time: 56.8 us -> 57 us (level)
  blocking collectives: 11.9 us -> 14.8 us
  starting transfers between devices: 17.4 us -> 15.9 us
  Pallas kernels: 19.1 us -> 17.9 us
    ppermute x3, starting transfers between devices: 6.08 us -> 2.83 us  [on_x(): return lax.ppermute(v, ('core', 'x'), pairs)]
    all_to_all x1, blocking collectives: 11.9 us -> 14.8 us  [per_device(): received = lax.all_to_all(terms, ('z', 'yhi'), 0, 0, tiled=True)]
    ppermute x3, waiting for transfers between devices: 6.53 us -> 3.97 us  [on_x(): return lax.ppermute(v, ('core', 'x'), pairs)]
    ppermute x3, waiting for transfers between devices: 0.01 us -> 2.32 us  [per_device(): lax.ppermute(block, PLANE, along(False, k))]
    ppermute x4, starting transfers between devices: 1.02 us -> 2.81 us  [to_core(): return lax.ppermute(v, 'core', [(0, 1), (1, 0)])]
    pallas_call x1, Pallas kernels: 17.6 us -> 16.4 us  [score(): pl.pallas_call(score_kernel, out_shape=jax.ShapeDtypeStruct((8, 8, 128),...]
  transfers between devices with their start and end apart: 13 -> 13, of which waited for: 3 -> 4; matrix products, arithmetic and copies ran while one was open for 2% -> 2% of each run, Pallas kernels for 0% -> 0%
where the time goes in v5:
time: 57 us; the launch traced here: 56.2 us
  Pallas kernels  17.9 us (31%)
  starting transfers between devices  15.9 us (28%)
  blocking collectives  14.8 us (26%)
  waiting for transfers between devices  6.3 us (11%)
  other arithmetic  1.04 us (2%)
    pallas_call x1, Pallas kernels, score(): pl.pallas_call(score_kernel, out_shape=jax.ShapeDtypeStruct((8, 8, 128),...  16.4 us
    all_to_all x1, blocking collectives, per_device(): received = lax.all_to_all(terms, ('z', 'yhi'), 0, 0, tiled=True)  14.8 us
    ppermute x3, starting transfers between devices, per_device(): lax.ppermute(block, PLANE, along(False, k))  5.98 us
    ppermute x3, starting transfers between devices, per_device(): lax.ppermute(own, PLANE, along(True, k))  4.32 us
    ppermute x3, waiting for transfers between devices, on_x(): return lax.ppermute(v, ('core', 'x'), pairs)  3.97 us
    ppermute x3, starting transfers between devices, on_x(): return lax.ppermute(v, ('core', 'x'), pairs)  2.83 us
    ppermute x4, starting transfers between devices, to_core(): return lax.ppermute(v, 'core', [(0, 1), (1, 0)])  2.81 us
    ppermute x3, waiting for transfers between devices, per_device(): lax.ppermute(block, PLANE, along(False, k))  2.32 us
  transfers between devices with their start and end apart: 13, of which 4 were waited for; matrix products, arithmetic and copies ran while one was open for 2% of the time, Pallas kernels for 0%

profile of v5, /device:TPU:8, one launch (start us, length us, event | category | flops | bytes accessed | tf_op | source)
XLA Modules:
  0.0 56.2 jit_solution(7632344838949253421)
XLA Ops:
  0.0 0.0 copy-start.1
  0.0 2.3 %collective-permute-start.2 = (bf16[256,128]{1,0:T(8,128)(2,1)}, bf16[256,128]{1,0:T(8,128)(2,1)S(1)}, u32[]{:S(2)}, u32[]{:S(2)}) collective-permute-start(bf16[256,128]{1,0:T(8,128)(2,1)} %bitcast.12), channel_id=1, source_target_pairs={{0,4},{4,0},{8,12},{12,8},{16,20},{20,16},{24,28},{28,24},{32,48},... | collective-permute-start | bytes 196616 | tf_op jit(solution)/shard_map/ppermute | solution.py:236
  2.3 1.3 %collective-permute-start.1 = (bf16[256,128]{1,0:T(8,128)(2,1)}, bf16[256,128]{1,0:T(8,128)(2,1)S(1)}, u32[]{:S(2)}, u32[]{:S(2)}) collective-permute-start(bf16[256,128]{1,0:T(8,128)(2,1)} %bitcast.13), channel_id=1, source_target_pairs={{0,68},{4,64},{8,76},{12,72},{16,84},{20,80},{24,92},{28,88},{32,5... | collective-permute-start | bytes 196616 | tf_op jit(solution)/shard_map/ppermute | solution.py:236
  3.6 0.7 %collective-permute-start = (bf16[256,128]{1,0:T(8,128)(2,1)}, bf16[256,128]{1,0:T(8,128)(2,1)S(1)}, u32[]{:S(2)}, u32[]{:S(2)}) collective-permute-start(bf16[256,128]{1,0:T(8,128)(2,1)} %bitcast.14), channel_id=1, source_target_pairs={{0,64},{4,68},{8,72},{12,76},{16,80},{20,84},{24,88},{28,92},{32,4... | collective-permute-start | bytes 196616 | tf_op jit(solution)/shard_map/ppermute | solution.py:236
  4.3 0.0 copy-done.1
  4.3 0.0 copy-start
  4.4 1.0 %pad_maximum_fusion.refs_8_ = bf16[1040,128]{1,0:T(8,128)(2,1)S(1)} fusion(bf16[16,128]{1,0:T(8,128)(2,1)S(1)} %broadcast_in_dim.3, bf16[1024,128]{1,0:T(8,128)(2,1)} %bitcast.11), kind=kLoop, calls=%fused_computation | loop fusion | flops 532480 | bytes 532480 | tf_op jit(solution)/shard_map/concatenate | solution.py:59
  5.4 2.8 %collective-permute-start.11 = (bf16[1040,128]{1,0:T(8,128)(2,1)S(1)}, bf16[1040,128]{1,0:T(8,128)(2,1)S(1)}, u32[]{:S(2)}, u32[]{:S(2)}) collective-permute-start(bf16[1040,128]{1,0:T(8,128)(2,1)S(1)} %pad_maximum_fusion.refs_8_), channel_id=1, source_target_pairs={{0,3},{1,0},{2,1},{3,2},{32,33},{33,34},{34,35},{35,32},{4,7},{5,4... | collective-permute-start | bytes 798728 | tf_op jit(solution)/shard_map/ppermute | solution.py:54
  8.2 0.0 collective-permute-start.10
  8.2 0.0 collective-permute-done.2
  8.2 0.0 collective-permute-done.1
  8.2 0.0 collective-permute-done
  8.2 0.0 copy-done
  8.3 4.0 %collective-permute-start.5 = (bf16[4,256,128]{2,1,0:T(8,128)(2,1)S(1)}, bf16[4,256,128]{2,1,0:T(8,128)(2,1)S(1)}, u32[]{:S(2)}, u32[]{:S(2)}) collective-permute-start(bf16[4,256,128]{2,1,0:T(8,128)(2,1)S(1)} %pad_maximum_fusion.1.refs_0_), channel_id=1, source_target_pairs={{0,16},{4,20},{8,24},{12,28},{16,0},{20,4},{24,8},{28,12},{32,36},... | collective-permute-start | bytes 786440 | tf_op jit(solution)/shard_map/ppermute | solution.py:241
  12.2 0.7 %collective-permute-start.4 = (bf16[4,256,128]{2,1,0:T(8,128)(2,1)S(1)}, bf16[4,256,128]{2,1,0:T(8,128)(2,1)S(1)}, u32[]{:S(2)}, u32[]{:S(2)}) collective-permute-start(bf16[4,256,128]{2,1,0:T(8,128)(2,1)S(1)} %pad_maximum_fusion.1.refs_0_), channel_id=1, source_target_pairs={{0,24},{4,28},{8,0},{12,4},{16,8},{20,12},{24,16},{28,20},{32,100}... | collective-permute-start | bytes 786440 | tf_op jit(solution)/shard_map/ppermute | solution.py:241
  12.9 1.3 %collective-permute-start.3 = (bf16[4,256,128]{2,1,0:T(8,128)(2,1)S(1)}, bf16[4,256,128]{2,1,0:T(8,128)(2,1)S(1)}, u32[]{:S(2)}, u32[]{:S(2)}) collective-permute-start(bf16[4,256,128]{2,1,0:T(8,128)(2,1)S(1)} %pad_maximum_fusion.1.refs_0_), channel_id=1, source_target_pairs={{0,8},{4,12},{8,16},{12,20},{16,24},{20,28},{24,0},{28,4},{32,96},... | collective-permute-start | bytes 786440 | tf_op jit(solution)/shard_map/ppermute | solution.py:241
  14.3 1.6 %collective-permute-done.10.refs_9_ = bf16[1040,128]{1,0:T(8,128)(2,1)S(1)} collective-permute-done((bf16[1040,128]{1,0:T(8,128)(2,1)S(1)}, bf16[1040,128]{1,0:T(8,128)(2,1)S(1)}, u32[]{:S(2)}, u32[]{:S(2)}) %collective-permute-start.10) | collective-permute-done | bytes 266272 | tf_op jit(solution)/shard_map/ppermute | solution.py:54
  15.8 0.0 collective-permute-start.12
  15.8 0.0 collective-permute-done.11.refs_10_
  15.8 2.3 %collective-permute-start.6 = (bf16[4,256,128]{2,1,0:T(8,128)(2,1)S(1)}, bf16[4,256,128]{2,1,0:T(8,128)(2,1)S(1)}, u32[]{:S(2)}, u32[]{:S(2)}) collective-permute-start(bf16[4,256,128]{2,1,0:T(8,128)(2,1)S(1)} %pad_maximum_fusion.1.refs_0_), channel_id=1, source_target_pairs={{0,32},{32,0},{1,33},{33,1},{2,34},{34,2},{3,35},{35,3},{4,36},{36... | collective-permute-start | bytes 786440 | tf_op jit(solution)/shard_map/ppermute | solution.py:45
  18.1 0.0 collective-permute-done.5.refs_3_
  18.1 0.1 collective-permute-start.9
  18.2 2.2 %collective-permute-done.4.refs_2_ = bf16[4,256,128]{2,1,0:T(8,128)(2,1)S(1)} collective-permute-done((bf16[4,256,128]{2,1,0:T(8,128)(2,1)S(1)}, bf16[4,256,128]{2,1,0:T(8,128)(2,1)S(1)}, u32[]{:S(2)}, u32[]{:S(2)}) %collective-permute-start.4) | collective-permute-done | bytes 262176 | tf_op jit(solution)/shard_map/ppermute | solution.py:241
  20.4 0.0 collective-permute-start.8
  20.4 0.1 collective-permute-done.3.refs_1_
  20.5 0.4 collective-permute-start.7
  21.0 0.1 stack.35.info_ref
  21.0 0.0 collective-permute-done.6.refs_4_
  21.0 2.4 %collective-permute-done.12.refs_11_ = bf16[1040,128]{1,0:T(8,128)(2,1)S(1)} collective-permute-done((bf16[1040,128]{1,0:T(8,128)(2,1)S(1)}, bf16[1040,128]{1,0:T(8,128)(2,1)S(1)}, u32[]{:S(2)}, u32[]{:S(2)}) %collective-permute-start.12) | collective-permute-done | bytes 266272 | tf_op jit(solution)/shard_map/ppermute | solution.py:54
  23.4 0.0 collective-permute-done.9.refs_7_
  23.5 0.0 collective-permute-done.8.refs_6_
  23.5 0.0 collective-permute-done.7.refs_5_
  23.5 16.4 %shard_map.37 = f32[8,8,128]{2,1,0:T(8,128)S(1)} custom-call(s32[5]{0:T(128)S(1)} %stack.35.info_ref, bf16[4,256,128]{2,1,0:T(8,128)(2,1)S(1)} %pad_maximum_fusion.1.refs_0_, bf16[4,256,128]{2,1,0:T(8,128)(2,1)S(1)} %collective-permute-done.3.refs_1_, bf16[4,256,128]{2,1,0:T(8,128)(2,1)S(1)} %collective-permute-done.4.refs_2_, ...), custom_call_target="tpu_custom_call" | custom-call | tf_op jit(solution)/shard_map/pallas_call | solution.py:199
  39.9 14.8 %all_to_all.5.r_ref = f32[8,8,128]{2,1,0:T(8,128)} all-to-all(f32[8,8,128]{2,1,0:T(8,128)S(1)} %shard_map.37), channel_id=1, replica_groups=mesh['ylo'=2,'core'=2,'z'=4,'yhi'=2,'x'=4] {'z','yhi'}, dimensions={0} | all-to-all | bytes 65536 | tf_op jit(solution)/shard_map/all_to_all | solution.py:244
  54.7 1.5 %shard_map.38 = f32[32,256]{1,0:T(8,128)} custom-call(f32[8,8,128]{2,1,0:T(8,128)} %all_to_all.5.r_ref), custom_call_target="tpu_custom_call" | custom-call | tf_op jit(solution)/shard_map/pallas_call | solution.py:224
  (4 shorter events, 0.1 us)
Async XLA Ops:
  0.0 4.3 %copy-start.1 = (s32[8]{0:T(128)S(1)}, s32[8]{0:T(128)}, u32[]{:S(2)}) copy-start(s32[8]{0:T(128)} %param.5) | copy-start | bytes 100
  0.0 8.2 %collective-permute-start.2 = (bf16[256,128]{1,0:T(8,128)(2,1)}, bf16[256,128]{1,0:T(8,128)(2,1)S(1)}, u32[]{:S(2)}, u32[]{:S(2)}) collective-permute-start(bf16[256,128]{1,0:T(8,128)(2,1)} %bitcast.12), channel_id=1, source_target_pairs={{0,4},{4,0},{8,12},{12,8},{16,20},{20,16},{24,28},{28,24},{32,48},... | collective-permute-start | bytes 196616 | tf_op jit(solution)/shard_map/ppermute | solution.py:236
  2.3 5.9 %collective-permute-start.1 = (bf16[256,128]{1,0:T(8,128)(2,1)}, bf16[256,128]{1,0:T(8,128)(2,1)S(1)}, u32[]{:S(2)}, u32[]{:S(2)}) collective-permute-start(bf16[256,128]{1,0:T(8,128)(2,1)} %bitcast.13), channel_id=1, source_target_pairs={{0,68},{4,64},{8,76},{12,72},{16,84},{20,80},{24,92},{28,88},{32,5... | collective-permute-start | bytes 196616 | tf_op jit(solution)/shard_map/ppermute | solution.py:236
  3.6 4.6 %collective-permute-start = (bf16[256,128]{1,0:T(8,128)(2,1)}, bf16[256,128]{1,0:T(8,128)(2,1)S(1)}, u32[]{:S(2)}, u32[]{:S(2)}) collective-permute-start(bf16[256,128]{1,0:T(8,128)(2,1)} %bitcast.14), channel_id=1, source_target_pairs={{0,64},{4,68},{8,72},{12,76},{16,80},{20,84},{24,88},{28,92},{32,4... | collective-permute-start | bytes 196616 | tf_op jit(solution)/shard_map/ppermute | solution.py:236
  4.3 3.9 %copy-start = (bf16[32,8,128]{2,1,0:T(8,128)(2,1)S(1)}, bf16[32,8,128]{2,1,0:T(8,128)(2,1)}, u32[]{:S(2)}) copy-start(bf16[32,8,128]{2,1,0:T(8,128)(2,1)} %param.3) | copy-start | bytes 196612
  5.4 10.5 %collective-permute-start.11 = (bf16[1040,128]{1,0:T(8,128)(2,1)S(1)}, bf16[1040,128]{1,0:T(8,128)(2,1)S(1)}, u32[]{:S(2)}, u32[]{:S(2)}) collective-permute-start(bf16[1040,128]{1,0:T(8,128)(2,1)S(1)} %pad_maximum_fusion.refs_8_), channel_id=1, source_target_pairs={{0,3},{1,0},{2,1},{3,2},{32,33},{33,34},{34,35},{35,32},{4,7},{5,4... | collective-permute-start | bytes 798728 | tf_op jit(solution)/shard_map/ppermute | solution.py:54
  8.2 7.6 %collective-permute-start.10 = (bf16[1040,128]{1,0:T(8,128)(2,1)S(1)}, bf16[1040,128]{1,0:T(8,128)(2,1)S(1)}, u32[]{:S(2)}, u32[]{:S(2)}) collective-permute-start(bf16[1040,128]{1,0:T(8,128)(2,1)S(1)} %pad_maximum_fusion.refs_8_), channel_id=1, source_target_pairs={{0,1},{1,2},{2,3},{3,0},{32,35},{33,32},{34,33},{35,34},{4,5},{5,6... | collective-permute-start | bytes 798728 | tf_op jit(solution)/shard_map/ppermute | solution.py:54
  8.3 9.9 %collective-permute-start.5 = (bf16[4,256,128]{2,1,0:T(8,128)(2,1)S(1)}, bf16[4,256,128]{2,1,0:T(8,128)(2,1)S(1)}, u32[]{:S(2)}, u32[]{:S(2)}) collective-permute-start(bf16[4,256,128]{2,1,0:T(8,128)(2,1)S(1)} %pad_maximum_fusion.1.refs_0_), channel_id=1, source_target_pairs={{0,16},{4,20},{8,24},{12,28},{16,0},{20,4},{24,8},{28,12},{32,36},... | collective-permute-start | bytes 786440 | tf_op jit(solution)/shard_map/ppermute | solution.py:241
  12.2 8.2 %collective-permute-start.4 = (bf16[4,256,128]{2,1,0:T(8,128)(2,1)S(1)}, bf16[4,256,128]{2,1,0:T(8,128)(2,1)S(1)}, u32[]{:S(2)}, u32[]{:S(2)}) collective-permute-start(bf16[4,256,128]{2,1,0:T(8,128)(2,1)S(1)} %pad_maximum_fusion.1.refs_0_), channel_id=1, source_target_pairs={{0,24},{4,28},{8,0},{12,4},{16,8},{20,12},{24,16},{28,20},{32,100}... | collective-permute-start | bytes 786440 | tf_op jit(solution)/shard_map/ppermute | solution.py:241
  12.9 7.6 %collective-permute-start.3 = (bf16[4,256,128]{2,1,0:T(8,128)(2,1)S(1)}, bf16[4,256,128]{2,1,0:T(8,128)(2,1)S(1)}, u32[]{:S(2)}, u32[]{:S(2)}) collective-permute-start(bf16[4,256,128]{2,1,0:T(8,128)(2,1)S(1)} %pad_maximum_fusion.1.refs_0_), channel_id=1, source_target_pairs={{0,8},{4,12},{8,16},{12,20},{16,24},{20,28},{24,0},{28,4},{32,96},... | collective-permute-start | bytes 786440 | tf_op jit(solution)/shard_map/ppermute | solution.py:241
  15.8 7.6 %collective-permute-start.12 = (bf16[1040,128]{1,0:T(8,128)(2,1)S(1)}, bf16[1040,128]{1,0:T(8,128)(2,1)S(1)}, u32[]{:S(2)}, u32[]{:S(2)}) collective-permute-start(bf16[1040,128]{1,0:T(8,128)(2,1)S(1)} %collective-permute-done.10.refs_9_), channel_id=1, source_target_pairs={{0,1},{1,2},{2,3},{3,0},{32,35},{33,32},{34,33},{35,34},{4,5},{5,6... | collective-permute-start | bytes 798728 | tf_op jit(solution)/shard_map/ppermute | solution.py:54
  15.8 5.2 %collective-permute-start.6 = (bf16[4,256,128]{2,1,0:T(8,128)(2,1)S(1)}, bf16[4,256,128]{2,1,0:T(8,128)(2,1)S(1)}, u32[]{:S(2)}, u32[]{:S(2)}) collective-permute-start(bf16[4,256,128]{2,1,0:T(8,128)(2,1)S(1)} %pad_maximum_fusion.1.refs_0_), channel_id=1, source_target_pairs={{0,32},{32,0},{1,33},{33,1},{2,34},{34,2},{3,35},{35,3},{4,36},{36... | collective-permute-start | bytes 786440 | tf_op jit(solution)/shard_map/ppermute | solution.py:45
  18.1 5.3 %collective-permute-start.9 = (bf16[4,256,128]{2,1,0:T(8,128)(2,1)S(1)}, bf16[4,256,128]{2,1,0:T(8,128)(2,1)S(1)}, u32[]{:S(2)}, u32[]{:S(2)}) collective-permute-start(bf16[4,256,128]{2,1,0:T(8,128)(2,1)S(1)} %collective-permute-done.5.refs_3_), channel_id=1, source_target_pairs={{0,32},{32,0},{1,33},{33,1},{2,34},{34,2},{3,35},{35,3},{4,36},{36... | collective-permute-start | bytes 786440 | tf_op jit(solution)/shard_map/ppermute | solution.py:45
  20.4 3.0 %collective-permute-start.8 = (bf16[4,256,128]{2,1,0:T(8,128)(2,1)S(1)}, bf16[4,256,128]{2,1,0:T(8,128)(2,1)S(1)}, u32[]{:S(2)}, u32[]{:S(2)}) collective-permute-start(bf16[4,256,128]{2,1,0:T(8,128)(2,1)S(1)} %collective-permute-done.4.refs_2_), channel_id=1, source_target_pairs={{0,32},{32,0},{1,33},{33,1},{2,34},{34,2},{3,35},{35,3},{4,36},{36... | collective-permute-start | bytes 786440 | tf_op jit(solution)/shard_map/ppermute | solution.py:45
  20.5 2.9 %collective-permute-start.7 = (bf16[4,256,128]{2,1,0:T(8,128)(2,1)S(1)}, bf16[4,256,128]{2,1,0:T(8,128)(2,1)S(1)}, u32[]{:S(2)}, u32[]{:S(2)}) collective-permute-start(bf16[4,256,128]{2,1,0:T(8,128)(2,1)S(1)} %collective-permute-done.3.refs_1_), channel_id=1, source_target_pairs={{0,32},{32,0},{1,33},{33,1},{2,34},{34,2},{3,35},{35,3},{4,36},{36... | collective-permute-start | bytes 786440 | tf_op jit(solution)/shard_map/ppermute | solution.py:45

commit v6 on v5

v6 whole, which is shorter than its diff:
```python
import functools

import jax
import jax.numpy as jnp
from jax import lax
from jax.experimental import pallas as pl
from jax.experimental.pallas import tpu as pltpu
from jax.sharding import Mesh
from jax.sharding import PartitionSpec as P

NAMES = ("ylo", "core", "z", "yhi", "x")
SIZES = (2, 2, 4, 2, 4)
PLANE = ("ylo", "core", "z", "yhi")
SHIFTS = (0, 1, -1, 2)
OWN, SLOTS, WIDTH = 8, 128, 128
DEPTH = 16
LOWEST = -3.0e38
UNITS = 384


def plane_pairs(move):
    def index(ylo, core, z, yhi):
        return ((ylo * 2 + core) * 4 + z) * 2 + yhi

    pairs = []
    for ylo in range(2):
        for core in range(2):
            for z in range(4):
                for yhi in range(2):
                    y2, core2, z2 = move(2 * yhi + ylo, core, z)
                    y2, z2 = y2 % 4, z2 % 4
                    pairs.append((index(ylo, core, z, yhi), index(y2 % 2, core2, z2, y2 // 2)))
    return pairs


def along(first, shift):
    def move(y, core, z):
        if (core == 0) == first:
            return y + shift, core, z
        return y, core, z + shift

    return plane_pairs(move)


def to_core(v):
    return lax.ppermute(v, "core", [(0, 1), (1, 0)])


def on_x(v, shift):
    pairs = [
        (core * 4 + i, core * 4 + (i + (shift if core == 0 else -shift)) % 4)
        for core in range(2)
        for i in range(4)
    ]
    return lax.ppermute(v, ("core", "x"), pairs)


def with_lengths(passages, lengths):
    tail = jnp.pad(lengths.astype(passages.dtype), (0, WIDTH - OWN))
    return jnp.concatenate(
        [passages.reshape(OWN * SLOTS, WIDTH), jnp.broadcast_to(tail, (16, WIDTH))], axis=0
    )


def prepare_kernel(info_ref, *refs):
    pieces, p_ref, unit_ref = refs[:4], refs[4], refs[5]
    core, x = info_ref[2], info_ref[3]
    count = jnp.int32(0)
    for m in range(4):
        from_x = lax.rem(x + 4 - jnp.where(core == 0, SHIFTS[m], -SHIFTS[m]), 4)
        p_ref[pl.ds(pl.multiple_of(from_x * 1024, 1024), 1024), :] = pieces[m][0:1024, :]
        lengths = pieces[m][1024:1040, :].astype(jnp.float32)[0:8].astype(jnp.int32)
        units = lax.shift_right_logical(lengths + 15, 4)
        for i in range(OWN):
            for n in range(8):
                unit_ref[count + n] = from_x * 1024 + i * SLOTS + n * 16
            count = count + units[0, i]
            used = units[0, i]
            last = pl.multiple_of(from_x * 1024 + i * SLOTS + (used - 1) * 16, 16)
            both = p_ref[pl.ds(last, 16), :].astype(jnp.float32)
            second = jnp.where(lengths[0, i] == used * 16, both[8:16], both[0:8])
            p_ref[pl.ds(last, 16), :] = jnp.concatenate([both[0:8], second], axis=0).astype(p_ref.dtype)
    for i in range(DEPTH):
        unit_ref[count + i] = unit_ref[count - 1]
    unit_ref[UNITS - 1] = lax.div(count + DEPTH - 1, DEPTH)


def prepare(info, pieces):
    return pl.pallas_call(
        prepare_kernel,
        out_shape=[
            jax.ShapeDtypeStruct((4096, WIDTH), jnp.bfloat16),
            jax.ShapeDtypeStruct((UNITS,), jnp.int32),
        ],
        in_specs=[pl.BlockSpec(memory_space=pltpu.SMEM)]
        + [pl.BlockSpec(memory_space=pltpu.VMEM)] * 4,
        out_specs=[pl.BlockSpec(memory_space=pltpu.VMEM), pl.BlockSpec(memory_space=pltpu.SMEM)],
        compiler_params=pltpu.CompilerParams(vmem_limit_bytes=16 << 20),
        cost_estimate=pl.CostEstimate(flops=1 << 30, bytes_accessed=2 << 20, transcendentals=0),
    )(info, *pieces)


def best_dots(rows, places, p_ref, m_ref, s_ref, unit_ref, turns, *acc):
    acc = (acc[:DEPTH], acc[DEPTH:])
    nothing = jnp.zeros((16, 128), jnp.bfloat16)

    def push(g):
        for u in range(2):
            held = jnp.concatenate([ref[j] for ref, j in rows[g][2 * u : 2 * u + 2]], axis=1)
            pltpu.matmul_push_rhs(held, 0, u, transpose=True)

    def issue(unit, j, fresh=False):
        slots = p_ref[pl.ds(pl.multiple_of(unit, 16), 16), :]
        lhs = jnp.concatenate(
            [
                jnp.concatenate([slots, nothing], axis=1),
                jnp.concatenate([nothing, slots], axis=1),
            ],
            axis=0,
        )
        for u in range(2):
            pltpu.matmul_acc_lhs(acc[u][j], lhs, load_staged_rhs=0 if fresh else None)

    def take(unit, j):
        at = lax.shift_right_logical(unit, 7)
        begin = jnp.where(lax.bitwise_and(unit, 127) == 0, 32, at)
        tops = []
        held = [m_ref[b, begin] for b in range(8)]
        for u in range(2):
            d = pltpu.matmul_pop(acc[u][j])
            for half in range(2):
                top = jnp.maximum(d[16 * half : 16 * half + 8], d[16 * half + 8 : 16 * half + 16])
                tops += [top[:, 0:128], top[:, 128:256]]
        for b in range(8):
            m_ref[b, at] = jnp.maximum(held[b], tops[b])

    def turn(t, c):
        for j in range(DEPTH):
            take(unit_ref[t * DEPTH + j], j)
            issue(unit_ref[t * DEPTH + DEPTH + j], j)
        return c

    m_ref[:, 32] = jnp.full((8, 8, 128), LOWEST, jnp.float32)
    rows_ref = m_ref.reshape(8, 264, 128)
    push(0)
    for j in range(DEPTH):
        issue(unit_ref[j], j, fresh=j == 0)
    for g in range(len(rows)):
        lax.fori_loop(0, turns - 1, turn, 0)
        more = g + 1 < len(rows)
        if more:
            push(g + 1)
        last = (turns - 1) * DEPTH
        for j in range(DEPTH):
            take(unit_ref[last + j], j)
            if more:
                issue(unit_ref[j], j, fresh=j == 0)
        for o in range(4):
            for b in range(8):
                top = rows_ref[b, pl.ds(64 * o, 8, stride=8), :]
                for i in range(1, 8):
                    top = jnp.maximum(top, rows_ref[b, pl.ds(64 * o + i, 8, stride=8), :])
                lanes = slice(128 * (b % 2), 128 * (b % 2) + 128)
                s_ref[places[g][b // 2], 8 * o : 8 * o + 8, lanes] += top


def score_kernel(shifts, parts, info_ref, unit_ref, p_ref, *refs):
    n = 2 * len(shifts)
    rows, sums, out_ref, m_ref = refs[:n], refs[n : n + parts], refs[n + parts], refs[n + parts + 1]
    s_ref = refs[n + parts + 2] if parts else out_ref
    z, yhi, core, ylo = info_ref[0], info_ref[1], info_ref[2], info_ref[4]
    y = yhi * 2 + ylo

    def place(chain, k, j):
        from_z = lax.rem(z + 4 - jnp.where(chain == 0, SHIFTS[k], SHIFTS[j]), 4)
        from_y = lax.rem(y + 4 - jnp.where(chain == 0, SHIFTS[j], SHIFTS[k]), 4)
        return from_z * 2 + lax.shift_right_logical(from_y, 1)

    groups, places = [], []
    for i, k in enumerate(shifts):
        mine, other = rows[2 * i], rows[2 * i + 1]
        for j in (0, 2):
            groups.append([(mine, j), (mine, j + 1), (other, j), (other, j + 1)])
            places.append([place(chain, k, j + e) for chain in (core, 1 - core) for e in range(2)])
    total = jnp.zeros(s_ref.shape, jnp.float32)
    for part in sums:
        total = total + part[...]
    s_ref[...] = total
    pl.run_scoped(
        functools.partial(best_dots, groups, places, p_ref, m_ref, s_ref, unit_ref, unit_ref[UNITS - 1]),
        *[pltpu.ACC(u)((32, 256), jnp.float32) for u in range(2) for _ in range(DEPTH)],
    )
    if not parts:
        return

    lane = lax.broadcasted_iota(jnp.int32, (32, 256), 1)
    row = lax.broadcasted_iota(jnp.int32, (32, 256), 0)
    pick = jnp.where(lane // 8 == row, 1.0 / 32, 0.0).astype(jnp.bfloat16)
    rest = s_ref[...].reshape(256, 256)
    split = []
    for _ in range(3):
        split.append(rest.astype(jnp.bfloat16))
        rest = rest - split[-1].astype(jnp.float32)

    def add_up(acc):
        for part in split:
            pltpu.matmul_push_rhs(part, 0, 0, transpose=True)
            pltpu.matmul_acc_lhs(acc, pick, load_staged_rhs=0)
        return pltpu.matmul_pop(acc)

    r = pl.run_scoped(add_up, pltpu.ACC(0)((32, 256), jnp.float32))
    for g in range(8):
        c = r[:, 32 * g : 32 * g + 32]
        out_ref[g] = jnp.concatenate([c[0:8], c[8:16], c[16:24], c[24:32]], axis=1)


def score(info, units, slots, shifts, rows, sums=()):
    sums_shape = (8, 32, 256)
    return pl.pallas_call(
        functools.partial(score_kernel, shifts, len(sums)),
        out_shape=jax.ShapeDtypeStruct((8, 8, 128) if sums else sums_shape, jnp.float32),
        in_specs=[pl.BlockSpec(memory_space=pltpu.SMEM)] * 2
        + [pl.BlockSpec(memory_space=pltpu.VMEM)] * (1 + len(rows) + len(sums)),
        out_specs=pl.BlockSpec(memory_space=pltpu.VMEM),
        scratch_shapes=[pltpu.VMEM((8, 33, 8, 128), jnp.float32)]
        + ([pltpu.VMEM(sums_shape, jnp.float32)] if sums else []),
        compiler_params=pltpu.CompilerParams(vmem_limit_bytes=32 << 20),
        cost_estimate=pl.CostEstimate(
            flops=len(shifts) * 2048 * 4096 * 256 * 2, bytes_accessed=2 << 20, transcendentals=0
        ),
    )(info, units, slots, *rows, *sums)


def place_kernel(r_ref, o_ref):
    for g in range(4):
        o_ref[8 * g : 8 * g + 8, :] = jnp.concatenate(
            [r_ref[s][:, 32 * g : 32 * g + 32] for s in range(8)], axis=1
        )


def place(received):
    return pl.pallas_call(
        place_kernel,
        out_shape=jax.ShapeDtypeStruct((32, 256), jnp.float32),
        in_specs=[pl.BlockSpec(memory_space=pltpu.VMEM)],
        out_specs=pl.BlockSpec(memory_space=pltpu.VMEM),
    )(received)


def per_device(queries, passages, lengths):
    own = queries.reshape(256, 128)
    info = jnp.stack([lax.axis_index(name) for name in ("z", "yhi", "core", "x", "ylo")]).astype(jnp.int32)

    near = [own] + [lax.ppermute(own, PLANE, along(True, k)) for k in SHIFTS[1:]]
    filled = with_lengths(passages, lengths)
    once = on_x(filled, 1)
    moved = [filled, once, on_x(filled, -1), on_x(once, 1)]
    block = jnp.stack(near)
    slots, units = prepare(info, moved)
    mine = [block] + [lax.ppermute(block, PLANE, along(False, k)) for k in SHIFTS[1:]]
    first = score(info, units, slots, (0,), (block, to_core(block)))
    first, *late = lax.optimization_barrier((first, *mine[1:]))
    rows = [w for v in late for w in (v, to_core(v))]
    terms = score(info, units, slots, (1, 2, 3), rows, (first,))
    received = lax.all_to_all(terms, ("z", "yhi"), 0, 0, tiled=True)
    return place(received)


def solution(mesh):
    fine = Mesh(mesh.devices.reshape(SIZES), NAMES)
    corpus = ("z", "yhi", "x")
    query = ("ylo", "core")
    return jax.shard_map(
        per_device,
        mesh=fine,
        in_specs=(P(corpus, query, None), P(query + corpus, None, None), P(query + corpus)),
        out_specs=P(corpus, query),
        check_vma=False,
    )
```

time: 57 us -> 55.4 us (0.972)
  the two profiles are of different devices: /device:TPU:8 before, /device:TPU:0 now
where the time goes in v6:
time: 55.4 us; the launch traced here: 55.6 us
  starting transfers between devices  19.3 us (35%)
  Pallas kernels  19.2 us (35%)
  blocking collectives  11.4 us (21%)
  waiting for transfers between devices  3.85 us (7%)
  other arithmetic  1.7 us (3%)
    pallas_call x2, Pallas kernels, score(): pl.pallas_call(functools.partial(score_kernel, shifts, len(sums)), out_sh...  16.1 us
    all_to_all x1, blocking collectives, per_device(): received = lax.all_to_all(terms, ('z', 'yhi'), 0, 0, tiled=True)  11.4 us
    ppermute x3, starting transfers between devices, per_device(): lax.ppermute(own, PLANE, along(True, k))  6.43 us
    ppermute x3, starting transfers between devices, per_device(): lax.ppermute(block, PLANE, along(False, k))  5.16 us
    ppermute x4, starting transfers between devices, to_core(): return lax.ppermute(v, 'core', [(0, 1), (1, 0)])  4.03 us
    ppermute x3, starting transfers between devices, on_x(): return lax.ppermute(v, ('core', 'x'), pairs)  3.67 us
    ppermute x3, waiting for transfers between devices, on_x(): return lax.ppermute(v, ('core', 'x'), pairs)  2.17 us
    pallas_call x1, Pallas kernels, prepare(): pl.pallas_call(prepare_kernel, out_shape=[jax.ShapeDtypeStruct((4096, WID...  1.63 us
  transfers between devices with their start and end apart: 13, of which 6 were waited for; matrix products, arithmetic and copies ran while one was open for 0% of the time, Pallas kernels for 11%

profile of v6, /device:TPU:0, one launch (start us, length us, event | category | flops | bytes accessed | tf_op | source)
XLA Modules:
  0.0 55.6 jit_solution(15351666055512034204)
XLA Ops:
  0.0 0.7 %convert_element_type.5 = bf16[8]{0:T(256)(128)(2,1)S(1)} convert(s32[8]{0:T(128)} %param.5) | non-fusion elementwise | flops 8 | bytes 48 | tf_op jit(solution)/shard_map/convert_element_type | solution.py:59
  0.7 0.0 copy-start
  0.7 1.0 %pad_maximum_fusion.refs_0_ = bf16[1040,128]{1,0:T(8,128)(2,1)S(1)} fusion(bf16[16,128]{1,0:T(8,128)(2,1)S(1)} %broadcast_in_dim.3, bf16[1024,128]{1,0:T(8,128)(2,1)} %bitcast.11), kind=kLoop, calls=%fused_computation | loop fusion | flops 532480 | bytes 532480 | tf_op jit(solution)/shard_map/concatenate | solution.py:60
  1.7 1.6 %collective-permute-start = (bf16[1040,128]{1,0:T(8,128)(2,1)S(1)}, bf16[1040,128]{1,0:T(8,128)(2,1)S(1)}, u32[]{:S(2)}, u32[]{:S(2)}) collective-permute-start(bf16[1040,128]{1,0:T(8,128)(2,1)S(1)} %pad_maximum_fusion.refs_0_), channel_id=1, source_target_pairs={{0,1},{1,2},{2,3},{3,0},{32,35},{33,32},{34,33},{35,34},{4,5},{5,6... | collective-permute-start | bytes 798728 | tf_op jit(solution)/shard_map/ppermute | solution.py:55
  3.3 0.0 copy-done
  3.3 3.2 %collective-permute-start.5 = (bf16[256,128]{1,0:T(8,128)(2,1)S(1)}, bf16[256,128]{1,0:T(8,128)(2,1)S(1)}, u32[]{:S(2)}, u32[]{:S(2)}) collective-permute-start(bf16[256,128]{1,0:T(8,128)(2,1)S(1)} %bitcast.12), channel_id=1, source_target_pairs={{0,4},{4,0},{8,12},{12,8},{16,20},{20,16},{24,28},{28,24},{32,48},... | collective-permute-start | bytes 196616 | tf_op jit(solution)/shard_map/ppermute | solution.py:254
  6.5 0.7 %collective-permute-start.3 = (bf16[256,128]{1,0:T(8,128)(2,1)S(1)}, bf16[256,128]{1,0:T(8,128)(2,1)S(1)}, u32[]{:S(2)}, u32[]{:S(2)}) collective-permute-start(bf16[256,128]{1,0:T(8,128)(2,1)S(1)} %bitcast.13), channel_id=1, source_target_pairs={{0,64},{4,68},{8,72},{12,76},{16,80},{20,84},{24,88},{28,92},{32,4... | collective-permute-start | bytes 196616 | tf_op jit(solution)/shard_map/ppermute | solution.py:254
  7.2 2.6 %collective-permute-start.4 = (bf16[256,128]{1,0:T(8,128)(2,1)S(1)}, bf16[256,128]{1,0:T(8,128)(2,1)S(1)}, u32[]{:S(2)}, u32[]{:S(2)}) collective-permute-start(bf16[256,128]{1,0:T(8,128)(2,1)S(1)} %bitcast.14), channel_id=1, source_target_pairs={{0,68},{4,64},{8,76},{12,72},{16,84},{20,80},{24,92},{28,88},{32,5... | collective-permute-start | bytes 196616 | tf_op jit(solution)/shard_map/ppermute | solution.py:254
  9.8 1.7 %collective-permute-start.1 = (bf16[1040,128]{1,0:T(8,128)(2,1)S(1)}, bf16[1040,128]{1,0:T(8,128)(2,1)S(1)}, u32[]{:S(2)}, u32[]{:S(2)}) collective-permute-start(bf16[1040,128]{1,0:T(8,128)(2,1)S(1)} %pad_maximum_fusion.refs_0_), channel_id=1, source_target_pairs={{0,3},{1,0},{2,1},{3,2},{32,33},{33,34},{34,35},{35,32},{4,7},{5,4... | collective-permute-start | bytes 798728 | tf_op jit(solution)/shard_map/ppermute | solution.py:55
  11.5 0.0 collective-permute-done.refs_1_
  11.5 0.3 collective-permute-start.2
  11.8 0.0 collective-permute-done.5
  11.8 0.2 collective-permute-done.3
  12.0 0.0 collective-permute-done.4
  12.0 1.2 %collective-permute-start.6 = (bf16[4,256,128]{2,1,0:T(8,128)(2,1)S(1)}, bf16[4,256,128]{2,1,0:T(8,128)(2,1)S(1)}, u32[]{:S(2)}, u32[]{:S(2)}) collective-permute-start(bf16[4,256,128]{2,1,0:T(8,128)(2,1)S(1)} %pad_maximum_fusion.1.refs_0_), channel_id=1, source_target_pairs={{0,32},{32,0},{1,33},{33,1},{2,34},{34,2},{3,35},{35,3},{4,36},{36... | collective-permute-start | bytes 786440 | tf_op jit(solution)/shard_map/ppermute | solution.py:46
  13.2 0.1 stack.35.info_ref
  13.3 0.8 %collective-permute-start.7 = (bf16[4,256,128]{2,1,0:T(8,128)(2,1)S(1)}, bf16[4,256,128]{2,1,0:T(8,128)(2,1)S(1)}, u32[]{:S(2)}, u32[]{:S(2)}) collective-permute-start(bf16[4,256,128]{2,1,0:T(8,128)(2,1)S(1)} %pad_maximum_fusion.1.refs_0_), channel_id=1, source_target_pairs={{0,8},{4,12},{8,16},{12,20},{16,24},{20,28},{24,0},{28,4},{32,96},... | collective-permute-start | bytes 786440 | tf_op jit(solution)/shard_map/ppermute | solution.py:260
  14.2 2.4 %collective-permute-start.8 = (bf16[4,256,128]{2,1,0:T(8,128)(2,1)S(1)}, bf16[4,256,128]{2,1,0:T(8,128)(2,1)S(1)}, u32[]{:S(2)}, u32[]{:S(2)}) collective-permute-start(bf16[4,256,128]{2,1,0:T(8,128)(2,1)S(1)} %pad_maximum_fusion.1.refs_0_), channel_id=1, source_target_pairs={{0,24},{4,28},{8,0},{12,4},{16,8},{20,12},{24,16},{28,20},{32,100}... | collective-permute-start | bytes 786440 | tf_op jit(solution)/shard_map/ppermute | solution.py:260
  16.6 2.2 %collective-permute-done.1.refs_2_ = bf16[1040,128]{1,0:T(8,128)(2,1)S(1)} collective-permute-done((bf16[1040,128]{1,0:T(8,128)(2,1)S(1)}, bf16[1040,128]{1,0:T(8,128)(2,1)S(1)}, u32[]{:S(2)}, u32[]{:S(2)}) %collective-permute-start.1) | collective-permute-done | bytes 266272 | tf_op jit(solution)/shard_map/ppermute | solution.py:55
  18.7 1.9 %collective-permute-start.9 = (bf16[4,256,128]{2,1,0:T(8,128)(2,1)S(1)}, bf16[4,256,128]{2,1,0:T(8,128)(2,1)S(1)}, u32[]{:S(2)}, u32[]{:S(2)}) collective-permute-start(bf16[4,256,128]{2,1,0:T(8,128)(2,1)S(1)} %pad_maximum_fusion.1.refs_0_), channel_id=1, source_target_pairs={{0,16},{4,20},{8,24},{12,28},{16,0},{20,4},{24,8},{28,12},{32,36},... | collective-permute-start | bytes 786440 | tf_op jit(solution)/shard_map/ppermute | solution.py:260
  20.7 0.0 collective-permute-done.2.refs_3_
  20.7 1.6 %shard_map.37 = (bf16[4096,128]{1,0:T(8,128)(2,1)S(1)}, s32[384]{0:T(512)S(1)}) custom-call(s32[5]{0:T(128)S(1)} %stack.35.info_ref, bf16[1040,128]{1,0:T(8,128)(2,1)S(1)} %pad_maximum_fusion.refs_0_, bf16[1040,128]{1,0:T(8,128)(2,1)S(1)} %collective-permute-done.refs_1_, bf16[1040,128]{1,0:T(8,128)(2,1)S(1)} %collective-permute-done.1.refs_2_, ...), custom_call_target="tpu_custom_call" | custom-call | flops 1073741824 | bytes 2097152 | tf_op jit(solution)/shard_map/pallas_call | solution.py:89
  22.3 0.0 collective-permute-done.6.refs_1_
  22.3 4.2 %shard_map.38.refs_6_ = f32[8,32,256]{2,1,0:T(8,128)S(1)} custom-call(s32[5]{0:T(128)S(1)} %stack.35.info_ref, s32[384]{0:T(512)S(1)} %get-tuple-element.11.unit_ref, bf16[4096,128]{1,0:T(8,128)(2,1)S(1)} %get-tuple-element.12.p_ref, bf16[4,256,128]{2,1,0:T(8,128)(2,1)S(1)} %pad_maximum_fusion.1.refs_0_, bf16[4,256,128]{2,1,0:T(8,128)(2,1)S(1)} %collective-permute-done.6.refs_1_), custom_call_target="tpu_custom_call" | custom-call | flops 4294967296 | bytes 2097152 | tf_op jit(solution)/shard_map/pallas_call | solution.py:219
  26.5 0.0 collective-permute-done.7.refs_0_
  26.5 0.0 collective-permute-done.8.refs_2_
  26.6 0.1 collective-permute-done.9.refs_4_
  26.6 2.3 %collective-permute-start.10 = (bf16[4,256,128]{2,1,0:T(8,128)(2,1)S(1)}, bf16[4,256,128]{2,1,0:T(8,128)(2,1)S(1)}, u32[]{:S(2)}, u32[]{:S(2)}) collective-permute-start(bf16[4,256,128]{2,1,0:T(8,128)(2,1)S(1)} %collective-permute-done.7.refs_0_), channel_id=1, source_target_pairs={{0,32},{32,0},{1,33},{33,1},{2,34},{34,2},{3,35},{35,3},{4,36},{36... | collective-permute-start | bytes 786440 | tf_op jit(solution)/shard_map/ppermute | solution.py:46
  28.9 0.1 collective-permute-start.11
  29.0 0.4 collective-permute-start.12
  29.4 0.7 %collective-permute-done.10.refs_1_ = bf16[4,256,128]{2,1,0:T(8,128)(2,1)S(1)} collective-permute-done((bf16[4,256,128]{2,1,0:T(8,128)(2,1)S(1)}, bf16[4,256,128]{2,1,0:T(8,128)(2,1)S(1)}, u32[]{:S(2)}, u32[]{:S(2)}) %collective-permute-start.10) | collective-permute-done | bytes 262176 | tf_op jit(solution)/shard_map/ppermute | solution.py:46
  30.1 0.4 collective-permute-done.11.refs_3_
  30.5 0.4 collective-permute-done.12.refs_5_
  30.8 11.9 %shard_map.39 = f32[8,8,128]{2,1,0:T(8,128)S(1)} custom-call(s32[5]{0:T(128)S(1)} %stack.35.info_ref, s32[384]{0:T(512)S(1)} %get-tuple-element.11.unit_ref, bf16[4096,128]{1,0:T(8,128)(2,1)S(1)} %get-tuple-element.12.p_ref, bf16[4,256,128]{2,1,0:T(8,128)(2,1)S(1)} %collective-permute-done.7.refs_0_, ...), custom_call_target="tpu_custom_call" | custom-call | flops 12884901888 | bytes 2097152 | tf_op jit(solution)/shard_map/pallas_call | solution.py:219
  42.7 11.4 %all_to_all.5.r_ref = f32[8,8,128]{2,1,0:T(8,128)} all-to-all(f32[8,8,128]{2,1,0:T(8,128)S(1)} %shard_map.39), channel_id=1, replica_groups=mesh['ylo'=2,'core'=2,'z'=4,'yhi'=2,'x'=4] {'z','yhi'}, dimensions={0} | all-to-all | bytes 65536 | tf_op jit(solution)/shard_map/all_to_all | solution.py:265
  54.1 1.5 %shard_map.40 = f32[32,256]{1,0:T(8,128)} custom-call(f32[8,8,128]{2,1,0:T(8,128)} %all_to_all.5.r_ref), custom_call_target="tpu_custom_call" | custom-call | tf_op jit(solution)/shard_map/pallas_call | solution.py:242
  (3 shorter events, 0.0 us)
Async XLA Ops:
  0.7 2.7 %copy-start = (bf16[32,8,128]{2,1,0:T(8,128)(2,1)S(1)}, bf16[32,8,128]{2,1,0:T(8,128)(2,1)}, u32[]{:S(2)}) copy-start(bf16[32,8,128]{2,1,0:T(8,128)(2,1)} %param.3) | copy-start | bytes 196612
  1.7 9.8 %collective-permute-start = (bf16[1040,128]{1,0:T(8,128)(2,1)S(1)}, bf16[1040,128]{1,0:T(8,128)(2,1)S(1)}, u32[]{:S(2)}, u32[]{:S(2)}) collective-permute-start(bf16[1040,128]{1,0:T(8,128)(2,1)S(1)} %pad_maximum_fusion.refs_0_), channel_id=1, source_target_pairs={{0,1},{1,2},{2,3},{3,0},{32,35},{33,32},{34,33},{35,34},{4,5},{5,6... | collective-permute-start | bytes 798728 | tf_op jit(solution)/shard_map/ppermute | solution.py:55
  3.3 8.5 %collective-permute-start.5 = (bf16[256,128]{1,0:T(8,128)(2,1)S(1)}, bf16[256,128]{1,0:T(8,128)(2,1)S(1)}, u32[]{:S(2)}, u32[]{:S(2)}) collective-permute-start(bf16[256,128]{1,0:T(8,128)(2,1)S(1)} %bitcast.12), channel_id=1, source_target_pairs={{0,4},{4,0},{8,12},{12,8},{16,20},{20,16},{24,28},{28,24},{32,48},... | collective-permute-start | bytes 196616 | tf_op jit(solution)/shard_map/ppermute | solution.py:254
  6.5 5.5 %collective-permute-start.3 = (bf16[256,128]{1,0:T(8,128)(2,1)S(1)}, bf16[256,128]{1,0:T(8,128)(2,1)S(1)}, u32[]{:S(2)}, u32[]{:S(2)}) collective-permute-start(bf16[256,128]{1,0:T(8,128)(2,1)S(1)} %bitcast.13), channel_id=1, source_target_pairs={{0,64},{4,68},{8,72},{12,76},{16,80},{20,84},{24,88},{28,92},{32,4... | collective-permute-start | bytes 196616 | tf_op jit(solution)/shard_map/ppermute | solution.py:254
  7.2 4.8 %collective-permute-start.4 = (bf16[256,128]{1,0:T(8,128)(2,1)S(1)}, bf16[256,128]{1,0:T(8,128)(2,1)S(1)}, u32[]{:S(2)}, u32[]{:S(2)}) collective-permute-start(bf16[256,128]{1,0:T(8,128)(2,1)S(1)} %bitcast.14), channel_id=1, source_target_pairs={{0,68},{4,64},{8,76},{12,72},{16,84},{20,80},{24,92},{28,88},{32,5... | collective-permute-start | bytes 196616 | tf_op jit(solution)/shard_map/ppermute | solution.py:254
  9.8 9.0 %collective-permute-start.1 = (bf16[1040,128]{1,0:T(8,128)(2,1)S(1)}, bf16[1040,128]{1,0:T(8,128)(2,1)S(1)}, u32[]{:S(2)}, u32[]{:S(2)}) collective-permute-start(bf16[1040,128]{1,0:T(8,128)(2,1)S(1)} %pad_maximum_fusion.refs_0_), channel_id=1, source_target_pairs={{0,3},{1,0},{2,1},{3,2},{32,33},{33,34},{34,35},{35,32},{4,7},{5,4... | collective-permute-start | bytes 798728 | tf_op jit(solution)/shard_map/ppermute | solution.py:55
  11.5 9.1 %collective-permute-start.2 = (bf16[1040,128]{1,0:T(8,128)(2,1)S(1)}, bf16[1040,128]{1,0:T(8,128)(2,1)S(1)}, u32[]{:S(2)}, u32[]{:S(2)}) collective-permute-start(bf16[1040,128]{1,0:T(8,128)(2,1)S(1)} %collective-permute-done.refs_1_), channel_id=1, source_target_pairs={{0,1},{1,2},{2,3},{3,0},{32,35},{33,32},{34,33},{35,34},{4,5},{5,6... | collective-permute-start | bytes 798728 | tf_op jit(solution)/shard_map/ppermute | solution.py:55
  12.0 10.3 %collective-permute-start.6 = (bf16[4,256,128]{2,1,0:T(8,128)(2,1)S(1)}, bf16[4,256,128]{2,1,0:T(8,128)(2,1)S(1)}, u32[]{:S(2)}, u32[]{:S(2)}) collective-permute-start(bf16[4,256,128]{2,1,0:T(8,128)(2,1)S(1)} %pad_maximum_fusion.1.refs_0_), channel_id=1, source_target_pairs={{0,32},{32,0},{1,33},{33,1},{2,34},{34,2},{3,35},{35,3},{4,36},{36... | collective-permute-start | bytes 786440 | tf_op jit(solution)/shard_map/ppermute | solution.py:46
  13.3 13.2 %collective-permute-start.7 = (bf16[4,256,128]{2,1,0:T(8,128)(2,1)S(1)}, bf16[4,256,128]{2,1,0:T(8,128)(2,1)S(1)}, u32[]{:S(2)}, u32[]{:S(2)}) collective-permute-start(bf16[4,256,128]{2,1,0:T(8,128)(2,1)S(1)} %pad_maximum_fusion.1.refs_0_), channel_id=1, source_target_pairs={{0,8},{4,12},{8,16},{12,20},{16,24},{20,28},{24,0},{28,4},{32,96},... | collective-permute-start | bytes 786440 | tf_op jit(solution)/shard_map/ppermute | solution.py:260
  14.2 12.4 %collective-permute-start.8 = (bf16[4,256,128]{2,1,0:T(8,128)(2,1)S(1)}, bf16[4,256,128]{2,1,0:T(8,128)(2,1)S(1)}, u32[]{:S(2)}, u32[]{:S(2)}) collective-permute-start(bf16[4,256,128]{2,1,0:T(8,128)(2,1)S(1)} %pad_maximum_fusion.1.refs_0_), channel_id=1, source_target_pairs={{0,24},{4,28},{8,0},{12,4},{16,8},{20,12},{24,16},{28,20},{32,100}... | collective-permute-start | bytes 786440 | tf_op jit(solution)/shard_map/ppermute | solution.py:260
  18.7 7.9 %collective-permute-start.9 = (bf16[4,256,128]{2,1,0:T(8,128)(2,1)S(1)}, bf16[4,256,128]{2,1,0:T(8,128)(2,1)S(1)}, u32[]{:S(2)}, u32[]{:S(2)}) collective-permute-start(bf16[4,256,128]{2,1,0:T(8,128)(2,1)S(1)} %pad_maximum_fusion.1.refs_0_), channel_id=1, source_target_pairs={{0,16},{4,20},{8,24},{12,28},{16,0},{20,4},{24,8},{28,12},{32,36},... | collective-permute-start | bytes 786440 | tf_op jit(solution)/shard_map/ppermute | solution.py:260
  26.6 3.5 %collective-permute-start.10 = (bf16[4,256,128]{2,1,0:T(8,128)(2,1)S(1)}, bf16[4,256,128]{2,1,0:T(8,128)(2,1)S(1)}, u32[]{:S(2)}, u32[]{:S(2)}) collective-permute-start(bf16[4,256,128]{2,1,0:T(8,128)(2,1)S(1)} %collective-permute-done.7.refs_0_), channel_id=1, source_target_pairs={{0,32},{32,0},{1,33},{33,1},{2,34},{34,2},{3,35},{35,3},{4,36},{36... | collective-permute-start | bytes 786440 | tf_op jit(solution)/shard_map/ppermute | solution.py:46
  28.9 1.5 %collective-permute-start.11 = (bf16[4,256,128]{2,1,0:T(8,128)(2,1)S(1)}, bf16[4,256,128]{2,1,0:T(8,128)(2,1)S(1)}, u32[]{:S(2)}, u32[]{:S(2)}) collective-permute-start(bf16[4,256,128]{2,1,0:T(8,128)(2,1)S(1)} %collective-permute-done.8.refs_2_), channel_id=1, source_target_pairs={{0,32},{32,0},{1,33},{33,1},{2,34},{34,2},{3,35},{35,3},{4,36},{36... | collective-permute-start | bytes 786440 | tf_op jit(solution)/shard_map/ppermute | solution.py:46
  29.0 1.8 %collective-permute-start.12 = (bf16[4,256,128]{2,1,0:T(8,128)(2,1)S(1)}, bf16[4,256,128]{2,1,0:T(8,128)(2,1)S(1)}, u32[]{:S(2)}, u32[]{:S(2)}) collective-permute-start(bf16[4,256,128]{2,1,0:T(8,128)(2,1)S(1)} %collective-permute-done.9.refs_4_), channel_id=1, source_target_pairs={{0,32},{32,0},{1,33},{33,1},{2,34},{34,2},{3,35},{35,3},{4,36},{36... | collective-permute-start | bytes 786440 | tf_op jit(solution)/shard_map/ppermute | solution.py:46

commit v7 on v6

--- a/solution.py
+++ b/solution.py
@@ -62,9 +62,7 @@
     )
 
 
-def prepare_kernel(info_ref, *refs):
-    pieces, p_ref, unit_ref = refs[:4], refs[4], refs[5]
-    core, x = info_ref[2], info_ref[3]
+def prepare(core, x, pieces, p_ref, unit_ref):
     count = jnp.int32(0)
     for m in range(4):
         from_x = lax.rem(x + 4 - jnp.where(core == 0, SHIFTS[m], -SHIFTS[m]), 4)
@@ -83,21 +81,6 @@
     for i in range(DEPTH):
         unit_ref[count + i] = unit_ref[count - 1]
     unit_ref[UNITS - 1] = lax.div(count + DEPTH - 1, DEPTH)
-
-
-def prepare(info, pieces):
-    return pl.pallas_call(
-        prepare_kernel,
-        out_shape=[
-            jax.ShapeDtypeStruct((4096, WIDTH), jnp.bfloat16),
-            jax.ShapeDtypeStruct((UNITS,), jnp.int32),
-        ],
-        in_specs=[pl.BlockSpec(memory_space=pltpu.SMEM)]
-        + [pl.BlockSpec(memory_space=pltpu.VMEM)] * 4,
-        out_specs=[pl.BlockSpec(memory_space=pltpu.VMEM), pl.BlockSpec(memory_space=pltpu.SMEM)],
-        compiler_params=pltpu.CompilerParams(vmem_limit_bytes=16 << 20),
-        cost_estimate=pl.CostEstimate(flops=1 << 30, bytes_accessed=2 << 20, transcendentals=0),
-    )(info, *pieces)
 
 
 def best_dots(rows, places, p_ref, m_ref, s_ref, unit_ref, turns, *acc):
@@ -164,10 +147,22 @@
                 s_ref[places[g][b // 2], 8 * o : 8 * o + 8, lanes] += top
 
 
-def score_kernel(shifts, parts, info_ref, unit_ref, p_ref, *refs):
+def first_kernel(info_ref, *refs):
+    pieces, rows, (p_ref, unit_ref, s_ref, m_ref) = refs[:4], refs[4:6], refs[6:]
+    prepare(info_ref[2], info_ref[3], pieces, p_ref, unit_ref)
+    s_ref[...] = jnp.zeros_like(s_ref)
+    score_rows(info_ref, unit_ref, p_ref, (0,), rows, s_ref, m_ref)
+
+
+def last_kernel(shifts, info_ref, unit_ref, p_ref, *refs):
     n = 2 * len(shifts)
-    rows, sums, out_ref, m_ref = refs[:n], refs[n : n + parts], refs[n + parts], refs[n + parts + 1]
-    s_ref = refs[n + parts + 2] if parts else out_ref
+    rows, (sum_ref, out_ref, s_ref, m_ref) = refs[:n], refs[n:]
+    s_ref[...] = sum_ref[...]
+    score_rows(info_ref, unit_ref, p_ref, shifts, rows, s_ref, m_ref)
+    pack(s_ref, out_ref)
+
+
+def score_rows(info_ref, unit_ref, p_ref, shifts, rows, s_ref, m_ref):
     z, yhi, core, ylo = info_ref[0], info_ref[1], info_ref[2], info_ref[4]
     y = yhi * 2 + ylo
 
@@ -182,17 +177,13 @@
         for j in (0, 2):
             groups.append([(mine, j), (mine, j + 1), (other, j), (other, j + 1)])
             places.append([place(chain, k, j + e) for chain in (core, 1 - core) for e in range(2)])
-    total = jnp.zeros(s_ref.shape, jnp.float32)
-    for part in sums:
-        total = total + part[...]
-    s_ref[...] = total
     pl.run_scoped(
         functools.partial(best_dots, groups, places, p_ref, m_ref, s_ref, unit_ref, unit_ref[UNITS - 1]),
         *[pltpu.ACC(u)((32, 256), jnp.float32) for u in range(2) for _ in range(DEPTH)],
     )
-    if not parts:
-        return
-
+
+
+def pack(s_ref, out_ref):
     lane = lax.broadcasted_iota(jnp.int32, (32, 256), 1)
     row = lax.broadcasted_iota(jnp.int32, (32, 256), 0)
     pick = jnp.where(lane // 8 == row, 1.0 / 32, 0.0).astype(jnp.bfloat16)
@@ -214,21 +205,47 @@
         out_ref[g] = jnp.concatenate([c[0:8], c[8:16], c[16:24], c[24:32]], axis=1)
 
 
-def score(info, units, slots, shifts, rows, sums=()):
-    sums_shape = (8, 32, 256)
+SUMS = (8, 32, 256)
+
+
+def cost(arrays):
+    return pl.CostEstimate(
+        flops=arrays * 2048 * 4096 * 256 * 2, bytes_accessed=2 << 20, transcendentals=0
+    )
+
+
+def score_first(info, pieces, rows):
     return pl.pallas_call(
-        functools.partial(score_kernel, shifts, len(sums)),
-        out_shape=jax.ShapeDtypeStruct((8, 8, 128) if sums else sums_shape, jnp.float32),
+        first_kernel,
+        out_shape=[
+            jax.ShapeDtypeStruct((4096, WIDTH), jnp.bfloat16),
+            jax.ShapeDtypeStruct((UNITS,), jnp.int32),
+            jax.ShapeDtypeStruct(SUMS, jnp.float32),
+        ],
+        in_specs=[pl.BlockSpec(memory_space=pltpu.SMEM)]
+        + [pl.BlockSpec(memory_space=pltpu.VMEM)] * 6,
+        out_specs=[
+            pl.BlockSpec(memory_space=pltpu.VMEM),
+            pl.BlockSpec(memory_space=pltpu.SMEM),
+            pl.BlockSpec(memory_space=pltpu.VMEM),
+        ],
+        scratch_shapes=[pltpu.VMEM((8, 33, 8, 128), jnp.float32)],
+        compiler_params=pltpu.CompilerParams(vmem_limit_bytes=32 << 20),
+        cost_estimate=cost(1),
+    )(info, *pieces, *rows)
+
+
+def score_last(info, units, slots, shifts, rows, sums):
+    return pl.pallas_call(
+        functools.partial(last_kernel, shifts),
+        out_shape=jax.ShapeDtypeStruct((8, 8, 128), jnp.float32),
         in_specs=[pl.BlockSpec(memory_space=pltpu.SMEM)] * 2
-        + [pl.BlockSpec(memory_space=pltpu.VMEM)] * (1 + len(rows) + len(sums)),
+        + [pl.BlockSpec(memory_space=pltpu.VMEM)] * (2 + len(rows)),
         out_specs=pl.BlockSpec(memory_space=pltpu.VMEM),
-        scratch_shapes=[pltpu.VMEM((8, 33, 8, 128), jnp.float32)]
-        + ([pltpu.VMEM(sums_shape, jnp.float32)] if sums else []),
+        scratch_shapes=[pltpu.VMEM(SUMS, jnp.float32), pltpu.VMEM((8, 33, 8, 128), jnp.float32)],
         compiler_params=pltpu.CompilerParams(vmem_limit_bytes=32 << 20),
-        cost_estimate=pl.CostEstimate(
-            flops=len(shifts) * 2048 * 4096 * 256 * 2, bytes_accessed=2 << 20, transcendentals=0
-        ),
-    )(info, units, slots, *rows, *sums)
+        cost_estimate=cost(len(shifts)),
+    )(info, units, slots, *rows, sums)
 
 
 def place_kernel(r_ref, o_ref):
@@ -253,15 +270,13 @@
 
     near = [own] + [lax.ppermute(own, PLANE, along(True, k)) for k in SHIFTS[1:]]
     filled = with_lengths(passages, lengths)
-    once = on_x(filled, 1)
-    moved = [filled, once, on_x(filled, -1), on_x(once, 1)]
+    moved = [filled] + [on_x(filled, k) for k in SHIFTS[1:]]
     block = jnp.stack(near)
-    slots, units = prepare(info, moved)
-    mine = [block] + [lax.ppermute(block, PLANE, along(False, k)) for k in SHIFTS[1:]]
-    first = score(info, units, slots, (0,), (block, to_core(block)))
-    first, *late = lax.optimization_barrier((first, *mine[1:]))
-    rows = [w for v in late for w in (v, to_core(v))]
-    terms = score(info, units, slots, (1, 2, 3), rows, (first,))
+    mine = [lax.ppermute(block, PLANE, along(False, k)) for k in SHIFTS[1:]]
+    slots, units, sums = score_first(info, moved, (block, to_core(block)))
+    sums, mine[0] = lax.optimization_barrier((sums, mine[0]))
+    rows = [w for v in mine for w in (v, to_core(v))]
+    terms = score_last(info, units, slots, (1, 2, 3), rows, sums)
     received = lax.all_to_all(terms, ("z", "yhi"), 0, 0, tiled=True)
     return place(received)
 

time: 55.4 us -> 60.9 us (1.099); the launches traced: 55.6 us -> 59.8 us
  starting transfers between devices: 19.3 us -> 24.2 us
  other arithmetic: 1.7 us -> 1.04 us
    ppermute x3, starting transfers between devices: 5.16 us -> 11.9 us  [per_device(): mine = [lax.ppermute(block, PLANE, along(False, k)) for k in SHIFTS[1:]]]
    ppermute x4, starting transfers between devices: 4.03 us -> 0.66 us  [to_core(): return lax.ppermute(v, 'core', [(0, 1), (1, 0)])]
    ppermute x3, starting transfers between devices: 3.67 us -> 5.12 us  [on_x(): return lax.ppermute(v, ('core', 'x'), pairs)]
    convert_element_type x1, other arithmetic: 0.66 us -> 0.01 us  [with_lengths(): tail = jnp.pad(lengths.astype(passages.dtype), (0, WIDTH - OWN))]
    pallas_call x3 -> x2, Pallas kernels: 17.7 us -> 18.2 us  [the longest x1 12.8 us: score_last(): pl.pallas_call(functools.partial(last_kernel, shifts), out_shape=jax.Shap...]
  transfers between devices with their start and end apart: 13 -> 13, of which waited for: 6 -> 5; matrix products, arithmetic and copies ran while one was open for 0% -> 2% of each run, Pallas kernels for 11% -> 9%
where the time goes in v7:
time: 60.9 us; the launch traced here: 59.8 us
  starting transfers between devices  24.2 us (40%)
  Pallas kernels  19.7 us (32%)
  blocking collectives  10.8 us (18%)
  waiting for transfers between devices  3.92 us (6%)
  other arithmetic  1.04 us (2%)
    pallas_call x1, Pallas kernels, score_last(): pl.pallas_call(functools.partial(last_kernel, shifts), out_shape=jax.Shap...  12.8 us
    ppermute x3, starting transfers between devices, per_device(): mine = [lax.ppermute(block, PLANE, along(False, k)) for k in SHIFTS[1:]]  11.9 us
    all_to_all x1, blocking collectives, per_device(): received = lax.all_to_all(terms, ('z', 'yhi'), 0, 0, tiled=True)  10.8 us
    ppermute x3, starting transfers between devices, per_device(): lax.ppermute(own, PLANE, along(True, k))  6.51 us
    pallas_call x1, Pallas kernels, score_first(): pl.pallas_call(first_kernel, out_shape=[jax.ShapeDtypeStruct((4096, WIDTH...  5.36 us
    ppermute x3, starting transfers between devices, on_x(): return lax.ppermute(v, ('core', 'x'), pairs)  5.12 us
    ppermute x3, waiting for transfers between devices, on_x(): return lax.ppermute(v, ('core', 'x'), pairs)  2.05 us
    ppermute x4, waiting for transfers between devices, to_core(): return lax.ppermute(v, 'core', [(0, 1), (1, 0)])  1.53 us
  transfers between devices with their start and end apart: 13, of which 5 were waited for; matrix products, arithmetic and copies ran while one was open for 2% of the time, Pallas kernels for 9%

profile of v7, /device:TPU:0, one launch (start us, length us, event | category | flops | bytes accessed | tf_op | source)
XLA Modules:
  0.0 59.8 jit_solution(14043073231997700635)
XLA Ops:
  0.0 0.0 copy-start.1
  0.0 3.3 %collective-permute-start.5 = (bf16[256,128]{1,0:T(8,128)(2,1)}, bf16[256,128]{1,0:T(8,128)(2,1)S(1)}, u32[]{:S(2)}, u32[]{:S(2)}) collective-permute-start(bf16[256,128]{1,0:T(8,128)(2,1)} %bitcast.12), channel_id=1, source_target_pairs={{0,4},{4,0},{8,12},{12,8},{16,20},{20,16},{24,28},{28,24},{32,48},... | collective-permute-start | bytes 196616 | tf_op jit(solution)/shard_map/ppermute | solution.py:271
  3.3 0.7 %collective-permute-start.3 = (bf16[256,128]{1,0:T(8,128)(2,1)}, bf16[256,128]{1,0:T(8,128)(2,1)S(1)}, u32[]{:S(2)}, u32[]{:S(2)}) collective-permute-start(bf16[256,128]{1,0:T(8,128)(2,1)} %bitcast.13), channel_id=1, source_target_pairs={{0,64},{4,68},{8,72},{12,76},{16,80},{20,84},{24,88},{28,92},{32,4... | collective-permute-start | bytes 196616 | tf_op jit(solution)/shard_map/ppermute | solution.py:271
  4.0 2.6 %collective-permute-start.4 = (bf16[256,128]{1,0:T(8,128)(2,1)}, bf16[256,128]{1,0:T(8,128)(2,1)S(1)}, u32[]{:S(2)}, u32[]{:S(2)}) collective-permute-start(bf16[256,128]{1,0:T(8,128)(2,1)} %bitcast.14), channel_id=1, source_target_pairs={{0,68},{4,64},{8,76},{12,72},{16,84},{20,80},{24,92},{28,88},{32,5... | collective-permute-start | bytes 196616 | tf_op jit(solution)/shard_map/ppermute | solution.py:271
  6.5 0.0 copy-done.1
  6.5 0.0 copy-start
  6.6 1.0 %pad_maximum_fusion.refs_0_ = bf16[1040,128]{1,0:T(8,128)(2,1)S(1)} fusion(bf16[16,128]{1,0:T(8,128)(2,1)S(1)} %broadcast_in_dim.3, bf16[1024,128]{1,0:T(8,128)(2,1)} %bitcast.11), kind=kLoop, calls=%fused_computation | loop fusion | flops 532480 | bytes 532480 | tf_op jit(solution)/shard_map/concatenate | solution.py:60
  7.6 1.6 %collective-permute-start = (bf16[1040,128]{1,0:T(8,128)(2,1)S(1)}, bf16[1040,128]{1,0:T(8,128)(2,1)S(1)}, u32[]{:S(2)}, u32[]{:S(2)}) collective-permute-start(bf16[1040,128]{1,0:T(8,128)(2,1)S(1)} %pad_maximum_fusion.refs_0_), channel_id=1, source_target_pairs={{0,1},{1,2},{2,3},{3,0},{32,35},{33,32},{34,33},{35,34},{4,5},{5,6... | collective-permute-start | bytes 798728 | tf_op jit(solution)/shard_map/ppermute | solution.py:55
  9.1 1.7 %collective-permute-start.1 = (bf16[1040,128]{1,0:T(8,128)(2,1)S(1)}, bf16[1040,128]{1,0:T(8,128)(2,1)S(1)}, u32[]{:S(2)}, u32[]{:S(2)}) collective-permute-start(bf16[1040,128]{1,0:T(8,128)(2,1)S(1)} %pad_maximum_fusion.refs_0_), channel_id=1, source_target_pairs={{0,3},{1,0},{2,1},{3,2},{32,33},{33,34},{34,35},{35,32},{4,7},{5,4... | collective-permute-start | bytes 798728 | tf_op jit(solution)/shard_map/ppermute | solution.py:55
  10.9 0.0 collective-permute-done.5
  10.9 1.8 %collective-permute-start.2 = (bf16[1040,128]{1,0:T(8,128)(2,1)S(1)}, bf16[1040,128]{1,0:T(8,128)(2,1)S(1)}, u32[]{:S(2)}, u32[]{:S(2)}) collective-permute-start(bf16[1040,128]{1,0:T(8,128)(2,1)S(1)} %pad_maximum_fusion.refs_0_), channel_id=1, source_target_pairs={{0,2},{1,3},{2,0},{3,1},{32,34},{33,35},{34,32},{35,33},{4,6},{5,7... | collective-permute-start | bytes 798728 | tf_op jit(solution)/shard_map/ppermute | solution.py:55
  12.7 0.0 collective-permute-done.3
  12.7 0.0 collective-permute-done.4
  12.7 0.0 copy-done
  12.7 0.1 collective-permute-start.6
  12.8 0.1 stack.35.info_ref
  12.9 1.9 %collective-permute-start.7 = (bf16[4,256,128]{2,1,0:T(8,128)(2,1)S(1)}, bf16[4,256,128]{2,1,0:T(8,128)(2,1)S(1)}, u32[]{:S(2)}, u32[]{:S(2)}) collective-permute-start(bf16[4,256,128]{2,1,0:T(8,128)(2,1)S(1)} %pad_maximum_fusion.1.refs_4_), channel_id=1, source_target_pairs={{0,8},{4,12},{8,16},{12,20},{16,24},{20,28},{24,0},{28,4},{32,96},... | collective-permute-start | bytes 786440 | tf_op jit(solution)/shard_map/ppermute | solution.py:275
  14.8 2.0 %collective-permute-done.refs_1_ = bf16[1040,128]{1,0:T(8,128)(2,1)S(1)} collective-permute-done((bf16[1040,128]{1,0:T(8,128)(2,1)S(1)}, bf16[1040,128]{1,0:T(8,128)(2,1)S(1)}, u32[]{:S(2)}, u32[]{:S(2)}) %collective-permute-start) | collective-permute-done | bytes 266272 | tf_op jit(solution)/shard_map/ppermute | solution.py:55
  16.9 8.4 %collective-permute-start.9 = (bf16[4,256,128]{2,1,0:T(8,128)(2,1)S(1)}, bf16[4,256,128]{2,1,0:T(8,128)(2,1)S(1)}, u32[]{:S(2)}, u32[]{:S(2)}) collective-permute-start(bf16[4,256,128]{2,1,0:T(8,128)(2,1)S(1)} %pad_maximum_fusion.1.refs_4_), channel_id=1, source_target_pairs={{0,24},{4,28},{8,0},{12,4},{16,8},{20,12},{24,16},{28,20},{32,100}... | collective-permute-start | bytes 786440 | tf_op jit(solution)/shard_map/ppermute | solution.py:275
  25.3 0.0 collective-permute-done.1.refs_2_
  25.3 1.6 %collective-permute-start.11 = (bf16[4,256,128]{2,1,0:T(8,128)(2,1)S(1)}, bf16[4,256,128]{2,1,0:T(8,128)(2,1)S(1)}, u32[]{:S(2)}, u32[]{:S(2)}) collective-permute-start(bf16[4,256,128]{2,1,0:T(8,128)(2,1)S(1)} %pad_maximum_fusion.1.refs_4_), channel_id=1, source_target_pairs={{0,16},{4,20},{8,24},{12,28},{16,0},{20,4},{24,8},{28,12},{32,36},... | collective-permute-start | bytes 786440 | tf_op jit(solution)/shard_map/ppermute | solution.py:275
  26.9 0.0 collective-permute-done.2.refs_3_
  26.9 0.0 collective-permute-done.6.refs_5_
  26.9 5.4 %shard_map.37 = (bf16[4096,128]{1,0:T(8,128)(2,1)S(1)}, s32[384]{0:T(512)S(1)}, f32[8,32,256]{2,1,0:T(8,128)S(1)}) custom-call(s32[5]{0:T(128)S(1)} %stack.35.info_ref, bf16[1040,128]{1,0:T(8,128)(2,1)S(1)} %pad_maximum_fusion.refs_0_, bf16[1040,128]{1,0:T(8,128)(2,1)S(1)} %collective-permute-done.refs_1_, ...), custom_call_target="tpu_custom_call" | custom-call | flops 4294967296 | bytes 2097152 | tf_op jit(solution)/shard_map/pallas_call | solution.py:218
  32.3 0.0 collective-permute-done.7.refs_0_
  32.3 0.1 collective-permute-start.8
  32.4 0.0 collective-permute-done.9.refs_2_
  32.4 0.5 collective-permute-start.10
  32.9 0.3 collective-permute-done.11.refs_4_
  33.2 0.0 collective-permute-start.12
  33.2 0.7 %collective-permute-done.8.refs_1_ = bf16[4,256,128]{2,1,0:T(8,128)(2,1)S(1)} collective-permute-done((bf16[4,256,128]{2,1,0:T(8,128)(2,1)S(1)}, bf16[4,256,128]{2,1,0:T(8,128)(2,1)S(1)}, u32[]{:S(2)}, u32[]{:S(2)}) %collective-permute-start.8) | collective-permute-done | bytes 262176 | tf_op jit(solution)/shard_map/ppermute | solution.py:46
  33.9 0.4 collective-permute-done.10.refs_3_
  34.3 0.5 collective-permute-done.12.refs_5_
  34.7 12.8 %shard_map.38 = f32[8,8,128]{2,1,0:T(8,128)S(1)} custom-call(s32[5]{0:T(128)S(1)} %stack.35.info_ref, s32[384]{0:T(512)S(1)} %get-tuple-element.10.unit_ref, bf16[4096,128]{1,0:T(8,128)(2,1)S(1)} %get-tuple-element.11.p_ref, bf16[4,256,128]{2,1,0:T(8,128)(2,1)S(1)} %collective-permute-done.7.refs_0_, ...), custom_call_target="tpu_custom_call" | custom-call | flops 12884901888 | bytes 2097152 | tf_op jit(solution)/shard_map/pallas_call | solution.py:239
  47.5 10.8 %all_to_all.5.r_ref = f32[8,8,128]{2,1,0:T(8,128)} all-to-all(f32[8,8,128]{2,1,0:T(8,128)S(1)} %shard_map.38), channel_id=1, replica_groups=mesh['ylo'=2,'core'=2,'z'=4,'yhi'=2,'x'=4] {'z','yhi'}, dimensions={0} | all-to-all | bytes 65536 | tf_op jit(solution)/shard_map/all_to_all | solution.py:280
  58.4 1.5 %shard_map.39 = f32[32,256]{1,0:T(8,128)} custom-call(f32[8,8,128]{2,1,0:T(8,128)} %all_to_all.5.r_ref), custom_call_target="tpu_custom_call" | custom-call | tf_op jit(solution)/shard_map/pallas_call | solution.py:259
  (4 shorter events, 0.1 us)
Async XLA Ops:
  0.0 6.5 %copy-start.1 = (s32[8]{0:T(128)S(1)}, s32[8]{0:T(128)}, u32[]{:S(2)}) copy-start(s32[8]{0:T(128)} %param.5) | copy-start | bytes 100
  0.0 10.9 %collective-permute-start.5 = (bf16[256,128]{1,0:T(8,128)(2,1)}, bf16[256,128]{1,0:T(8,128)(2,1)S(1)}, u32[]{:S(2)}, u32[]{:S(2)}) collective-permute-start(bf16[256,128]{1,0:T(8,128)(2,1)} %bitcast.12), channel_id=1, source_target_pairs={{0,4},{4,0},{8,12},{12,8},{16,20},{20,16},{24,28},{28,24},{32,48},... | collective-permute-start | bytes 196616 | tf_op jit(solution)/shard_map/ppermute | solution.py:271
  3.3 9.4 %collective-permute-start.3 = (bf16[256,128]{1,0:T(8,128)(2,1)}, bf16[256,128]{1,0:T(8,128)(2,1)S(1)}, u32[]{:S(2)}, u32[]{:S(2)}) collective-permute-start(bf16[256,128]{1,0:T(8,128)(2,1)} %bitcast.13), channel_id=1, source_target_pairs={{0,64},{4,68},{8,72},{12,76},{16,80},{20,84},{24,88},{28,92},{32,4... | collective-permute-start | bytes 196616 | tf_op jit(solution)/shard_map/ppermute | solution.py:271
  4.0 8.7 %collective-permute-start.4 = (bf16[256,128]{1,0:T(8,128)(2,1)}, bf16[256,128]{1,0:T(8,128)(2,1)S(1)}, u32[]{:S(2)}, u32[]{:S(2)}) collective-permute-start(bf16[256,128]{1,0:T(8,128)(2,1)} %bitcast.14), channel_id=1, source_target_pairs={{0,68},{4,64},{8,76},{12,72},{16,84},{20,80},{24,92},{28,88},{32,5... | collective-permute-start | bytes 196616 | tf_op jit(solution)/shard_map/ppermute | solution.py:271
  6.5 6.1 %copy-start = (bf16[32,8,128]{2,1,0:T(8,128)(2,1)S(1)}, bf16[32,8,128]{2,1,0:T(8,128)(2,1)}, u32[]{:S(2)}) copy-start(bf16[32,8,128]{2,1,0:T(8,128)(2,1)} %param.3) | copy-start | bytes 196612
  7.6 9.3 %collective-permute-start = (bf16[1040,128]{1,0:T(8,128)(2,1)S(1)}, bf16[1040,128]{1,0:T(8,128)(2,1)S(1)}, u32[]{:S(2)}, u32[]{:S(2)}) collective-permute-start(bf16[1040,128]{1,0:T(8,128)(2,1)S(1)} %pad_maximum_fusion.refs_0_), channel_id=1, source_target_pairs={{0,1},{1,2},{2,3},{3,0},{32,35},{33,32},{34,33},{35,34},{4,5},{5,6... | collective-permute-start | bytes 798728 | tf_op jit(solution)/shard_map/ppermute | solution.py:55
  9.1 16.2 %collective-permute-start.1 = (bf16[1040,128]{1,0:T(8,128)(2,1)S(1)}, bf16[1040,128]{1,0:T(8,128)(2,1)S(1)}, u32[]{:S(2)}, u32[]{:S(2)}) collective-permute-start(bf16[1040,128]{1,0:T(8,128)(2,1)S(1)} %pad_maximum_fusion.refs_0_), channel_id=1, source_target_pairs={{0,3},{1,0},{2,1},{3,2},{32,33},{33,34},{34,35},{35,32},{4,7},{5,4... | collective-permute-start | bytes 798728 | tf_op jit(solution)/shard_map/ppermute | solution.py:55
  10.9 16.0 %collective-permute-start.2 = (bf16[1040,128]{1,0:T(8,128)(2,1)S(1)}, bf16[1040,128]{1,0:T(8,128)(2,1)S(1)}, u32[]{:S(2)}, u32[]{:S(2)}) collective-permute-start(bf16[1040,128]{1,0:T(8,128)(2,1)S(1)} %pad_maximum_fusion.refs_0_), channel_id=1, source_target_pairs={{0,2},{1,3},{2,0},{3,1},{32,34},{33,35},{34,32},{35,33},{4,6},{5,7... | collective-permute-start | bytes 798728 | tf_op jit(solution)/shard_map/ppermute | solution.py:55
  12.7 14.1 %collective-permute-start.6 = (bf16[4,256,128]{2,1,0:T(8,128)(2,1)S(1)}, bf16[4,256,128]{2,1,0:T(8,128)(2,1)S(1)}, u32[]{:S(2)}, u32[]{:S(2)}) collective-permute-start(bf16[4,256,128]{2,1,0:T(8,128)(2,1)S(1)} %pad_maximum_fusion.1.refs_4_), channel_id=1, source_target_pairs={{0,32},{32,0},{1,33},{33,1},{2,34},{34,2},{3,35},{35,3},{4,36},{36... | collective-permute-start | bytes 786440 | tf_op jit(solution)/shard_map/ppermute | solution.py:46
  12.9 19.3 %collective-permute-start.7 = (bf16[4,256,128]{2,1,0:T(8,128)(2,1)S(1)}, bf16[4,256,128]{2,1,0:T(8,128)(2,1)S(1)}, u32[]{:S(2)}, u32[]{:S(2)}) collective-permute-start(bf16[4,256,128]{2,1,0:T(8,128)(2,1)S(1)} %pad_maximum_fusion.1.refs_4_), channel_id=1, source_target_pairs={{0,8},{4,12},{8,16},{12,20},{16,24},{20,28},{24,0},{28,4},{32,96},... | collective-permute-start | bytes 786440 | tf_op jit(solution)/shard_map/ppermute | solution.py:275
  16.9 15.5 %collective-permute-start.9 = (bf16[4,256,128]{2,1,0:T(8,128)(2,1)S(1)}, bf16[4,256,128]{2,1,0:T(8,128)(2,1)S(1)}, u32[]{:S(2)}, u32[]{:S(2)}) collective-permute-start(bf16[4,256,128]{2,1,0:T(8,128)(2,1)S(1)} %pad_maximum_fusion.1.refs_4_), channel_id=1, source_target_pairs={{0,24},{4,28},{8,0},{12,4},{16,8},{20,12},{24,16},{28,20},{32,100}... | collective-permute-start | bytes 786440 | tf_op jit(solution)/shard_map/ppermute | solution.py:275
  25.3 7.9 %collective-permute-start.11 = (bf16[4,256,128]{2,1,0:T(8,128)(2,1)S(1)}, bf16[4,256,128]{2,1,0:T(8,128)(2,1)S(1)}, u32[]{:S(2)}, u32[]{:S(2)}) collective-permute-start(bf16[4,256,128]{2,1,0:T(8,128)(2,1)S(1)} %pad_maximum_fusion.1.refs_4_), channel_id=1, source_target_pairs={{0,16},{4,20},{8,24},{12,28},{16,0},{20,4},{24,8},{28,12},{32,36},... | collective-permute-start | bytes 786440 | tf_op jit(solution)/shard_map/ppermute | solution.py:275
  32.3 1.6 %collective-permute-start.8 = (bf16[4,256,128]{2,1,0:T(8,128)(2,1)S(1)}, bf16[4,256,128]{2,1,0:T(8,128)(2,1)S(1)}, u32[]{:S(2)}, u32[]{:S(2)}) collective-permute-start(bf16[4,256,128]{2,1,0:T(8,128)(2,1)S(1)} %collective-permute-done.7.refs_0_), channel_id=1, source_target_pairs={{0,32},{32,0},{1,33},{33,1},{2,34},{34,2},{3,35},{35,3},{4,36},{36... | collective-permute-start | bytes 786440 | tf_op jit(solution)/shard_map/ppermute | solution.py:46
  32.4 1.9 %collective-permute-start.10 = (bf16[4,256,128]{2,1,0:T(8,128)(2,1)S(1)}, bf16[4,256,128]{2,1,0:T(8,128)(2,1)S(1)}, u32[]{:S(2)}, u32[]{:S(2)}) collective-permute-start(bf16[4,256,128]{2,1,0:T(8,128)(2,1)S(1)} %collective-permute-done.9.refs_2_), channel_id=1, source_target_pairs={{0,32},{32,0},{1,33},{33,1},{2,34},{34,2},{3,35},{35,3},{4,36},{36... | collective-permute-start | bytes 786440 | tf_op jit(solution)/shard_map/ppermute | solution.py:46
  33.2 1.5 %collective-permute-start.12 = (bf16[4,256,128]{2,1,0:T(8,128)(2,1)S(1)}, bf16[4,256,128]{2,1,0:T(8,128)(2,1)S(1)}, u32[]{:S(2)}, u32[]{:S(2)}) collective-permute-start(bf16[4,256,128]{2,1,0:T(8,128)(2,1)S(1)} %collective-permute-done.11.refs_4_), channel_id=1, source_target_pairs={{0,32},{32,0},{1,33},{33,1},{2,34},{34,2},{3,35},{35,3},{4,36},{36... | collective-permute-start | bytes 786440 | tf_op jit(solution)/shard_map/ppermute | solution.py:46

commit v8 on v7

--- a/solution.py
+++ b/solution.py
@@ -270,11 +270,12 @@
 
     near = [own] + [lax.ppermute(own, PLANE, along(True, k)) for k in SHIFTS[1:]]
     filled = with_lengths(passages, lengths)
-    moved = [filled] + [on_x(filled, k) for k in SHIFTS[1:]]
+    once = on_x(filled, 1)
+    moved = [filled, once, on_x(filled, -1), on_x(once, 1)]
     block = jnp.stack(near)
     mine = [lax.ppermute(block, PLANE, along(False, k)) for k in SHIFTS[1:]]
     slots, units, sums = score_first(info, moved, (block, to_core(block)))
-    sums, mine[0] = lax.optimization_barrier((sums, mine[0]))
+    sums, mine[2] = lax.optimization_barrier((sums, mine[2]))
     rows = [w for v in mine for w in (v, to_core(v))]
     terms = score_last(info, units, slots, (1, 2, 3), rows, sums)
     received = lax.all_to_all(terms, ("z", "yhi"), 0, 0, tiled=True)

time: 60.9 us -> 58.1 us (0.954)
  starting transfers between devices: 24.2 us -> 18.5 us
  blocking collectives: 10.8 us -> 12.2 us
  waiting for transfers between devices: 3.92 us -> 5 us
  other arithmetic: 1.04 us -> 1.7 us
    ppermute x3, starting transfers between devices: 11.9 us -> 6.03 us  [per_device(): mine = [lax.ppermute(block, PLANE, along(False, k)) for k in SHIFTS[1:]]]
    ppermute x4, starting transfers between devices: 0.66 us -> 2.39 us  [to_core(): return lax.ppermute(v, 'core', [(0, 1), (1, 0)])]
    ppermute x3, starting transfers between devices: 5.12 us -> 3.67 us  [on_x(): return lax.ppermute(v, ('core', 'x'), pairs)]
    all_to_all x1, blocking collectives: 10.8 us -> 12.2 us  [per_device(): received = lax.all_to_all(terms, ('z', 'yhi'), 0, 0, tiled=True)]
    convert_element_type x1, other arithmetic: 0.01 us -> 0.66 us  [with_lengths(): tail = jnp.pad(lengths.astype(passages.dtype), (0, WIDTH - OWN))]
  transfers between devices with their start and end apart: 13 -> 13, of which waited for: 5 -> 4; matrix products, arithmetic and copies ran while one was open for 2% -> 0% of each run, Pallas kernels for 9% -> 9%
where the time goes in v8:
time: 58.1 us; the launch traced here: 57.3 us
  Pallas kernels  19.6 us (34%)
  starting transfers between devices  18.5 us (32%)
  blocking collectives  12.2 us (21%)
  waiting for transfers between devices  5 us (9%)
  other arithmetic  1.7 us (3%)
    pallas_call x1, Pallas kernels, score_last(): pl.pallas_call(functools.partial(last_kernel, shifts), out_shape=jax.Shap...  12.8 us
    all_to_all x1, blocking collectives, per_device(): received = lax.all_to_all(terms, ('z', 'yhi'), 0, 0, tiled=True)  12.2 us
    ppermute x3, starting transfers between devices, per_device(): lax.ppermute(own, PLANE, along(True, k))  6.43 us
    ppermute x3, starting transfers between devices, per_device(): mine = [lax.ppermute(block, PLANE, along(False, k)) for k in SHIFTS[1:]]  6.03 us
    pallas_call x1, Pallas kernels, score_first(): pl.pallas_call(first_kernel, out_shape=[jax.ShapeDtypeStruct((4096, WIDTH...  5.35 us
    ppermute x3, starting transfers between devices, on_x(): return lax.ppermute(v, ('core', 'x'), pairs)  3.67 us
    ppermute x3, waiting for transfers between devices, on_x(): return lax.ppermute(v, ('core', 'x'), pairs)  2.5 us
    ppermute x4, starting transfers between devices, to_core(): return lax.ppermute(v, 'core', [(0, 1), (1, 0)])  2.39 us
  transfers between devices with their start and end apart: 13, of which 4 were waited for; matrix products, arithmetic and copies ran while one was open for 0% of the time, Pallas kernels for 9%

profile of v8, /device:TPU:0, one launch (start us, length us, event | category | flops | bytes accessed | tf_op | source)
XLA Modules:
  0.0 57.3 jit_solution(6076746951275311101)
XLA Ops:
  0.0 0.7 %convert_element_type.5 = bf16[8]{0:T(256)(128)(2,1)S(1)} convert(s32[8]{0:T(128)} %param.5) | non-fusion elementwise | flops 8 | bytes 48 | tf_op jit(solution)/shard_map/convert_element_type | solution.py:59
  0.7 0.0 copy-start
  0.7 1.0 %pad_maximum_fusion.refs_0_ = bf16[1040,128]{1,0:T(8,128)(2,1)S(1)} fusion(bf16[16,128]{1,0:T(8,128)(2,1)S(1)} %broadcast_in_dim.3, bf16[1024,128]{1,0:T(8,128)(2,1)} %bitcast.11), kind=kLoop, calls=%fused_computation | loop fusion | flops 532480 | bytes 532480 | tf_op jit(solution)/shard_map/concatenate | solution.py:60
  1.7 1.6 %collective-permute-start = (bf16[1040,128]{1,0:T(8,128)(2,1)S(1)}, bf16[1040,128]{1,0:T(8,128)(2,1)S(1)}, u32[]{:S(2)}, u32[]{:S(2)}) collective-permute-start(bf16[1040,128]{1,0:T(8,128)(2,1)S(1)} %pad_maximum_fusion.refs_0_), channel_id=1, source_target_pairs={{0,1},{1,2},{2,3},{3,0},{32,35},{33,32},{34,33},{35,34},{4,5},{5,6... | collective-permute-start | bytes 798728 | tf_op jit(solution)/shard_map/ppermute | solution.py:55
  3.3 0.0 copy-done
  3.3 3.2 %collective-permute-start.5 = (bf16[256,128]{1,0:T(8,128)(2,1)S(1)}, bf16[256,128]{1,0:T(8,128)(2,1)S(1)}, u32[]{:S(2)}, u32[]{:S(2)}) collective-permute-start(bf16[256,128]{1,0:T(8,128)(2,1)S(1)} %bitcast.12), channel_id=1, source_target_pairs={{0,4},{4,0},{8,12},{12,8},{16,20},{20,16},{24,28},{28,24},{32,48},... | collective-permute-start | bytes 196616 | tf_op jit(solution)/shard_map/ppermute | solution.py:271
  6.5 0.7 %collective-permute-start.3 = (bf16[256,128]{1,0:T(8,128)(2,1)S(1)}, bf16[256,128]{1,0:T(8,128)(2,1)S(1)}, u32[]{:S(2)}, u32[]{:S(2)}) collective-permute-start(bf16[256,128]{1,0:T(8,128)(2,1)S(1)} %bitcast.13), channel_id=1, source_target_pairs={{0,64},{4,68},{8,72},{12,76},{16,80},{20,84},{24,88},{28,92},{32,4... | collective-permute-start | bytes 196616 | tf_op jit(solution)/shard_map/ppermute | solution.py:271
  7.2 2.6 %collective-permute-start.4 = (bf16[256,128]{1,0:T(8,128)(2,1)S(1)}, bf16[256,128]{1,0:T(8,128)(2,1)S(1)}, u32[]{:S(2)}, u32[]{:S(2)}) collective-permute-start(bf16[256,128]{1,0:T(8,128)(2,1)S(1)} %bitcast.14), channel_id=1, source_target_pairs={{0,68},{4,64},{8,76},{12,72},{16,84},{20,80},{24,92},{28,88},{32,5... | collective-permute-start | bytes 196616 | tf_op jit(solution)/shard_map/ppermute | solution.py:271
  9.8 1.7 %collective-permute-start.1 = (bf16[1040,128]{1,0:T(8,128)(2,1)S(1)}, bf16[1040,128]{1,0:T(8,128)(2,1)S(1)}, u32[]{:S(2)}, u32[]{:S(2)}) collective-permute-start(bf16[1040,128]{1,0:T(8,128)(2,1)S(1)} %pad_maximum_fusion.refs_0_), channel_id=1, source_target_pairs={{0,3},{1,0},{2,1},{3,2},{32,33},{33,34},{34,35},{35,32},{4,7},{5,4... | collective-permute-start | bytes 798728 | tf_op jit(solution)/shard_map/ppermute | solution.py:55
  11.5 0.0 collective-permute-done.refs_1_
  11.5 0.3 collective-permute-start.2
  11.8 0.0 collective-permute-done.5
  11.8 0.2 collective-permute-done.3
  12.0 0.0 collective-permute-done.4
  12.0 4.1 %collective-permute-start.9 = (bf16[4,256,128]{2,1,0:T(8,128)(2,1)S(1)}, bf16[4,256,128]{2,1,0:T(8,128)(2,1)S(1)}, u32[]{:S(2)}, u32[]{:S(2)}) collective-permute-start(bf16[4,256,128]{2,1,0:T(8,128)(2,1)S(1)} %pad_maximum_fusion.1.refs_4_), channel_id=1, source_target_pairs={{0,24},{4,28},{8,0},{12,4},{16,8},{20,12},{24,16},{28,20},{32,100}... | collective-permute-start | bytes 786440 | tf_op jit(solution)/shard_map/ppermute | solution.py:276
  16.2 0.0 collective-permute-start.7
  16.2 0.0 collective-permute-start.6
  16.2 0.1 stack.35.info_ref
  16.2 2.5 %collective-permute-done.1.refs_2_ = bf16[1040,128]{1,0:T(8,128)(2,1)S(1)} collective-permute-done((bf16[1040,128]{1,0:T(8,128)(2,1)S(1)}, bf16[1040,128]{1,0:T(8,128)(2,1)S(1)}, u32[]{:S(2)}, u32[]{:S(2)}) %collective-permute-start.1) | collective-permute-done | bytes 266272 | tf_op jit(solution)/shard_map/ppermute | solution.py:55
  18.7 1.9 %collective-permute-start.11 = (bf16[4,256,128]{2,1,0:T(8,128)(2,1)S(1)}, bf16[4,256,128]{2,1,0:T(8,128)(2,1)S(1)}, u32[]{:S(2)}, u32[]{:S(2)}) collective-permute-start(bf16[4,256,128]{2,1,0:T(8,128)(2,1)S(1)} %pad_maximum_fusion.1.refs_4_), channel_id=1, source_target_pairs={{0,16},{4,20},{8,24},{12,28},{16,0},{20,4},{24,8},{28,12},{32,36},... | collective-permute-start | bytes 786440 | tf_op jit(solution)/shard_map/ppermute | solution.py:276
  20.7 0.0 collective-permute-done.9.refs_2_
  20.7 2.3 %collective-permute-start.10 = (bf16[4,256,128]{2,1,0:T(8,128)(2,1)S(1)}, bf16[4,256,128]{2,1,0:T(8,128)(2,1)S(1)}, u32[]{:S(2)}, u32[]{:S(2)}) collective-permute-start(bf16[4,256,128]{2,1,0:T(8,128)(2,1)S(1)} %collective-permute-done.9.refs_2_), channel_id=1, source_target_pairs={{0,32},{32,0},{1,33},{33,1},{2,34},{34,2},{3,35},{35,3},{4,36},{36... | collective-permute-start | bytes 786440 | tf_op jit(solution)/shard_map/ppermute | solution.py:46
  23.0 0.8 %collective-permute-done.7.refs_0_ = bf16[4,256,128]{2,1,0:T(8,128)(2,1)S(1)} collective-permute-done((bf16[4,256,128]{2,1,0:T(8,128)(2,1)S(1)}, bf16[4,256,128]{2,1,0:T(8,128)(2,1)S(1)}, u32[]{:S(2)}, u32[]{:S(2)}) %collective-permute-start.7) | collective-permute-done | bytes 262176 | tf_op jit(solution)/shard_map/ppermute | solution.py:276
  23.7 0.0 collective-permute-start.8
  23.7 0.0 collective-permute-done.6.refs_5_
  23.7 0.0 collective-permute-done.2.refs_3_
  23.7 5.3 %shard_map.37 = (bf16[4096,128]{1,0:T(8,128)(2,1)S(1)}, s32[384]{0:T(512)S(1)}, f32[8,32,256]{2,1,0:T(8,128)S(1)}) custom-call(s32[5]{0:T(128)S(1)} %stack.35.info_ref, bf16[1040,128]{1,0:T(8,128)(2,1)S(1)} %pad_maximum_fusion.refs_0_, bf16[1040,128]{1,0:T(8,128)(2,1)S(1)} %collective-permute-done.refs_1_, ...), custom_call_target="tpu_custom_call" | custom-call | flops 4294967296 | bytes 2097152 | tf_op jit(solution)/shard_map/pallas_call | solution.py:218
  29.1 0.0 collective-permute-done.11.refs_4_
  29.1 0.1 collective-permute-start.12
  29.2 0.0 collective-permute-done.10.refs_3_
  29.2 0.0 collective-permute-done.8.refs_1_
  29.2 1.5 %collective-permute-done.12.refs_5_ = bf16[4,256,128]{2,1,0:T(8,128)(2,1)S(1)} collective-permute-done((bf16[4,256,128]{2,1,0:T(8,128)(2,1)S(1)}, bf16[4,256,128]{2,1,0:T(8,128)(2,1)S(1)}, u32[]{:S(2)}, u32[]{:S(2)}) %collective-permute-start.12) | collective-permute-done | bytes 262176 | tf_op jit(solution)/shard_map/ppermute | solution.py:46
  30.7 12.8 %shard_map.38 = f32[8,8,128]{2,1,0:T(8,128)S(1)} custom-call(s32[5]{0:T(128)S(1)} %stack.35.info_ref, s32[384]{0:T(512)S(1)} %get-tuple-element.10.unit_ref, bf16[4096,128]{1,0:T(8,128)(2,1)S(1)} %get-tuple-element.11.p_ref, bf16[4,256,128]{2,1,0:T(8,128)(2,1)S(1)} %collective-permute-done.7.refs_0_, ...), custom_call_target="tpu_custom_call" | custom-call | flops 12884901888 | bytes 2097152 | tf_op jit(solution)/shard_map/pallas_call | solution.py:239
  43.6 12.2 %all_to_all.5.r_ref = f32[8,8,128]{2,1,0:T(8,128)} all-to-all(f32[8,8,128]{2,1,0:T(8,128)S(1)} %shard_map.38), channel_id=1, replica_groups=mesh['ylo'=2,'core'=2,'z'=4,'yhi'=2,'x'=4] {'z','yhi'}, dimensions={0} | all-to-all | bytes 65536 | tf_op jit(solution)/shard_map/all_to_all | solution.py:281
  55.8 1.5 %shard_map.39 = f32[32,256]{1,0:T(8,128)} custom-call(f32[8,8,128]{2,1,0:T(8,128)} %all_to_all.5.r_ref), custom_call_target="tpu_custom_call" | custom-call | tf_op jit(solution)/shard_map/pallas_call | solution.py:259
  (3 shorter events, 0.0 us)
Async XLA Ops:
  0.7 2.7 %copy-start = (bf16[32,8,128]{2,1,0:T(8,128)(2,1)S(1)}, bf16[32,8,128]{2,1,0:T(8,128)(2,1)}, u32[]{:S(2)}) copy-start(bf16[32,8,128]{2,1,0:T(8,128)(2,1)} %param.3) | copy-start | bytes 196612
  1.7 9.8 %collective-permute-start = (bf16[1040,128]{1,0:T(8,128)(2,1)S(1)}, bf16[1040,128]{1,0:T(8,128)(2,1)S(1)}, u32[]{:S(2)}, u32[]{:S(2)}) collective-permute-start(bf16[1040,128]{1,0:T(8,128)(2,1)S(1)} %pad_maximum_fusion.refs_0_), channel_id=1, source_target_pairs={{0,1},{1,2},{2,3},{3,0},{32,35},{33,32},{34,33},{35,34},{4,5},{5,6... | collective-permute-start | bytes 798728 | tf_op jit(solution)/shard_map/ppermute | solution.py:55
  3.3 8.5 %collective-permute-start.5 = (bf16[256,128]{1,0:T(8,128)(2,1)S(1)}, bf16[256,128]{1,0:T(8,128)(2,1)S(1)}, u32[]{:S(2)}, u32[]{:S(2)}) collective-permute-start(bf16[256,128]{1,0:T(8,128)(2,1)S(1)} %bitcast.12), channel_id=1, source_target_pairs={{0,4},{4,0},{8,12},{12,8},{16,20},{20,16},{24,28},{28,24},{32,48},... | collective-permute-start | bytes 196616 | tf_op jit(solution)/shard_map/ppermute | solution.py:271
  6.5 5.5 %collective-permute-start.3 = (bf16[256,128]{1,0:T(8,128)(2,1)S(1)}, bf16[256,128]{1,0:T(8,128)(2,1)S(1)}, u32[]{:S(2)}, u32[]{:S(2)}) collective-permute-start(bf16[256,128]{1,0:T(8,128)(2,1)S(1)} %bitcast.13), channel_id=1, source_target_pairs={{0,64},{4,68},{8,72},{12,76},{16,80},{20,84},{24,88},{28,92},{32,4... | collective-permute-start | bytes 196616 | tf_op jit(solution)/shard_map/ppermute | solution.py:271
  7.2 4.8 %collective-permute-start.4 = (bf16[256,128]{1,0:T(8,128)(2,1)S(1)}, bf16[256,128]{1,0:T(8,128)(2,1)S(1)}, u32[]{:S(2)}, u32[]{:S(2)}) collective-permute-start(bf16[256,128]{1,0:T(8,128)(2,1)S(1)} %bitcast.14), channel_id=1, source_target_pairs={{0,68},{4,64},{8,76},{12,72},{16,84},{20,80},{24,92},{28,88},{32,5... | collective-permute-start | bytes 196616 | tf_op jit(solution)/shard_map/ppermute | solution.py:271
  9.8 9.0 %collective-permute-start.1 = (bf16[1040,128]{1,0:T(8,128)(2,1)S(1)}, bf16[1040,128]{1,0:T(8,128)(2,1)S(1)}, u32[]{:S(2)}, u32[]{:S(2)}) collective-permute-start(bf16[1040,128]{1,0:T(8,128)(2,1)S(1)} %pad_maximum_fusion.refs_0_), channel_id=1, source_target_pairs={{0,3},{1,0},{2,1},{3,2},{32,33},{33,34},{34,35},{35,32},{4,7},{5,4... | collective-permute-start | bytes 798728 | tf_op jit(solution)/shard_map/ppermute | solution.py:55
  11.5 12.2 %collective-permute-start.2 = (bf16[1040,128]{1,0:T(8,128)(2,1)S(1)}, bf16[1040,128]{1,0:T(8,128)(2,1)S(1)}, u32[]{:S(2)}, u32[]{:S(2)}) collective-permute-start(bf16[1040,128]{1,0:T(8,128)(2,1)S(1)} %collective-permute-done.refs_1_), channel_id=1, source_target_pairs={{0,1},{1,2},{2,3},{3,0},{32,35},{33,32},{34,33},{35,34},{4,5},{5,6... | collective-permute-start | bytes 798728 | tf_op jit(solution)/shard_map/ppermute | solution.py:55
  12.0 8.6 %collective-permute-start.9 = (bf16[4,256,128]{2,1,0:T(8,128)(2,1)S(1)}, bf16[4,256,128]{2,1,0:T(8,128)(2,1)S(1)}, u32[]{:S(2)}, u32[]{:S(2)}) collective-permute-start(bf16[4,256,128]{2,1,0:T(8,128)(2,1)S(1)} %pad_maximum_fusion.1.refs_4_), channel_id=1, source_target_pairs={{0,24},{4,28},{8,0},{12,4},{16,8},{20,12},{24,16},{28,20},{32,100}... | collective-permute-start | bytes 786440 | tf_op jit(solution)/shard_map/ppermute | solution.py:276
  16.2 7.6 %collective-permute-start.7 = (bf16[4,256,128]{2,1,0:T(8,128)(2,1)S(1)}, bf16[4,256,128]{2,1,0:T(8,128)(2,1)S(1)}, u32[]{:S(2)}, u32[]{:S(2)}) collective-permute-start(bf16[4,256,128]{2,1,0:T(8,128)(2,1)S(1)} %pad_maximum_fusion.1.refs_4_), channel_id=1, source_target_pairs={{0,8},{4,12},{8,16},{12,20},{16,24},{20,28},{24,0},{28,4},{32,96},... | collective-permute-start | bytes 786440 | tf_op jit(solution)/shard_map/ppermute | solution.py:276
  16.2 7.6 %collective-permute-start.6 = (bf16[4,256,128]{2,1,0:T(8,128)(2,1)S(1)}, bf16[4,256,128]{2,1,0:T(8,128)(2,1)S(1)}, u32[]{:S(2)}, u32[]{:S(2)}) collective-permute-start(bf16[4,256,128]{2,1,0:T(8,128)(2,1)S(1)} %pad_maximum_fusion.1.refs_4_), channel_id=1, source_target_pairs={{0,32},{32,0},{1,33},{33,1},{2,34},{34,2},{3,35},{35,3},{4,36},{36... | collective-permute-start | bytes 786440 | tf_op jit(solution)/shard_map/ppermute | solution.py:46
  18.7 10.4 %collective-permute-start.11 = (bf16[4,256,128]{2,1,0:T(8,128)(2,1)S(1)}, bf16[4,256,128]{2,1,0:T(8,128)(2,1)S(1)}, u32[]{:S(2)}, u32[]{:S(2)}) collective-permute-start(bf16[4,256,128]{2,1,0:T(8,128)(2,1)S(1)} %pad_maximum_fusion.1.refs_4_), channel_id=1, source_target_pairs={{0,16},{4,20},{8,24},{12,28},{16,0},{20,4},{24,8},{28,12},{32,36},... | collective-permute-start | bytes 786440 | tf_op jit(solution)/shard_map/ppermute | solution.py:276
  20.7 8.5 %collective-permute-start.10 = (bf16[4,256,128]{2,1,0:T(8,128)(2,1)S(1)}, bf16[4,256,128]{2,1,0:T(8,128)(2,1)S(1)}, u32[]{:S(2)}, u32[]{:S(2)}) collective-permute-start(bf16[4,256,128]{2,1,0:T(8,128)(2,1)S(1)} %collective-permute-done.9.refs_2_), channel_id=1, source_target_pairs={{0,32},{32,0},{1,33},{33,1},{2,34},{34,2},{3,35},{35,3},{4,36},{36... | collective-permute-start | bytes 786440 | tf_op jit(solution)/shard_map/ppermute | solution.py:46
  23.7 5.5 %collective-permute-start.8 = (bf16[4,256,128]{2,1,0:T(8,128)(2,1)S(1)}, bf16[4,256,128]{2,1,0:T(8,128)(2,1)S(1)}, u32[]{:S(2)}, u32[]{:S(2)}) collective-permute-start(bf16[4,256,128]{2,1,0:T(8,128)(2,1)S(1)} %collective-permute-done.7.refs_0_), channel_id=1, source_target_pairs={{0,32},{32,0},{1,33},{33,1},{2,34},{34,2},{3,35},{35,3},{4,36},{36... | collective-permute-start | bytes 786440 | tf_op jit(solution)/shard_map/ppermute | solution.py:46
  29.1 1.6 %collective-permute-start.12 = (bf16[4,256,128]{2,1,0:T(8,128)(2,1)S(1)}, bf16[4,256,128]{2,1,0:T(8,128)(2,1)S(1)}, u32[]{:S(2)}, u32[]{:S(2)}) collective-permute-start(bf16[4,256,128]{2,1,0:T(8,128)(2,1)S(1)} %collective-permute-done.11.refs_4_), channel_id=1, source_target_pairs={{0,32},{32,0},{1,33},{33,1},{2,34},{34,2},{3,35},{35,3},{4,36},{36... | collective-permute-start | bytes 786440 | tf_op jit(solution)/shard_map/ppermute | solution.py:46

commit v9 on v5

--- a/solution.py
+++ b/solution.py
@@ -11,7 +11,6 @@
 NAMES = ("ylo", "core", "z", "yhi", "x")
 SIZES = (2, 2, 4, 2, 4)
 PLANE = ("ylo", "core", "z", "yhi")
-SHIFTS = (0, 1, -1, 2)
 OWN, SLOTS, WIDTH = 8, 128, 128
 DEPTH = 16
 LOWEST = -3.0e38
@@ -27,16 +26,15 @@
             for z in range(4):
                 for yhi in range(2):
                     y2, core2, z2 = move(2 * yhi + ylo, core, z)
-                    y2, z2 = y2 % 4, z2 % 4
                     pairs.append((index(ylo, core, z, yhi), index(y2 % 2, core2, z2, y2 // 2)))
     return pairs
 
 
-def along(first, shift):
+def along(first, mask):
     def move(y, core, z):
         if (core == 0) == first:
-            return y + shift, core, z
-        return y, core, z + shift
+            return y ^ mask, core, z
+        return y, core, z ^ mask
 
     return plane_pairs(move)
 
@@ -45,9 +43,9 @@
     return lax.ppermute(v, "core", [(0, 1), (1, 0)])
 
 
-def on_x(v, shift):
+def on_x(v, mask, other_mask):
     pairs = [
-        (core * 4 + i, core * 4 + (i + (shift if core == 0 else -shift)) % 4)
+        (core * 4 + i, core * 4 + (i ^ (mask if core == 0 else other_mask)))
         for core in range(2)
         for i in range(4)
     ]
@@ -100,7 +98,6 @@
         issue(unit_ref[j], j, fresh=j == 0)
 
     def group(g, carry):
-        push(jnp.minimum(g + 1, 7))
 
         def turn(t, c):
             for j in range(DEPTH):
@@ -109,6 +106,7 @@
             return c
 
         lax.fori_loop(0, turns - 1, turn, 0)
+        push(jnp.minimum(g + 1, 7))
         last = (turns - 1) * DEPTH
         for j in range(DEPTH):
             take(unit_ref[last + j], j)
@@ -134,8 +132,7 @@
 def score_kernel(info_ref, *refs):
     rows, pieces, out_ref = refs[:8], refs[8:12], refs[12]
     w_ref, p_ref, m_ref, s_ref, unit_ref = refs[13:]
-    z, yhi, core, x, ylo = (info_ref[i] for i in range(5))
-    mate = 2 - ylo
+    z, yhi, core, x = (info_ref[i] for i in range(4))
 
     for kind in range(2):
 
@@ -145,13 +142,13 @@
                 for j in range(4):
                     same = (a < 4) == (kind == 0)
                     dz, dy = (a % 4, j) if same else (j, a % 4)
-                    h = {0: 0, 3: 1}.get(dy, (mate != dy).astype(jnp.int32))
-                    half = 128 * (dy in (1, 2))
+                    h = dy // 2
+                    half = 128 * (dy % 2)
                     w_ref[(dz * 2 + h) * 2 + a // 4, :, half : half + 128] = rows[a][j]
 
     count = jnp.int32(0)
     for m in range(4):
-        from_x = lax.rem(x + 4 - jnp.where(core == 0, SHIFTS[m], -SHIFTS[m]), 4)
+        from_x = lax.bitwise_xor(x, jnp.where(core == 0, (0, 1, 3, 2)[m], (0, 3, 1, 2)[m]))
         p_ref[pl.ds(pl.multiple_of(from_x * 1024, 1024), 1024), :] = pieces[m][0:1024, :]
         lengths = pieces[m][1024:1040, :].astype(jnp.float32)[0:8].astype(jnp.int32)
         units = lax.shift_right_logical(lengths + 15, 4)
@@ -191,7 +188,7 @@
     r = pl.run_scoped(add_up, pltpu.ACC(0)((32, 256), jnp.float32))
     for g in range(8):
         c = r[:, 32 * g : 32 * g + 32]
-        place = lax.rem(z + 4 - SHIFTS[g // 2], 4) * 2 + (yhi if g % 2 == 0 else 1 - yhi)
+        place = lax.bitwise_xor(z * 2 + yhi, g)
         out_ref[place] = jnp.concatenate([c[0:8], c[8:16], c[16:24], c[24:32]], axis=1)
 
 
@@ -231,14 +228,14 @@
 
 def per_device(queries, passages, lengths):
     own = queries.reshape(256, 128)
-    info = jnp.stack([lax.axis_index(name) for name in ("z", "yhi", "core", "x", "ylo")]).astype(jnp.int32)
-
-    near = [own] + [lax.ppermute(own, PLANE, along(True, k)) for k in SHIFTS[1:]]
+    info = jnp.stack([lax.axis_index(name) for name in ("z", "yhi", "core", "x")]).astype(jnp.int32)
+
+    near = [own] + [lax.ppermute(own, PLANE, along(True, k)) for k in range(1, 4)]
     filled = with_lengths(passages, lengths)
-    once = on_x(filled, 1)
-    moved = [filled, once, on_x(filled, -1), on_x(once, 1)]
+    once = on_x(filled, 1, 3)
+    moved = [filled, once, on_x(filled, 3, 1), on_x(once, 3, 1)]
     block = jnp.stack(near)
-    mine = [block] + [lax.ppermute(block, PLANE, along(False, k)) for k in SHIFTS[1:]]
+    mine = [block] + [lax.ppermute(block, PLANE, along(False, k)) for k in range(1, 4)]
     other = [to_core(v) for v in mine]
     terms = score(info, mine + other, moved)
     received = lax.all_to_all(terms, ("z", "yhi"), 0, 0, tiled=True)

time: 57 us -> 55.5 us (0.974)
  the two profiles are of different devices: /device:TPU:8 before, /device:TPU:0 now
where the time goes in v9:
time: 55.5 us; the launch traced here: 55.2 us
  Pallas kernels  16.4 us (30%)
  blocking collectives  15.8 us (28%)
  starting transfers between devices  15 us (27%)
  waiting for transfers between devices  6.82 us (12%)
  other arithmetic  1.12 us (2%)
    all_to_all x1, blocking collectives, per_device(): received = lax.all_to_all(terms, ('z', 'yhi'), 0, 0, tiled=True)  15.8 us
    pallas_call x1, Pallas kernels, score(): pl.pallas_call(score_kernel, out_shape=jax.ShapeDtypeStruct((8, 8, 128),...  14.9 us
    ppermute x3, starting transfers between devices, on_x(): return lax.ppermute(v, ('core', 'x'), pairs)  5.63 us
    ppermute x3, starting transfers between devices, per_device(): lax.ppermute(block, PLANE, along(False, k))  5.07 us
    ppermute x3, waiting for transfers between devices, per_device(): lax.ppermute(block, PLANE, along(False, k))  4.42 us
    ppermute x3, starting transfers between devices, per_device(): lax.ppermute(own, PLANE, along(True, k))  4.09 us
    pallas_call x1, Pallas kernels, place(): pl.pallas_call(place_kernel, out_shape=jax.ShapeDtypeStruct((32, 256), jn...  1.46 us
  transfers between devices with their start and end apart: 13, of which 8 were waited for; matrix products, arithmetic and copies ran while one was open for 2% of the time, Pallas kernels for 0%

profile of v9, /device:TPU:0, one launch (start us, length us, event | category | flops | bytes accessed | tf_op | source)
XLA Modules:
  0.0 55.2 jit_solution(2464882522751643990)
XLA Ops:
  0.0 0.0 copy-start.1
  0.0 3.1 %collective-permute-start.2 = (bf16[256,128]{1,0:T(8,128)(2,1)}, bf16[256,128]{1,0:T(8,128)(2,1)S(1)}, u32[]{:S(2)}, u32[]{:S(2)}) collective-permute-start(bf16[256,128]{1,0:T(8,128)(2,1)} %bitcast.11), channel_id=1, source_target_pairs={{0,68},{4,64},{8,76},{12,72},{16,84},{20,80},{24,92},{28,88},{32,5... | collective-permute-start | bytes 196616 | tf_op jit(solution)/shard_map/ppermute | solution.py:233
  3.1 0.6 %collective-permute-start.1 = (bf16[256,128]{1,0:T(8,128)(2,1)}, bf16[256,128]{1,0:T(8,128)(2,1)S(1)}, u32[]{:S(2)}, u32[]{:S(2)}) collective-permute-start(bf16[256,128]{1,0:T(8,128)(2,1)} %bitcast.12), channel_id=1, source_target_pairs={{0,4},{4,0},{8,12},{12,8},{16,20},{20,16},{24,28},{28,24},{32,48},... | collective-permute-start | bytes 196616 | tf_op jit(solution)/shard_map/ppermute | solution.py:233
  3.7 0.4 collective-permute-start
  4.1 0.0 copy-done.1
  4.1 0.0 copy-start
  4.1 1.0 %pad_maximum_fusion.refs_8_ = bf16[1040,128]{1,0:T(8,128)(2,1)S(1)} fusion(bf16[16,128]{1,0:T(8,128)(2,1)S(1)} %broadcast_in_dim.3, bf16[1024,128]{1,0:T(8,128)(2,1)} %bitcast.10), kind=kLoop, calls=%fused_computation | loop fusion | flops 532480 | bytes 532480 | tf_op jit(solution)/shard_map/concatenate | solution.py:57
  5.1 2.9 %collective-permute-start.11 = (bf16[1040,128]{1,0:T(8,128)(2,1)S(1)}, bf16[1040,128]{1,0:T(8,128)(2,1)S(1)}, u32[]{:S(2)}, u32[]{:S(2)}) collective-permute-start(bf16[1040,128]{1,0:T(8,128)(2,1)S(1)} %pad_maximum_fusion.refs_8_), channel_id=1, source_target_pairs={{0,3},{1,2},{2,1},{3,0},{32,33},{33,32},{34,35},{35,34},{4,7},{5,6... | collective-permute-start | bytes 798728 | tf_op jit(solution)/shard_map/ppermute | solution.py:52
  8.1 0.2 collective-permute-start.10
  8.3 0.0 collective-permute-done.2
  8.3 0.8 %collective-permute-done.1 = bf16[256,128]{1,0:T(8,128)(2,1)S(1)} collective-permute-done((bf16[256,128]{1,0:T(8,128)(2,1)}, bf16[256,128]{1,0:T(8,128)(2,1)S(1)}, u32[]{:S(2)}, u32[]{:S(2)}) %collective-permute-start.1) | collective-permute-done | bytes 65568 | tf_op jit(solution)/shard_map/ppermute | solution.py:233
  9.1 0.0 collective-permute-done
  9.1 0.0 copy-done
  9.1 4.1 %collective-permute-start.5 = (bf16[4,256,128]{2,1,0:T(8,128)(2,1)S(1)}, bf16[4,256,128]{2,1,0:T(8,128)(2,1)S(1)}, u32[]{:S(2)}, u32[]{:S(2)}) collective-permute-start(bf16[4,256,128]{2,1,0:T(8,128)(2,1)S(1)} %pad_maximum_fusion.1.refs_0_), channel_id=1, source_target_pairs={{0,24},{4,28},{8,16},{12,20},{16,8},{20,12},{24,0},{28,4},{32,100}... | collective-permute-start | bytes 786440 | tf_op jit(solution)/shard_map/ppermute | solution.py:238
  13.2 0.0 collective-permute-start.4
  13.2 0.9 %collective-permute-start.3 = (bf16[4,256,128]{2,1,0:T(8,128)(2,1)S(1)}, bf16[4,256,128]{2,1,0:T(8,128)(2,1)S(1)}, u32[]{:S(2)}, u32[]{:S(2)}) collective-permute-start(bf16[4,256,128]{2,1,0:T(8,128)(2,1)S(1)} %pad_maximum_fusion.1.refs_0_), channel_id=1, source_target_pairs={{0,8},{4,12},{8,0},{12,4},{16,24},{20,28},{24,16},{28,20},{32,96},... | collective-permute-start | bytes 786440 | tf_op jit(solution)/shard_map/ppermute | solution.py:238
  14.2 0.3 collective-permute-done.10.refs_9_
  14.5 2.5 %collective-permute-start.12 = (bf16[1040,128]{1,0:T(8,128)(2,1)S(1)}, bf16[1040,128]{1,0:T(8,128)(2,1)S(1)}, u32[]{:S(2)}, u32[]{:S(2)}) collective-permute-start(bf16[1040,128]{1,0:T(8,128)(2,1)S(1)} %collective-permute-done.10.refs_9_), channel_id=1, source_target_pairs={{0,3},{1,2},{2,1},{3,0},{32,33},{33,32},{34,35},{35,34},{4,7},{5,6... | collective-permute-start | bytes 798728 | tf_op jit(solution)/shard_map/ppermute | solution.py:52
  17.0 0.0 collective-permute-done.11.refs_10_
  17.0 0.0 collective-permute-start.6
  17.0 3.0 %collective-permute-done.5.refs_3_ = bf16[4,256,128]{2,1,0:T(8,128)(2,1)S(1)} collective-permute-done((bf16[4,256,128]{2,1,0:T(8,128)(2,1)S(1)}, bf16[4,256,128]{2,1,0:T(8,128)(2,1)S(1)}, u32[]{:S(2)}, u32[]{:S(2)}) %collective-permute-start.5) | collective-permute-done | bytes 262176 | tf_op jit(solution)/shard_map/ppermute | solution.py:238
  19.9 0.0 collective-permute-start.9
  19.9 1.2 %collective-permute-done.4.refs_2_ = bf16[4,256,128]{2,1,0:T(8,128)(2,1)S(1)} collective-permute-done((bf16[4,256,128]{2,1,0:T(8,128)(2,1)S(1)}, bf16[4,256,128]{2,1,0:T(8,128)(2,1)S(1)}, u32[]{:S(2)}, u32[]{:S(2)}) %collective-permute-start.4) | collective-permute-done | bytes 262176 | tf_op jit(solution)/shard_map/ppermute | solution.py:238
  21.1 0.0 collective-permute-start.8
  21.1 0.3 collective-permute-done.3.refs_1_
  21.4 0.2 collective-permute-start.7
  21.6 0.1 pad_add_fusion.info_ref
  21.7 0.0 collective-permute-done.6.refs_4_
  21.7 0.4 collective-permute-done.12.refs_11_
  22.1 0.0 collective-permute-done.9.refs_7_
  22.1 0.5 collective-permute-done.8.refs_6_
  22.7 0.4 collective-permute-done.7.refs_5_
  23.0 14.9 %shard_map.37 = f32[8,8,128]{2,1,0:T(8,128)S(1)} custom-call(s32[4]{0:T(128)S(1)} %pad_add_fusion.info_ref, bf16[4,256,128]{2,1,0:T(8,128)(2,1)S(1)} %pad_maximum_fusion.1.refs_0_, bf16[4,256,128]{2,1,0:T(8,128)(2,1)S(1)} %collective-permute-done.3.refs_1_, bf16[4,256,128]{2,1,0:T(8,128)(2,1)S(1)} %collective-permute-done.4.refs_2_, ...), custom_call_target="tpu_custom_call" | custom-call | tf_op jit(solution)/shard_map/pallas_call | solution.py:196
  38.0 15.8 %all_to_all.5.r_ref = f32[8,8,128]{2,1,0:T(8,128)} all-to-all(f32[8,8,128]{2,1,0:T(8,128)S(1)} %shard_map.37), channel_id=1, replica_groups=mesh['ylo'=2,'core'=2,'z'=4,'yhi'=2,'x'=4] {'z','yhi'}, dimensions={0} | all-to-all | bytes 65536 | tf_op jit(solution)/shard_map/all_to_all | solution.py:241
  53.8 1.5 %shard_map.38 = f32[32,256]{1,0:T(8,128)} custom-call(f32[8,8,128]{2,1,0:T(8,128)} %all_to_all.5.r_ref), custom_call_target="tpu_custom_call" | custom-call | tf_op jit(solution)/shard_map/pallas_call | solution.py:221
  (4 shorter events, 0.1 us)
Async XLA Ops:
  0.0 4.1 %copy-start.1 = (s32[8]{0:T(128)S(1)}, s32[8]{0:T(128)}, u32[]{:S(2)}) copy-start(s32[8]{0:T(128)} %param.5) | copy-start | bytes 100
  0.0 8.3 %collective-permute-start.2 = (bf16[256,128]{1,0:T(8,128)(2,1)}, bf16[256,128]{1,0:T(8,128)(2,1)S(1)}, u32[]{:S(2)}, u32[]{:S(2)}) collective-permute-start(bf16[256,128]{1,0:T(8,128)(2,1)} %bitcast.11), channel_id=1, source_target_pairs={{0,68},{4,64},{8,76},{12,72},{16,84},{20,80},{24,92},{28,88},{32,5... | collective-permute-start | bytes 196616 | tf_op jit(solution)/shard_map/ppermute | solution.py:233
  3.1 6.0 %collective-permute-start.1 = (bf16[256,128]{1,0:T(8,128)(2,1)}, bf16[256,128]{1,0:T(8,128)(2,1)S(1)}, u32[]{:S(2)}, u32[]{:S(2)}) collective-permute-start(bf16[256,128]{1,0:T(8,128)(2,1)} %bitcast.12), channel_id=1, source_target_pairs={{0,4},{4,0},{8,12},{12,8},{16,20},{20,16},{24,28},{28,24},{32,48},... | collective-permute-start | bytes 196616 | tf_op jit(solution)/shard_map/ppermute | solution.py:233
  3.7 5.4 %collective-permute-start = (bf16[256,128]{1,0:T(8,128)(2,1)}, bf16[256,128]{1,0:T(8,128)(2,1)S(1)}, u32[]{:S(2)}, u32[]{:S(2)}) collective-permute-start(bf16[256,128]{1,0:T(8,128)(2,1)} %bitcast.13), channel_id=1, source_target_pairs={{0,64},{4,68},{8,72},{12,76},{16,80},{20,84},{24,88},{28,92},{32,4... | collective-permute-start | bytes 196616 | tf_op jit(solution)/shard_map/ppermute | solution.py:233
  4.1 5.0 %copy-start = (bf16[32,8,128]{2,1,0:T(8,128)(2,1)S(1)}, bf16[32,8,128]{2,1,0:T(8,128)(2,1)}, u32[]{:S(2)}) copy-start(bf16[32,8,128]{2,1,0:T(8,128)(2,1)} %param.3) | copy-start | bytes 196612
  5.1 11.8 %collective-permute-start.11 = (bf16[1040,128]{1,0:T(8,128)(2,1)S(1)}, bf16[1040,128]{1,0:T(8,128)(2,1)S(1)}, u32[]{:S(2)}, u32[]{:S(2)}) collective-permute-start(bf16[1040,128]{1,0:T(8,128)(2,1)S(1)} %pad_maximum_fusion.refs_8_), channel_id=1, source_target_pairs={{0,3},{1,2},{2,1},{3,0},{32,33},{33,32},{34,35},{35,34},{4,7},{5,6... | collective-permute-start | bytes 798728 | tf_op jit(solution)/shard_map/ppermute | solution.py:52
  8.1 6.4 %collective-permute-start.10 = (bf16[1040,128]{1,0:T(8,128)(2,1)S(1)}, bf16[1040,128]{1,0:T(8,128)(2,1)S(1)}, u32[]{:S(2)}, u32[]{:S(2)}) collective-permute-start(bf16[1040,128]{1,0:T(8,128)(2,1)S(1)} %pad_maximum_fusion.refs_8_), channel_id=1, source_target_pairs={{0,1},{1,0},{2,3},{3,2},{32,35},{33,34},{34,33},{35,32},{4,5},{5,4... | collective-permute-start | bytes 798728 | tf_op jit(solution)/shard_map/ppermute | solution.py:52
  9.1 10.8 %collective-permute-start.5 = (bf16[4,256,128]{2,1,0:T(8,128)(2,1)S(1)}, bf16[4,256,128]{2,1,0:T(8,128)(2,1)S(1)}, u32[]{:S(2)}, u32[]{:S(2)}) collective-permute-start(bf16[4,256,128]{2,1,0:T(8,128)(2,1)S(1)} %pad_maximum_fusion.1.refs_0_), channel_id=1, source_target_pairs={{0,24},{4,28},{8,16},{12,20},{16,8},{20,12},{24,0},{28,4},{32,100}... | collective-permute-start | bytes 786440 | tf_op jit(solution)/shard_map/ppermute | solution.py:238
  13.2 7.9 %collective-permute-start.4 = (bf16[4,256,128]{2,1,0:T(8,128)(2,1)S(1)}, bf16[4,256,128]{2,1,0:T(8,128)(2,1)S(1)}, u32[]{:S(2)}, u32[]{:S(2)}) collective-permute-start(bf16[4,256,128]{2,1,0:T(8,128)(2,1)S(1)} %pad_maximum_fusion.1.refs_0_), channel_id=1, source_target_pairs={{0,16},{4,20},{8,24},{12,28},{16,0},{20,4},{24,8},{28,12},{32,36},... | collective-permute-start | bytes 786440 | tf_op jit(solution)/shard_map/ppermute | solution.py:238
  13.2 8.1 %collective-permute-start.3 = (bf16[4,256,128]{2,1,0:T(8,128)(2,1)S(1)}, bf16[4,256,128]{2,1,0:T(8,128)(2,1)S(1)}, u32[]{:S(2)}, u32[]{:S(2)}) collective-permute-start(bf16[4,256,128]{2,1,0:T(8,128)(2,1)S(1)} %pad_maximum_fusion.1.refs_0_), channel_id=1, source_target_pairs={{0,8},{4,12},{8,0},{12,4},{16,24},{20,28},{24,16},{28,20},{32,96},... | collective-permute-start | bytes 786440 | tf_op jit(solution)/shard_map/ppermute | solution.py:238
  14.5 7.6 %collective-permute-start.12 = (bf16[1040,128]{1,0:T(8,128)(2,1)S(1)}, bf16[1040,128]{1,0:T(8,128)(2,1)S(1)}, u32[]{:S(2)}, u32[]{:S(2)}) collective-permute-start(bf16[1040,128]{1,0:T(8,128)(2,1)S(1)} %collective-permute-done.10.refs_9_), channel_id=1, source_target_pairs={{0,3},{1,2},{2,1},{3,0},{32,33},{33,32},{34,35},{35,34},{4,7},{5,6... | collective-permute-start | bytes 798728 | tf_op jit(solution)/shard_map/ppermute | solution.py:52
  17.0 4.8 %collective-permute-start.6 = (bf16[4,256,128]{2,1,0:T(8,128)(2,1)S(1)}, bf16[4,256,128]{2,1,0:T(8,128)(2,1)S(1)}, u32[]{:S(2)}, u32[]{:S(2)}) collective-permute-start(bf16[4,256,128]{2,1,0:T(8,128)(2,1)S(1)} %pad_maximum_fusion.1.refs_0_), channel_id=1, source_target_pairs={{0,32},{32,0},{1,33},{33,1},{2,34},{34,2},{3,35},{35,3},{4,36},{36... | collective-permute-start | bytes 786440 | tf_op jit(solution)/shard_map/ppermute | solution.py:43
  19.9 2.2 %collective-permute-start.9 = (bf16[4,256,128]{2,1,0:T(8,128)(2,1)S(1)}, bf16[4,256,128]{2,1,0:T(8,128)(2,1)S(1)}, u32[]{:S(2)}, u32[]{:S(2)}) collective-permute-start(bf16[4,256,128]{2,1,0:T(8,128)(2,1)S(1)} %collective-permute-done.5.refs_3_), channel_id=1, source_target_pairs={{0,32},{32,0},{1,33},{33,1},{2,34},{34,2},{3,35},{35,3},{4,36},{36... | collective-permute-start | bytes 786440 | tf_op jit(solution)/shard_map/ppermute | solution.py:43
  21.1 1.5 %collective-permute-start.8 = (bf16[4,256,128]{2,1,0:T(8,128)(2,1)S(1)}, bf16[4,256,128]{2,1,0:T(8,128)(2,1)S(1)}, u32[]{:S(2)}, u32[]{:S(2)}) collective-permute-start(bf16[4,256,128]{2,1,0:T(8,128)(2,1)S(1)} %collective-permute-done.4.refs_2_), channel_id=1, source_target_pairs={{0,32},{32,0},{1,33},{33,1},{2,34},{34,2},{3,35},{35,3},{4,36},{36... | collective-permute-start | bytes 786440 | tf_op jit(solution)/shard_map/ppermute | solution.py:43
  21.4 1.6 %collective-permute-start.7 = (bf16[4,256,128]{2,1,0:T(8,128)(2,1)S(1)}, bf16[4,256,128]{2,1,0:T(8,128)(2,1)S(1)}, u32[]{:S(2)}, u32[]{:S(2)}) collective-permute-start(bf16[4,256,128]{2,1,0:T(8,128)(2,1)S(1)} %collective-permute-done.3.refs_1_), channel_id=1, source_target_pairs={{0,32},{32,0},{1,33},{33,1},{2,34},{34,2},{3,35},{35,3},{4,36},{36... | collective-permute-start | bytes 786440 | tf_op jit(solution)/shard_map/ppermute | solution.py:43

commit v10 on v9

--- a/solution.py
+++ b/solution.py
@@ -12,6 +12,7 @@
 SIZES = (2, 2, 4, 2, 4)
 PLANE = ("ylo", "core", "z", "yhi")
 OWN, SLOTS, WIDTH = 8, 128, 128
+PERMUTED = 4
 DEPTH = 16
 LOWEST = -3.0e38
 
@@ -55,7 +56,7 @@
 def with_lengths(passages, lengths):
     tail = jnp.pad(lengths.astype(passages.dtype), (0, WIDTH - OWN))
     return jnp.concatenate(
-        [passages.reshape(OWN * SLOTS, WIDTH), jnp.broadcast_to(tail, (16, WIDTH))], axis=0
+        [passages.reshape(-1, WIDTH), jnp.broadcast_to(tail, (16, WIDTH))], axis=0
     )
 
 
@@ -130,8 +131,8 @@
 
 
 def score_kernel(info_ref, *refs):
-    rows, pieces, out_ref = refs[:8], refs[8:12], refs[12]
-    w_ref, p_ref, m_ref, s_ref, unit_ref = refs[13:]
+    rows, pieces, rest_ref, out_ref = refs[:8], refs[8:12], refs[12], refs[13]
+    w_ref, p_ref, m_ref, s_ref, unit_ref = refs[14:]
     z, yhi, core, x = (info_ref[i] for i in range(4))
 
     for kind in range(2):
@@ -147,10 +148,13 @@
                     w_ref[(dz * 2 + h) * 2 + a // 4, :, half : half + 128] = rows[a][j]
 
     count = jnp.int32(0)
+    cut = PERMUTED * SLOTS
+    for i in range(4):
+        p_ref[1024 * i + cut : 1024 * i + 1024, :] = rest_ref[i * (1024 - cut) : (i + 1) * (1024 - cut), :]
     for m in range(4):
         from_x = lax.bitwise_xor(x, jnp.where(core == 0, (0, 1, 3, 2)[m], (0, 3, 1, 2)[m]))
-        p_ref[pl.ds(pl.multiple_of(from_x * 1024, 1024), 1024), :] = pieces[m][0:1024, :]
-        lengths = pieces[m][1024:1040, :].astype(jnp.float32)[0:8].astype(jnp.int32)
+        p_ref[pl.ds(pl.multiple_of(from_x * 1024, 1024), cut), :] = pieces[m][0:cut, :]
+        lengths = pieces[m][cut : cut + 16, :].astype(jnp.float32)[0:8].astype(jnp.int32)
         units = lax.shift_right_logical(lengths + 15, 4)
         for i in range(OWN):
             for n in range(8):
@@ -192,12 +196,12 @@
         out_ref[place] = jnp.concatenate([c[0:8], c[8:16], c[16:24], c[24:32]], axis=1)
 
 
-def score(info, rows, pieces):
+def score(info, rows, pieces, rest):
     return pl.pallas_call(
         score_kernel,
         out_shape=jax.ShapeDtypeStruct((8, 8, 128), jnp.float32),
         in_specs=[pl.BlockSpec(memory_space=pltpu.SMEM)]
-        + [pl.BlockSpec(memory_space=pltpu.VMEM)] * 12,
+        + [pl.BlockSpec(memory_space=pltpu.VMEM)] * 13,
         out_specs=pl.BlockSpec(memory_space=pltpu.VMEM),
         scratch_shapes=[
             pltpu.VMEM((16, 256, 256), jnp.bfloat16),
@@ -207,7 +211,7 @@
             pltpu.SMEM((256 + DEPTH,), jnp.int32),
         ],
         compiler_params=pltpu.CompilerParams(vmem_limit_bytes=32 << 20),
-    )(info, *rows, *pieces)
+    )(info, *rows, *pieces, rest)
 
 
 def place_kernel(r_ref, o_ref):
@@ -231,13 +235,14 @@
     info = jnp.stack([lax.axis_index(name) for name in ("z", "yhi", "core", "x")]).astype(jnp.int32)
 
     near = [own] + [lax.ppermute(own, PLANE, along(True, k)) for k in range(1, 4)]
-    filled = with_lengths(passages, lengths)
+    filled = with_lengths(passages[:PERMUTED], lengths)
+    rest = lax.all_gather(passages[PERMUTED:].reshape(-1, WIDTH), "x", axis=0, tiled=True)
     once = on_x(filled, 1, 3)
     moved = [filled, once, on_x(filled, 3, 1), on_x(once, 3, 1)]
     block = jnp.stack(near)
     mine = [block] + [lax.ppermute(block, PLANE, along(False, k)) for k in range(1, 4)]
     other = [to_core(v) for v in mine]
-    terms = score(info, mine + other, moved)
+    terms = score(info, mine + other, moved, rest)
     received = lax.all_to_all(terms, ("z", "yhi"), 0, 0, tiled=True)
     return place(received)
 

time: 55.5 us -> 70.5 us (1.27)
  blocking collectives: 15.8 us -> 27.7 us
  waiting for transfers between devices: 6.82 us -> 9.79 us
  Pallas kernels: 16.4 us -> 17.7 us
  starting transfers between devices: 15 us -> 14 us
    all_gather x0 -> x1, blocking collectives: none -> 12.9 us  [per_device(): lax.all_gather(passages[PERMUTED:].reshape(-1, WIDTH), 'x', axis=0, tiled...]
    ppermute x3, waiting for transfers between devices: 4.42 us -> 0.01 us  [per_device(): lax.ppermute(block, PLANE, along(False, k))]
    ppermute x3, waiting for transfers between devices: 0.8 us -> 4.99 us  [per_device(): lax.ppermute(own, PLANE, along(True, k))]
    ppermute x3, waiting for transfers between devices: 0.67 us -> 4.79 us  [on_x(): return lax.ppermute(v, ('core', 'x'), pairs)]
    ppermute x3, starting transfers between devices: 5.63 us -> 4.28 us  [on_x(): return lax.ppermute(v, ('core', 'x'), pairs)]
    pallas_call x1, Pallas kernels: 14.9 us -> 16.2 us  [score(): pl.pallas_call(score_kernel, out_shape=jax.ShapeDtypeStruct((8, 8, 128),...]
    all_to_all x1, blocking collectives: 15.8 us -> 14.8 us  [per_device(): received = lax.all_to_all(terms, ('z', 'yhi'), 0, 0, tiled=True)]
    concatenate x1, other arithmetic: 1 us -> 0.01 us  [with_lengths(): jnp.concatenate([passages.reshape(-1, WIDTH), jnp.broadcast_to(tail, (16,...]
  transfers between devices with their start and end apart: 13 -> 13, of which waited for: 8 -> 4; matrix products, arithmetic and copies ran while one was open for 2% -> 0% of each run, Pallas kernels for 0% -> 0%
where the time goes in v10:
time: 70.5 us; the launch traced here: 70.4 us
  blocking collectives  27.7 us (39%)
  Pallas kernels  17.7 us (25%)
  starting transfers between devices  14 us (20%)
  waiting for transfers between devices  9.79 us (14%)
  other arithmetic  1.01 us (1%)
    pallas_call x1, Pallas kernels, score(): pl.pallas_call(score_kernel, out_shape=jax.ShapeDtypeStruct((8, 8, 128),...  16.2 us
    all_to_all x1, blocking collectives, per_device(): received = lax.all_to_all(terms, ('z', 'yhi'), 0, 0, tiled=True)  14.8 us
    all_gather x1, blocking collectives, per_device(): lax.all_gather(passages[PERMUTED:].reshape(-1, WIDTH), 'x', axis=0, tiled...  12.9 us
    ppermute x3, starting transfers between devices, per_device(): lax.ppermute(block, PLANE, along(False, k))  5.07 us
    ppermute x3, waiting for transfers between devices, per_device(): lax.ppermute(own, PLANE, along(True, k))  4.99 us
    ppermute x3, waiting for transfers between devices, on_x(): return lax.ppermute(v, ('core', 'x'), pairs)  4.79 us
    ppermute x3, starting transfers between devices, on_x(): return lax.ppermute(v, ('core', 'x'), pairs)  4.28 us
    ppermute x3, starting transfers between devices, per_device(): lax.ppermute(own, PLANE, along(True, k))  4.09 us
  transfers between devices with their start and end apart: 13, of which 4 were waited for; matrix products, arithmetic and copies ran while one was open for 0% of the time, Pallas kernels for 0%

profile of v10, /device:TPU:0, one launch (start us, length us, event | category | flops | bytes accessed | tf_op | source)
XLA Modules:
  0.0 70.4 jit_solution(10423755072985388525)
XLA Ops:
  0.0 3.1 %collective-permute-start.2 = (bf16[256,128]{1,0:T(8,128)(2,1)}, bf16[256,128]{1,0:T(8,128)(2,1)S(1)}, u32[]{:S(2)}, u32[]{:S(2)}) collective-permute-start(bf16[256,128]{1,0:T(8,128)(2,1)} %bitcast.13), channel_id=1, source_target_pairs={{0,68},{4,64},{8,76},{12,72},{16,84},{20,80},{24,92},{28,88},{32,5... | collective-permute-start | bytes 196616 | tf_op jit(solution)/shard_map/ppermute | solution.py:237
  3.1 0.6 collective-permute-start.1
  3.7 0.4 collective-permute-start
  4.1 1.6 %collective-permute-done.2 = bf16[256,128]{1,0:T(8,128)(2,1)S(1)} collective-permute-done((bf16[256,128]{1,0:T(8,128)(2,1)}, bf16[256,128]{1,0:T(8,128)(2,1)S(1)}, u32[]{:S(2)}, u32[]{:S(2)}) %collective-permute-start.2) | collective-permute-done | bytes 65568 | tf_op jit(solution)/shard_map/ppermute | solution.py:237
  5.7 3.4 %collective-permute-done.1 = bf16[256,128]{1,0:T(8,128)(2,1)S(1)} collective-permute-done((bf16[256,128]{1,0:T(8,128)(2,1)}, bf16[256,128]{1,0:T(8,128)(2,1)S(1)}, u32[]{:S(2)}, u32[]{:S(2)}) %collective-permute-start.1) | collective-permute-done | bytes 65568 | tf_op jit(solution)/shard_map/ppermute | solution.py:237
  9.1 0.0 collective-permute-done
  9.1 0.0 copy-start
  9.1 0.9 %pad_maximum_fusion.refs_0_ = bf16[4,256,128]{2,1,0:T(8,128)(2,1)S(1)} fusion(bf16[1,256,128]{2,1,0:T(8,128)(2,1)S(1)} %bitcast.17, bf16[1,256,128]{2,1,0:T(8,128)(2,1)S(1)} %bitcast.18, bf16[1,256,128]{2,1,0:T(8,128)(2,1)S(1)} %bitcast.19, bf16[1,256,128]{2,1,0:T(8,128)(2,1)} %bitcast.16), kind=kLoop, calls=%fused_computation | loop fusion | flops 393216 | bytes 524288 | tf_op jit(solution)/shard_map/stack | solution.py:242
  10.0 0.0 copy-start.1
  10.0 4.1 %collective-permute-start.5 = (bf16[4,256,128]{2,1,0:T(8,128)(2,1)S(1)}, bf16[4,256,128]{2,1,0:T(8,128)(2,1)S(1)}, u32[]{:S(2)}, u32[]{:S(2)}) collective-permute-start(bf16[4,256,128]{2,1,0:T(8,128)(2,1)S(1)} %pad_maximum_fusion.refs_0_), channel_id=1, source_target_pairs={{0,24},{4,28},{8,16},{12,20},{16,8},{20,12},{24,0},{28,4},{32,100}... | collective-permute-start | bytes 786440 | tf_op jit(solution)/shard_map/ppermute | solution.py:243
  14.1 0.0 collective-permute-start.4
  14.1 0.9 %collective-permute-start.3 = (bf16[4,256,128]{2,1,0:T(8,128)(2,1)S(1)}, bf16[4,256,128]{2,1,0:T(8,128)(2,1)S(1)}, u32[]{:S(2)}, u32[]{:S(2)}) collective-permute-start(bf16[4,256,128]{2,1,0:T(8,128)(2,1)S(1)} %pad_maximum_fusion.refs_0_), channel_id=1, source_target_pairs={{0,8},{4,12},{8,0},{12,4},{16,24},{20,28},{24,16},{28,20},{32,96},... | collective-permute-start | bytes 786440 | tf_op jit(solution)/shard_map/ppermute | solution.py:243
  15.1 0.0 copy-done
  15.1 0.0 copy-done.1
  15.2 2.8 %collective-permute-start.11 = (bf16[528,128]{1,0:T(8,128)(2,1)S(1)}, bf16[528,128]{1,0:T(8,128)(2,1)S(1)}, u32[]{:S(2)}, u32[]{:S(2)}) collective-permute-start(bf16[528,128]{1,0:T(8,128)(2,1)S(1)} %pad_maximum_fusion.1.refs_8_), channel_id=1, source_target_pairs={{0,3},{1,2},{2,1},{3,0},{32,33},{33,32},{34,35},{35,34},{4,7},{5,6... | collective-permute-start | bytes 405512 | tf_op jit(solution)/shard_map/ppermute | solution.py:53
  18.0 0.2 collective-permute-start.10
  18.2 3.2 %collective-permute-done.11.refs_10_ = bf16[528,128]{1,0:T(8,128)(2,1)S(1)} collective-permute-done((bf16[528,128]{1,0:T(8,128)(2,1)S(1)}, bf16[528,128]{1,0:T(8,128)(2,1)S(1)}, u32[]{:S(2)}, u32[]{:S(2)}) %collective-permute-start.11) | collective-permute-done | bytes 135200 | tf_op jit(solution)/shard_map/ppermute | solution.py:53
  21.5 0.0 collective-permute-start.6
  21.5 1.5 %collective-permute-done.10.refs_9_ = bf16[528,128]{1,0:T(8,128)(2,1)S(1)} collective-permute-done((bf16[528,128]{1,0:T(8,128)(2,1)S(1)}, bf16[528,128]{1,0:T(8,128)(2,1)S(1)}, u32[]{:S(2)}, u32[]{:S(2)}) %collective-permute-start.10) | collective-permute-done | bytes 135200 | tf_op jit(solution)/shard_map/ppermute | solution.py:53
  23.0 1.2 %collective-permute-start.12 = (bf16[528,128]{1,0:T(8,128)(2,1)S(1)}, bf16[528,128]{1,0:T(8,128)(2,1)S(1)}, u32[]{:S(2)}, u32[]{:S(2)}) collective-permute-start(bf16[528,128]{1,0:T(8,128)(2,1)S(1)} %collective-permute-done.10.refs_9_), channel_id=1, source_target_pairs={{0,3},{1,2},{2,1},{3,0},{32,33},{33,32},{34,35},{35,34},{4,7},{5,6... | collective-permute-start | bytes 405512 | tf_op jit(solution)/shard_map/ppermute | solution.py:53
  24.2 0.0 collective-permute-done.5.refs_3_
  24.2 0.0 collective-permute-start.9
  24.3 0.0 collective-permute-done.4.refs_2_
  24.3 0.5 collective-permute-start.8
  24.8 0.0 collective-permute-done.3.refs_1_
  24.8 0.1 collective-permute-start.7
  24.9 12.9 %all_gather.3.refs_12_ = bf16[2048,128]{1,0:T(8,128)(2,1)S(1)} all-gather(bf16[512,128]{1,0:T(8,128)(2,1)S(1)} %bitcast.11), channel_id=1, replica_groups=mesh['ylo'=2,'core'=2,'z'=4,'yhi'=2,'x'=4] {'x'}, dimensions={0}, use_global_device_ids=true | all-gather | bytes 655360 | tf_op jit(solution)/shard_map/all_gather | solution.py:239
  37.8 0.1 pad_add_fusion.info_ref
  37.9 0.0 collective-permute-done.12.refs_11_
  37.9 0.0 collective-permute-done.6.refs_4_
  37.9 0.0 collective-permute-done.9.refs_7_
  37.9 0.0 collective-permute-done.8.refs_6_
  37.9 0.0 collective-permute-done.7.refs_5_
  37.9 16.2 %shard_map.37 = f32[8,8,128]{2,1,0:T(8,128)S(1)} custom-call(s32[4]{0:T(128)S(1)} %pad_add_fusion.info_ref, bf16[4,256,128]{2,1,0:T(8,128)(2,1)S(1)} %pad_maximum_fusion.refs_0_, bf16[4,256,128]{2,1,0:T(8,128)(2,1)S(1)} %collective-permute-done.3.refs_1_, bf16[4,256,128]{2,1,0:T(8,128)(2,1)S(1)} %collective-permute-done.4.refs_2_, ...), custom_call_target="tpu_custom_call" | custom-call | tf_op jit(solution)/shard_map/pallas_call | solution.py:200
  54.1 14.8 %all_to_all.5.r_ref = f32[8,8,128]{2,1,0:T(8,128)} all-to-all(f32[8,8,128]{2,1,0:T(8,128)S(1)} %shard_map.37), channel_id=1, replica_groups=mesh['ylo'=2,'core'=2,'z'=4,'yhi'=2,'x'=4] {'z','yhi'}, dimensions={0} | all-to-all | bytes 65536 | tf_op jit(solution)/shard_map/all_to_all | solution.py:246
  68.9 1.5 %shard_map.38 = f32[32,256]{1,0:T(8,128)} custom-call(f32[8,8,128]{2,1,0:T(8,128)} %all_to_all.5.r_ref), custom_call_target="tpu_custom_call" | custom-call | tf_op jit(solution)/shard_map/pallas_call | solution.py:225
  (5 shorter events, 0.0 us)
Async XLA Ops:
  0.0 5.7 %collective-permute-start.2 = (bf16[256,128]{1,0:T(8,128)(2,1)}, bf16[256,128]{1,0:T(8,128)(2,1)S(1)}, u32[]{:S(2)}, u32[]{:S(2)}) collective-permute-start(bf16[256,128]{1,0:T(8,128)(2,1)} %bitcast.13), channel_id=1, source_target_pairs={{0,68},{4,64},{8,76},{12,72},{16,84},{20,80},{24,92},{28,88},{32,5... | collective-permute-start | bytes 196616 | tf_op jit(solution)/shard_map/ppermute | solution.py:237
  3.1 6.0 %collective-permute-start.1 = (bf16[256,128]{1,0:T(8,128)(2,1)}, bf16[256,128]{1,0:T(8,128)(2,1)S(1)}, u32[]{:S(2)}, u32[]{:S(2)}) collective-permute-start(bf16[256,128]{1,0:T(8,128)(2,1)} %bitcast.14), channel_id=1, source_target_pairs={{0,4},{4,0},{8,12},{12,8},{16,20},{20,16},{24,28},{28,24},{32,48},... | collective-permute-start | bytes 196616 | tf_op jit(solution)/shard_map/ppermute | solution.py:237
  3.7 5.4 %collective-permute-start = (bf16[256,128]{1,0:T(8,128)(2,1)}, bf16[256,128]{1,0:T(8,128)(2,1)S(1)}, u32[]{:S(2)}, u32[]{:S(2)}) collective-permute-start(bf16[256,128]{1,0:T(8,128)(2,1)} %bitcast.15), channel_id=1, source_target_pairs={{0,64},{4,68},{8,72},{12,76},{16,80},{20,84},{24,88},{28,92},{32,4... | collective-permute-start | bytes 196616 | tf_op jit(solution)/shard_map/ppermute | solution.py:237
  9.1 6.0 %copy-start = (bf16[8,128,128]{2,1,0:T(8,128)(2,1)S(1)}, bf16[8,128,128]{2,1,0:T(8,128)(2,1)}, u32[]{:S(2)}) copy-start(bf16[8,128,128]{2,1,0:T(8,128)(2,1)} %param.4) | copy-start | bytes 786436
  10.0 5.1 %copy-start.1 = (s32[8]{0:T(128)S(1)}, s32[8]{0:T(128)}, u32[]{:S(2)}) copy-start(s32[8]{0:T(128)} %param.5) | copy-start | bytes 100
  10.0 14.2 %collective-permute-start.5 = (bf16[4,256,128]{2,1,0:T(8,128)(2,1)S(1)}, bf16[4,256,128]{2,1,0:T(8,128)(2,1)S(1)}, u32[]{:S(2)}, u32[]{:S(2)}) collective-permute-start(bf16[4,256,128]{2,1,0:T(8,128)(2,1)S(1)} %pad_maximum_fusion.refs_0_), channel_id=1, source_target_pairs={{0,24},{4,28},{8,16},{12,20},{16,8},{20,12},{24,0},{28,4},{32,100}... | collective-permute-start | bytes 786440 | tf_op jit(solution)/shard_map/ppermute | solution.py:243
  14.1 10.1 %collective-permute-start.4 = (bf16[4,256,128]{2,1,0:T(8,128)(2,1)S(1)}, bf16[4,256,128]{2,1,0:T(8,128)(2,1)S(1)}, u32[]{:S(2)}, u32[]{:S(2)}) collective-permute-start(bf16[4,256,128]{2,1,0:T(8,128)(2,1)S(1)} %pad_maximum_fusion.refs_0_), channel_id=1, source_target_pairs={{0,16},{4,20},{8,24},{12,28},{16,0},{20,4},{24,8},{28,12},{32,36},... | collective-permute-start | bytes 786440 | tf_op jit(solution)/shard_map/ppermute | solution.py:243
  14.1 10.6 %collective-permute-start.3 = (bf16[4,256,128]{2,1,0:T(8,128)(2,1)S(1)}, bf16[4,256,128]{2,1,0:T(8,128)(2,1)S(1)}, u32[]{:S(2)}, u32[]{:S(2)}) collective-permute-start(bf16[4,256,128]{2,1,0:T(8,128)(2,1)S(1)} %pad_maximum_fusion.refs_0_), channel_id=1, source_target_pairs={{0,8},{4,12},{8,0},{12,4},{16,24},{20,28},{24,16},{28,20},{32,96},... | collective-permute-start | bytes 786440 | tf_op jit(solution)/shard_map/ppermute | solution.py:243
  15.2 6.3 %collective-permute-start.11 = (bf16[528,128]{1,0:T(8,128)(2,1)S(1)}, bf16[528,128]{1,0:T(8,128)(2,1)S(1)}, u32[]{:S(2)}, u32[]{:S(2)}) collective-permute-start(bf16[528,128]{1,0:T(8,128)(2,1)S(1)} %pad_maximum_fusion.1.refs_8_), channel_id=1, source_target_pairs={{0,3},{1,2},{2,1},{3,0},{32,33},{33,32},{34,35},{35,34},{4,7},{5,6... | collective-permute-start | bytes 405512 | tf_op jit(solution)/shard_map/ppermute | solution.py:53
  18.0 5.0 %collective-permute-start.10 = (bf16[528,128]{1,0:T(8,128)(2,1)S(1)}, bf16[528,128]{1,0:T(8,128)(2,1)S(1)}, u32[]{:S(2)}, u32[]{:S(2)}) collective-permute-start(bf16[528,128]{1,0:T(8,128)(2,1)S(1)} %pad_maximum_fusion.1.refs_8_), channel_id=1, source_target_pairs={{0,1},{1,0},{2,3},{3,2},{32,35},{33,34},{34,33},{35,32},{4,5},{5,4... | collective-permute-start | bytes 405512 | tf_op jit(solution)/shard_map/ppermute | solution.py:53
  21.5 16.4 %collective-permute-start.6 = (bf16[4,256,128]{2,1,0:T(8,128)(2,1)S(1)}, bf16[4,256,128]{2,1,0:T(8,128)(2,1)S(1)}, u32[]{:S(2)}, u32[]{:S(2)}) collective-permute-start(bf16[4,256,128]{2,1,0:T(8,128)(2,1)S(1)} %pad_maximum_fusion.refs_0_), channel_id=1, source_target_pairs={{0,32},{32,0},{1,33},{33,1},{2,34},{34,2},{3,35},{35,3},{4,36},{36... | collective-permute-start | bytes 786440 | tf_op jit(solution)/shard_map/ppermute | solution.py:44
  23.0 14.9 %collective-permute-start.12 = (bf16[528,128]{1,0:T(8,128)(2,1)S(1)}, bf16[528,128]{1,0:T(8,128)(2,1)S(1)}, u32[]{:S(2)}, u32[]{:S(2)}) collective-permute-start(bf16[528,128]{1,0:T(8,128)(2,1)S(1)} %collective-permute-done.10.refs_9_), channel_id=1, source_target_pairs={{0,3},{1,2},{2,1},{3,0},{32,33},{33,32},{34,35},{35,34},{4,7},{5,6... | collective-permute-start | bytes 405512 | tf_op jit(solution)/shard_map/ppermute | solution.py:53
  24.2 13.6 %collective-permute-start.9 = (bf16[4,256,128]{2,1,0:T(8,128)(2,1)S(1)}, bf16[4,256,128]{2,1,0:T(8,128)(2,1)S(1)}, u32[]{:S(2)}, u32[]{:S(2)}) collective-permute-start(bf16[4,256,128]{2,1,0:T(8,128)(2,1)S(1)} %collective-permute-done.5.refs_3_), channel_id=1, source_target_pairs={{0,32},{32,0},{1,33},{33,1},{2,34},{34,2},{3,35},{35,3},{4,36},{36... | collective-permute-start | bytes 786440 | tf_op jit(solution)/shard_map/ppermute | solution.py:44
  24.3 13.6 %collective-permute-start.8 = (bf16[4,256,128]{2,1,0:T(8,128)(2,1)S(1)}, bf16[4,256,128]{2,1,0:T(8,128)(2,1)S(1)}, u32[]{:S(2)}, u32[]{:S(2)}) collective-permute-start(bf16[4,256,128]{2,1,0:T(8,128)(2,1)S(1)} %collective-permute-done.4.refs_2_), channel_id=1, source_target_pairs={{0,32},{32,0},{1,33},{33,1},{2,34},{34,2},{3,35},{35,3},{4,36},{36... | collective-permute-start | bytes 786440 | tf_op jit(solution)/shard_map/ppermute | solution.py:44
  24.8 13.1 %collective-permute-start.7 = (bf16[4,256,128]{2,1,0:T(8,128)(2,1)S(1)}, bf16[4,256,128]{2,1,0:T(8,128)(2,1)S(1)}, u32[]{:S(2)}, u32[]{:S(2)}) collective-permute-start(bf16[4,256,128]{2,1,0:T(8,128)(2,1)S(1)} %collective-permute-done.3.refs_1_), channel_id=1, source_target_pairs={{0,32},{32,0},{1,33},{33,1},{2,34},{34,2},{3,35},{35,3},{4,36},{36... | collective-permute-start | bytes 786440 | tf_op jit(solution)/shard_map/ppermute | solution.py:44

commit v11 on v9

--- a/solution.py
+++ b/solution.py
@@ -54,18 +54,22 @@
 
 def with_lengths(passages, lengths):
     tail = jnp.pad(lengths.astype(passages.dtype), (0, WIDTH - OWN))
+    slot = lax.broadcasted_iota(jnp.int32, passages.shape, 1)
+    before = jnp.concatenate([passages[:, :8], passages[:, :-8]], axis=1)
+    filled = jnp.where(slot < lengths[:, None, None], passages, before)
     return jnp.concatenate(
-        [passages.reshape(OWN * SLOTS, WIDTH), jnp.broadcast_to(tail, (16, WIDTH))], axis=0
+        [filled.reshape(OWN * SLOTS, WIDTH), jnp.broadcast_to(tail, (16, WIDTH))], axis=0
     )
 
 
-def best_dots(w_ref, p_ref, m_ref, s_ref, unit_ref, turns, *acc):
+def best_dots(rows, places, p_ref, m_ref, s_ref, unit_ref, turns, *acc):
     acc = (acc[:DEPTH], acc[DEPTH:])
     nothing = jnp.zeros((16, 128), jnp.bfloat16)
 
     def push(g):
         for u in range(2):
-            pltpu.matmul_push_rhs(w_ref[g * 2 + u], 0, u, transpose=True)
+            held = jnp.concatenate([ref[j] for ref, j in rows[g][2 * u : 2 * u + 2]], axis=1)
+            pltpu.matmul_push_rhs(held, 0, u, transpose=True)
 
     def issue(unit, j, fresh=False):
         slots = p_ref[pl.ds(pl.multiple_of(unit, 16), 16), :]
@@ -92,59 +96,49 @@
         for b in range(8):
             m_ref[b, at] = jnp.maximum(held[b], tops[b])
 
+    def turn(t, c):
+        for j in range(DEPTH):
+            take(unit_ref[t * DEPTH + j], j)
+            issue(unit_ref[t * DEPTH + DEPTH + j], j)
+        return c
+
     m_ref[:, 32] = jnp.full((8, 8, 128), LOWEST, jnp.float32)
+    rows_ref = m_ref.reshape(8, 264, 128)
     push(0)
     for j in range(DEPTH):
         issue(unit_ref[j], j, fresh=j == 0)
-
-    def group(g, carry):
-
-        def turn(t, c):
-            for j in range(DEPTH):
-                take(unit_ref[t * DEPTH + j], j)
-                issue(unit_ref[t * DEPTH + DEPTH + j], j)
-            return c
-
+    for g in range(len(rows)):
         lax.fori_loop(0, turns - 1, turn, 0)
-        push(jnp.minimum(g + 1, 7))
+        more = g + 1 < len(rows)
+        if more:
+            push(g + 1)
         last = (turns - 1) * DEPTH
         for j in range(DEPTH):
             take(unit_ref[last + j], j)
-            issue(unit_ref[j], j, fresh=j == 0)
-        rows_ref = m_ref.reshape(8, 264, 128)
+            if more:
+                issue(unit_ref[j], j, fresh=j == 0)
         for o in range(4):
-            for side in range(2):
-                total = None
-                for b in range(side, 8, 2):
-                    top = rows_ref[b, pl.ds(64 * o, 8, stride=8), :]
-                    for i in range(1, 8):
-                        top = jnp.maximum(top, rows_ref[b, pl.ds(64 * o + i, 8, stride=8), :])
-                    total = top if total is None else total + top
-                s_ref[g, 8 * o : 8 * o + 8, 128 * side : 128 * side + 128] = total
-        return carry
-
-    lax.fori_loop(0, 8, group, 0)
-    for u in range(2):
-        for j in range(DEPTH):
-            m_ref[0, 0] = pltpu.matmul_pop(acc[u][j])[0:8, 0:128]
+            for b in range(8):
+                top = rows_ref[b, pl.ds(64 * o, 8, stride=8), :]
+                for i in range(1, 8):
+                    top = jnp.maximum(top, rows_ref[b, pl.ds(64 * o + i, 8, stride=8), :])
+                lanes = slice(128 * (b % 2), 128 * (b % 2) + 128)
+                s_ref[places[g][b // 2], 8 * o : 8 * o + 8, lanes] += top
 
 
 def score_kernel(info_ref, *refs):
     rows, pieces, out_ref = refs[:8], refs[8:12], refs[12]
-    w_ref, p_ref, m_ref, s_ref, unit_ref = refs[13:]
+    p_ref, m_ref, s_ref, unit_ref = refs[13:]
     z, yhi, core, x = (info_ref[i] for i in range(4))
 
-    for kind in range(2):
-
-        @pl.when(core == kind)
-        def _():
-            for a in range(8):
-                for j in range(4):
-                    same = (a < 4) == (kind == 0)
-                    dz, dy = (a % 4, j) if same else (j, a % 4)
-                    h = dy // 2
-                    half = 128 * (dy % 2)
-                    w_ref[(dz * 2 + h) * 2 + a // 4, :, half : half + 128] = rows[a][j]
+    groups, places = [], []
+    for k in range(4):
+        for j in (0, 2):
+            groups.append([(rows[c + k], e) for c in (0, 4) for e in (j, j + 1)])
+            by_chain = [[k * 2 + e // 2, e * 2 + k // 2] for e in (j, j + 1)]
+            places.append(
+                [jnp.where(chain == 0, p, q) for chain in (core, 1 - core) for p, q in by_chain]
+            )
 
     count = jnp.int32(0)
     for m in range(4):
@@ -156,17 +150,13 @@
             for n in range(8):
                 unit_ref[count + n] = from_x * 1024 + i * SLOTS + n * 16
             count = count + units[0, i]
-            used = units[0, i]
-            last = pl.multiple_of(from_x * 1024 + i * SLOTS + (used - 1) * 16, 16)
-            both = p_ref[pl.ds(last, 16), :].astype(jnp.float32)
-            second = jnp.where(lengths[0, i] == used * 16, both[8:16], both[0:8])
-            p_ref[pl.ds(last, 16), :] = jnp.concatenate([both[0:8], second], axis=0).astype(p_ref.dtype)
     for i in range(DEPTH):
         unit_ref[count + i] = unit_ref[count - 1]
     turns = lax.div(count + DEPTH - 1, DEPTH)
 
+    s_ref[...] = jnp.zeros_like(s_ref)
     pl.run_scoped(
-        functools.partial(best_dots, w_ref, p_ref, m_ref, s_ref, unit_ref, turns),
+        functools.partial(best_dots, groups, places, p_ref, m_ref, s_ref, unit_ref, turns),
         *[pltpu.ACC(u)((32, 256), jnp.float32) for u in range(2) for _ in range(DEPTH)],
     )
 
@@ -200,7 +190,6 @@
         + [pl.BlockSpec(memory_space=pltpu.VMEM)] * 12,
         out_specs=pl.BlockSpec(memory_space=pltpu.VMEM),
         scratch_shapes=[
-            pltpu.VMEM((16, 256, 256), jnp.bfloat16),
             pltpu.VMEM((4096, 128), jnp.bfloat16),
             pltpu.VMEM((8, 33, 8, 128), jnp.float32),
             pltpu.VMEM((8, 32, 256), jnp.float32),

time: 55.5 us -> 55.3 us (level)
  local copies, waits for them, and re-layouts: 0.02 us -> 1.02 us
  other arithmetic: 1.12 us -> 0.31 us
    concatenate x1, other arithmetic: 1 us -> 0.02 us  [with_lengths(): jnp.concatenate([filled.reshape(OWN * SLOTS, WIDTH), jnp.broadcast_to(tai...]
    unnamed x4 -> x6, local copies, waits for them, and re-layouts: 0.01 us -> 0.66 us
  transfers between devices with their start and end apart: 13 -> 13, of which waited for: 8 -> 8; matrix products, arithmetic and copies ran while one was open for 2% -> 1% of each run, Pallas kernels for 0% -> 0%
where the time goes in v11:
time: 55.3 us; the launch traced here: 55 us
  blocking collectives  16 us (29%)
  Pallas kernels  15.9 us (29%)
  starting transfers between devices  14.8 us (27%)
  waiting for transfers between devices  6.82 us (12%)
  local copies, waits for them, and re-layouts  1.02 us (2%)
    all_to_all x1, blocking collectives, per_device(): received = lax.all_to_all(terms, ('z', 'yhi'), 0, 0, tiled=True)  16 us
    pallas_call x1, Pallas kernels, score(): pl.pallas_call(score_kernel, out_shape=jax.ShapeDtypeStruct((8, 8, 128),...  14.5 us
    ppermute x3, starting transfers between devices, on_x(): return lax.ppermute(v, ('core', 'x'), pairs)  5.42 us
    ppermute x3, starting transfers between devices, per_device(): lax.ppermute(block, PLANE, along(False, k))  5.07 us
    ppermute x3, waiting for transfers between devices, per_device(): lax.ppermute(block, PLANE, along(False, k))  4.42 us
    ppermute x3, starting transfers between devices, per_device(): lax.ppermute(own, PLANE, along(True, k))  4.09 us
    pallas_call x1, Pallas kernels, place(): pl.pallas_call(place_kernel, out_shape=jax.ShapeDtypeStruct((32, 256), jn...  1.46 us
  transfers between devices with their start and end apart: 13, of which 8 were waited for; matrix products, arithmetic and copies ran while one was open for 1% of the time, Pallas kernels for 0%

profile of v11, /device:TPU:0, one launch (start us, length us, event | category | flops | bytes accessed | tf_op | source)
XLA Modules:
  0.0 55.0 jit_solution(17467974925809254676)
XLA Ops:
  0.0 0.0 copy-start
  0.0 3.1 %collective-permute-start.2 = (bf16[256,128]{1,0:T(8,128)(2,1)}, bf16[256,128]{1,0:T(8,128)(2,1)S(1)}, u32[]{:S(2)}, u32[]{:S(2)}) collective-permute-start(bf16[256,128]{1,0:T(8,128)(2,1)} %bitcast.11), channel_id=1, source_target_pairs={{0,68},{4,64},{8,76},{12,72},{16,84},{20,80},{24,92},{28,88},{32,5... | collective-permute-start | bytes 196616 | tf_op jit(solution)/shard_map/ppermute | solution.py:222
  3.1 0.6 %collective-permute-start.1 = (bf16[256,128]{1,0:T(8,128)(2,1)}, bf16[256,128]{1,0:T(8,128)(2,1)S(1)}, u32[]{:S(2)}, u32[]{:S(2)}) collective-permute-start(bf16[256,128]{1,0:T(8,128)(2,1)} %bitcast.12), channel_id=1, source_target_pairs={{0,4},{4,0},{8,12},{12,8},{16,20},{20,16},{24,28},{28,24},{32,48},... | collective-permute-start | bytes 196616 | tf_op jit(solution)/shard_map/ppermute | solution.py:222
  3.7 0.4 collective-permute-start
  4.1 0.0 copy-start.2
  4.1 0.0 slice-start
  4.1 0.0 slice-start.1
  4.1 0.6 %copy-done.2 = s32[8]{0:T(128)S(1)} copy-done((s32[8]{0:T(128)S(1)}, s32[8]{0:T(128)}, u32[]{:S(2)}) %copy-start.2) | copy-done | bytes 56
  4.8 0.0 copy-done
  4.8 0.1 slice-done
  4.8 0.3 slice-done.1
  5.1 0.2 fusion
  5.3 0.0 copy-start.1
  5.3 2.9 %collective-permute-start.11 = (bf16[1040,128]{1,0:T(8,128)(2,1)S(1)}, bf16[1040,128]{1,0:T(8,128)(2,1)S(1)}, u32[]{:S(2)}, u32[]{:S(2)}) collective-permute-start(bf16[1040,128]{1,0:T(8,128)(2,1)S(1)} %pad_maximum_fusion.refs_8_), channel_id=1, source_target_pairs={{0,3},{1,2},{2,1},{3,0},{32,33},{33,32},{34,35},{35,34},{4,7},{5,6... | collective-permute-start | bytes 798728 | tf_op jit(solution)/shard_map/ppermute | solution.py:52
  8.3 0.2 collective-permute-start.10
  8.5 0.0 collective-permute-done.2
  8.5 0.6 %collective-permute-done.1 = bf16[256,128]{1,0:T(8,128)(2,1)S(1)} collective-permute-done((bf16[256,128]{1,0:T(8,128)(2,1)}, bf16[256,128]{1,0:T(8,128)(2,1)S(1)}, u32[]{:S(2)}, u32[]{:S(2)}) %collective-permute-start.1) | collective-permute-done | bytes 65568 | tf_op jit(solution)/shard_map/ppermute | solution.py:222
  9.1 0.0 collective-permute-done
  9.1 0.0 copy-done.1
  9.1 4.1 %collective-permute-start.5 = (bf16[4,256,128]{2,1,0:T(8,128)(2,1)S(1)}, bf16[4,256,128]{2,1,0:T(8,128)(2,1)S(1)}, u32[]{:S(2)}, u32[]{:S(2)}) collective-permute-start(bf16[4,256,128]{2,1,0:T(8,128)(2,1)S(1)} %pad_maximum_fusion.1.refs_0_), channel_id=1, source_target_pairs={{0,24},{4,28},{8,16},{12,20},{16,8},{20,12},{24,0},{28,4},{32,100}... | collective-permute-start | bytes 786440 | tf_op jit(solution)/shard_map/ppermute | solution.py:227
  13.2 0.0 collective-permute-start.4
  13.2 0.9 %collective-permute-start.3 = (bf16[4,256,128]{2,1,0:T(8,128)(2,1)S(1)}, bf16[4,256,128]{2,1,0:T(8,128)(2,1)S(1)}, u32[]{:S(2)}, u32[]{:S(2)}) collective-permute-start(bf16[4,256,128]{2,1,0:T(8,128)(2,1)S(1)} %pad_maximum_fusion.1.refs_0_), channel_id=1, source_target_pairs={{0,8},{4,12},{8,0},{12,4},{16,24},{20,28},{24,16},{28,20},{32,96},... | collective-permute-start | bytes 786440 | tf_op jit(solution)/shard_map/ppermute | solution.py:227
  14.2 0.5 collective-permute-done.10.refs_9_
  14.7 2.3 %collective-permute-start.12 = (bf16[1040,128]{1,0:T(8,128)(2,1)S(1)}, bf16[1040,128]{1,0:T(8,128)(2,1)S(1)}, u32[]{:S(2)}, u32[]{:S(2)}) collective-permute-start(bf16[1040,128]{1,0:T(8,128)(2,1)S(1)} %collective-permute-done.10.refs_9_), channel_id=1, source_target_pairs={{0,3},{1,2},{2,1},{3,0},{32,33},{33,32},{34,35},{35,34},{4,7},{5,6... | collective-permute-start | bytes 798728 | tf_op jit(solution)/shard_map/ppermute | solution.py:52
  17.0 0.0 collective-permute-done.11.refs_10_
  17.0 0.0 collective-permute-start.6
  17.0 3.0 %collective-permute-done.5.refs_3_ = bf16[4,256,128]{2,1,0:T(8,128)(2,1)S(1)} collective-permute-done((bf16[4,256,128]{2,1,0:T(8,128)(2,1)S(1)}, bf16[4,256,128]{2,1,0:T(8,128)(2,1)S(1)}, u32[]{:S(2)}, u32[]{:S(2)}) %collective-permute-start.5) | collective-permute-done | bytes 262176 | tf_op jit(solution)/shard_map/ppermute | solution.py:227
  19.9 0.0 collective-permute-start.9
  19.9 1.2 %collective-permute-done.4.refs_2_ = bf16[4,256,128]{2,1,0:T(8,128)(2,1)S(1)} collective-permute-done((bf16[4,256,128]{2,1,0:T(8,128)(2,1)S(1)}, bf16[4,256,128]{2,1,0:T(8,128)(2,1)S(1)}, u32[]{:S(2)}, u32[]{:S(2)}) %collective-permute-start.4) | collective-permute-done | bytes 262176 | tf_op jit(solution)/shard_map/ppermute | solution.py:227
  21.1 0.0 collective-permute-start.8
  21.1 0.3 collective-permute-done.3.refs_1_
  21.4 0.2 collective-permute-start.7
  21.6 0.1 pad_add_fusion.info_ref
  21.7 0.0 collective-permute-done.6.refs_4_
  21.7 0.6 %collective-permute-done.12.refs_11_ = bf16[1040,128]{1,0:T(8,128)(2,1)S(1)} collective-permute-done((bf16[1040,128]{1,0:T(8,128)(2,1)S(1)}, bf16[1040,128]{1,0:T(8,128)(2,1)S(1)}, u32[]{:S(2)}, u32[]{:S(2)}) %collective-permute-start.12) | collective-permute-done | bytes 266272 | tf_op jit(solution)/shard_map/ppermute | solution.py:52
  22.3 0.0 collective-permute-done.9.refs_7_
  22.3 0.3 collective-permute-done.8.refs_6_
  22.7 0.4 collective-permute-done.7.refs_5_
  23.0 14.5 %shard_map.37 = f32[8,8,128]{2,1,0:T(8,128)S(1)} custom-call(s32[4]{0:T(128)S(1)} %pad_add_fusion.info_ref, bf16[4,256,128]{2,1,0:T(8,128)(2,1)S(1)} %pad_maximum_fusion.1.refs_0_, bf16[4,256,128]{2,1,0:T(8,128)(2,1)S(1)} %collective-permute-done.3.refs_1_, bf16[4,256,128]{2,1,0:T(8,128)(2,1)S(1)} %collective-permute-done.4.refs_2_, ...), custom_call_target="tpu_custom_call" | custom-call | tf_op jit(solution)/shard_map/pallas_call | solution.py:186
  37.5 16.0 %all_to_all.5.r_ref = f32[8,8,128]{2,1,0:T(8,128)} all-to-all(f32[8,8,128]{2,1,0:T(8,128)S(1)} %shard_map.37), channel_id=1, replica_groups=mesh['ylo'=2,'core'=2,'z'=4,'yhi'=2,'x'=4] {'z','yhi'}, dimensions={0} | all-to-all | bytes 65536 | tf_op jit(solution)/shard_map/all_to_all | solution.py:230
  53.5 1.5 %shard_map.38 = f32[32,256]{1,0:T(8,128)} custom-call(f32[8,8,128]{2,1,0:T(8,128)} %all_to_all.5.r_ref), custom_call_target="tpu_custom_call" | custom-call | tf_op jit(solution)/shard_map/pallas_call | solution.py:210
  (5 shorter events, 0.1 us)
Async XLA Ops:
  0.0 4.8 %copy-start = (bf16[8,128,128]{2,1,0:T(8,128)(2,1)S(1)}, bf16[8,128,128]{2,1,0:T(8,128)(2,1)}, u32[]{:S(2)}) copy-start(bf16[8,128,128]{2,1,0:T(8,128)(2,1)} %param.4) | copy-start | bytes 786436
  0.0 8.5 %collective-permute-start.2 = (bf16[256,128]{1,0:T(8,128)(2,1)}, bf16[256,128]{1,0:T(8,128)(2,1)S(1)}, u32[]{:S(2)}, u32[]{:S(2)}) collective-permute-start(bf16[256,128]{1,0:T(8,128)(2,1)} %bitcast.11), channel_id=1, source_target_pairs={{0,68},{4,64},{8,76},{12,72},{16,84},{20,80},{24,92},{28,88},{32,5... | collective-permute-start | bytes 196616 | tf_op jit(solution)/shard_map/ppermute | solution.py:222
  3.1 6.0 %collective-permute-start.1 = (bf16[256,128]{1,0:T(8,128)(2,1)}, bf16[256,128]{1,0:T(8,128)(2,1)S(1)}, u32[]{:S(2)}, u32[]{:S(2)}) collective-permute-start(bf16[256,128]{1,0:T(8,128)(2,1)} %bitcast.12), channel_id=1, source_target_pairs={{0,4},{4,0},{8,12},{12,8},{16,20},{20,16},{24,28},{28,24},{32,48},... | collective-permute-start | bytes 196616 | tf_op jit(solution)/shard_map/ppermute | solution.py:222
  3.7 5.4 %collective-permute-start = (bf16[256,128]{1,0:T(8,128)(2,1)}, bf16[256,128]{1,0:T(8,128)(2,1)S(1)}, u32[]{:S(2)}, u32[]{:S(2)}) collective-permute-start(bf16[256,128]{1,0:T(8,128)(2,1)} %bitcast.13), channel_id=1, source_target_pairs={{0,64},{4,68},{8,72},{12,76},{16,80},{20,84},{24,88},{28,92},{32,4... | collective-permute-start | bytes 196616 | tf_op jit(solution)/shard_map/ppermute | solution.py:222
  4.1 0.7 %copy-start.2 = (s32[8]{0:T(128)S(1)}, s32[8]{0:T(128)}, u32[]{:S(2)}) copy-start(s32[8]{0:T(128)} %param.5) | copy-start | bytes 100
  4.1 0.7 %slice-start = ((bf16[8,128,128]{2,1,0:T(8,128)(2,1)}), bf16[8,8,128]{2,1,0:T(8,128)(2,1)S(1)}, s32[]{:S(2)}) async-start(bf16[8,128,128]{2,1,0:T(8,128)(2,1)} %param.4), calls=%async_computation.1 | async-start | bytes 32768 | tf_op jit(solution)/shard_map/slice | solution.py:58
  4.1 1.0 %slice-start.1 = ((bf16[8,128,128]{2,1,0:T(8,128)(2,1)}), bf16[8,120,128]{2,1,0:T(8,128)(2,1)S(1)}, s32[]{:S(2)}) async-start(bf16[8,128,128]{2,1,0:T(8,128)(2,1)} %param.4), calls=%async_computation.2 | async-start | bytes 491520 | tf_op jit(solution)/shard_map/slice | solution.py:58
  5.3 3.8 %copy-start.1 = (bf16[32,8,128]{2,1,0:T(8,128)(2,1)S(1)}, bf16[32,8,128]{2,1,0:T(8,128)(2,1)}, u32[]{:S(2)}) copy-start(bf16[32,8,128]{2,1,0:T(8,128)(2,1)} %param.3) | copy-start | bytes 196612
  5.3 11.6 %collective-permute-start.11 = (bf16[1040,128]{1,0:T(8,128)(2,1)S(1)}, bf16[1040,128]{1,0:T(8,128)(2,1)S(1)}, u32[]{:S(2)}, u32[]{:S(2)}) collective-permute-start(bf16[1040,128]{1,0:T(8,128)(2,1)S(1)} %pad_maximum_fusion.refs_8_), channel_id=1, source_target_pairs={{0,3},{1,2},{2,1},{3,0},{32,33},{33,32},{34,35},{35,34},{4,7},{5,6... | collective-permute-start | bytes 798728 | tf_op jit(solution)/shard_map/ppermute | solution.py:52
  8.3 6.4 %collective-permute-start.10 = (bf16[1040,128]{1,0:T(8,128)(2,1)S(1)}, bf16[1040,128]{1,0:T(8,128)(2,1)S(1)}, u32[]{:S(2)}, u32[]{:S(2)}) collective-permute-start(bf16[1040,128]{1,0:T(8,128)(2,1)S(1)} %pad_maximum_fusion.refs_8_), channel_id=1, source_target_pairs={{0,1},{1,0},{2,3},{3,2},{32,35},{33,34},{34,33},{35,32},{4,5},{5,4... | collective-permute-start | bytes 798728 | tf_op jit(solution)/shard_map/ppermute | solution.py:52
  9.1 10.8 %collective-permute-start.5 = (bf16[4,256,128]{2,1,0:T(8,128)(2,1)S(1)}, bf16[4,256,128]{2,1,0:T(8,128)(2,1)S(1)}, u32[]{:S(2)}, u32[]{:S(2)}) collective-permute-start(bf16[4,256,128]{2,1,0:T(8,128)(2,1)S(1)} %pad_maximum_fusion.1.refs_0_), channel_id=1, source_target_pairs={{0,24},{4,28},{8,16},{12,20},{16,8},{20,12},{24,0},{28,4},{32,100}... | collective-permute-start | bytes 786440 | tf_op jit(solution)/shard_map/ppermute | solution.py:227
  13.2 7.9 %collective-permute-start.4 = (bf16[4,256,128]{2,1,0:T(8,128)(2,1)S(1)}, bf16[4,256,128]{2,1,0:T(8,128)(2,1)S(1)}, u32[]{:S(2)}, u32[]{:S(2)}) collective-permute-start(bf16[4,256,128]{2,1,0:T(8,128)(2,1)S(1)} %pad_maximum_fusion.1.refs_0_), channel_id=1, source_target_pairs={{0,16},{4,20},{8,24},{12,28},{16,0},{20,4},{24,8},{28,12},{32,36},... | collective-permute-start | bytes 786440 | tf_op jit(solution)/shard_map/ppermute | solution.py:227
  13.2 8.1 %collective-permute-start.3 = (bf16[4,256,128]{2,1,0:T(8,128)(2,1)S(1)}, bf16[4,256,128]{2,1,0:T(8,128)(2,1)S(1)}, u32[]{:S(2)}, u32[]{:S(2)}) collective-permute-start(bf16[4,256,128]{2,1,0:T(8,128)(2,1)S(1)} %pad_maximum_fusion.1.refs_0_), channel_id=1, source_target_pairs={{0,8},{4,12},{8,0},{12,4},{16,24},{20,28},{24,16},{28,20},{32,96},... | collective-permute-start | bytes 786440 | tf_op jit(solution)/shard_map/ppermute | solution.py:227
  14.7 7.6 %collective-permute-start.12 = (bf16[1040,128]{1,0:T(8,128)(2,1)S(1)}, bf16[1040,128]{1,0:T(8,128)(2,1)S(1)}, u32[]{:S(2)}, u32[]{:S(2)}) collective-permute-start(bf16[1040,128]{1,0:T(8,128)(2,1)S(1)} %collective-permute-done.10.refs_9_), channel_id=1, source_target_pairs={{0,3},{1,2},{2,1},{3,0},{32,33},{33,32},{34,35},{35,34},{4,7},{5,6... | collective-permute-start | bytes 798728 | tf_op jit(solution)/shard_map/ppermute | solution.py:52
  17.0 4.8 %collective-permute-start.6 = (bf16[4,256,128]{2,1,0:T(8,128)(2,1)S(1)}, bf16[4,256,128]{2,1,0:T(8,128)(2,1)S(1)}, u32[]{:S(2)}, u32[]{:S(2)}) collective-permute-start(bf16[4,256,128]{2,1,0:T(8,128)(2,1)S(1)} %pad_maximum_fusion.1.refs_0_), channel_id=1, source_target_pairs={{0,32},{32,0},{1,33},{33,1},{2,34},{34,2},{3,35},{35,3},{4,36},{36... | collective-permute-start | bytes 786440 | tf_op jit(solution)/shard_map/ppermute | solution.py:43
  19.9 2.4 %collective-permute-start.9 = (bf16[4,256,128]{2,1,0:T(8,128)(2,1)S(1)}, bf16[4,256,128]{2,1,0:T(8,128)(2,1)S(1)}, u32[]{:S(2)}, u32[]{:S(2)}) collective-permute-start(bf16[4,256,128]{2,1,0:T(8,128)(2,1)S(1)} %collective-permute-done.5.refs_3_), channel_id=1, source_target_pairs={{0,32},{32,0},{1,33},{33,1},{2,34},{34,2},{3,35},{35,3},{4,36},{36... | collective-permute-start | bytes 786440 | tf_op jit(solution)/shard_map/ppermute | solution.py:43
  21.1 1.5 %collective-permute-start.8 = (bf16[4,256,128]{2,1,0:T(8,128)(2,1)S(1)}, bf16[4,256,128]{2,1,0:T(8,128)(2,1)S(1)}, u32[]{:S(2)}, u32[]{:S(2)}) collective-permute-start(bf16[4,256,128]{2,1,0:T(8,128)(2,1)S(1)} %collective-permute-done.4.refs_2_), channel_id=1, source_target_pairs={{0,32},{32,0},{1,33},{33,1},{2,34},{34,2},{3,35},{35,3},{4,36},{36... | collective-permute-start | bytes 786440 | tf_op jit(solution)/shard_map/ppermute | solution.py:43
  21.4 1.6 %collective-permute-start.7 = (bf16[4,256,128]{2,1,0:T(8,128)(2,1)S(1)}, bf16[4,256,128]{2,1,0:T(8,128)(2,1)S(1)}, u32[]{:S(2)}, u32[]{:S(2)}) collective-permute-start(bf16[4,256,128]{2,1,0:T(8,128)(2,1)S(1)} %collective-permute-done.3.refs_1_), channel_id=1, source_target_pairs={{0,32},{32,0},{1,33},{33,1},{2,34},{34,2},{3,35},{35,3},{4,36},{36... | collective-permute-start | bytes 786440 | tf_op jit(solution)/shard_map/ppermute | solution.py:43

commit v12 on v11

--- a/solution.py
+++ b/solution.py
@@ -127,9 +127,9 @@
 
 
 def score_kernel(info_ref, *refs):
-    rows, pieces, out_ref = refs[:8], refs[8:12], refs[12]
-    p_ref, m_ref, s_ref, unit_ref = refs[13:]
-    z, yhi, core, x = (info_ref[i] for i in range(4))
+    rows, pieces, outs = refs[:8], refs[8:12], refs[12:20]
+    p_ref, m_ref, s_ref, unit_ref = refs[20:]
+    core, x = info_ref[2], info_ref[3]
 
     groups, places = [], []
     for k in range(4):
@@ -178,17 +178,16 @@
     r = pl.run_scoped(add_up, pltpu.ACC(0)((32, 256), jnp.float32))
     for g in range(8):
         c = r[:, 32 * g : 32 * g + 32]
-        place = lax.bitwise_xor(z * 2 + yhi, g)
-        out_ref[place] = jnp.concatenate([c[0:8], c[8:16], c[16:24], c[24:32]], axis=1)
+        outs[g][...] = jnp.concatenate([c[0:8], c[8:16], c[16:24], c[24:32]], axis=1)
 
 
 def score(info, rows, pieces):
     return pl.pallas_call(
         score_kernel,
-        out_shape=jax.ShapeDtypeStruct((8, 8, 128), jnp.float32),
+        out_shape=[jax.ShapeDtypeStruct((8, 128), jnp.float32)] * 8,
         in_specs=[pl.BlockSpec(memory_space=pltpu.SMEM)]
         + [pl.BlockSpec(memory_space=pltpu.VMEM)] * 12,
-        out_specs=pl.BlockSpec(memory_space=pltpu.VMEM),
+        out_specs=[pl.BlockSpec(memory_space=pltpu.VMEM)] * 8,
         scratch_shapes=[
             pltpu.VMEM((4096, 128), jnp.bfloat16),
             pltpu.VMEM((8, 33, 8, 128), jnp.float32),
@@ -199,20 +198,29 @@
     )(info, *rows, *pieces)
 
 
-def place_kernel(r_ref, o_ref):
+def place_kernel(info_ref, *refs):
+    parts, o_ref, held_ref = refs[:8], refs[8], refs[9]
+    for g in range(8):
+        held_ref[lax.bitwise_xor(info_ref[0] * 2 + info_ref[1], g)] = parts[g][...]
     for g in range(4):
         o_ref[8 * g : 8 * g + 8, :] = jnp.concatenate(
-            [r_ref[s][:, 32 * g : 32 * g + 32] for s in range(8)], axis=1
+            [held_ref[s][:, 32 * g : 32 * g + 32] for s in range(8)], axis=1
         )
 
 
-def place(received):
+def place(info, parts):
     return pl.pallas_call(
         place_kernel,
         out_shape=jax.ShapeDtypeStruct((32, 256), jnp.float32),
-        in_specs=[pl.BlockSpec(memory_space=pltpu.VMEM)],
+        in_specs=[pl.BlockSpec(memory_space=pltpu.SMEM)]
+        + [pl.BlockSpec(memory_space=pltpu.VMEM)] * 8,
         out_specs=pl.BlockSpec(memory_space=pltpu.VMEM),
-    )(received)
+        scratch_shapes=[pltpu.VMEM((8, 8, 128), jnp.float32)],
+    )(info, *parts)
+
+
+def home(v, g):
+    return lax.ppermute(v, ("z", "yhi"), [(i, i ^ g) for i in range(8)])
 
 
 def per_device(queries, passages, lengths):
@@ -227,8 +235,7 @@
     mine = [block] + [lax.ppermute(block, PLANE, along(False, k)) for k in range(1, 4)]
     other = [to_core(v) for v in mine]
     terms = score(info, mine + other, moved)
-    received = lax.all_to_all(terms, ("z", "yhi"), 0, 0, tiled=True)
-    return place(received)
+    return place(info, [terms[0]] + [home(terms[g], g) for g in range(1, 8)])
 
 
 def solution(mesh):

time: 55.3 us -> 61.8 us (1.12)
  blocking collectives: 16 us -> 0 us
  starting transfers between devices: 14.8 us -> 30 us
  waiting for transfers between devices: 6.82 us -> 12.3 us
  Pallas kernels: 15.9 us -> 17.2 us
    all_to_all x1 -> x0, blocking collectives: 16 us -> none  [per_device(): received = lax.all_to_all(terms, ('z', 'yhi'), 0, 0, tiled=True)]
    ppermute x0 -> x7, starting transfers between devices: none -> 15.1 us  [home(): return lax.ppermute(v, ('z', 'yhi'), [(i, i ^ g) for i in range(8)])]
    ppermute x0 -> x7, waiting for transfers between devices: none -> 5.44 us  [home(): return lax.ppermute(v, ('z', 'yhi'), [(i, i ^ g) for i in range(8)])]
    pallas_call x1, Pallas kernels: 14.5 us -> 15.7 us  [score(): pl.pallas_call(score_kernel, out_shape=[jax.ShapeDtypeStruct((8, 128), jn...]
    unnamed x6 -> x24, local copies, waits for them, and re-layouts: 0.66 us -> 1.24 us
  transfers between devices with their start and end apart: 13 -> 20, of which waited for: 8 -> 10; matrix products, arithmetic and copies ran while one was open for 1% -> 1% of each run, Pallas kernels for 0% -> 0%
where the time goes in v12:
time: 61.8 us; the launch traced here: 61.5 us
  starting transfers between devices  30 us (49%)
  Pallas kernels  17.2 us (28%)
  waiting for transfers between devices  12.3 us (20%)
  local copies, waits for them, and re-layouts  1.61 us (3%)
    pallas_call x1, Pallas kernels, score(): pl.pallas_call(score_kernel, out_shape=[jax.ShapeDtypeStruct((8, 128), jn...  15.7 us
    ppermute x7, starting transfers between devices, home(): return lax.ppermute(v, ('z', 'yhi'), [(i, i ^ g) for i in range(8)])  15.1 us
    ppermute x7, waiting for transfers between devices, home(): return lax.ppermute(v, ('z', 'yhi'), [(i, i ^ g) for i in range(8)])  5.44 us
    ppermute x3, starting transfers between devices, on_x(): return lax.ppermute(v, ('core', 'x'), pairs)  5.42 us
    ppermute x3, starting transfers between devices, per_device(): lax.ppermute(block, PLANE, along(False, k))  5.07 us
    ppermute x3, waiting for transfers between devices, per_device(): lax.ppermute(block, PLANE, along(False, k))  4.42 us
    ppermute x3, starting transfers between devices, per_device(): lax.ppermute(own, PLANE, along(True, k))  4.09 us
    pallas_call x1, Pallas kernels, place(): pl.pallas_call(place_kernel, out_shape=jax.ShapeDtypeStruct((32, 256), jn...  1.53 us
  transfers between devices with their start and end apart: 20, of which 10 were waited for; matrix products, arithmetic and copies ran while one was open for 1% of the time, Pallas kernels for 0%

profile of v12, /device:TPU:0, one launch (start us, length us, event | category | flops | bytes accessed | tf_op | source)
XLA Modules:
  0.0 61.5 jit_solution(10313874329799229653)
XLA Ops:
  0.0 0.0 copy-start.2
  0.0 3.1 %collective-permute-start.2 = (bf16[256,128]{1,0:T(8,128)(2,1)}, bf16[256,128]{1,0:T(8,128)(2,1)S(1)}, u32[]{:S(2)}, u32[]{:S(2)}) collective-permute-start(bf16[256,128]{1,0:T(8,128)(2,1)} %bitcast.11), channel_id=1, source_target_pairs={{0,68},{4,64},{8,76},{12,72},{16,84},{20,80},{24,92},{28,88},{32,5... | collective-permute-start | bytes 196616 | tf_op jit(solution)/shard_map/ppermute | solution.py:230
  3.1 0.6 %collective-permute-start.1 = (bf16[256,128]{1,0:T(8,128)(2,1)}, bf16[256,128]{1,0:T(8,128)(2,1)S(1)}, u32[]{:S(2)}, u32[]{:S(2)}) collective-permute-start(bf16[256,128]{1,0:T(8,128)(2,1)} %bitcast.12), channel_id=1, source_target_pairs={{0,4},{4,0},{8,12},{12,8},{16,20},{20,16},{24,28},{28,24},{32,48},... | collective-permute-start | bytes 196616 | tf_op jit(solution)/shard_map/ppermute | solution.py:230
  3.7 0.4 collective-permute-start
  4.1 0.0 copy-start.11
  4.1 0.0 slice-start
  4.1 0.6 %copy-done.11 = s32[8]{0:T(128)S(1)} copy-done((s32[8]{0:T(128)S(1)}, s32[8]{0:T(128)}, u32[]{:S(2)}) %copy-start.11) | copy-done | bytes 56
  4.8 0.0 copy-done.2
  4.8 0.1 slice-done
  4.8 0.3 slice-done.1
  5.1 0.2 fusion
  5.3 0.0 copy-start.3
  5.3 2.9 %collective-permute-start.11 = (bf16[1040,128]{1,0:T(8,128)(2,1)S(1)}, bf16[1040,128]{1,0:T(8,128)(2,1)S(1)}, u32[]{:S(2)}, u32[]{:S(2)}) collective-permute-start(bf16[1040,128]{1,0:T(8,128)(2,1)S(1)} %pad_maximum_fusion.refs_8_), channel_id=1, source_target_pairs={{0,3},{1,2},{2,1},{3,0},{32,33},{33,32},{34,35},{35,34},{4,7},{5,6... | collective-permute-start | bytes 798728 | tf_op jit(solution)/shard_map/ppermute | solution.py:52
  8.3 0.2 collective-permute-start.10
  8.5 0.0 collective-permute-done.2
  8.5 0.6 collective-permute-done.1
  9.1 0.0 collective-permute-done
  9.1 0.0 copy-done.3
  9.1 4.1 %collective-permute-start.5 = (bf16[4,256,128]{2,1,0:T(8,128)(2,1)S(1)}, bf16[4,256,128]{2,1,0:T(8,128)(2,1)S(1)}, u32[]{:S(2)}, u32[]{:S(2)}) collective-permute-start(bf16[4,256,128]{2,1,0:T(8,128)(2,1)S(1)} %pad_maximum_fusion.1.refs_0_), channel_id=1, source_target_pairs={{0,24},{4,28},{8,16},{12,20},{16,8},{20,12},{24,0},{28,4},{32,100}... | collective-permute-start | bytes 786440 | tf_op jit(solution)/shard_map/ppermute | solution.py:235
  13.2 0.0 collective-permute-start.4
  13.2 0.9 %collective-permute-start.3 = (bf16[4,256,128]{2,1,0:T(8,128)(2,1)S(1)}, bf16[4,256,128]{2,1,0:T(8,128)(2,1)S(1)}, u32[]{:S(2)}, u32[]{:S(2)}) collective-permute-start(bf16[4,256,128]{2,1,0:T(8,128)(2,1)S(1)} %pad_maximum_fusion.1.refs_0_), channel_id=1, source_target_pairs={{0,8},{4,12},{8,0},{12,4},{16,24},{20,28},{24,16},{28,20},{32,96},... | collective-permute-start | bytes 786440 | tf_op jit(solution)/shard_map/ppermute | solution.py:235
  14.2 0.5 collective-permute-done.10.refs_9_
  14.7 2.3 %collective-permute-start.12 = (bf16[1040,128]{1,0:T(8,128)(2,1)S(1)}, bf16[1040,128]{1,0:T(8,128)(2,1)S(1)}, u32[]{:S(2)}, u32[]{:S(2)}) collective-permute-start(bf16[1040,128]{1,0:T(8,128)(2,1)S(1)} %collective-permute-done.10.refs_9_), channel_id=1, source_target_pairs={{0,3},{1,2},{2,1},{3,0},{32,33},{33,32},{34,35},{35,34},{4,7},{5,6... | collective-permute-start | bytes 798728 | tf_op jit(solution)/shard_map/ppermute | solution.py:52
  17.0 0.0 collective-permute-done.11.refs_10_
  17.0 0.0 collective-permute-start.6
  17.0 3.0 %collective-permute-done.5.refs_3_ = bf16[4,256,128]{2,1,0:T(8,128)(2,1)S(1)} collective-permute-done((bf16[4,256,128]{2,1,0:T(8,128)(2,1)S(1)}, bf16[4,256,128]{2,1,0:T(8,128)(2,1)S(1)}, u32[]{:S(2)}, u32[]{:S(2)}) %collective-permute-start.5) | collective-permute-done | bytes 262176 | tf_op jit(solution)/shard_map/ppermute | solution.py:235
  19.9 0.0 collective-permute-start.9
  19.9 1.2 %collective-permute-done.4.refs_2_ = bf16[4,256,128]{2,1,0:T(8,128)(2,1)S(1)} collective-permute-done((bf16[4,256,128]{2,1,0:T(8,128)(2,1)S(1)}, bf16[4,256,128]{2,1,0:T(8,128)(2,1)S(1)}, u32[]{:S(2)}, u32[]{:S(2)}) %collective-permute-start.4) | collective-permute-done | bytes 262176 | tf_op jit(solution)/shard_map/ppermute | solution.py:235
  21.1 0.0 collective-permute-start.8
  21.1 0.3 collective-permute-done.3.refs_1_
  21.4 0.2 collective-permute-start.7
  21.6 0.1 pad_add_fusion.info_ref
  21.7 0.0 collective-permute-done.6.refs_4_
  21.7 0.6 collective-permute-done.12.refs_11_
  22.3 0.0 collective-permute-done.9.refs_7_
  22.3 0.3 collective-permute-done.8.refs_6_
  22.7 0.4 collective-permute-done.7.refs_5_
  23.0 15.7 %shard_map.37 = (f32[8,128]{1,0:T(8,128)S(1)}, f32[8,128]{1,0:T(8,128)S(1)}, f32[8,128]{1,0:T(8,128)S(1)}, f32[8,128]{1,0:T(8,128)S(1)}, f32[8,128]{1,0:T(8,128)...) custom-call(s32[4]{0:T(128)S(1)} %pad_add_fusion.info_ref, ...), custom_call_target="tpu_custom_call" | custom-call | tf_op jit(solution)/shard_map/pallas_call | solution.py:185
  38.7 0.0 copy-done
  38.8 0.0 copy-start.1
  38.8 2.7 %collective-permute-start.13 = (f32[8,128]{1,0:T(8,128)S(1)}, f32[8,128]{1,0:T(8,128)S(1)}, u32[]{:S(2)}, u32[]{:S(2)}) collective-permute-start(f32[8,128]{1,0:T(8,128)S(1)} %get-tuple-element.14), channel_id=1, source_target_pairs={{0,4},{4,0},{8,12},{12,8},{16,20},{20,16},{24,28},{28,24},{1,5},{5... | collective-permute-start | bytes 12296 | tf_op jit(solution)/shard_map/ppermute | solution.py:223
  41.4 0.6 collective-permute-start.14
  42.0 1.8 %collective-permute-start.15 = (f32[8,128]{1,0:T(8,128)S(1)}, f32[8,128]{1,0:T(8,128)S(1)}, u32[]{:S(2)}, u32[]{:S(2)}) collective-permute-start(f32[8,128]{1,0:T(8,128)S(1)} %get-tuple-element.16), channel_id=1, source_target_pairs={{0,12},{4,8},{8,4},{12,0},{16,28},{20,24},{24,20},{28,16},{1,13},{... | collective-permute-start | bytes 12296 | tf_op jit(solution)/shard_map/ppermute | solution.py:223
  43.8 4.4 %collective-permute-start.16 = (f32[8,128]{1,0:T(8,128)S(1)}, f32[8,128]{1,0:T(8,128)S(1)}, u32[]{:S(2)}, u32[]{:S(2)}) collective-permute-start(f32[8,128]{1,0:T(8,128)S(1)} %get-tuple-element.17), channel_id=1, source_target_pairs={{0,16},{4,20},{8,24},{12,28},{16,0},{20,4},{24,8},{28,12},{1,17},{... | collective-permute-start | bytes 12296 | tf_op jit(solution)/shard_map/ppermute | solution.py:223
  48.3 0.0 copy-done.1
  48.3 1.4 %collective-permute-start.17 = (f32[8,128]{1,0:T(8,128)S(1)}, f32[8,128]{1,0:T(8,128)S(1)}, u32[]{:S(2)}, u32[]{:S(2)}) collective-permute-start(f32[8,128]{1,0:T(8,128)S(1)} %get-tuple-element.18), channel_id=1, source_target_pairs={{0,20},{4,16},{8,28},{12,24},{16,4},{20,0},{24,12},{28,8},{1,21},{... | collective-permute-start | bytes 12296 | tf_op jit(solution)/shard_map/ppermute | solution.py:223
  49.6 0.0 collective-permute-done.13.refs_1_
  49.6 2.5 %collective-permute-start.18 = (f32[8,128]{1,0:T(8,128)S(1)}, f32[8,128]{1,0:T(8,128)S(1)}, u32[]{:S(2)}, u32[]{:S(2)}) collective-permute-start(f32[8,128]{1,0:T(8,128)S(1)} %get-tuple-element.19), channel_id=1, source_target_pairs={{0,24},{4,28},{8,16},{12,20},{16,8},{20,12},{24,0},{28,4},{1,25},{... | collective-permute-start | bytes 12296 | tf_op jit(solution)/shard_map/ppermute | solution.py:223
  52.2 0.0 collective-permute-done.14.refs_2_
  52.2 1.8 %collective-permute-start.19 = (f32[8,128]{1,0:T(8,128)S(1)}, f32[8,128]{1,0:T(8,128)S(1)}, u32[]{:S(2)}, u32[]{:S(2)}) collective-permute-start(f32[8,128]{1,0:T(8,128)S(1)} %get-tuple-element.20), channel_id=1, source_target_pairs={{0,28},{4,24},{8,20},{12,16},{16,12},{20,8},{24,4},{28,0},{1,29},{... | collective-permute-start | bytes 12296 | tf_op jit(solution)/shard_map/ppermute | solution.py:223
  53.9 0.0 collective-permute-done.15.refs_3_
  53.9 0.0 collective-permute-done.16.refs_4_
  53.9 0.0 copy-start.7
  54.0 1.9 %collective-permute-done.17.refs_5_ = f32[8,128]{1,0:T(8,128)S(1)} collective-permute-done((f32[8,128]{1,0:T(8,128)S(1)}, f32[8,128]{1,0:T(8,128)S(1)}, u32[]{:S(2)}, u32[]{:S(2)}) %collective-permute-start.17) | collective-permute-done | bytes 4128 | tf_op jit(solution)/shard_map/ppermute | solution.py:223
  55.8 0.0 collective-permute-done.18.refs_6_
  55.8 3.6 %collective-permute-done.19.refs_7_ = f32[8,128]{1,0:T(8,128)S(1)} collective-permute-done((f32[8,128]{1,0:T(8,128)S(1)}, f32[8,128]{1,0:T(8,128)S(1)}, u32[]{:S(2)}, u32[]{:S(2)}) %collective-permute-start.19) | collective-permute-done | bytes 4128 | tf_op jit(solution)/shard_map/ppermute | solution.py:223
  59.4 0.0 copy-done.4
  59.4 0.0 copy-done.5
  59.4 0.0 copy-done.6
  59.4 0.0 copy-done.7
  59.4 0.0 copy-done.8
  59.4 0.0 copy-done.9
  59.4 0.5 copy-done.10
  60.0 1.5 %shard_map.38 = f32[32,256]{1,0:T(8,128)} custom-call(s32[4]{0:T(128)} %copy-done, f32[8,128]{1,0:T(8,128)} %copy-done.1, f32[8,128]{1,0:T(8,128)} %copy-done.4, f32[8,128]{1,0:T(8,128)} %copy-done.5, f32[8,128]{1,0:T(8,128)} %copy-done.6, f32[8,128]{1,0:T(8,128)} %copy-done.7, f32[8,128]{1,0:T(8,128)} %copy-done.8, f32[8,128]{1,0:T(8,128)} %copy-done.9, ...), custom_call_target="tpu_custom_call" | custom-call | tf_op jit(solution)/shard_map/pallas_call | solution.py:212
  (13 shorter events, 0.1 us)
Async XLA Ops:
  0.0 4.8 %copy-start.2 = (bf16[8,128,128]{2,1,0:T(8,128)(2,1)S(1)}, bf16[8,128,128]{2,1,0:T(8,128)(2,1)}, u32[]{:S(2)}) copy-start(bf16[8,128,128]{2,1,0:T(8,128)(2,1)} %param.4) | copy-start | bytes 786436
  0.0 8.5 %collective-permute-start.2 = (bf16[256,128]{1,0:T(8,128)(2,1)}, bf16[256,128]{1,0:T(8,128)(2,1)S(1)}, u32[]{:S(2)}, u32[]{:S(2)}) collective-permute-start(bf16[256,128]{1,0:T(8,128)(2,1)} %bitcast.11), channel_id=1, source_target_pairs={{0,68},{4,64},{8,76},{12,72},{16,84},{20,80},{24,92},{28,88},{32,5... | collective-permute-start | bytes 196616 | tf_op jit(solution)/shard_map/ppermute | solution.py:230
  3.1 6.0 %collective-permute-start.1 = (bf16[256,128]{1,0:T(8,128)(2,1)}, bf16[256,128]{1,0:T(8,128)(2,1)S(1)}, u32[]{:S(2)}, u32[]{:S(2)}) collective-permute-start(bf16[256,128]{1,0:T(8,128)(2,1)} %bitcast.12), channel_id=1, source_target_pairs={{0,4},{4,0},{8,12},{12,8},{16,20},{20,16},{24,28},{28,24},{32,48},... | collective-permute-start | bytes 196616 | tf_op jit(solution)/shard_map/ppermute | solution.py:230
  3.7 5.4 %collective-permute-start = (bf16[256,128]{1,0:T(8,128)(2,1)}, bf16[256,128]{1,0:T(8,128)(2,1)S(1)}, u32[]{:S(2)}, u32[]{:S(2)}) collective-permute-start(bf16[256,128]{1,0:T(8,128)(2,1)} %bitcast.13), channel_id=1, source_target_pairs={{0,64},{4,68},{8,72},{12,76},{16,80},{20,84},{24,88},{28,92},{32,4... | collective-permute-start | bytes 196616 | tf_op jit(solution)/shard_map/ppermute | solution.py:230
  4.1 0.7 %copy-start.11 = (s32[8]{0:T(128)S(1)}, s32[8]{0:T(128)}, u32[]{:S(2)}) copy-start(s32[8]{0:T(128)} %param.5) | copy-start | bytes 100
  4.1 0.7 %slice-start = ((bf16[8,128,128]{2,1,0:T(8,128)(2,1)}), bf16[8,8,128]{2,1,0:T(8,128)(2,1)S(1)}, s32[]{:S(2)}) async-start(bf16[8,128,128]{2,1,0:T(8,128)(2,1)} %param.4), calls=%async_computation | async-start | bytes 32768 | tf_op jit(solution)/shard_map/slice | solution.py:58
  4.1 1.0 %slice-start.1 = ((bf16[8,128,128]{2,1,0:T(8,128)(2,1)}), bf16[8,120,128]{2,1,0:T(8,128)(2,1)S(1)}, s32[]{:S(2)}) async-start(bf16[8,128,128]{2,1,0:T(8,128)(2,1)} %param.4), calls=%async_computation.1 | async-start | bytes 491520 | tf_op jit(solution)/shard_map/slice | solution.py:58
  5.3 3.8 %copy-start.3 = (bf16[32,8,128]{2,1,0:T(8,128)(2,1)S(1)}, bf16[32,8,128]{2,1,0:T(8,128)(2,1)}, u32[]{:S(2)}) copy-start(bf16[32,8,128]{2,1,0:T(8,128)(2,1)} %param.3) | copy-start | bytes 196612
  5.3 11.6 %collective-permute-start.11 = (bf16[1040,128]{1,0:T(8,128)(2,1)S(1)}, bf16[1040,128]{1,0:T(8,128)(2,1)S(1)}, u32[]{:S(2)}, u32[]{:S(2)}) collective-permute-start(bf16[1040,128]{1,0:T(8,128)(2,1)S(1)} %pad_maximum_fusion.refs_8_), channel_id=1, source_target_pairs={{0,3},{1,2},{2,1},{3,0},{32,33},{33,32},{34,35},{35,34},{4,7},{5,6... | collective-permute-start | bytes 798728 | tf_op jit(solution)/shard_map/ppermute | solution.py:52
  8.3 6.4 %collective-permute-start.10 = (bf16[1040,128]{1,0:T(8,128)(2,1)S(1)}, bf16[1040,128]{1,0:T(8,128)(2,1)S(1)}, u32[]{:S(2)}, u32[]{:S(2)}) collective-permute-start(bf16[1040,128]{1,0:T(8,128)(2,1)S(1)} %pad_maximum_fusion.refs_8_), channel_id=1, source_target_pairs={{0,1},{1,0},{2,3},{3,2},{32,35},{33,34},{34,33},{35,32},{4,5},{5,4... | collective-permute-start | bytes 798728 | tf_op jit(solution)/shard_map/ppermute | solution.py:52
  9.1 10.8 %collective-permute-start.5 = (bf16[4,256,128]{2,1,0:T(8,128)(2,1)S(1)}, bf16[4,256,128]{2,1,0:T(8,128)(2,1)S(1)}, u32[]{:S(2)}, u32[]{:S(2)}) collective-permute-start(bf16[4,256,128]{2,1,0:T(8,128)(2,1)S(1)} %pad_maximum_fusion.1.refs_0_), channel_id=1, source_target_pairs={{0,24},{4,28},{8,16},{12,20},{16,8},{20,12},{24,0},{28,4},{32,100}... | collective-permute-start | bytes 786440 | tf_op jit(solution)/shard_map/ppermute | solution.py:235
  13.2 7.9 %collective-permute-start.4 = (bf16[4,256,128]{2,1,0:T(8,128)(2,1)S(1)}, bf16[4,256,128]{2,1,0:T(8,128)(2,1)S(1)}, u32[]{:S(2)}, u32[]{:S(2)}) collective-permute-start(bf16[4,256,128]{2,1,0:T(8,128)(2,1)S(1)} %pad_maximum_fusion.1.refs_0_), channel_id=1, source_target_pairs={{0,16},{4,20},{8,24},{12,28},{16,0},{20,4},{24,8},{28,12},{32,36},... | collective-permute-start | bytes 786440 | tf_op jit(solution)/shard_map/ppermute | solution.py:235
  13.2 8.1 %collective-permute-start.3 = (bf16[4,256,128]{2,1,0:T(8,128)(2,1)S(1)}, bf16[4,256,128]{2,1,0:T(8,128)(2,1)S(1)}, u32[]{:S(2)}, u32[]{:S(2)}) collective-permute-start(bf16[4,256,128]{2,1,0:T(8,128)(2,1)S(1)} %pad_maximum_fusion.1.refs_0_), channel_id=1, source_target_pairs={{0,8},{4,12},{8,0},{12,4},{16,24},{20,28},{24,16},{28,20},{32,96},... | collective-permute-start | bytes 786440 | tf_op jit(solution)/shard_map/ppermute | solution.py:235
  14.7 7.6 %collective-permute-start.12 = (bf16[1040,128]{1,0:T(8,128)(2,1)S(1)}, bf16[1040,128]{1,0:T(8,128)(2,1)S(1)}, u32[]{:S(2)}, u32[]{:S(2)}) collective-permute-start(bf16[1040,128]{1,0:T(8,128)(2,1)S(1)} %collective-permute-done.10.refs_9_), channel_id=1, source_target_pairs={{0,3},{1,2},{2,1},{3,0},{32,33},{33,32},{34,35},{35,34},{4,7},{5,6... | collective-permute-start | bytes 798728 | tf_op jit(solution)/shard_map/ppermute | solution.py:52
  17.0 4.8 %collective-permute-start.6 = (bf16[4,256,128]{2,1,0:T(8,128)(2,1)S(1)}, bf16[4,256,128]{2,1,0:T(8,128)(2,1)S(1)}, u32[]{:S(2)}, u32[]{:S(2)}) collective-permute-start(bf16[4,256,128]{2,1,0:T(8,128)(2,1)S(1)} %pad_maximum_fusion.1.refs_0_), channel_id=1, source_target_pairs={{0,32},{32,0},{1,33},{33,1},{2,34},{34,2},{3,35},{35,3},{4,36},{36... | collective-permute-start | bytes 786440 | tf_op jit(solution)/shard_map/ppermute | solution.py:43
  19.9 2.4 %collective-permute-start.9 = (bf16[4,256,128]{2,1,0:T(8,128)(2,1)S(1)}, bf16[4,256,128]{2,1,0:T(8,128)(2,1)S(1)}, u32[]{:S(2)}, u32[]{:S(2)}) collective-permute-start(bf16[4,256,128]{2,1,0:T(8,128)(2,1)S(1)} %collective-permute-done.5.refs_3_), channel_id=1, source_target_pairs={{0,32},{32,0},{1,33},{33,1},{2,34},{34,2},{3,35},{35,3},{4,36},{36... | collective-permute-start | bytes 786440 | tf_op jit(solution)/shard_map/ppermute | solution.py:43
  21.1 1.5 %collective-permute-start.8 = (bf16[4,256,128]{2,1,0:T(8,128)(2,1)S(1)}, bf16[4,256,128]{2,1,0:T(8,128)(2,1)S(1)}, u32[]{:S(2)}, u32[]{:S(2)}) collective-permute-start(bf16[4,256,128]{2,1,0:T(8,128)(2,1)S(1)} %collective-permute-done.4.refs_2_), channel_id=1, source_target_pairs={{0,32},{32,0},{1,33},{33,1},{2,34},{34,2},{3,35},{35,3},{4,36},{36... | collective-permute-start | bytes 786440 | tf_op jit(solution)/shard_map/ppermute | solution.py:43
  21.4 1.6 %collective-permute-start.7 = (bf16[4,256,128]{2,1,0:T(8,128)(2,1)S(1)}, bf16[4,256,128]{2,1,0:T(8,128)(2,1)S(1)}, u32[]{:S(2)}, u32[]{:S(2)}) collective-permute-start(bf16[4,256,128]{2,1,0:T(8,128)(2,1)S(1)} %collective-permute-done.3.refs_1_), channel_id=1, source_target_pairs={{0,32},{32,0},{1,33},{33,1},{2,34},{34,2},{3,35},{35,3},{4,36},{36... | collective-permute-start | bytes 786440 | tf_op jit(solution)/shard_map/ppermute | solution.py:43
  21.7 17.0 %copy-start = (s32[4]{0:T(128)}, s32[4]{0:T(128)S(1)}, u32[]{:S(2)}) copy-start(s32[4]{0:T(128)S(1)} %pad_add_fusion.info_ref) | copy-start | bytes 52
  38.8 9.5 %copy-start.1 = (f32[8,128]{1,0:T(8,128)}, f32[8,128]{1,0:T(8,128)S(1)}, u32[]{:S(2)}) copy-start(f32[8,128]{1,0:T(8,128)S(1)} %get-tuple-element.13.refs_0_) | copy-start | bytes 12292
  38.8 10.9 %collective-permute-start.13 = (f32[8,128]{1,0:T(8,128)S(1)}, f32[8,128]{1,0:T(8,128)S(1)}, u32[]{:S(2)}, u32[]{:S(2)}) collective-permute-start(f32[8,128]{1,0:T(8,128)S(1)} %get-tuple-element.14), channel_id=1, source_target_pairs={{0,4},{4,0},{8,12},{12,8},{16,20},{20,16},{24,28},{28,24},{1,5},{5... | collective-permute-start | bytes 12296 | tf_op jit(solution)/shard_map/ppermute | solution.py:223
  41.4 10.7 %collective-permute-start.14 = (f32[8,128]{1,0:T(8,128)S(1)}, f32[8,128]{1,0:T(8,128)S(1)}, u32[]{:S(2)}, u32[]{:S(2)}) collective-permute-start(f32[8,128]{1,0:T(8,128)S(1)} %get-tuple-element.15), channel_id=1, source_target_pairs={{0,8},{4,12},{8,0},{12,4},{16,24},{20,28},{24,16},{28,20},{1,9},{5... | collective-permute-start | bytes 12296 | tf_op jit(solution)/shard_map/ppermute | solution.py:223
  42.0 11.9 %collective-permute-start.15 = (f32[8,128]{1,0:T(8,128)S(1)}, f32[8,128]{1,0:T(8,128)S(1)}, u32[]{:S(2)}, u32[]{:S(2)}) collective-permute-start(f32[8,128]{1,0:T(8,128)S(1)} %get-tuple-element.16), channel_id=1, source_target_pairs={{0,12},{4,8},{8,4},{12,0},{16,28},{20,24},{24,20},{28,16},{1,13},{... | collective-permute-start | bytes 12296 | tf_op jit(solution)/shard_map/ppermute | solution.py:223
  43.8 10.1 %collective-permute-start.16 = (f32[8,128]{1,0:T(8,128)S(1)}, f32[8,128]{1,0:T(8,128)S(1)}, u32[]{:S(2)}, u32[]{:S(2)}) collective-permute-start(f32[8,128]{1,0:T(8,128)S(1)} %get-tuple-element.17), channel_id=1, source_target_pairs={{0,16},{4,20},{8,24},{12,28},{16,0},{20,4},{24,8},{28,12},{1,17},{... | collective-permute-start | bytes 12296 | tf_op jit(solution)/shard_map/ppermute | solution.py:223
  48.3 7.5 %collective-permute-start.17 = (f32[8,128]{1,0:T(8,128)S(1)}, f32[8,128]{1,0:T(8,128)S(1)}, u32[]{:S(2)}, u32[]{:S(2)}) collective-permute-start(f32[8,128]{1,0:T(8,128)S(1)} %get-tuple-element.18), channel_id=1, source_target_pairs={{0,20},{4,16},{8,28},{12,24},{16,4},{20,0},{24,12},{28,8},{1,21},{... | collective-permute-start | bytes 12296 | tf_op jit(solution)/shard_map/ppermute | solution.py:223
  49.6 9.8 %copy-start.4 = (f32[8,128]{1,0:T(8,128)}, f32[8,128]{1,0:T(8,128)S(1)}, u32[]{:S(2)}) copy-start(f32[8,128]{1,0:T(8,128)S(1)} %collective-permute-done.13.refs_1_) | copy-start | bytes 12292
  49.6 6.2 %collective-permute-start.18 = (f32[8,128]{1,0:T(8,128)S(1)}, f32[8,128]{1,0:T(8,128)S(1)}, u32[]{:S(2)}, u32[]{:S(2)}) collective-permute-start(f32[8,128]{1,0:T(8,128)S(1)} %get-tuple-element.19), channel_id=1, source_target_pairs={{0,24},{4,28},{8,16},{12,20},{16,8},{20,12},{24,0},{28,4},{1,25},{... | collective-permute-start | bytes 12296 | tf_op jit(solution)/shard_map/ppermute | solution.py:223
  52.2 7.2 %copy-start.5 = (f32[8,128]{1,0:T(8,128)}, f32[8,128]{1,0:T(8,128)S(1)}, u32[]{:S(2)}) copy-start(f32[8,128]{1,0:T(8,128)S(1)} %collective-permute-done.14.refs_2_) | copy-start | bytes 12292
  52.2 7.2 %collective-permute-start.19 = (f32[8,128]{1,0:T(8,128)S(1)}, f32[8,128]{1,0:T(8,128)S(1)}, u32[]{:S(2)}, u32[]{:S(2)}) collective-permute-start(f32[8,128]{1,0:T(8,128)S(1)} %get-tuple-element.20), channel_id=1, source_target_pairs={{0,28},{4,24},{8,20},{12,16},{16,12},{20,8},{24,4},{28,0},{1,29},{... | collective-permute-start | bytes 12296 | tf_op jit(solution)/shard_map/ppermute | solution.py:223
  53.9 5.5 %copy-start.6 = (f32[8,128]{1,0:T(8,128)}, f32[8,128]{1,0:T(8,128)S(1)}, u32[]{:S(2)}) copy-start(f32[8,128]{1,0:T(8,128)S(1)} %collective-permute-done.15.refs_3_) | copy-start | bytes 12292
  53.9 5.5 %copy-start.7 = (f32[8,128]{1,0:T(8,128)}, f32[8,128]{1,0:T(8,128)S(1)}, u32[]{:S(2)}) copy-start(f32[8,128]{1,0:T(8,128)S(1)} %collective-permute-done.16.refs_4_) | copy-start | bytes 12292
  55.8 3.6 %copy-start.8 = (f32[8,128]{1,0:T(8,128)}, f32[8,128]{1,0:T(8,128)S(1)}, u32[]{:S(2)}) copy-start(f32[8,128]{1,0:T(8,128)S(1)} %collective-permute-done.17.refs_5_) | copy-start | bytes 12292
  55.8 3.6 %copy-start.9 = (f32[8,128]{1,0:T(8,128)}, f32[8,128]{1,0:T(8,128)S(1)}, u32[]{:S(2)}) copy-start(f32[8,128]{1,0:T(8,128)S(1)} %collective-permute-done.18.refs_6_) | copy-start | bytes 12292
  59.4 0.6 copy-start.10

commit v13 on v11

--- a/solution.py
+++ b/solution.py
@@ -222,7 +222,8 @@
     near = [own] + [lax.ppermute(own, PLANE, along(True, k)) for k in range(1, 4)]
     filled = with_lengths(passages, lengths)
     once = on_x(filled, 1, 3)
-    moved = [filled, once, on_x(filled, 3, 1), on_x(once, 3, 1)]
+    once, later = lax.optimization_barrier((once, filled))
+    moved = [filled, once, on_x(later, 3, 1), on_x(once, 3, 1)]
     block = jnp.stack(near)
     mine = [block] + [lax.ppermute(block, PLANE, along(False, k)) for k in range(1, 4)]
     other = [to_core(v) for v in mine]

time: 55.3 us -> 56.3 us (1.018)
  blocking collectives: 16 us -> 13.5 us
  waiting for transfers between devices: 6.82 us -> 9.01 us
  Pallas kernels: 15.9 us -> 17.2 us
    all_to_all x1, blocking collectives: 16 us -> 13.5 us  [per_device(): received = lax.all_to_all(terms, ('z', 'yhi'), 0, 0, tiled=True)]
    ppermute x3, waiting for transfers between devices: 1.09 us -> 2.97 us  [on_x(): return lax.ppermute(v, ('core', 'x'), pairs)]
    ppermute x3, waiting for transfers between devices: 0.59 us -> 2.08 us  [per_device(): lax.ppermute(own, PLANE, along(True, k))]
    pallas_call x1, Pallas kernels: 14.5 us -> 15.7 us  [score(): pl.pallas_call(score_kernel, out_shape=jax.ShapeDtypeStruct((8, 8, 128),...]
    ppermute x4, waiting for transfers between devices: 0.72 us -> 0.01 us  [to_core(): return lax.ppermute(v, 'core', [(0, 1), (1, 0)])]
  transfers between devices with their start and end apart: 13 -> 13, of which waited for: 8 -> 6; matrix products, arithmetic and copies ran while one was open for 1% -> 1% of each run, Pallas kernels for 0% -> 0%
where the time goes in v13:
time: 56.3 us; the launch traced here: 55.5 us
  Pallas kernels  17.2 us (31%)
  starting transfers between devices  14.4 us (26%)
  blocking collectives  13.5 us (24%)
  waiting for transfers between devices  9.01 us (16%)
  local copies, waits for them, and re-layouts  1.02 us (2%)
    pallas_call x1, Pallas kernels, score(): pl.pallas_call(score_kernel, out_shape=jax.ShapeDtypeStruct((8, 8, 128),...  15.7 us
    all_to_all x1, blocking collectives, per_device(): received = lax.all_to_all(terms, ('z', 'yhi'), 0, 0, tiled=True)  13.5 us
    ppermute x3, starting transfers between devices, per_device(): lax.ppermute(block, PLANE, along(False, k))  5.07 us
    ppermute x3, starting transfers between devices, on_x(): return lax.ppermute(v, ('core', 'x'), pairs)  4.89 us
    ppermute x3, starting transfers between devices, per_device(): lax.ppermute(own, PLANE, along(True, k))  4.09 us
    ppermute x3, waiting for transfers between devices, per_device(): lax.ppermute(block, PLANE, along(False, k))  3.95 us
    ppermute x3, waiting for transfers between devices, on_x(): return lax.ppermute(v, ('core', 'x'), pairs)  2.97 us
    ppermute x3, waiting for transfers between devices, per_device(): lax.ppermute(own, PLANE, along(True, k))  2.08 us
  transfers between devices with their start and end apart: 13, of which 6 were waited for; matrix products, arithmetic and copies ran while one was open for 1% of the time, Pallas kernels for 0%

profile of v13, /device:TPU:0, one launch (start us, length us, event | category | flops | bytes accessed | tf_op | source)
XLA Modules:
  0.0 55.5 jit_solution(4647715946364982973)
XLA Ops:
  0.0 0.0 copy-start
  0.0 3.1 %collective-permute-start.2 = (bf16[256,128]{1,0:T(8,128)(2,1)}, bf16[256,128]{1,0:T(8,128)(2,1)S(1)}, u32[]{:S(2)}, u32[]{:S(2)}) collective-permute-start(bf16[256,128]{1,0:T(8,128)(2,1)} %bitcast.11), channel_id=1, source_target_pairs={{0,68},{4,64},{8,76},{12,72},{16,84},{20,80},{24,92},{28,88},{32,5... | collective-permute-start | bytes 196616 | tf_op jit(solution)/shard_map/ppermute | solution.py:222
  3.1 0.6 %collective-permute-start.1 = (bf16[256,128]{1,0:T(8,128)(2,1)}, bf16[256,128]{1,0:T(8,128)(2,1)S(1)}, u32[]{:S(2)}, u32[]{:S(2)}) collective-permute-start(bf16[256,128]{1,0:T(8,128)(2,1)} %bitcast.12), channel_id=1, source_target_pairs={{0,4},{4,0},{8,12},{12,8},{16,20},{20,16},{24,28},{28,24},{32,48},... | collective-permute-start | bytes 196616 | tf_op jit(solution)/shard_map/ppermute | solution.py:222
  3.7 0.4 collective-permute-start
  4.1 0.0 copy-start.2
  4.1 0.0 slice-start
  4.1 0.0 slice-start.1
  4.1 0.6 %copy-done.2 = s32[8]{0:T(128)S(1)} copy-done((s32[8]{0:T(128)S(1)}, s32[8]{0:T(128)}, u32[]{:S(2)}) %copy-start.2) | copy-done | bytes 56
  4.8 0.0 copy-done
  4.8 0.1 slice-done
  4.8 0.3 slice-done.1
  5.1 0.2 fusion
  5.3 0.0 copy-start.1
  5.3 1.7 %collective-permute-start.10 = (bf16[1040,128]{1,0:T(8,128)(2,1)S(1)}, bf16[1040,128]{1,0:T(8,128)(2,1)S(1)}, u32[]{:S(2)}, u32[]{:S(2)}) collective-permute-start(bf16[1040,128]{1,0:T(8,128)(2,1)S(1)} %pad_maximum_fusion.refs_8_), channel_id=1, source_target_pairs={{0,1},{1,0},{2,3},{3,2},{32,35},{33,34},{34,33},{35,32},{4,5},{5,4... | collective-permute-start | bytes 798728 | tf_op jit(solution)/shard_map/ppermute | solution.py:52
  7.0 0.0 collective-permute-done.2
  7.0 2.1 %collective-permute-done.1 = bf16[256,128]{1,0:T(8,128)(2,1)S(1)} collective-permute-done((bf16[256,128]{1,0:T(8,128)(2,1)}, bf16[256,128]{1,0:T(8,128)(2,1)S(1)}, u32[]{:S(2)}, u32[]{:S(2)}) %collective-permute-start.1) | collective-permute-done | bytes 65568 | tf_op jit(solution)/shard_map/ppermute | solution.py:222
  9.1 0.0 collective-permute-done
  9.1 0.0 copy-done.1
  9.1 0.1 collective-permute-start.6
  9.2 4.1 %collective-permute-start.5 = (bf16[4,256,128]{2,1,0:T(8,128)(2,1)S(1)}, bf16[4,256,128]{2,1,0:T(8,128)(2,1)S(1)}, u32[]{:S(2)}, u32[]{:S(2)}) collective-permute-start(bf16[4,256,128]{2,1,0:T(8,128)(2,1)S(1)} %pad_maximum_fusion.1.refs_0_), channel_id=1, source_target_pairs={{0,24},{4,28},{8,16},{12,20},{16,8},{20,12},{24,0},{28,4},{32,100}... | collective-permute-start | bytes 786440 | tf_op jit(solution)/shard_map/ppermute | solution.py:228
  13.3 0.0 collective-permute-start.4
  13.3 0.9 %collective-permute-start.3 = (bf16[4,256,128]{2,1,0:T(8,128)(2,1)S(1)}, bf16[4,256,128]{2,1,0:T(8,128)(2,1)S(1)}, u32[]{:S(2)}, u32[]{:S(2)}) collective-permute-start(bf16[4,256,128]{2,1,0:T(8,128)(2,1)S(1)} %pad_maximum_fusion.1.refs_0_), channel_id=1, source_target_pairs={{0,8},{4,12},{8,0},{12,4},{16,24},{20,28},{24,16},{28,20},{32,96},... | collective-permute-start | bytes 786440 | tf_op jit(solution)/shard_map/ppermute | solution.py:228
  14.3 0.0 collective-permute-done.10.refs_9_
  14.3 2.8 %collective-permute-start.11 = (bf16[1040,128]{1,0:T(8,128)(2,1)S(1)}, bf16[1040,128]{1,0:T(8,128)(2,1)S(1)}, u32[]{:S(2)}, u32[]{:S(2)}) collective-permute-start(bf16[1040,128]{1,0:T(8,128)(2,1)S(1)} %pad_maximum_fusion.refs_8_), channel_id=1, source_target_pairs={{0,3},{1,2},{2,1},{3,0},{32,33},{33,32},{34,35},{35,34},{4,7},{5,6... | collective-permute-start | bytes 798728 | tf_op jit(solution)/shard_map/ppermute | solution.py:52
  17.1 0.0 collective-permute-done.6.refs_4_
  17.1 0.5 collective-permute-start.12
  17.5 2.5 %collective-permute-done.5.refs_3_ = bf16[4,256,128]{2,1,0:T(8,128)(2,1)S(1)} collective-permute-done((bf16[4,256,128]{2,1,0:T(8,128)(2,1)S(1)}, bf16[4,256,128]{2,1,0:T(8,128)(2,1)S(1)}, u32[]{:S(2)}, u32[]{:S(2)}) %collective-permute-start.5) | collective-permute-done | bytes 262176 | tf_op jit(solution)/shard_map/ppermute | solution.py:228
  20.0 0.0 collective-permute-start.9
  20.0 1.2 %collective-permute-done.4.refs_2_ = bf16[4,256,128]{2,1,0:T(8,128)(2,1)S(1)} collective-permute-done((bf16[4,256,128]{2,1,0:T(8,128)(2,1)S(1)}, bf16[4,256,128]{2,1,0:T(8,128)(2,1)S(1)}, u32[]{:S(2)}, u32[]{:S(2)}) %collective-permute-start.4) | collective-permute-done | bytes 262176 | tf_op jit(solution)/shard_map/ppermute | solution.py:228
  21.2 0.0 collective-permute-start.8
  21.2 0.3 collective-permute-done.3.refs_1_
  21.5 0.2 collective-permute-start.7
  21.7 0.1 pad_add_fusion.info_ref
  21.8 0.1 collective-permute-done.11.refs_10_
  21.9 2.9 %collective-permute-done.12.refs_11_ = bf16[1040,128]{1,0:T(8,128)(2,1)S(1)} collective-permute-done((bf16[1040,128]{1,0:T(8,128)(2,1)S(1)}, bf16[1040,128]{1,0:T(8,128)(2,1)S(1)}, u32[]{:S(2)}, u32[]{:S(2)}) %collective-permute-start.12) | collective-permute-done | bytes 266272 | tf_op jit(solution)/shard_map/ppermute | solution.py:52
  24.8 0.0 collective-permute-done.9.refs_7_
  24.8 0.0 collective-permute-done.8.refs_6_
  24.8 0.0 collective-permute-done.7.refs_5_
  24.8 15.7 %shard_map.37 = f32[8,8,128]{2,1,0:T(8,128)S(1)} custom-call(s32[4]{0:T(128)S(1)} %pad_add_fusion.info_ref, bf16[4,256,128]{2,1,0:T(8,128)(2,1)S(1)} %pad_maximum_fusion.1.refs_0_, bf16[4,256,128]{2,1,0:T(8,128)(2,1)S(1)} %collective-permute-done.3.refs_1_, bf16[4,256,128]{2,1,0:T(8,128)(2,1)S(1)} %collective-permute-done.4.refs_2_, ...), custom_call_target="tpu_custom_call" | custom-call | tf_op jit(solution)/shard_map/pallas_call | solution.py:186
  40.5 13.5 %all_to_all.5.r_ref = f32[8,8,128]{2,1,0:T(8,128)} all-to-all(f32[8,8,128]{2,1,0:T(8,128)S(1)} %shard_map.37), channel_id=1, replica_groups=mesh['ylo'=2,'core'=2,'z'=4,'yhi'=2,'x'=4] {'z','yhi'}, dimensions={0} | all-to-all | bytes 65536 | tf_op jit(solution)/shard_map/all_to_all | solution.py:231
  54.0 1.5 %shard_map.38 = f32[32,256]{1,0:T(8,128)} custom-call(f32[8,8,128]{2,1,0:T(8,128)} %all_to_all.5.r_ref), custom_call_target="tpu_custom_call" | custom-call | tf_op jit(solution)/shard_map/pallas_call | solution.py:210
  (5 shorter events, 0.1 us)
Async XLA Ops:
  0.0 4.8 %copy-start = (bf16[8,128,128]{2,1,0:T(8,128)(2,1)S(1)}, bf16[8,128,128]{2,1,0:T(8,128)(2,1)}, u32[]{:S(2)}) copy-start(bf16[8,128,128]{2,1,0:T(8,128)(2,1)} %param.4) | copy-start | bytes 786436
  0.0 7.0 %collective-permute-start.2 = (bf16[256,128]{1,0:T(8,128)(2,1)}, bf16[256,128]{1,0:T(8,128)(2,1)S(1)}, u32[]{:S(2)}, u32[]{:S(2)}) collective-permute-start(bf16[256,128]{1,0:T(8,128)(2,1)} %bitcast.11), channel_id=1, source_target_pairs={{0,68},{4,64},{8,76},{12,72},{16,84},{20,80},{24,92},{28,88},{32,5... | collective-permute-start | bytes 196616 | tf_op jit(solution)/shard_map/ppermute | solution.py:222
  3.1 6.0 %collective-permute-start.1 = (bf16[256,128]{1,0:T(8,128)(2,1)}, bf16[256,128]{1,0:T(8,128)(2,1)S(1)}, u32[]{:S(2)}, u32[]{:S(2)}) collective-permute-start(bf16[256,128]{1,0:T(8,128)(2,1)} %bitcast.12), channel_id=1, source_target_pairs={{0,4},{4,0},{8,12},{12,8},{16,20},{20,16},{24,28},{28,24},{32,48},... | collective-permute-start | bytes 196616 | tf_op jit(solution)/shard_map/ppermute | solution.py:222
  3.7 5.4 %collective-permute-start = (bf16[256,128]{1,0:T(8,128)(2,1)}, bf16[256,128]{1,0:T(8,128)(2,1)S(1)}, u32[]{:S(2)}, u32[]{:S(2)}) collective-permute-start(bf16[256,128]{1,0:T(8,128)(2,1)} %bitcast.13), channel_id=1, source_target_pairs={{0,64},{4,68},{8,72},{12,76},{16,80},{20,84},{24,88},{28,92},{32,4... | collective-permute-start | bytes 196616 | tf_op jit(solution)/shard_map/ppermute | solution.py:222
  4.1 0.7 %copy-start.2 = (s32[8]{0:T(128)S(1)}, s32[8]{0:T(128)}, u32[]{:S(2)}) copy-start(s32[8]{0:T(128)} %param.5) | copy-start | bytes 100
  4.1 0.7 %slice-start = ((bf16[8,128,128]{2,1,0:T(8,128)(2,1)}), bf16[8,8,128]{2,1,0:T(8,128)(2,1)S(1)}, s32[]{:S(2)}) async-start(bf16[8,128,128]{2,1,0:T(8,128)(2,1)} %param.4), calls=%async_computation.1 | async-start | bytes 32768 | tf_op jit(solution)/shard_map/slice | solution.py:58
  4.1 1.0 %slice-start.1 = ((bf16[8,128,128]{2,1,0:T(8,128)(2,1)}), bf16[8,120,128]{2,1,0:T(8,128)(2,1)S(1)}, s32[]{:S(2)}) async-start(bf16[8,128,128]{2,1,0:T(8,128)(2,1)} %param.4), calls=%async_computation.2 | async-start | bytes 491520 | tf_op jit(solution)/shard_map/slice | solution.py:58
  5.3 3.8 %copy-start.1 = (bf16[32,8,128]{2,1,0:T(8,128)(2,1)S(1)}, bf16[32,8,128]{2,1,0:T(8,128)(2,1)}, u32[]{:S(2)}) copy-start(bf16[32,8,128]{2,1,0:T(8,128)(2,1)} %param.3) | copy-start | bytes 196612
  5.3 8.9 %collective-permute-start.10 = (bf16[1040,128]{1,0:T(8,128)(2,1)S(1)}, bf16[1040,128]{1,0:T(8,128)(2,1)S(1)}, u32[]{:S(2)}, u32[]{:S(2)}) collective-permute-start(bf16[1040,128]{1,0:T(8,128)(2,1)S(1)} %pad_maximum_fusion.refs_8_), channel_id=1, source_target_pairs={{0,1},{1,0},{2,3},{3,2},{32,35},{33,34},{34,33},{35,32},{4,5},{5,4... | collective-permute-start | bytes 798728 | tf_op jit(solution)/shard_map/ppermute | solution.py:52
  9.1 7.9 %collective-permute-start.6 = (bf16[4,256,128]{2,1,0:T(8,128)(2,1)S(1)}, bf16[4,256,128]{2,1,0:T(8,128)(2,1)S(1)}, u32[]{:S(2)}, u32[]{:S(2)}) collective-permute-start(bf16[4,256,128]{2,1,0:T(8,128)(2,1)S(1)} %pad_maximum_fusion.1.refs_0_), channel_id=1, source_target_pairs={{0,32},{32,0},{1,33},{33,1},{2,34},{34,2},{3,35},{35,3},{4,36},{36... | collective-permute-start | bytes 786440 | tf_op jit(solution)/shard_map/ppermute | solution.py:43
  9.2 10.8 %collective-permute-start.5 = (bf16[4,256,128]{2,1,0:T(8,128)(2,1)S(1)}, bf16[4,256,128]{2,1,0:T(8,128)(2,1)S(1)}, u32[]{:S(2)}, u32[]{:S(2)}) collective-permute-start(bf16[4,256,128]{2,1,0:T(8,128)(2,1)S(1)} %pad_maximum_fusion.1.refs_0_), channel_id=1, source_target_pairs={{0,24},{4,28},{8,16},{12,20},{16,8},{20,12},{24,0},{28,4},{32,100}... | collective-permute-start | bytes 786440 | tf_op jit(solution)/shard_map/ppermute | solution.py:228
  13.3 7.9 %collective-permute-start.4 = (bf16[4,256,128]{2,1,0:T(8,128)(2,1)S(1)}, bf16[4,256,128]{2,1,0:T(8,128)(2,1)S(1)}, u32[]{:S(2)}, u32[]{:S(2)}) collective-permute-start(bf16[4,256,128]{2,1,0:T(8,128)(2,1)S(1)} %pad_maximum_fusion.1.refs_0_), channel_id=1, source_target_pairs={{0,16},{4,20},{8,24},{12,28},{16,0},{20,4},{24,8},{28,12},{32,36},... | collective-permute-start | bytes 786440 | tf_op jit(solution)/shard_map/ppermute | solution.py:228
  13.3 8.1 %collective-permute-start.3 = (bf16[4,256,128]{2,1,0:T(8,128)(2,1)S(1)}, bf16[4,256,128]{2,1,0:T(8,128)(2,1)S(1)}, u32[]{:S(2)}, u32[]{:S(2)}) collective-permute-start(bf16[4,256,128]{2,1,0:T(8,128)(2,1)S(1)} %pad_maximum_fusion.1.refs_0_), channel_id=1, source_target_pairs={{0,8},{4,12},{8,0},{12,4},{16,24},{20,28},{24,16},{28,20},{32,96},... | collective-permute-start | bytes 786440 | tf_op jit(solution)/shard_map/ppermute | solution.py:228
  14.3 7.6 %collective-permute-start.11 = (bf16[1040,128]{1,0:T(8,128)(2,1)S(1)}, bf16[1040,128]{1,0:T(8,128)(2,1)S(1)}, u32[]{:S(2)}, u32[]{:S(2)}) collective-permute-start(bf16[1040,128]{1,0:T(8,128)(2,1)S(1)} %pad_maximum_fusion.refs_8_), channel_id=1, source_target_pairs={{0,3},{1,2},{2,1},{3,0},{32,33},{33,32},{34,35},{35,34},{4,7},{5,6... | collective-permute-start | bytes 798728 | tf_op jit(solution)/shard_map/ppermute | solution.py:52
  17.1 7.7 %collective-permute-start.12 = (bf16[1040,128]{1,0:T(8,128)(2,1)S(1)}, bf16[1040,128]{1,0:T(8,128)(2,1)S(1)}, u32[]{:S(2)}, u32[]{:S(2)}) collective-permute-start(bf16[1040,128]{1,0:T(8,128)(2,1)S(1)} %collective-permute-done.10.refs_9_), channel_id=1, source_target_pairs={{0,3},{1,2},{2,1},{3,0},{32,33},{33,32},{34,35},{35,34},{4,7},{5,6... | collective-permute-start | bytes 798728 | tf_op jit(solution)/shard_map/ppermute | solution.py:52
  20.0 4.7 %collective-permute-start.9 = (bf16[4,256,128]{2,1,0:T(8,128)(2,1)S(1)}, bf16[4,256,128]{2,1,0:T(8,128)(2,1)S(1)}, u32[]{:S(2)}, u32[]{:S(2)}) collective-permute-start(bf16[4,256,128]{2,1,0:T(8,128)(2,1)S(1)} %collective-permute-done.5.refs_3_), channel_id=1, source_target_pairs={{0,32},{32,0},{1,33},{33,1},{2,34},{34,2},{3,35},{35,3},{4,36},{36... | collective-permute-start | bytes 786440 | tf_op jit(solution)/shard_map/ppermute | solution.py:43
  21.2 3.6 %collective-permute-start.8 = (bf16[4,256,128]{2,1,0:T(8,128)(2,1)S(1)}, bf16[4,256,128]{2,1,0:T(8,128)(2,1)S(1)}, u32[]{:S(2)}, u32[]{:S(2)}) collective-permute-start(bf16[4,256,128]{2,1,0:T(8,128)(2,1)S(1)} %collective-permute-done.4.refs_2_), channel_id=1, source_target_pairs={{0,32},{32,0},{1,33},{33,1},{2,34},{34,2},{3,35},{35,3},{4,36},{36... | collective-permute-start | bytes 786440 | tf_op jit(solution)/shard_map/ppermute | solution.py:43
  21.5 3.3 %collective-permute-start.7 = (bf16[4,256,128]{2,1,0:T(8,128)(2,1)S(1)}, bf16[4,256,128]{2,1,0:T(8,128)(2,1)S(1)}, u32[]{:S(2)}, u32[]{:S(2)}) collective-permute-start(bf16[4,256,128]{2,1,0:T(8,128)(2,1)S(1)} %collective-permute-done.3.refs_1_), channel_id=1, source_target_pairs={{0,32},{32,0},{1,33},{33,1},{2,34},{34,2},{3,35},{35,3},{4,36},{36... | collective-permute-start | bytes 786440 | tf_op jit(solution)/shard_map/ppermute | solution.py:43

commit v14 on v11

--- a/solution.py
+++ b/solution.py
@@ -54,11 +54,8 @@
 
 def with_lengths(passages, lengths):
     tail = jnp.pad(lengths.astype(passages.dtype), (0, WIDTH - OWN))
-    slot = lax.broadcasted_iota(jnp.int32, passages.shape, 1)
-    before = jnp.concatenate([passages[:, :8], passages[:, :-8]], axis=1)
-    filled = jnp.where(slot < lengths[:, None, None], passages, before)
     return jnp.concatenate(
-        [filled.reshape(OWN * SLOTS, WIDTH), jnp.broadcast_to(tail, (16, WIDTH))], axis=0
+        [passages.reshape(OWN * SLOTS, WIDTH), jnp.broadcast_to(tail, (16, WIDTH))], axis=0
     )
 
 
@@ -150,6 +147,11 @@
             for n in range(8):
                 unit_ref[count + n] = from_x * 1024 + i * SLOTS + n * 16
             count = count + units[0, i]
+            used = units[0, i]
+            last = pl.multiple_of(from_x * 1024 + i * SLOTS + (used - 1) * 16, 16)
+            both = p_ref[pl.ds(last, 16), :].astype(jnp.float32)
+            second = jnp.where(lengths[0, i] == used * 16, both[8:16], both[0:8])
+            p_ref[pl.ds(last, 16), :] = jnp.concatenate([both[0:8], second], axis=0).astype(p_ref.dtype)
     for i in range(DEPTH):
         unit_ref[count + i] = unit_ref[count - 1]
     turns = lax.div(count + DEPTH - 1, DEPTH)

time: 55.3 us -> 55.7 us (level); the launches traced: 55 us -> 56.1 us
  Pallas kernels: 15.9 us -> 17.2 us
  local copies, waits for them, and re-layouts: 1.02 us -> 0.02 us
  other arithmetic: 0.31 us -> 1.12 us
    pallas_call x1, Pallas kernels: 14.5 us -> 15.8 us  [score(): pl.pallas_call(score_kernel, out_shape=jax.ShapeDtypeStruct((8, 8, 128),...]
    concatenate x1, other arithmetic: 0.02 us -> 1 us  [with_lengths(): jnp.concatenate([passages.reshape(OWN * SLOTS, WIDTH), jnp.broadcast_to(t...]
    unnamed x6 -> x4, local copies, waits for them, and re-layouts: 0.66 us -> 0.01 us
  transfers between devices with their start and end apart: 13 -> 13, of which waited for: 8 -> 8; matrix products, arithmetic and copies ran while one was open for 1% -> 2% of each run, Pallas kernels for 0% -> 0%
where the time goes in v14:
time: 55.7 us; the launch traced here: 56.1 us
  Pallas kernels  17.2 us (31%)
  blocking collectives  15.8 us (28%)
  starting transfers between devices  15 us (27%)
  waiting for transfers between devices  6.82 us (12%)
  other arithmetic  1.12 us (2%)
    all_to_all x1, blocking collectives, per_device(): received = lax.all_to_all(terms, ('z', 'yhi'), 0, 0, tiled=True)  15.8 us
    pallas_call x1, Pallas kernels, score(): pl.pallas_call(score_kernel, out_shape=jax.ShapeDtypeStruct((8, 8, 128),...  15.8 us
    ppermute x3, starting transfers between devices, on_x(): return lax.ppermute(v, ('core', 'x'), pairs)  5.63 us
    ppermute x3, starting transfers between devices, per_device(): lax.ppermute(block, PLANE, along(False, k))  5.07 us
    ppermute x3, waiting for transfers between devices, per_device(): lax.ppermute(block, PLANE, along(False, k))  4.42 us
    ppermute x3, starting transfers between devices, per_device(): lax.ppermute(own, PLANE, along(True, k))  4.09 us
    pallas_call x1, Pallas kernels, place(): pl.pallas_call(place_kernel, out_shape=jax.ShapeDtypeStruct((32, 256), jn...  1.46 us
  transfers between devices with their start and end apart: 13, of which 8 were waited for; matrix products, arithmetic and copies ran while one was open for 2% of the time, Pallas kernels for 0%

profile of v14, /device:TPU:0, one launch (start us, length us, event | category | flops | bytes accessed | tf_op | source)
XLA Modules:
  0.0 56.1 jit_solution(13892821579509945706)
XLA Ops:
  0.0 0.0 copy-start.1
  0.0 3.1 %collective-permute-start.2 = (bf16[256,128]{1,0:T(8,128)(2,1)}, bf16[256,128]{1,0:T(8,128)(2,1)S(1)}, u32[]{:S(2)}, u32[]{:S(2)}) collective-permute-start(bf16[256,128]{1,0:T(8,128)(2,1)} %bitcast.11), channel_id=1, source_target_pairs={{0,68},{4,64},{8,76},{12,72},{16,84},{20,80},{24,92},{28,88},{32,5... | collective-permute-start | bytes 196616 | tf_op jit(solution)/shard_map/ppermute | solution.py:224
  3.1 0.6 %collective-permute-start.1 = (bf16[256,128]{1,0:T(8,128)(2,1)}, bf16[256,128]{1,0:T(8,128)(2,1)S(1)}, u32[]{:S(2)}, u32[]{:S(2)}) collective-permute-start(bf16[256,128]{1,0:T(8,128)(2,1)} %bitcast.12), channel_id=1, source_target_pairs={{0,4},{4,0},{8,12},{12,8},{16,20},{20,16},{24,28},{28,24},{32,48},... | collective-permute-start | bytes 196616 | tf_op jit(solution)/shard_map/ppermute | solution.py:224
  3.7 0.4 collective-permute-start
  4.1 0.0 copy-done.1
  4.1 0.0 copy-start
  4.1 1.0 %pad_maximum_fusion.refs_8_ = bf16[1040,128]{1,0:T(8,128)(2,1)S(1)} fusion(bf16[16,128]{1,0:T(8,128)(2,1)S(1)} %broadcast_in_dim.3, bf16[1024,128]{1,0:T(8,128)(2,1)} %bitcast.10), kind=kLoop, calls=%fused_computation | loop fusion | flops 532480 | bytes 532480 | tf_op jit(solution)/shard_map/concatenate | solution.py:57
  5.1 2.9 %collective-permute-start.11 = (bf16[1040,128]{1,0:T(8,128)(2,1)S(1)}, bf16[1040,128]{1,0:T(8,128)(2,1)S(1)}, u32[]{:S(2)}, u32[]{:S(2)}) collective-permute-start(bf16[1040,128]{1,0:T(8,128)(2,1)S(1)} %pad_maximum_fusion.refs_8_), channel_id=1, source_target_pairs={{0,3},{1,2},{2,1},{3,0},{32,33},{33,32},{34,35},{35,34},{4,7},{5,6... | collective-permute-start | bytes 798728 | tf_op jit(solution)/shard_map/ppermute | solution.py:52
  8.1 0.2 collective-permute-start.10
  8.3 0.0 collective-permute-done.2
  8.3 0.8 %collective-permute-done.1 = bf16[256,128]{1,0:T(8,128)(2,1)S(1)} collective-permute-done((bf16[256,128]{1,0:T(8,128)(2,1)}, bf16[256,128]{1,0:T(8,128)(2,1)S(1)}, u32[]{:S(2)}, u32[]{:S(2)}) %collective-permute-start.1) | collective-permute-done | bytes 65568 | tf_op jit(solution)/shard_map/ppermute | solution.py:224
  9.1 0.0 collective-permute-done
  9.1 0.0 copy-done
  9.1 4.1 %collective-permute-start.5 = (bf16[4,256,128]{2,1,0:T(8,128)(2,1)S(1)}, bf16[4,256,128]{2,1,0:T(8,128)(2,1)S(1)}, u32[]{:S(2)}, u32[]{:S(2)}) collective-permute-start(bf16[4,256,128]{2,1,0:T(8,128)(2,1)S(1)} %pad_maximum_fusion.1.refs_0_), channel_id=1, source_target_pairs={{0,24},{4,28},{8,16},{12,20},{16,8},{20,12},{24,0},{28,4},{32,100}... | collective-permute-start | bytes 786440 | tf_op jit(solution)/shard_map/ppermute | solution.py:229
  13.2 0.0 collective-permute-start.4
  13.2 0.9 %collective-permute-start.3 = (bf16[4,256,128]{2,1,0:T(8,128)(2,1)S(1)}, bf16[4,256,128]{2,1,0:T(8,128)(2,1)S(1)}, u32[]{:S(2)}, u32[]{:S(2)}) collective-permute-start(bf16[4,256,128]{2,1,0:T(8,128)(2,1)S(1)} %pad_maximum_fusion.1.refs_0_), channel_id=1, source_target_pairs={{0,8},{4,12},{8,0},{12,4},{16,24},{20,28},{24,16},{28,20},{32,96},... | collective-permute-start | bytes 786440 | tf_op jit(solution)/shard_map/ppermute | solution.py:229
  14.2 0.3 collective-permute-done.10.refs_9_
  14.5 2.5 %collective-permute-start.12 = (bf16[1040,128]{1,0:T(8,128)(2,1)S(1)}, bf16[1040,128]{1,0:T(8,128)(2,1)S(1)}, u32[]{:S(2)}, u32[]{:S(2)}) collective-permute-start(bf16[1040,128]{1,0:T(8,128)(2,1)S(1)} %collective-permute-done.10.refs_9_), channel_id=1, source_target_pairs={{0,3},{1,2},{2,1},{3,0},{32,33},{33,32},{34,35},{35,34},{4,7},{5,6... | collective-permute-start | bytes 798728 | tf_op jit(solution)/shard_map/ppermute | solution.py:52
  17.0 0.0 collective-permute-done.11.refs_10_
  17.0 0.0 collective-permute-start.6
  17.0 3.0 %collective-permute-done.5.refs_3_ = bf16[4,256,128]{2,1,0:T(8,128)(2,1)S(1)} collective-permute-done((bf16[4,256,128]{2,1,0:T(8,128)(2,1)S(1)}, bf16[4,256,128]{2,1,0:T(8,128)(2,1)S(1)}, u32[]{:S(2)}, u32[]{:S(2)}) %collective-permute-start.5) | collective-permute-done | bytes 262176 | tf_op jit(solution)/shard_map/ppermute | solution.py:229
  19.9 0.0 collective-permute-start.9
  19.9 1.2 %collective-permute-done.4.refs_2_ = bf16[4,256,128]{2,1,0:T(8,128)(2,1)S(1)} collective-permute-done((bf16[4,256,128]{2,1,0:T(8,128)(2,1)S(1)}, bf16[4,256,128]{2,1,0:T(8,128)(2,1)S(1)}, u32[]{:S(2)}, u32[]{:S(2)}) %collective-permute-start.4) | collective-permute-done | bytes 262176 | tf_op jit(solution)/shard_map/ppermute | solution.py:229
  21.1 0.0 collective-permute-start.8
  21.1 0.3 collective-permute-done.3.refs_1_
  21.4 0.2 collective-permute-start.7
  21.6 0.1 pad_add_fusion.info_ref
  21.7 0.0 collective-permute-done.6.refs_4_
  21.7 0.4 collective-permute-done.12.refs_11_
  22.1 0.0 collective-permute-done.9.refs_7_
  22.1 0.5 collective-permute-done.8.refs_6_
  22.7 0.4 collective-permute-done.7.refs_5_
  23.0 15.8 %shard_map.37 = f32[8,8,128]{2,1,0:T(8,128)S(1)} custom-call(s32[4]{0:T(128)S(1)} %pad_add_fusion.info_ref, bf16[4,256,128]{2,1,0:T(8,128)(2,1)S(1)} %pad_maximum_fusion.1.refs_0_, bf16[4,256,128]{2,1,0:T(8,128)(2,1)S(1)} %collective-permute-done.3.refs_1_, bf16[4,256,128]{2,1,0:T(8,128)(2,1)S(1)} %collective-permute-done.4.refs_2_, ...), custom_call_target="tpu_custom_call" | custom-call | tf_op jit(solution)/shard_map/pallas_call | solution.py:188
  38.8 15.8 %all_to_all.5.r_ref = f32[8,8,128]{2,1,0:T(8,128)} all-to-all(f32[8,8,128]{2,1,0:T(8,128)S(1)} %shard_map.37), channel_id=1, replica_groups=mesh['ylo'=2,'core'=2,'z'=4,'yhi'=2,'x'=4] {'z','yhi'}, dimensions={0} | all-to-all | bytes 65536 | tf_op jit(solution)/shard_map/all_to_all | solution.py:232
  54.6 1.5 %shard_map.38 = f32[32,256]{1,0:T(8,128)} custom-call(f32[8,8,128]{2,1,0:T(8,128)} %all_to_all.5.r_ref), custom_call_target="tpu_custom_call" | custom-call | tf_op jit(solution)/shard_map/pallas_call | solution.py:212
  (4 shorter events, 0.1 us)
Async XLA Ops:
  0.0 4.1 %copy-start.1 = (s32[8]{0:T(128)S(1)}, s32[8]{0:T(128)}, u32[]{:S(2)}) copy-start(s32[8]{0:T(128)} %param.5) | copy-start | bytes 100
  0.0 8.3 %collective-permute-start.2 = (bf16[256,128]{1,0:T(8,128)(2,1)}, bf16[256,128]{1,0:T(8,128)(2,1)S(1)}, u32[]{:S(2)}, u32[]{:S(2)}) collective-permute-start(bf16[256,128]{1,0:T(8,128)(2,1)} %bitcast.11), channel_id=1, source_target_pairs={{0,68},{4,64},{8,76},{12,72},{16,84},{20,80},{24,92},{28,88},{32,5... | collective-permute-start | bytes 196616 | tf_op jit(solution)/shard_map/ppermute | solution.py:224
  3.1 6.0 %collective-permute-start.1 = (bf16[256,128]{1,0:T(8,128)(2,1)}, bf16[256,128]{1,0:T(8,128)(2,1)S(1)}, u32[]{:S(2)}, u32[]{:S(2)}) collective-permute-start(bf16[256,128]{1,0:T(8,128)(2,1)} %bitcast.12), channel_id=1, source_target_pairs={{0,4},{4,0},{8,12},{12,8},{16,20},{20,16},{24,28},{28,24},{32,48},... | collective-permute-start | bytes 196616 | tf_op jit(solution)/shard_map/ppermute | solution.py:224
  3.7 5.4 %collective-permute-start = (bf16[256,128]{1,0:T(8,128)(2,1)}, bf16[256,128]{1,0:T(8,128)(2,1)S(1)}, u32[]{:S(2)}, u32[]{:S(2)}) collective-permute-start(bf16[256,128]{1,0:T(8,128)(2,1)} %bitcast.13), channel_id=1, source_target_pairs={{0,64},{4,68},{8,72},{12,76},{16,80},{20,84},{24,88},{28,92},{32,4... | collective-permute-start | bytes 196616 | tf_op jit(solution)/shard_map/ppermute | solution.py:224
  4.1 5.0 %copy-start = (bf16[32,8,128]{2,1,0:T(8,128)(2,1)S(1)}, bf16[32,8,128]{2,1,0:T(8,128)(2,1)}, u32[]{:S(2)}) copy-start(bf16[32,8,128]{2,1,0:T(8,128)(2,1)} %param.3) | copy-start | bytes 196612
  5.1 11.8 %collective-permute-start.11 = (bf16[1040,128]{1,0:T(8,128)(2,1)S(1)}, bf16[1040,128]{1,0:T(8,128)(2,1)S(1)}, u32[]{:S(2)}, u32[]{:S(2)}) collective-permute-start(bf16[1040,128]{1,0:T(8,128)(2,1)S(1)} %pad_maximum_fusion.refs_8_), channel_id=1, source_target_pairs={{0,3},{1,2},{2,1},{3,0},{32,33},{33,32},{34,35},{35,34},{4,7},{5,6... | collective-permute-start | bytes 798728 | tf_op jit(solution)/shard_map/ppermute | solution.py:52
  8.1 6.4 %collective-permute-start.10 = (bf16[1040,128]{1,0:T(8,128)(2,1)S(1)}, bf16[1040,128]{1,0:T(8,128)(2,1)S(1)}, u32[]{:S(2)}, u32[]{:S(2)}) collective-permute-start(bf16[1040,128]{1,0:T(8,128)(2,1)S(1)} %pad_maximum_fusion.refs_8_), channel_id=1, source_target_pairs={{0,1},{1,0},{2,3},{3,2},{32,35},{33,34},{34,33},{35,32},{4,5},{5,4... | collective-permute-start | bytes 798728 | tf_op jit(solution)/shard_map/ppermute | solution.py:52
  9.1 10.8 %collective-permute-start.5 = (bf16[4,256,128]{2,1,0:T(8,128)(2,1)S(1)}, bf16[4,256,128]{2,1,0:T(8,128)(2,1)S(1)}, u32[]{:S(2)}, u32[]{:S(2)}) collective-permute-start(bf16[4,256,128]{2,1,0:T(8,128)(2,1)S(1)} %pad_maximum_fusion.1.refs_0_), channel_id=1, source_target_pairs={{0,24},{4,28},{8,16},{12,20},{16,8},{20,12},{24,0},{28,4},{32,100}... | collective-permute-start | bytes 786440 | tf_op jit(solution)/shard_map/ppermute | solution.py:229
  13.2 7.9 %collective-permute-start.4 = (bf16[4,256,128]{2,1,0:T(8,128)(2,1)S(1)}, bf16[4,256,128]{2,1,0:T(8,128)(2,1)S(1)}, u32[]{:S(2)}, u32[]{:S(2)}) collective-permute-start(bf16[4,256,128]{2,1,0:T(8,128)(2,1)S(1)} %pad_maximum_fusion.1.refs_0_), channel_id=1, source_target_pairs={{0,16},{4,20},{8,24},{12,28},{16,0},{20,4},{24,8},{28,12},{32,36},... | collective-permute-start | bytes 786440 | tf_op jit(solution)/shard_map/ppermute | solution.py:229
  13.2 8.1 %collective-permute-start.3 = (bf16[4,256,128]{2,1,0:T(8,128)(2,1)S(1)}, bf16[4,256,128]{2,1,0:T(8,128)(2,1)S(1)}, u32[]{:S(2)}, u32[]{:S(2)}) collective-permute-start(bf16[4,256,128]{2,1,0:T(8,128)(2,1)S(1)} %pad_maximum_fusion.1.refs_0_), channel_id=1, source_target_pairs={{0,8},{4,12},{8,0},{12,4},{16,24},{20,28},{24,16},{28,20},{32,96},... | collective-permute-start | bytes 786440 | tf_op jit(solution)/shard_map/ppermute | solution.py:229
  14.5 7.6 %collective-permute-start.12 = (bf16[1040,128]{1,0:T(8,128)(2,1)S(1)}, bf16[1040,128]{1,0:T(8,128)(2,1)S(1)}, u32[]{:S(2)}, u32[]{:S(2)}) collective-permute-start(bf16[1040,128]{1,0:T(8,128)(2,1)S(1)} %collective-permute-done.10.refs_9_), channel_id=1, source_target_pairs={{0,3},{1,2},{2,1},{3,0},{32,33},{33,32},{34,35},{35,34},{4,7},{5,6... | collective-permute-start | bytes 798728 | tf_op jit(solution)/shard_map/ppermute | solution.py:52
  17.0 4.8 %collective-permute-start.6 = (bf16[4,256,128]{2,1,0:T(8,128)(2,1)S(1)}, bf16[4,256,128]{2,1,0:T(8,128)(2,1)S(1)}, u32[]{:S(2)}, u32[]{:S(2)}) collective-permute-start(bf16[4,256,128]{2,1,0:T(8,128)(2,1)S(1)} %pad_maximum_fusion.1.refs_0_), channel_id=1, source_target_pairs={{0,32},{32,0},{1,33},{33,1},{2,34},{34,2},{3,35},{35,3},{4,36},{36... | collective-permute-start | bytes 786440 | tf_op jit(solution)/shard_map/ppermute | solution.py:43
  19.9 2.2 %collective-permute-start.9 = (bf16[4,256,128]{2,1,0:T(8,128)(2,1)S(1)}, bf16[4,256,128]{2,1,0:T(8,128)(2,1)S(1)}, u32[]{:S(2)}, u32[]{:S(2)}) collective-permute-start(bf16[4,256,128]{2,1,0:T(8,128)(2,1)S(1)} %collective-permute-done.5.refs_3_), channel_id=1, source_target_pairs={{0,32},{32,0},{1,33},{33,1},{2,34},{34,2},{3,35},{35,3},{4,36},{36... | collective-permute-start | bytes 786440 | tf_op jit(solution)/shard_map/ppermute | solution.py:43
  21.1 1.5 %collective-permute-start.8 = (bf16[4,256,128]{2,1,0:T(8,128)(2,1)S(1)}, bf16[4,256,128]{2,1,0:T(8,128)(2,1)S(1)}, u32[]{:S(2)}, u32[]{:S(2)}) collective-permute-start(bf16[4,256,128]{2,1,0:T(8,128)(2,1)S(1)} %collective-permute-done.4.refs_2_), channel_id=1, source_target_pairs={{0,32},{32,0},{1,33},{33,1},{2,34},{34,2},{3,35},{35,3},{4,36},{36... | collective-permute-start | bytes 786440 | tf_op jit(solution)/shard_map/ppermute | solution.py:43
  21.4 1.6 %collective-permute-start.7 = (bf16[4,256,128]{2,1,0:T(8,128)(2,1)S(1)}, bf16[4,256,128]{2,1,0:T(8,128)(2,1)S(1)}, u32[]{:S(2)}, u32[]{:S(2)}) collective-permute-start(bf16[4,256,128]{2,1,0:T(8,128)(2,1)S(1)} %collective-permute-done.3.refs_1_), channel_id=1, source_target_pairs={{0,32},{32,0},{1,33},{33,1},{2,34},{34,2},{3,35},{35,3},{4,36},{36... | collective-permute-start | bytes 786440 | tf_op jit(solution)/shard_map/ppermute | solution.py:43

commit v15 on v14

--- a/solution.py
+++ b/solution.py
@@ -59,7 +59,7 @@
     )
 
 
-def best_dots(rows, places, p_ref, m_ref, s_ref, unit_ref, turns, *acc):
+def best_dots(rows, p_ref, m_ref, s_ref, unit_ref, turns, *acc):
     acc = (acc[:DEPTH], acc[DEPTH:])
     nothing = jnp.zeros((16, 128), jnp.bfloat16)
 
@@ -120,7 +120,7 @@
                 for i in range(1, 8):
                     top = jnp.maximum(top, rows_ref[b, pl.ds(64 * o + i, 8, stride=8), :])
                 lanes = slice(128 * (b % 2), 128 * (b % 2) + 128)
-                s_ref[places[g][b // 2], 8 * o : 8 * o + 8, lanes] += top
+                s_ref[4 * g + b // 2, 8 * o : 8 * o + 8, lanes] = top
 
 
 def score_kernel(info_ref, *refs):
@@ -128,14 +128,9 @@
     p_ref, m_ref, s_ref, unit_ref = refs[13:]
     z, yhi, core, x = (info_ref[i] for i in range(4))
 
-    groups, places = [], []
-    for k in range(4):
-        for j in (0, 2):
-            groups.append([(rows[c + k], e) for c in (0, 4) for e in (j, j + 1)])
-            by_chain = [[k * 2 + e // 2, e * 2 + k // 2] for e in (j, j + 1)]
-            places.append(
-                [jnp.where(chain == 0, p, q) for chain in (core, 1 - core) for p, q in by_chain]
-            )
+    groups = [
+        [(rows[c + k], e) for c in (0, 4) for e in (j, j + 1)] for k in range(4) for j in (0, 2)
+    ]
 
     count = jnp.int32(0)
     for m in range(4):
@@ -156,16 +151,22 @@
         unit_ref[count + i] = unit_ref[count - 1]
     turns = lax.div(count + DEPTH - 1, DEPTH)
 
-    s_ref[...] = jnp.zeros_like(s_ref)
     pl.run_scoped(
-        functools.partial(best_dots, groups, places, p_ref, m_ref, s_ref, unit_ref, turns),
+        functools.partial(best_dots, groups, p_ref, m_ref, s_ref, unit_ref, turns),
         *[pltpu.ACC(u)((32, 256), jnp.float32) for u in range(2) for _ in range(DEPTH)],
     )
 
     lane = lax.broadcasted_iota(jnp.int32, (32, 256), 1)
     row = lax.broadcasted_iota(jnp.int32, (32, 256), 0)
     pick = jnp.where(lane // 8 == row, 1.0 / 32, 0.0).astype(jnp.bfloat16)
-    rest = s_ref[...].reshape(256, 256)
+    totals = []
+    for dz in range(4):
+        for h in range(2):
+            places = [(dz * 2 + h) * 4 + core * 2 + e for e in range(2)]
+            places += [(k * 2 + dz // 2) * 4 + (1 - core) * 2 + dz % 2 for k in (2 * h, 2 * h + 1)]
+            a, b, c, d = (s_ref[i] for i in places)
+            totals.append((a + b) + (c + d))
+    rest = jnp.concatenate(totals, axis=0)
     parts = []
     for _ in range(3):
         parts.append(rest.astype(jnp.bfloat16))
@@ -194,7 +195,7 @@
         scratch_shapes=[
             pltpu.VMEM((4096, 128), jnp.bfloat16),
             pltpu.VMEM((8, 33, 8, 128), jnp.float32),
-            pltpu.VMEM((8, 32, 256), jnp.float32),
+            pltpu.VMEM((32, 32, 256), jnp.float32),
             pltpu.SMEM((256 + DEPTH,), jnp.int32),
         ],
         compiler_params=pltpu.CompilerParams(vmem_limit_bytes=32 << 20),

time: 55.7 us -> 55.2 us (level); the launches traced: 56.1 us -> 54.9 us
  blocking collectives: 15.8 us -> 13.5 us
  Pallas kernels: 17.2 us -> 18.4 us
    all_to_all x1, blocking collectives: 15.8 us -> 13.5 us  [per_device(): received = lax.all_to_all(terms, ('z', 'yhi'), 0, 0, tiled=True)]
    pallas_call x1, Pallas kernels: 15.8 us -> 16.9 us  [score(): pl.pallas_call(score_kernel, out_shape=jax.ShapeDtypeStruct((8, 8, 128),...]
where the time goes in v15:
time: 55.2 us; the launch traced here: 54.9 us
  Pallas kernels  18.4 us (33%)
  starting transfers between devices  15 us (27%)
  blocking collectives  13.5 us (24%)
  waiting for transfers between devices  6.82 us (12%)
  other arithmetic  1.12 us (2%)
    pallas_call x1, Pallas kernels, score(): pl.pallas_call(score_kernel, out_shape=jax.ShapeDtypeStruct((8, 8, 128),...  16.9 us
    all_to_all x1, blocking collectives, per_device(): received = lax.all_to_all(terms, ('z', 'yhi'), 0, 0, tiled=True)  13.5 us
    ppermute x3, starting transfers between devices, on_x(): return lax.ppermute(v, ('core', 'x'), pairs)  5.63 us
    ppermute x3, starting transfers between devices, per_device(): lax.ppermute(block, PLANE, along(False, k))  5.07 us
    ppermute x3, waiting for transfers between devices, per_device(): lax.ppermute(block, PLANE, along(False, k))  4.42 us
    ppermute x3, starting transfers between devices, per_device(): lax.ppermute(own, PLANE, along(True, k))  4.09 us
    pallas_call x1, Pallas kernels, place(): pl.pallas_call(place_kernel, out_shape=jax.ShapeDtypeStruct((32, 256), jn...  1.46 us
  transfers between devices with their start and end apart: 13, of which 8 were waited for; matrix products, arithmetic and copies ran while one was open for 2% of the time, Pallas kernels for 0%

profile of v15, /device:TPU:0, one launch (start us, length us, event | category | flops | bytes accessed | tf_op | source)
XLA Modules:
  0.0 54.9 jit_solution(11328992717632262373)
XLA Ops:
  0.0 0.0 copy-start.1
  0.0 3.1 %collective-permute-start.2 = (bf16[256,128]{1,0:T(8,128)(2,1)}, bf16[256,128]{1,0:T(8,128)(2,1)S(1)}, u32[]{:S(2)}, u32[]{:S(2)}) collective-permute-start(bf16[256,128]{1,0:T(8,128)(2,1)} %bitcast.11), channel_id=1, source_target_pairs={{0,68},{4,64},{8,76},{12,72},{16,84},{20,80},{24,92},{28,88},{32,5... | collective-permute-start | bytes 196616 | tf_op jit(solution)/shard_map/ppermute | solution.py:225
  3.1 0.6 %collective-permute-start.1 = (bf16[256,128]{1,0:T(8,128)(2,1)}, bf16[256,128]{1,0:T(8,128)(2,1)S(1)}, u32[]{:S(2)}, u32[]{:S(2)}) collective-permute-start(bf16[256,128]{1,0:T(8,128)(2,1)} %bitcast.12), channel_id=1, source_target_pairs={{0,4},{4,0},{8,12},{12,8},{16,20},{20,16},{24,28},{28,24},{32,48},... | collective-permute-start | bytes 196616 | tf_op jit(solution)/shard_map/ppermute | solution.py:225
  3.7 0.4 collective-permute-start
  4.1 0.0 copy-done.1
  4.1 0.0 copy-start
  4.1 1.0 %pad_maximum_fusion.refs_8_ = bf16[1040,128]{1,0:T(8,128)(2,1)S(1)} fusion(bf16[16,128]{1,0:T(8,128)(2,1)S(1)} %broadcast_in_dim.3, bf16[1024,128]{1,0:T(8,128)(2,1)} %bitcast.10), kind=kLoop, calls=%fused_computation | loop fusion | flops 532480 | bytes 532480 | tf_op jit(solution)/shard_map/concatenate | solution.py:57
  5.1 2.9 %collective-permute-start.11 = (bf16[1040,128]{1,0:T(8,128)(2,1)S(1)}, bf16[1040,128]{1,0:T(8,128)(2,1)S(1)}, u32[]{:S(2)}, u32[]{:S(2)}) collective-permute-start(bf16[1040,128]{1,0:T(8,128)(2,1)S(1)} %pad_maximum_fusion.refs_8_), channel_id=1, source_target_pairs={{0,3},{1,2},{2,1},{3,0},{32,33},{33,32},{34,35},{35,34},{4,7},{5,6... | collective-permute-start | bytes 798728 | tf_op jit(solution)/shard_map/ppermute | solution.py:52
  8.1 0.2 collective-permute-start.10
  8.3 0.0 collective-permute-done.2
  8.3 0.8 %collective-permute-done.1 = bf16[256,128]{1,0:T(8,128)(2,1)S(1)} collective-permute-done((bf16[256,128]{1,0:T(8,128)(2,1)}, bf16[256,128]{1,0:T(8,128)(2,1)S(1)}, u32[]{:S(2)}, u32[]{:S(2)}) %collective-permute-start.1) | collective-permute-done | bytes 65568 | tf_op jit(solution)/shard_map/ppermute | solution.py:225
  9.1 0.0 collective-permute-done
  9.1 0.0 copy-done
  9.1 4.1 %collective-permute-start.5 = (bf16[4,256,128]{2,1,0:T(8,128)(2,1)S(1)}, bf16[4,256,128]{2,1,0:T(8,128)(2,1)S(1)}, u32[]{:S(2)}, u32[]{:S(2)}) collective-permute-start(bf16[4,256,128]{2,1,0:T(8,128)(2,1)S(1)} %pad_maximum_fusion.1.refs_0_), channel_id=1, source_target_pairs={{0,24},{4,28},{8,16},{12,20},{16,8},{20,12},{24,0},{28,4},{32,100}... | collective-permute-start | bytes 786440 | tf_op jit(solution)/shard_map/ppermute | solution.py:230
  13.2 0.0 collective-permute-start.4
  13.2 0.9 %collective-permute-start.3 = (bf16[4,256,128]{2,1,0:T(8,128)(2,1)S(1)}, bf16[4,256,128]{2,1,0:T(8,128)(2,1)S(1)}, u32[]{:S(2)}, u32[]{:S(2)}) collective-permute-start(bf16[4,256,128]{2,1,0:T(8,128)(2,1)S(1)} %pad_maximum_fusion.1.refs_0_), channel_id=1, source_target_pairs={{0,8},{4,12},{8,0},{12,4},{16,24},{20,28},{24,16},{28,20},{32,96},... | collective-permute-start | bytes 786440 | tf_op jit(solution)/shard_map/ppermute | solution.py:230
  14.2 0.3 collective-permute-done.10.refs_9_
  14.5 2.5 %collective-permute-start.12 = (bf16[1040,128]{1,0:T(8,128)(2,1)S(1)}, bf16[1040,128]{1,0:T(8,128)(2,1)S(1)}, u32[]{:S(2)}, u32[]{:S(2)}) collective-permute-start(bf16[1040,128]{1,0:T(8,128)(2,1)S(1)} %collective-permute-done.10.refs_9_), channel_id=1, source_target_pairs={{0,3},{1,2},{2,1},{3,0},{32,33},{33,32},{34,35},{35,34},{4,7},{5,6... | collective-permute-start | bytes 798728 | tf_op jit(solution)/shard_map/ppermute | solution.py:52
  17.0 0.0 collective-permute-done.11.refs_10_
  17.0 0.0 collective-permute-start.6
  17.0 3.0 %collective-permute-done.5.refs_3_ = bf16[4,256,128]{2,1,0:T(8,128)(2,1)S(1)} collective-permute-done((bf16[4,256,128]{2,1,0:T(8,128)(2,1)S(1)}, bf16[4,256,128]{2,1,0:T(8,128)(2,1)S(1)}, u32[]{:S(2)}, u32[]{:S(2)}) %collective-permute-start.5) | collective-permute-done | bytes 262176 | tf_op jit(solution)/shard_map/ppermute | solution.py:230
  19.9 0.0 collective-permute-start.9
  19.9 1.2 %collective-permute-done.4.refs_2_ = bf16[4,256,128]{2,1,0:T(8,128)(2,1)S(1)} collective-permute-done((bf16[4,256,128]{2,1,0:T(8,128)(2,1)S(1)}, bf16[4,256,128]{2,1,0:T(8,128)(2,1)S(1)}, u32[]{:S(2)}, u32[]{:S(2)}) %collective-permute-start.4) | collective-permute-done | bytes 262176 | tf_op jit(solution)/shard_map/ppermute | solution.py:230
  21.1 0.0 collective-permute-start.8
  21.1 0.3 collective-permute-done.3.refs_1_
  21.4 0.2 collective-permute-start.7
  21.6 0.1 pad_add_fusion.info_ref
  21.7 0.0 collective-permute-done.6.refs_4_
  21.7 0.4 collective-permute-done.12.refs_11_
  22.1 0.0 collective-permute-done.9.refs_7_
  22.1 0.5 %collective-permute-done.8.refs_6_ = bf16[4,256,128]{2,1,0:T(8,128)(2,1)S(1)} collective-permute-done((bf16[4,256,128]{2,1,0:T(8,128)(2,1)S(1)}, bf16[4,256,128]{2,1,0:T(8,128)(2,1)S(1)}, u32[]{:S(2)}, u32[]{:S(2)}) %collective-permute-start.8) | collective-permute-done | bytes 262176 | tf_op jit(solution)/shard_map/ppermute | solution.py:43
  22.7 0.4 collective-permute-done.7.refs_5_
  23.0 16.9 %shard_map.37 = f32[8,8,128]{2,1,0:T(8,128)S(1)} custom-call(s32[4]{0:T(128)S(1)} %pad_add_fusion.info_ref, bf16[4,256,128]{2,1,0:T(8,128)(2,1)S(1)} %pad_maximum_fusion.1.refs_0_, bf16[4,256,128]{2,1,0:T(8,128)(2,1)S(1)} %collective-permute-done.3.refs_1_, bf16[4,256,128]{2,1,0:T(8,128)(2,1)S(1)} %collective-permute-done.4.refs_2_, ...), custom_call_target="tpu_custom_call" | custom-call | tf_op jit(solution)/shard_map/pallas_call | solution.py:189
  40.0 13.5 %all_to_all.5.r_ref = f32[8,8,128]{2,1,0:T(8,128)} all-to-all(f32[8,8,128]{2,1,0:T(8,128)S(1)} %shard_map.37), channel_id=1, replica_groups=mesh['ylo'=2,'core'=2,'z'=4,'yhi'=2,'x'=4] {'z','yhi'}, dimensions={0} | all-to-all | bytes 65536 | tf_op jit(solution)/shard_map/all_to_all | solution.py:233
  53.5 1.5 %shard_map.38 = f32[32,256]{1,0:T(8,128)} custom-call(f32[8,8,128]{2,1,0:T(8,128)} %all_to_all.5.r_ref), custom_call_target="tpu_custom_call" | custom-call | tf_op jit(solution)/shard_map/pallas_call | solution.py:213
  (4 shorter events, 0.1 us)
Async XLA Ops:
  0.0 4.1 %copy-start.1 = (s32[8]{0:T(128)S(1)}, s32[8]{0:T(128)}, u32[]{:S(2)}) copy-start(s32[8]{0:T(128)} %param.5) | copy-start | bytes 100
  0.0 8.3 %collective-permute-start.2 = (bf16[256,128]{1,0:T(8,128)(2,1)}, bf16[256,128]{1,0:T(8,128)(2,1)S(1)}, u32[]{:S(2)}, u32[]{:S(2)}) collective-permute-start(bf16[256,128]{1,0:T(8,128)(2,1)} %bitcast.11), channel_id=1, source_target_pairs={{0,68},{4,64},{8,76},{12,72},{16,84},{20,80},{24,92},{28,88},{32,5... | collective-permute-start | bytes 196616 | tf_op jit(solution)/shard_map/ppermute | solution.py:225
  3.1 6.0 %collective-permute-start.1 = (bf16[256,128]{1,0:T(8,128)(2,1)}, bf16[256,128]{1,0:T(8,128)(2,1)S(1)}, u32[]{:S(2)}, u32[]{:S(2)}) collective-permute-start(bf16[256,128]{1,0:T(8,128)(2,1)} %bitcast.12), channel_id=1, source_target_pairs={{0,4},{4,0},{8,12},{12,8},{16,20},{20,16},{24,28},{28,24},{32,48},... | collective-permute-start | bytes 196616 | tf_op jit(solution)/shard_map/ppermute | solution.py:225
  3.7 5.4 %collective-permute-start = (bf16[256,128]{1,0:T(8,128)(2,1)}, bf16[256,128]{1,0:T(8,128)(2,1)S(1)}, u32[]{:S(2)}, u32[]{:S(2)}) collective-permute-start(bf16[256,128]{1,0:T(8,128)(2,1)} %bitcast.13), channel_id=1, source_target_pairs={{0,64},{4,68},{8,72},{12,76},{16,80},{20,84},{24,88},{28,92},{32,4... | collective-permute-start | bytes 196616 | tf_op jit(solution)/shard_map/ppermute | solution.py:225
  4.1 5.0 %copy-start = (bf16[32,8,128]{2,1,0:T(8,128)(2,1)S(1)}, bf16[32,8,128]{2,1,0:T(8,128)(2,1)}, u32[]{:S(2)}) copy-start(bf16[32,8,128]{2,1,0:T(8,128)(2,1)} %param.3) | copy-start | bytes 196612
  5.1 11.8 %collective-permute-start.11 = (bf16[1040,128]{1,0:T(8,128)(2,1)S(1)}, bf16[1040,128]{1,0:T(8,128)(2,1)S(1)}, u32[]{:S(2)}, u32[]{:S(2)}) collective-permute-start(bf16[1040,128]{1,0:T(8,128)(2,1)S(1)} %pad_maximum_fusion.refs_8_), channel_id=1, source_target_pairs={{0,3},{1,2},{2,1},{3,0},{32,33},{33,32},{34,35},{35,34},{4,7},{5,6... | collective-permute-start | bytes 798728 | tf_op jit(solution)/shard_map/ppermute | solution.py:52
  8.1 6.4 %collective-permute-start.10 = (bf16[1040,128]{1,0:T(8,128)(2,1)S(1)}, bf16[1040,128]{1,0:T(8,128)(2,1)S(1)}, u32[]{:S(2)}, u32[]{:S(2)}) collective-permute-start(bf16[1040,128]{1,0:T(8,128)(2,1)S(1)} %pad_maximum_fusion.refs_8_), channel_id=1, source_target_pairs={{0,1},{1,0},{2,3},{3,2},{32,35},{33,34},{34,33},{35,32},{4,5},{5,4... | collective-permute-start | bytes 798728 | tf_op jit(solution)/shard_map/ppermute | solution.py:52
  9.1 10.8 %collective-permute-start.5 = (bf16[4,256,128]{2,1,0:T(8,128)(2,1)S(1)}, bf16[4,256,128]{2,1,0:T(8,128)(2,1)S(1)}, u32[]{:S(2)}, u32[]{:S(2)}) collective-permute-start(bf16[4,256,128]{2,1,0:T(8,128)(2,1)S(1)} %pad_maximum_fusion.1.refs_0_), channel_id=1, source_target_pairs={{0,24},{4,28},{8,16},{12,20},{16,8},{20,12},{24,0},{28,4},{32,100}... | collective-permute-start | bytes 786440 | tf_op jit(solution)/shard_map/ppermute | solution.py:230
  13.2 7.9 %collective-permute-start.4 = (bf16[4,256,128]{2,1,0:T(8,128)(2,1)S(1)}, bf16[4,256,128]{2,1,0:T(8,128)(2,1)S(1)}, u32[]{:S(2)}, u32[]{:S(2)}) collective-permute-start(bf16[4,256,128]{2,1,0:T(8,128)(2,1)S(1)} %pad_maximum_fusion.1.refs_0_), channel_id=1, source_target_pairs={{0,16},{4,20},{8,24},{12,28},{16,0},{20,4},{24,8},{28,12},{32,36},... | collective-permute-start | bytes 786440 | tf_op jit(solution)/shard_map/ppermute | solution.py:230
  13.2 8.1 %collective-permute-start.3 = (bf16[4,256,128]{2,1,0:T(8,128)(2,1)S(1)}, bf16[4,256,128]{2,1,0:T(8,128)(2,1)S(1)}, u32[]{:S(2)}, u32[]{:S(2)}) collective-permute-start(bf16[4,256,128]{2,1,0:T(8,128)(2,1)S(1)} %pad_maximum_fusion.1.refs_0_), channel_id=1, source_target_pairs={{0,8},{4,12},{8,0},{12,4},{16,24},{20,28},{24,16},{28,20},{32,96},... | collective-permute-start | bytes 786440 | tf_op jit(solution)/shard_map/ppermute | solution.py:230
  14.5 7.6 %collective-permute-start.12 = (bf16[1040,128]{1,0:T(8,128)(2,1)S(1)}, bf16[1040,128]{1,0:T(8,128)(2,1)S(1)}, u32[]{:S(2)}, u32[]{:S(2)}) collective-permute-start(bf16[1040,128]{1,0:T(8,128)(2,1)S(1)} %collective-permute-done.10.refs_9_), channel_id=1, source_target_pairs={{0,3},{1,2},{2,1},{3,0},{32,33},{33,32},{34,35},{35,34},{4,7},{5,6... | collective-permute-start | bytes 798728 | tf_op jit(solution)/shard_map/ppermute | solution.py:52
  17.0 4.8 %collective-permute-start.6 = (bf16[4,256,128]{2,1,0:T(8,128)(2,1)S(1)}, bf16[4,256,128]{2,1,0:T(8,128)(2,1)S(1)}, u32[]{:S(2)}, u32[]{:S(2)}) collective-permute-start(bf16[4,256,128]{2,1,0:T(8,128)(2,1)S(1)} %pad_maximum_fusion.1.refs_0_), channel_id=1, source_target_pairs={{0,32},{32,0},{1,33},{33,1},{2,34},{34,2},{3,35},{35,3},{4,36},{36... | collective-permute-start | bytes 786440 | tf_op jit(solution)/shard_map/ppermute | solution.py:43
  19.9 2.2 %collective-permute-start.9 = (bf16[4,256,128]{2,1,0:T(8,128)(2,1)S(1)}, bf16[4,256,128]{2,1,0:T(8,128)(2,1)S(1)}, u32[]{:S(2)}, u32[]{:S(2)}) collective-permute-start(bf16[4,256,128]{2,1,0:T(8,128)(2,1)S(1)} %collective-permute-done.5.refs_3_), channel_id=1, source_target_pairs={{0,32},{32,0},{1,33},{33,1},{2,34},{34,2},{3,35},{35,3},{4,36},{36... | collective-permute-start | bytes 786440 | tf_op jit(solution)/shard_map/ppermute | solution.py:43
  21.1 1.5 %collective-permute-start.8 = (bf16[4,256,128]{2,1,0:T(8,128)(2,1)S(1)}, bf16[4,256,128]{2,1,0:T(8,128)(2,1)S(1)}, u32[]{:S(2)}, u32[]{:S(2)}) collective-permute-start(bf16[4,256,128]{2,1,0:T(8,128)(2,1)S(1)} %collective-permute-done.4.refs_2_), channel_id=1, source_target_pairs={{0,32},{32,0},{1,33},{33,1},{2,34},{34,2},{3,35},{35,3},{4,36},{36... | collective-permute-start | bytes 786440 | tf_op jit(solution)/shard_map/ppermute | solution.py:43
  21.4 1.6 %collective-permute-start.7 = (bf16[4,256,128]{2,1,0:T(8,128)(2,1)S(1)}, bf16[4,256,128]{2,1,0:T(8,128)(2,1)S(1)}, u32[]{:S(2)}, u32[]{:S(2)}) collective-permute-start(bf16[4,256,128]{2,1,0:T(8,128)(2,1)S(1)} %collective-permute-done.3.refs_1_), channel_id=1, source_target_pairs={{0,32},{32,0},{1,33},{33,1},{2,34},{34,2},{3,35},{35,3},{4,36},{36... | collective-permute-start | bytes 786440 | tf_op jit(solution)/shard_map/ppermute | solution.py:43

commit v16 on v15

--- a/solution.py
+++ b/solution.py
@@ -218,16 +218,21 @@
     )(received)
 
 
+def in_order(send):
+    sent = {k: send(k) for k in (1, 3, 2)}
+    return [sent[k] for k in (1, 2, 3)]
+
+
 def per_device(queries, passages, lengths):
     own = queries.reshape(256, 128)
     info = jnp.stack([lax.axis_index(name) for name in ("z", "yhi", "core", "x")]).astype(jnp.int32)
 
-    near = [own] + [lax.ppermute(own, PLANE, along(True, k)) for k in range(1, 4)]
+    near = [own] + in_order(lambda k: lax.ppermute(own, PLANE, along(True, k)))
     filled = with_lengths(passages, lengths)
     once = on_x(filled, 1, 3)
     moved = [filled, once, on_x(filled, 3, 1), on_x(once, 3, 1)]
     block = jnp.stack(near)
-    mine = [block] + [lax.ppermute(block, PLANE, along(False, k)) for k in range(1, 4)]
+    mine = [block] + in_order(lambda k: lax.ppermute(block, PLANE, along(False, k)))
     other = [to_core(v) for v in mine]
     terms = score(info, mine + other, moved)
     received = lax.all_to_all(terms, ("z", "yhi"), 0, 0, tiled=True)

time: 55.2 us -> 55.7 us (level); the launches traced: 54.9 us -> 56.2 us
  blocking collectives: 13.5 us -> 16 us
  Pallas kernels: 18.4 us -> 17.2 us
    all_to_all x1, blocking collectives: 13.5 us -> 16 us  [per_device(): received = lax.all_to_all(terms, ('z', 'yhi'), 0, 0, tiled=True)]
    pallas_call x1, Pallas kernels: 16.9 us -> 15.7 us  [score(): pl.pallas_call(score_kernel, out_shape=jax.ShapeDtypeStruct((8, 8, 128),...]
where the time goes in v16:
time: 55.7 us; the launch traced here: 56.2 us
  Pallas kernels  17.2 us (31%)
  blocking collectives  16 us (29%)
  starting transfers between devices  15 us (27%)
  waiting for transfers between devices  6.82 us (12%)
  other arithmetic  1.12 us (2%)
    all_to_all x1, blocking collectives, per_device(): received = lax.all_to_all(terms, ('z', 'yhi'), 0, 0, tiled=True)  16 us
    pallas_call x1, Pallas kernels, score(): pl.pallas_call(score_kernel, out_shape=jax.ShapeDtypeStruct((8, 8, 128),...  15.7 us
    ppermute x3, starting transfers between devices, on_x(): return lax.ppermute(v, ('core', 'x'), pairs)  5.63 us
    ppermute x3, starting transfers between devices, per_device(): lax.ppermute(block, PLANE, along(False, k))  5.07 us
    ppermute x3, waiting for transfers between devices, per_device(): lax.ppermute(block, PLANE, along(False, k))  4.42 us
    ppermute x3, starting transfers between devices, per_device(): near = [own] + in_order(lambda k: lax.ppermute(own, PLANE, along(True, k)))  4.09 us
    pallas_call x1, Pallas kernels, place(): pl.pallas_call(place_kernel, out_shape=jax.ShapeDtypeStruct((32, 256), jn...  1.46 us
  transfers between devices with their start and end apart: 13, of which 8 were waited for; matrix products, arithmetic and copies ran while one was open for 2% of the time, Pallas kernels for 0%

profile of v16, /device:TPU:0, one launch (start us, length us, event | category | flops | bytes accessed | tf_op | source)
XLA Modules:
  0.0 56.2 jit_solution(11328992717632262373)
XLA Ops:
  0.0 0.0 copy-start.1
  0.0 3.1 %collective-permute-start.2 = (bf16[256,128]{1,0:T(8,128)(2,1)}, bf16[256,128]{1,0:T(8,128)(2,1)S(1)}, u32[]{:S(2)}, u32[]{:S(2)}) collective-permute-start(bf16[256,128]{1,0:T(8,128)(2,1)} %bitcast.11), channel_id=1, source_target_pairs={{0,68},{4,64},{8,76},{12,72},{16,84},{20,80},{24,92},{28,88},{32,5... | collective-permute-start | bytes 196616 | tf_op jit(solution)/shard_map/ppermute | solution.py:230
  3.1 0.6 %collective-permute-start.1 = (bf16[256,128]{1,0:T(8,128)(2,1)}, bf16[256,128]{1,0:T(8,128)(2,1)S(1)}, u32[]{:S(2)}, u32[]{:S(2)}) collective-permute-start(bf16[256,128]{1,0:T(8,128)(2,1)} %bitcast.12), channel_id=1, source_target_pairs={{0,4},{4,0},{8,12},{12,8},{16,20},{20,16},{24,28},{28,24},{32,48},... | collective-permute-start | bytes 196616 | tf_op jit(solution)/shard_map/ppermute | solution.py:230
  3.7 0.4 collective-permute-start
  4.1 0.0 copy-done.1
  4.1 0.0 copy-start
  4.1 1.0 %pad_maximum_fusion.refs_8_ = bf16[1040,128]{1,0:T(8,128)(2,1)S(1)} fusion(bf16[16,128]{1,0:T(8,128)(2,1)S(1)} %broadcast_in_dim.3, bf16[1024,128]{1,0:T(8,128)(2,1)} %bitcast.10), kind=kLoop, calls=%fused_computation | loop fusion | flops 532480 | bytes 532480 | tf_op jit(solution)/shard_map/concatenate | solution.py:57
  5.1 2.9 %collective-permute-start.11 = (bf16[1040,128]{1,0:T(8,128)(2,1)S(1)}, bf16[1040,128]{1,0:T(8,128)(2,1)S(1)}, u32[]{:S(2)}, u32[]{:S(2)}) collective-permute-start(bf16[1040,128]{1,0:T(8,128)(2,1)S(1)} %pad_maximum_fusion.refs_8_), channel_id=1, source_target_pairs={{0,3},{1,2},{2,1},{3,0},{32,33},{33,32},{34,35},{35,34},{4,7},{5,6... | collective-permute-start | bytes 798728 | tf_op jit(solution)/shard_map/ppermute | solution.py:52
  8.1 0.2 collective-permute-start.10
  8.3 0.0 collective-permute-done.2
  8.3 0.8 %collective-permute-done.1 = bf16[256,128]{1,0:T(8,128)(2,1)S(1)} collective-permute-done((bf16[256,128]{1,0:T(8,128)(2,1)}, bf16[256,128]{1,0:T(8,128)(2,1)S(1)}, u32[]{:S(2)}, u32[]{:S(2)}) %collective-permute-start.1) | collective-permute-done | bytes 65568 | tf_op jit(solution)/shard_map/ppermute | solution.py:230
  9.1 0.0 collective-permute-done
  9.1 0.0 copy-done
  9.1 4.1 %collective-permute-start.5 = (bf16[4,256,128]{2,1,0:T(8,128)(2,1)S(1)}, bf16[4,256,128]{2,1,0:T(8,128)(2,1)S(1)}, u32[]{:S(2)}, u32[]{:S(2)}) collective-permute-start(bf16[4,256,128]{2,1,0:T(8,128)(2,1)S(1)} %pad_maximum_fusion.1.refs_0_), channel_id=1, source_target_pairs={{0,24},{4,28},{8,16},{12,20},{16,8},{20,12},{24,0},{28,4},{32,100}... | collective-permute-start | bytes 786440 | tf_op jit(solution)/shard_map/ppermute | solution.py:235
  13.2 0.0 collective-permute-start.4
  13.2 0.9 %collective-permute-start.3 = (bf16[4,256,128]{2,1,0:T(8,128)(2,1)S(1)}, bf16[4,256,128]{2,1,0:T(8,128)(2,1)S(1)}, u32[]{:S(2)}, u32[]{:S(2)}) collective-permute-start(bf16[4,256,128]{2,1,0:T(8,128)(2,1)S(1)} %pad_maximum_fusion.1.refs_0_), channel_id=1, source_target_pairs={{0,8},{4,12},{8,0},{12,4},{16,24},{20,28},{24,16},{28,20},{32,96},... | collective-permute-start | bytes 786440 | tf_op jit(solution)/shard_map/ppermute | solution.py:235
  14.2 0.3 collective-permute-done.10.refs_9_
  14.5 2.5 %collective-permute-start.12 = (bf16[1040,128]{1,0:T(8,128)(2,1)S(1)}, bf16[1040,128]{1,0:T(8,128)(2,1)S(1)}, u32[]{:S(2)}, u32[]{:S(2)}) collective-permute-start(bf16[1040,128]{1,0:T(8,128)(2,1)S(1)} %collective-permute-done.10.refs_9_), channel_id=1, source_target_pairs={{0,3},{1,2},{2,1},{3,0},{32,33},{33,32},{34,35},{35,34},{4,7},{5,6... | collective-permute-start | bytes 798728 | tf_op jit(solution)/shard_map/ppermute | solution.py:52
  17.0 0.0 collective-permute-done.11.refs_10_
  17.0 0.0 collective-permute-start.6
  17.0 3.0 %collective-permute-done.5.refs_3_ = bf16[4,256,128]{2,1,0:T(8,128)(2,1)S(1)} collective-permute-done((bf16[4,256,128]{2,1,0:T(8,128)(2,1)S(1)}, bf16[4,256,128]{2,1,0:T(8,128)(2,1)S(1)}, u32[]{:S(2)}, u32[]{:S(2)}) %collective-permute-start.5) | collective-permute-done | bytes 262176 | tf_op jit(solution)/shard_map/ppermute | solution.py:235
  19.9 0.0 collective-permute-start.9
  19.9 1.2 %collective-permute-done.4.refs_2_ = bf16[4,256,128]{2,1,0:T(8,128)(2,1)S(1)} collective-permute-done((bf16[4,256,128]{2,1,0:T(8,128)(2,1)S(1)}, bf16[4,256,128]{2,1,0:T(8,128)(2,1)S(1)}, u32[]{:S(2)}, u32[]{:S(2)}) %collective-permute-start.4) | collective-permute-done | bytes 262176 | tf_op jit(solution)/shard_map/ppermute | solution.py:235
  21.1 0.0 collective-permute-start.8
  21.1 0.3 collective-permute-done.3.refs_1_
  21.4 0.2 collective-permute-start.7
  21.6 0.1 pad_add_fusion.info_ref
  21.7 0.0 collective-permute-done.6.refs_4_
  21.7 0.4 collective-permute-done.12.refs_11_
  22.1 0.0 collective-permute-done.9.refs_7_
  22.1 0.5 collective-permute-done.8.refs_6_
  22.7 0.4 collective-permute-done.7.refs_5_
  23.0 15.7 %shard_map.37 = f32[8,8,128]{2,1,0:T(8,128)S(1)} custom-call(s32[4]{0:T(128)S(1)} %pad_add_fusion.info_ref, bf16[4,256,128]{2,1,0:T(8,128)(2,1)S(1)} %pad_maximum_fusion.1.refs_0_, bf16[4,256,128]{2,1,0:T(8,128)(2,1)S(1)} %collective-permute-done.3.refs_1_, bf16[4,256,128]{2,1,0:T(8,128)(2,1)S(1)} %collective-permute-done.4.refs_2_, ...), custom_call_target="tpu_custom_call" | custom-call | tf_op jit(solution)/shard_map/pallas_call | solution.py:189
  38.7 16.0 %all_to_all.5.r_ref = f32[8,8,128]{2,1,0:T(8,128)} all-to-all(f32[8,8,128]{2,1,0:T(8,128)S(1)} %shard_map.37), channel_id=1, replica_groups=mesh['ylo'=2,'core'=2,'z'=4,'yhi'=2,'x'=4] {'z','yhi'}, dimensions={0} | all-to-all | bytes 65536 | tf_op jit(solution)/shard_map/all_to_all | solution.py:238
  54.7 1.5 %shard_map.38 = f32[32,256]{1,0:T(8,128)} custom-call(f32[8,8,128]{2,1,0:T(8,128)} %all_to_all.5.r_ref), custom_call_target="tpu_custom_call" | custom-call | tf_op jit(solution)/shard_map/pallas_call | solution.py:213
  (4 shorter events, 0.1 us)
Async XLA Ops:
  0.0 4.1 %copy-start.1 = (s32[8]{0:T(128)S(1)}, s32[8]{0:T(128)}, u32[]{:S(2)}) copy-start(s32[8]{0:T(128)} %param.5) | copy-start | bytes 100
  0.0 8.3 %collective-permute-start.2 = (bf16[256,128]{1,0:T(8,128)(2,1)}, bf16[256,128]{1,0:T(8,128)(2,1)S(1)}, u32[]{:S(2)}, u32[]{:S(2)}) collective-permute-start(bf16[256,128]{1,0:T(8,128)(2,1)} %bitcast.11), channel_id=1, source_target_pairs={{0,68},{4,64},{8,76},{12,72},{16,84},{20,80},{24,92},{28,88},{32,5... | collective-permute-start | bytes 196616 | tf_op jit(solution)/shard_map/ppermute | solution.py:230
  3.1 6.0 %collective-permute-start.1 = (bf16[256,128]{1,0:T(8,128)(2,1)}, bf16[256,128]{1,0:T(8,128)(2,1)S(1)}, u32[]{:S(2)}, u32[]{:S(2)}) collective-permute-start(bf16[256,128]{1,0:T(8,128)(2,1)} %bitcast.12), channel_id=1, source_target_pairs={{0,4},{4,0},{8,12},{12,8},{16,20},{20,16},{24,28},{28,24},{32,48},... | collective-permute-start | bytes 196616 | tf_op jit(solution)/shard_map/ppermute | solution.py:230
  3.7 5.4 %collective-permute-start = (bf16[256,128]{1,0:T(8,128)(2,1)}, bf16[256,128]{1,0:T(8,128)(2,1)S(1)}, u32[]{:S(2)}, u32[]{:S(2)}) collective-permute-start(bf16[256,128]{1,0:T(8,128)(2,1)} %bitcast.13), channel_id=1, source_target_pairs={{0,64},{4,68},{8,72},{12,76},{16,80},{20,84},{24,88},{28,92},{32,4... | collective-permute-start | bytes 196616 | tf_op jit(solution)/shard_map/ppermute | solution.py:230
  4.1 5.0 %copy-start = (bf16[32,8,128]{2,1,0:T(8,128)(2,1)S(1)}, bf16[32,8,128]{2,1,0:T(8,128)(2,1)}, u32[]{:S(2)}) copy-start(bf16[32,8,128]{2,1,0:T(8,128)(2,1)} %param.3) | copy-start | bytes 196612
  5.1 11.8 %collective-permute-start.11 = (bf16[1040,128]{1,0:T(8,128)(2,1)S(1)}, bf16[1040,128]{1,0:T(8,128)(2,1)S(1)}, u32[]{:S(2)}, u32[]{:S(2)}) collective-permute-start(bf16[1040,128]{1,0:T(8,128)(2,1)S(1)} %pad_maximum_fusion.refs_8_), channel_id=1, source_target_pairs={{0,3},{1,2},{2,1},{3,0},{32,33},{33,32},{34,35},{35,34},{4,7},{5,6... | collective-permute-start | bytes 798728 | tf_op jit(solution)/shard_map/ppermute | solution.py:52
  8.1 6.4 %collective-permute-start.10 = (bf16[1040,128]{1,0:T(8,128)(2,1)S(1)}, bf16[1040,128]{1,0:T(8,128)(2,1)S(1)}, u32[]{:S(2)}, u32[]{:S(2)}) collective-permute-start(bf16[1040,128]{1,0:T(8,128)(2,1)S(1)} %pad_maximum_fusion.refs_8_), channel_id=1, source_target_pairs={{0,1},{1,0},{2,3},{3,2},{32,35},{33,34},{34,33},{35,32},{4,5},{5,4... | collective-permute-start | bytes 798728 | tf_op jit(solution)/shard_map/ppermute | solution.py:52
  9.1 10.8 %collective-permute-start.5 = (bf16[4,256,128]{2,1,0:T(8,128)(2,1)S(1)}, bf16[4,256,128]{2,1,0:T(8,128)(2,1)S(1)}, u32[]{:S(2)}, u32[]{:S(2)}) collective-permute-start(bf16[4,256,128]{2,1,0:T(8,128)(2,1)S(1)} %pad_maximum_fusion.1.refs_0_), channel_id=1, source_target_pairs={{0,24},{4,28},{8,16},{12,20},{16,8},{20,12},{24,0},{28,4},{32,100}... | collective-permute-start | bytes 786440 | tf_op jit(solution)/shard_map/ppermute | solution.py:235
  13.2 7.9 %collective-permute-start.4 = (bf16[4,256,128]{2,1,0:T(8,128)(2,1)S(1)}, bf16[4,256,128]{2,1,0:T(8,128)(2,1)S(1)}, u32[]{:S(2)}, u32[]{:S(2)}) collective-permute-start(bf16[4,256,128]{2,1,0:T(8,128)(2,1)S(1)} %pad_maximum_fusion.1.refs_0_), channel_id=1, source_target_pairs={{0,16},{4,20},{8,24},{12,28},{16,0},{20,4},{24,8},{28,12},{32,36},... | collective-permute-start | bytes 786440 | tf_op jit(solution)/shard_map/ppermute | solution.py:235
  13.2 8.1 %collective-permute-start.3 = (bf16[4,256,128]{2,1,0:T(8,128)(2,1)S(1)}, bf16[4,256,128]{2,1,0:T(8,128)(2,1)S(1)}, u32[]{:S(2)}, u32[]{:S(2)}) collective-permute-start(bf16[4,256,128]{2,1,0:T(8,128)(2,1)S(1)} %pad_maximum_fusion.1.refs_0_), channel_id=1, source_target_pairs={{0,8},{4,12},{8,0},{12,4},{16,24},{20,28},{24,16},{28,20},{32,96},... | collective-permute-start | bytes 786440 | tf_op jit(solution)/shard_map/ppermute | solution.py:235
  14.5 7.6 %collective-permute-start.12 = (bf16[1040,128]{1,0:T(8,128)(2,1)S(1)}, bf16[1040,128]{1,0:T(8,128)(2,1)S(1)}, u32[]{:S(2)}, u32[]{:S(2)}) collective-permute-start(bf16[1040,128]{1,0:T(8,128)(2,1)S(1)} %collective-permute-done.10.refs_9_), channel_id=1, source_target_pairs={{0,3},{1,2},{2,1},{3,0},{32,33},{33,32},{34,35},{35,34},{4,7},{5,6... | collective-permute-start | bytes 798728 | tf_op jit(solution)/shard_map/ppermute | solution.py:52
  17.0 4.8 %collective-permute-start.6 = (bf16[4,256,128]{2,1,0:T(8,128)(2,1)S(1)}, bf16[4,256,128]{2,1,0:T(8,128)(2,1)S(1)}, u32[]{:S(2)}, u32[]{:S(2)}) collective-permute-start(bf16[4,256,128]{2,1,0:T(8,128)(2,1)S(1)} %pad_maximum_fusion.1.refs_0_), channel_id=1, source_target_pairs={{0,32},{32,0},{1,33},{33,1},{2,34},{34,2},{3,35},{35,3},{4,36},{36... | collective-permute-start | bytes 786440 | tf_op jit(solution)/shard_map/ppermute | solution.py:43
  19.9 2.2 %collective-permute-start.9 = (bf16[4,256,128]{2,1,0:T(8,128)(2,1)S(1)}, bf16[4,256,128]{2,1,0:T(8,128)(2,1)S(1)}, u32[]{:S(2)}, u32[]{:S(2)}) collective-permute-start(bf16[4,256,128]{2,1,0:T(8,128)(2,1)S(1)} %collective-permute-done.5.refs_3_), channel_id=1, source_target_pairs={{0,32},{32,0},{1,33},{33,1},{2,34},{34,2},{3,35},{35,3},{4,36},{36... | collective-permute-start | bytes 786440 | tf_op jit(solution)/shard_map/ppermute | solution.py:43
  21.1 1.5 %collective-permute-start.8 = (bf16[4,256,128]{2,1,0:T(8,128)(2,1)S(1)}, bf16[4,256,128]{2,1,0:T(8,128)(2,1)S(1)}, u32[]{:S(2)}, u32[]{:S(2)}) collective-permute-start(bf16[4,256,128]{2,1,0:T(8,128)(2,1)S(1)} %collective-permute-done.4.refs_2_), channel_id=1, source_target_pairs={{0,32},{32,0},{1,33},{33,1},{2,34},{34,2},{3,35},{35,3},{4,36},{36... | collective-permute-start | bytes 786440 | tf_op jit(solution)/shard_map/ppermute | solution.py:43
  21.4 1.6 %collective-permute-start.7 = (bf16[4,256,128]{2,1,0:T(8,128)(2,1)S(1)}, bf16[4,256,128]{2,1,0:T(8,128)(2,1)S(1)}, u32[]{:S(2)}, u32[]{:S(2)}) collective-permute-start(bf16[4,256,128]{2,1,0:T(8,128)(2,1)S(1)} %collective-permute-done.3.refs_1_), channel_id=1, source_target_pairs={{0,32},{32,0},{1,33},{33,1},{2,34},{34,2},{3,35},{35,3},{4,36},{36... | collective-permute-start | bytes 786440 | tf_op jit(solution)/shard_map/ppermute | solution.py:43
